TPU v7x, 128 devices: a whole 4x4x4 slice. The times are simulated.
128 devices in a mesh: section: 8 (over x_lo, z), fsdp: 16 (over x_hi, y, core).
Axes of the slice: x: 4 (x_hi: 2, x_lo: 2; x = x_hi * 2 + x_lo), y: 4, z: 4, core: 2. Of those that a mesh axis runs over, the one named last changes fastest.
Arguments:
- section_inputs: bfloat16 [2, 8, 4096, 7168], P(None, 'section', 'fsdp'), may hold values from -15 to 15
- value_cotangent: bfloat16 [2, 8, 4096, 512], P(None, 'section', 'fsdp'), may hold values from -6 to 6
- down_weight: bfloat16 [8, 7168, 512], P('section', 'fsdp'), may hold values from -0.0625 to 0.0625
- up_weight: bfloat16 [8, 7168, 512], P('section', 'fsdp'), may hold values from -0.0625 to 0.0625
- down_gain: bfloat16 [8, 7168], P('section'), may hold values from 0.099609375 to 1.8984375
- up_gain: bfloat16 [8, 7168], P('section'), may hold values from 0.099609375 to 1.8984375
- image_rows: bfloat16 [2, 1024, 7168], P(None, 'fsdp'), may hold values from -15 to 15
- image_route: int32 [2, 16, 16], replicated, may hold values from 0 to 15, as said below
Outputs:
- values: bfloat16 [2, 8, 4096, 512], P(None, 'section', 'fsdp')
- input_grad: bfloat16 [2, 8, 4096, 7168], P(None, 'section', 'fsdp')
- weight_grad: float32 [8, 7168, 512], P('section', 'fsdp')
- gain_grad: float32 [8, 7168], P('section', 'fsdp')
Inputs may be any that keep to these rules, and one draw needn't show every extreme that they name: `image_route`: one fsdp index sends at most 2 blocks of a pipe to any one index, and in each pipe some index takes 2 blocks from every index.
All inputs are finite; a program needn't handle non-finite values.
Results may differ from a plain program's by a relative error of at most 0.03.
Values may be sent and summed in bfloat16 or wider, within the bound.
No kernel may reach another device: no remote copies, remote signals or barrier semaphores. Data moves between devices by JAX's collectives and lax.ppermute only.
A program may use at most 192 MiB of HBM per device.

v0:
```python
import jax
import jax.numpy as jnp
from jax import lax
from jax.experimental import pallas as pl
from jax.experimental.pallas import tpu as pltpu
from jax.sharding import PartitionSpec as P

BLOCK_ROWS = 4
CAP = 2
EPSILON = 1e-05
TOKENS = 256
HEAD = 128
VMEM_BYTES = 60 * 1024 * 1024
F32 = jnp.float32
BF16 = jnp.bfloat16

X_CHIPS, Y_CHIPS = 2, 4
CHIPS = X_CHIPS * Y_CHIPS
CORE, LIVE, FLAG, PART, PIPE = 8, 9, 10, 12, 15


def fsdp_route(step):
    route = []
    for x in range(X_CHIPS):
        for y in range(Y_CHIPS):
            for core in range(2):
                to_x, to_y, to_core = step(x, y, core)
                target = (to_x % X_CHIPS * Y_CHIPS + to_y % Y_CHIPS) * 2 + to_core % 2
                route.append(((x * Y_CHIPS + y) * 2 + core, target))
    return route


def to_next(block):
    return lax.ppermute(block, "fsdp", fsdp_route(lambda x, y, core: (x, y + 1, core)))


def to_previous(block):
    return lax.ppermute(block, "fsdp", fsdp_route(lambda x, y, core: (x, y - 1, core)))


def to_across(block):
    return lax.ppermute(block, "fsdp", fsdp_route(lambda x, y, core: (x + 1, y, core)))


def to_sibling(block):
    return lax.ppermute(block, "fsdp", fsdp_route(lambda x, y, core: (x, y, core + 1)))


def to_mirror(block):
    count = lax.axis_size("section")
    return lax.ppermute(block, "section", [(s, count - 1 - s) for s in range(count)])


def columns(chip, size):
    return pl.ds(pl.multiple_of(chip * size, 128), size)


def prepare_kernel(table, x_ref, ct_ref, perm_ref, im0, im1, im2, head_ref, ct_out, inverse_out, rows):
    pipe, step = pl.program_id(0), pl.program_id(1)
    _, _, tokens, width = x_ref.shape
    pair = width // CHIPS
    rows[...] = x_ref[0, 0]

    @pl.when((table[FLAG + pipe] == 1) & (step * tokens < table[LIVE]))
    def _():
        row = lax.broadcasted_iota(jnp.int32, (tokens, 1), 0) + step * tokens
        live = row < table[LIVE]
        for part, image in enumerate((im0, im1, im2)):
            where = pl.ds(pl.multiple_of(table[PART + part], 128), image.shape[1])
            arrived = jnp.dot(perm_ref[...], image[...], preferred_element_type=F32).astype(BF16)
            rows[:, where] = jnp.where(live, arrived, rows[:, where])

    @pl.when((table[PIPE] == pipe) & (step * tokens < head_ref.shape[0]))
    def _():
        head_ref[pl.ds(pl.multiple_of(step * tokens, tokens), tokens)] = rows[...]

    total = jnp.zeros((tokens, 1), F32)
    for chip in range(CHIPS):
        part = rows[:, chip * pair : (chip + 1) * pair].astype(F32)
        total = total + jnp.sum(part * part, axis=1, keepdims=True)
    inverse = lax.rsqrt(total / width + EPSILON)
    ct_out[0, 0] = (ct_ref[0, 0].astype(F32) * inverse).astype(BF16)
    inverse_out[0] = jnp.broadcast_to(inverse, inverse_out.shape[1:])


def prepare(table, section_inputs, cotangent, perm, images):
    pipes, _, tokens, width = section_inputs.shape
    kv = cotangent.shape[3]
    tile = 64
    ct_spec = pl.BlockSpec((1, 1, tile, kv), lambda p, t: (p, 0, t, 0))
    whole = pl.BlockSpec(memory_space=pltpu.VMEM)
    return pl.pallas_call(
        prepare_kernel,
        grid=(pipes, tokens // tile),
        in_specs=[
            pl.BlockSpec(memory_space=pltpu.SMEM),
            pl.BlockSpec((1, 1, tile, width), lambda p, t: (p, 0, t, 0)),
            ct_spec,
            pl.BlockSpec((tile, perm.shape[1]), lambda p, t: (t, 0)),
            whole,
            whole,
            whole,
        ],
        out_specs=[
            pl.BlockSpec((HEAD, width), lambda p, t: (0, 0)),
            ct_spec,
            pl.BlockSpec((1, tile, 128), lambda p, t: (p, t, 0)),
        ],
        out_shape=[
            jax.ShapeDtypeStruct((HEAD, width), BF16),
            jax.ShapeDtypeStruct(cotangent.shape, BF16),
            jax.ShapeDtypeStruct((pipes, tokens, 128), F32),
        ],
        scratch_shapes=[pltpu.VMEM((tile, width), BF16)],
        compiler_params=pltpu.CompilerParams(vmem_limit_bytes=VMEM_BYTES),
        cost_estimate=pl.CostEstimate(
            flops=8 * pipes * tokens * width, bytes_accessed=12_000_000, transcendentals=0
        ),
        name="prepare",
    )(table, section_inputs, cotangent, perm, *images)


def start_rows(table, pipe, x_ref, head_ref, rows, sems, chip):
    pair = rows.shape[1] // CHIPS
    where = columns(chip, pair)
    tail = rows.shape[0] - HEAD
    flag = table[FLAG + pipe] == 1
    top = rows.at[pl.ds(0, HEAD), where]
    plain = pltpu.make_async_copy(x_ref.at[pipe, 0, pl.ds(0, HEAD), where], top, sems.at[0])
    placed = pltpu.make_async_copy(head_ref.at[:, where], top, sems.at[0])
    rest = pltpu.make_async_copy(
        x_ref.at[pipe, 0, pl.ds(HEAD, tail), where], rows.at[pl.ds(HEAD, tail), where], sems.at[1]
    )

    @pl.when(flag)
    def _():
        placed.start()

    @pl.when(jnp.logical_not(flag))
    def _():
        plain.start()

    rest.start()
    return plain, rest


def products(pipe, table, x, sibling_x, head, sibling_head, ct, sibling_ct, groups):
    _, _, tokens, width = x.shape
    pair = width // CHIPS
    half = pair // 2
    kv = ct.shape[3]
    place = {r: (g, i) for g, group in enumerate(groups) for i, r in enumerate(group)}
    order = [r for group in groups for r in group]

    def kernel(table, x_ref, sibling_x_ref, head_ref, sibling_head_ref, own_ct, other_ct, *refs):
        outs = refs[: len(groups)]
        own, other, sems = refs[len(groups) :]
        waits = {}
        for r in order:
            waits[r] = start_rows(table, pipe, x_ref, head_ref, own, sems.at[r, 0], table[r])
            waits[r] += start_rows(
                table, pipe, sibling_x_ref, sibling_head_ref, other, sems.at[r, 1], table[r]
            )
        contract = (((0,), (0,)), ((), ()))

        def block(r, low):
            where = columns(table[r], pair)
            product = lax.dot_general(
                own[:, where][:, low : low + half], own_ct[0, 0], contract, preferred_element_type=F32
            )
            product += lax.dot_general(
                other[:, where][:, low : low + half], other_ct[0, 0], contract, preferred_element_type=F32
            )
            out, at = place[r]
            outs[out][at] = product.astype(BF16)

        for r in order:
            for copy in waits[r]:
                copy.wait()
            pl.when(table[CORE] == 0)(lambda: block(r, 0))
            pl.when(table[CORE] == 1)(lambda: block(r, half))

    anywhere = pl.BlockSpec(memory_space=pl.ANY)
    ct_spec = pl.BlockSpec((1, 1, tokens, kv), lambda i: (pipe, 0, 0, 0))
    return pl.pallas_call(
        kernel,
        grid=(1,),
        in_specs=[pl.BlockSpec(memory_space=pltpu.SMEM)] + [anywhere] * 4 + [ct_spec] * 2,
        out_specs=[pl.BlockSpec((len(g), half, kv), lambda i: (0, 0, 0)) for g in groups],
        out_shape=[jax.ShapeDtypeStruct((len(g), half, kv), BF16) for g in groups],
        scratch_shapes=[
            pltpu.VMEM((tokens, width), BF16),
            pltpu.VMEM((tokens, width), BF16),
            pltpu.SemaphoreType.DMA((CHIPS, 2, 2)),
        ],
        compiler_params=pltpu.CompilerParams(vmem_limit_bytes=VMEM_BYTES),
        cost_estimate=pl.CostEstimate(
            flops=4 * tokens * width * kv, bytes_accessed=12_000_000, transcendentals=0
        ),
        name="products",
    )(table, x, sibling_x, head, sibling_head, ct, sibling_ct)


def layer(pipe, table, x, head, cotangent, scaled_ct, inverse, gain, own, sibling, carried):
    _, _, tokens, width = x.shape
    pair = width // CHIPS
    half = pair // 2
    kv = cotangent.shape[3]
    arrays = []
    for array, _ in [*own, *sibling]:
        if not any(array is known for known in arrays):
            arrays.append(array)
    position = [
        next(i for i, known in enumerate(arrays) if known is array) for array, _ in [*own, *sibling]
    ]
    index = [at for _, at in [*own, *sibling]]

    def kernel(table, x_ref, head_ref, ct_ref, scaled_ref, inverse_ref, gain_ref, *refs):
        pieces = refs[: len(arrays)]
        values_ref, grad_ref, rows, weight, grad, w_sems, x_sems, out_sems = refs[-8:]
        core = table[CORE]
        waits = []
        for r in range(CHIPS):
            copies = []
            for side in range(2):
                piece = side * CHIPS + r
                source = pieces[position[piece]]
                if index[piece] is not None:
                    source = source.at[index[piece]]
                at = table[r] * pair + (core if side == 0 else 1 - core) * half
                copy = pltpu.make_async_copy(
                    source, weight.at[pl.ds(pl.multiple_of(at, 64), half)], w_sems.at[piece]
                )
                copy.start()
                copies.append(copy)
            waits.append(copies + list(start_rows(table, pipe, x_ref, head_ref, rows, x_sems.at[r], table[r])))
        values = jnp.zeros((tokens, kv), F32)
        for r in range(CHIPS):
            for copy in waits[r]:
                copy.wait()
            where = columns(table[r], pair)
            block = weight[pl.ds(pl.multiple_of(table[r] * pair, 128), pair)]
            values += jnp.dot(rows[:, where] * gain_ref[:, where], block, preferred_element_type=F32)
        inv = inverse_ref[0, :, :1]
        values = values * inv
        values_ref[0, 0] = values.astype(BF16)
        centre = jnp.sum(values * ct_ref[0, 0].astype(F32), axis=1, keepdims=True) / width
        pull = inv * inv * centre
        outs = []
        for chip in range(CHIPS):
            where = slice(chip * pair, (chip + 1) * pair)
            back = lax.dot_general(
                scaled_ref[0, 0], weight[where], (((1,), (1,)), ((), ())), preferred_element_type=F32
            )
            grad[:, where] = (
                back * gain_ref[:, where].astype(F32) - rows[:, where].astype(F32) * pull
            ).astype(BF16)
            copy = pltpu.make_async_copy(
                grad.at[:, pl.ds(chip * pair, pair)],
                grad_ref.at[pipe, 0, :, pl.ds(chip * pair, pair)],
                out_sems.at[chip],
            )
            copy.start()
            outs.append(copy)
        for copy in outs:
            copy.wait()

    anywhere = pl.BlockSpec(memory_space=pl.ANY)
    ct_spec = pl.BlockSpec((1, 1, tokens, kv), lambda i: (pipe, 0, 0, 0))
    operands = [table, x, head, cotangent, scaled_ct, inverse, gain, *arrays, *carried]
    return pl.pallas_call(
        kernel,
        grid=(1,),
        in_specs=[
            pl.BlockSpec(memory_space=pltpu.SMEM),
            anywhere,
            anywhere,
            ct_spec,
            ct_spec,
            pl.BlockSpec((1, tokens, 128), lambda i: (pipe, 0, 0)),
            pl.BlockSpec((1, width), lambda i: (0, 0)),
        ]
        + [anywhere] * (len(arrays) + len(carried)),
        out_specs=[ct_spec, anywhere],
        out_shape=[
            jax.ShapeDtypeStruct(cotangent.shape, BF16),
            jax.ShapeDtypeStruct(x.shape, BF16),
        ],
        scratch_shapes=[
            pltpu.VMEM((tokens, width), BF16),
            pltpu.VMEM((width, kv), BF16),
            pltpu.VMEM((tokens, width), BF16),
            pltpu.SemaphoreType.DMA((2 * CHIPS,)),
            pltpu.SemaphoreType.DMA((CHIPS, 2)),
            pltpu.SemaphoreType.DMA((CHIPS,)),
        ],
        input_output_aliases={7 + len(arrays) + i: i for i in range(len(carried))},
        compiler_params=pltpu.CompilerParams(vmem_limit_bytes=VMEM_BYTES),
        cost_estimate=pl.CostEstimate(
            flops=4 * tokens * width * kv, bytes_accessed=16_000_000, transcendentals=0
        ),
        name="layer",
    )(*operands)


def route_images(image_rows, image_route, section_place, fsdp_place):
    fsdp_count = lax.axis_size("fsdp")
    section_count = lax.axis_size("section")
    ring = section_count // 2
    width = image_rows.shape[2]
    size = -(-width // (3 * 128)) * 128
    pipe = section_place // ring
    z = section_place % ring
    enc_rows = image_rows.shape[1]
    enc_count = enc_rows // BLOCK_ROWS
    head = fsdp_count * CAP * BLOCK_ROWS
    routes = lax.dynamic_index_in_dim(image_route, pipe, 0, keepdims=False)
    own_route = lax.dynamic_index_in_dim(routes, fsdp_place, 0, keepdims=False)
    ids = jnp.arange(enc_count, dtype=jnp.int32)
    earlier = (own_route[:, None] == own_route[None, :]) & (ids[None, :] < ids[:, None])
    slot_of = own_route * CAP + jnp.sum(earlier.astype(jnp.int32), axis=1)
    goes_to = jnp.repeat(slot_of * BLOCK_ROWS, BLOCK_ROWS) + jnp.tile(
        jnp.arange(BLOCK_ROWS, dtype=jnp.int32), enc_count
    )
    row_ids = jnp.arange(head, dtype=jnp.int32)
    select = (row_ids[:, None] == goes_to[None, :]).astype(BF16)
    from_end = jnp.where(pipe == 0, z, ring - 1 - z)
    own_part = jnp.where(from_end == ring - 1, 2, jnp.minimum(from_end, 1))
    starts = jnp.array([0, size, width - size], jnp.int32)
    start = jnp.where(own_part == 0, 0, jnp.where(own_part == 1, size, width - size))
    part = lax.dynamic_slice(image_rows, (pipe, 0, start), (1, enc_rows, size))[0]
    outgoing = jnp.dot(select, part, preferred_element_type=F32).astype(BF16)
    incoming = lax.all_to_all(outgoing, "fsdp", split_axis=0, concat_axis=0, tiled=True)
    end = section_count - 1
    images = [
        incoming,
        lax.ppermute(incoming, "section", [(1, 0), (end - 1, end)]),
        lax.ppermute(incoming, "section", [(ring - 1, 0), (end - ring + 1, end)]),
    ]
    arrivals = jnp.sum((routes == fsdp_place).astype(jnp.int32), axis=1)
    offsets = jnp.cumsum(arrivals) - arrivals
    slot_rows = CAP * BLOCK_ROWS
    within = row_ids % slot_rows
    lands = jnp.repeat(offsets, slot_rows) * BLOCK_ROWS + within
    valid = within < jnp.repeat(arrivals, slot_rows) * BLOCK_ROWS
    lands = jnp.where(valid, lands, -1)
    perm = (jnp.arange(TOKENS, dtype=jnp.int32)[:, None] == lands[None, :]).astype(BF16)
    numbers = jnp.concatenate(
        [
            (jnp.sum(arrivals) * BLOCK_ROWS)[None],
            (section_place == 0).astype(jnp.int32)[None],
            (section_place == end).astype(jnp.int32)[None],
            starts,
            pipe[None],
        ]
    )
    return images, perm, numbers, outgoing


def hold(value, *before):
    return lax.optimization_barrier((value, before))[0]


def per_device(
    section_inputs,
    value_cotangent,
    down_weight,
    up_weight,
    down_gain,
    up_gain,
    image_rows,
    image_route,
):
    section_place = lax.axis_index("section")
    fsdp_place = lax.axis_index("fsdp")
    core = fsdp_place % 2
    y = fsdp_place // 2 % Y_CHIPS
    x = fsdp_place // (2 * Y_CHIPS)
    r = jnp.arange(CHIPS, dtype=jnp.int32)
    chips = (x ^ (r // Y_CHIPS)) * Y_CHIPS + (y + r % Y_CHIPS) % Y_CHIPS

    images, perm, numbers, outgoing = route_images(image_rows, image_route, section_place, fsdp_place)
    table = jnp.concatenate([chips, core[None], numbers]).astype(jnp.int32)

    w0 = jnp.stack([down_weight[0], up_weight[0]])
    w3, w1, w4 = to_next(w0), to_previous(w0), to_across(w0)
    sibling_x = to_sibling(section_inputs)
    moved = {id(w0): to_sibling(w0)}
    w2 = to_next(w3)
    up4 = w4[1]
    up5 = to_previous(up4)
    down57 = to_across(jnp.stack([w1[0], w3[0]]))
    round2 = (w2, up5, down57)
    up7 = to_next(hold(up4, round2))
    up6 = to_previous(up5)
    down6 = to_across(w2[0])
    for array in (w1, w3, w4):
        moved[id(array)] = to_sibling(hold(array, round2))
    for array in (w2, up5, down57, up7, up6, down6):
        moved[id(array)] = to_sibling(array)
    head, scaled_ct, inverse = prepare(
        hold(table, round2, sibling_x), section_inputs, value_cotangent, perm, images
    )
    sibling_head = to_sibling(head)
    sibling_ct = to_sibling(scaled_ct)
    down_own = [(w0, 0), (w1, 0), (w2, 0), (w3, 0), (w4, 0), (down57, 0), (down6, None), (down57, 1)]
    up_own = [(w0, 1), (w1, 1), (w2, 1), (w3, 1), (w4, 1), (up5, None), (up6, None), (up7, None)]
    down_sibling = [(moved[id(array)], at) for array, at in down_own]
    up_sibling = [(moved[id(array)], at) for array, at in up_own]

    up_groups = ((2, 5), (6, 3), (1,), (7,), (0, 4))
    down_groups = ((6,), (5, 7, 4), (2,), (1, 3), (0,))
    up_blocks = products(
        1, hold(table, up7, up6, down6, *moved.values()), section_inputs, sibling_x, head, sibling_head, scaled_ct, sibling_ct, up_groups
    )
    down_blocks = products(
        0, hold(table, up_blocks[0]), section_inputs, sibling_x, head, sibling_head, scaled_ct, sibling_ct, down_groups
    )

    far0_near1, far1_back0, near0, back1, own01 = up_blocks
    below1 = to_next(far0_near1)
    above0 = to_previous(far1_back0)
    send2, send130, keep2, keep13, keep0 = down_blocks
    half = keep2.shape[1] // 2
    came2, came130 = to_across(send2), to_across(send130)
    filled = layer(
        0,
        hold(table, down_blocks[0]),
        section_inputs, head, value_cotangent, scaled_ct, inverse, down_gain, down_own, down_sibling, (),
    )
    below1, above0, came2 = hold((below1, above0, came2), filled[0])
    up_near = near0[0] + below1[0]
    up_back = back1[0] + above0[0]
    down_far = keep2[0] + came2[0]
    down_below = to_next(down_far[:half])
    down_above = to_previous(down_far[half:])
    below0 = to_next(up_near)
    above1 = to_previous(up_back)

    values, input_grad = layer(
        1,
        hold(table, up_near, up_back, down_far),
        section_inputs, head, value_cotangent, scaled_ct, inverse, up_gain, up_own, up_sibling, tuple(filled),
    )
    below0, above1, down_below, down_above, came130 = hold(
        (below0, above1, down_below, down_above, came130), values
    )
    across = own01[1].astype(F32) + below1[1].astype(F32) + above1.astype(F32)
    kept = own01[0].astype(F32) + below0.astype(F32) + above0[1].astype(F32)
    across = to_across(across.astype(BF16))
    ups = keep13[0] + came130[0]
    downs = keep13[1] + came130[1]
    ups = jnp.concatenate([ups[:half] + down_below, ups[half:]])
    downs = jnp.concatenate([downs[:half], downs[half:] + down_above])
    below = to_next(ups)
    above = to_previous(downs)
    up_share = kept + across.astype(F32)
    down_share = keep0[0].astype(F32) + came130[2].astype(F32) + below.astype(F32) + above.astype(F32)

    shard = down_weight.shape[1]

    def gradients(weight, share, gain):
        part = lax.dynamic_slice(gain[0], (fsdp_place * shard,), (shard,)).astype(F32)
        return part[:, None] * share, jnp.sum(weight[0].astype(F32) * share, axis=1)

    up_weight_grad, up_gain_grad = gradients(up_weight, up_share, up_gain)
    down_weight_grad, down_gain_grad = gradients(down_weight, down_share, down_gain)
    moved_weight = to_mirror(up_weight_grad.astype(BF16))
    moved_gain = to_mirror(up_gain_grad.astype(BF16))
    weight_grad = (down_weight_grad + moved_weight.astype(F32))[None]
    gain_grad = (down_gain_grad + moved_gain.astype(F32))[None]
    return (values, input_grad, weight_grad, gain_grad)


def solution(mesh):
    return jax.shard_map(
        per_device,
        mesh=mesh,
        in_specs=(
            P(None, "section", "fsdp", None),
            P(None, "section", "fsdp", None),
            P("section", "fsdp", None),
            P("section", "fsdp", None),
            P("section", None),
            P("section", None),
            P(None, "fsdp", None),
            P(),
        ),
        out_specs=(
            P(None, "section", "fsdp", None),
            P(None, "section", "fsdp", None),
            P("section", "fsdp", None),
            P("section", "fsdp"),
        ),
        check_vma=False,
    )
```

profile of v0, /device:TPU:1, one launch (start us, length us, event | category | flops | bytes accessed | tf_op | source)
XLA Modules:
  0.0 189.5 jit_solution(15993294470091819062)
XLA Ops:
  0.7 1.5 collective-permute-start.19
  2.2 1.8 constant_dynamic-update-slice_fusion.1
  4.0 1.8 constant_dynamic-update-slice_fusion.refs_0_
  5.8 1.4 collective-permute-start.1
  7.2 1.4 collective-permute-start.4
  8.6 2.7 %collective-permute-start = (bf16[2,448,512]{2,1,0:T(8,128)(2,1)}, bf16[2,448,512]{2,1,0:T(8,128)(2,1)}, u32[]{:S(2)}, u32[]{:S(2)}) collective-permute-start(bf16[2,448,512]{2,1,0:T(8,128)(2,1)} %constant_dynamic-update-slice_fusion.refs_0_), channel_id=1, source_target_pairs={{0,8},{1,9},{2,10},{3,11},{4,12},{5,13},{6,14},{7,15},{8,0},{9,1},... | collective-permute-start | bytes 2752520 | tf_op jit(solution)/shard_map/ppermute | solution.py:42
  11.4 0.9 collective-permute-start.9
  12.7 1.2 fusion
  13.9 3.5 %all-to-all-start = ((bf16[16,8,2432]{2,1,0:T(8,128)(2,1)}), bf16[16,8,2432]{2,1,0:T(8,128)(2,1)S(1)}, u32[]{:S(2)}, u32[]{:S(2)}) async-start(bf16[16,8,2432]{2,1,0:T(8,128)(2,1)} %fusion), calls=%async_computation | async-start | bytes 1245184 | tf_op jit(solution)/shard_map/all_to_all | solution.py:333
  17.4 12.1 %collective-permute-done.1.refs_3_ = bf16[2,448,512]{2,1,0:T(8,128)(2,1)S(1)} collective-permute-done((bf16[2,448,512]{2,1,0:T(8,128)(2,1)}, bf16[2,448,512]{2,1,0:T(8,128)(2,1)S(1)}, u32[]{:S(2)}, u32[]{:S(2)}) %collective-permute-start.1) | collective-permute-done | bytes 917536 | tf_op jit(solution)/shard_map/ppermute | solution.py:34
  29.5 1.4 slice.109
  30.9 1.0 pad_maximum_fusion
  31.9 2.5 %collective-permute-start.5 = (bf16[2,448,512]{2,1,0:T(8,128)(2,1)}, bf16[2,448,512]{2,1,0:T(8,128)(2,1)}, u32[]{:S(2)}, u32[]{:S(2)}) collective-permute-start(bf16[2,448,512]{2,1,0:T(8,128)(2,1)} %pad_maximum_fusion), channel_id=1, source_target_pairs={{0,8},{1,9},{2,10},{3,11},{4,12},{5,13},{6,14},{7,15},{8,0},{9,1},... | collective-permute-start | bytes 2752520 | tf_op jit(solution)/shard_map/ppermute | solution.py:42
  34.4 0.7 collective-permute-start.2
  35.1 1.8 slice_bitcast_fusion.1
  36.9 2.0 %collective-permute-start.3 = (bf16[448,512]{1,0:T(8,128)(2,1)}, bf16[448,512]{1,0:T(8,128)(2,1)S(1)}, u32[]{:S(2)}, u32[]{:S(2)}) collective-permute-start(bf16[448,512]{1,0:T(8,128)(2,1)} %slice_bitcast_fusion.1), channel_id=1, source_target_pairs={{0,6},{1,7},{2,0},{3,1},{4,2},{5,3},{6,4},{7,5},{8,14},{9,15},{10,... | collective-permute-start | bytes 1376264 | tf_op jit(solution)/shard_map/ppermute | solution.py:38
  38.9 0.6 convert_reduce_fusion
  40.8 0.7 concatenate.9.table
  41.5 1.3 collective-permute-start.20
  42.8 3.8 %collective-permute-done.3.refs_5_ = bf16[448,512]{1,0:T(8,128)(2,1)S(1)} collective-permute-done((bf16[448,512]{1,0:T(8,128)(2,1)}, bf16[448,512]{1,0:T(8,128)(2,1)S(1)}, u32[]{:S(2)}, u32[]{:S(2)}) %collective-permute-start.3) | collective-permute-done | bytes 458784 | tf_op jit(solution)/shard_map/ppermute | solution.py:38
  46.6 1.3 collective-permute-start.21
  47.9 10.2 %collective-permute-done.5.refs_5_ = bf16[2,448,512]{2,1,0:T(8,128)(2,1)} collective-permute-done((bf16[2,448,512]{2,1,0:T(8,128)(2,1)}, bf16[2,448,512]{2,1,0:T(8,128)(2,1)}, u32[]{:S(2)}, u32[]{:S(2)}) %collective-permute-start.5) | collective-permute-done | bytes 917536 | tf_op jit(solution)/shard_map/ppermute | solution.py:42
  58.1 1.3 collective-permute-start.7
  59.4 1.9 collective-permute-start.14
  61.3 0.7 fusion.10.perm_ref
  61.9 0.8 slice_bitcast_fusion
  63.6 2.7 %collective-permute-start.8 = (bf16[448,512]{1,0:T(8,128)(2,1)}, bf16[448,512]{1,0:T(8,128)(2,1)}, u32[]{:S(2)}, u32[]{:S(2)}) collective-permute-start(bf16[448,512]{1,0:T(8,128)(2,1)} %slice_bitcast_fusion), channel_id=1, source_target_pairs={{0,8},{1,9},{2,10},{3,11},{4,12},{5,13},{6,14},{7,15},{8,0},{9,1},... | collective-permute-start | bytes 1376264 | tf_op jit(solution)/shard_map/ppermute | solution.py:42
  66.3 2.5 %collective-permute-done.7.refs_6_ = bf16[448,512]{1,0:T(8,128)(2,1)} collective-permute-done((bf16[448,512]{1,0:T(8,128)(2,1)S(1)}, bf16[448,512]{1,0:T(8,128)(2,1)}, u32[]{:S(2)}, u32[]{:S(2)}) %collective-permute-start.7) | collective-permute-done | bytes 458784 | tf_op jit(solution)/shard_map/ppermute | solution.py:38
  68.8 2.3 %collective-permute-start.17 = (bf16[448,512]{1,0:T(8,128)(2,1)}, bf16[448,512]{1,0:T(8,128)(2,1)}, u32[]{:S(2)}, u32[]{:S(2)}) collective-permute-start(bf16[448,512]{1,0:T(8,128)(2,1)} %collective-permute-done.7.refs_6_), channel_id=1, source_target_pairs={{0,1},{1,0},{2,3},{3,2},{4,5},{5,4},{6,7},{7,6},{8,9},{9,8},{10,11... | collective-permute-start | bytes 1376264 | tf_op jit(solution)/shard_map/ppermute | solution.py:46
  71.2 9.3 %prepare.1 = (bf16[128,7168]{1,0:T(8,128)(2,1)}, bf16[2,1,256,512]{3,2,1,0:T(8,128)(2,1)}, f32[2,256,128]{2,1,0:T(8,128)}) custom-call(s32[16]{0:T(128)} %concatenate.9.table, bf16[2,1,256,7168]{3,2,1,0:T(8,128)(2,1)} %x_ref.9, bf16[2,1,256,512]{3,2,1,0:T(8,128)(2,1)} %ct_ref.5, bf16[256,128]{1,0:T(8,128)(2,1)} %fusion.10.perm_ref, ...), custom_call_target="tpu_custom_call" | custom-call | flops 29360128 | bytes 12000000 | tf_op jit(solution)/shard_map/prepare/pallas_call | solution.py:92
  80.5 0.5 collective-permute-start.12
  81.6 4.9 %collective-permute-done.16.refs_15_ = bf16[448,512]{1,0:T(8,128)(2,1)S(1)} collective-permute-done((bf16[448,512]{1,0:T(8,128)(2,1)}, bf16[448,512]{1,0:T(8,128)(2,1)S(1)}, u32[]{:S(2)}, u32[]{:S(2)}) %collective-permute-start.16) | collective-permute-done | bytes 458784 | tf_op jit(solution)/shard_map/ppermute | solution.py:46
  87.9 1.2 collective-permute-done.15.refs_12_
  89.2 2.7 %collective-permute-done.18.refs_13_ = bf16[448,512]{1,0:T(8,128)(2,1)S(1)} collective-permute-done((bf16[448,512]{1,0:T(8,128)(2,1)}, bf16[448,512]{1,0:T(8,128)(2,1)S(1)}, u32[]{:S(2)}, u32[]{:S(2)}) %collective-permute-start.18) | collective-permute-done | bytes 458784 | tf_op jit(solution)/shard_map/ppermute | solution.py:46
  91.9 0.7 copy-done.25
  92.7 0.8 copy-done.10
  93.5 1.2 copy-done.2
  94.7 10.3 %products.2 = (bf16[2,448,512]{2,1,0:T(8,128)(2,1)}, bf16[2,448,512]{2,1,0:T(8,128)(2,1)}, bf16[1,448,512]{2,1,0:T(8,128)(2,1)}, bf16[1,448,512]{2,1,0:T(8,128)(2,1)}, bf16[2,448,512]{2,1,0:T(8,128)(2,1)}) custom-call(s32[16]{0:T(128)} %concatenate.9.table, bf16[2,1,256,7168]{3,2,1,0:T(8,128)(2,1)} %x_ref.9, ...), custom_call_target="tpu_custom_call" | custom-call | flops 3758096384 | bytes 12000000 | tf_op jit(solution)/shard_map/products/pallas_call | solution.py:185
  105.1 2.9 %collective-permute-start.25 = (bf16[2,448,512]{2,1,0:T(8,128)(2,1)}, bf16[2,448,512]{2,1,0:T(8,128)(2,1)S(1)}, u32[]{:S(2)}, u32[]{:S(2)}) collective-permute-start(bf16[2,448,512]{2,1,0:T(8,128)(2,1)} %get-tuple-element.48), channel_id=1, source_target_pairs={{0,6},{1,7},{2,0},{3,1},{4,2},{5,3},{6,4},{7,5},{8,14},{9,15},{10,... | collective-permute-start | bytes 2752520 | tf_op jit(solution)/shard_map/ppermute | solution.py:38
  108.0 10.2 %products.3 = (bf16[1,448,512]{2,1,0:T(8,128)(2,1)}, bf16[3,448,512]{2,1,0:T(8,128)(2,1)}, bf16[1,448,512]{2,1,0:T(8,128)(2,1)}, bf16[2,448,512]{2,1,0:T(8,128)(2,1)}, bf16[1,448,512]{2,1,0:T(8,128)(2,1)}) custom-call(s32[16]{0:T(128)} %concatenate.9.table, bf16[2,1,256,7168]{3,2,1,0:T(8,128)(2,1)} %x_ref.9, ...), custom_call_target="tpu_custom_call" | custom-call | flops 3758096384 | bytes 12000000 | tf_op jit(solution)/shard_map/products/pallas_call | solution.py:185
  118.2 2.8 %collective-permute-start.26 = (bf16[1,448,512]{2,1,0:T(8,128)(2,1)}, bf16[1,448,512]{2,1,0:T(8,128)(2,1)}, u32[]{:S(2)}, u32[]{:S(2)}) collective-permute-start(bf16[1,448,512]{2,1,0:T(8,128)(2,1)} %get-tuple-element.50), channel_id=1, source_target_pairs={{0,8},{1,9},{2,10},{3,11},{4,12},{5,13},{6,14},{7,15},{8,0},{9,1},... | collective-permute-start | bytes 1376264 | tf_op jit(solution)/shard_map/ppermute | solution.py:42
  121.1 1.3 dynamic-slice_convert_fusion
  122.6 10.0 %layer.2 = (bf16[2,1,256,512]{3,2,1,0:T(8,128)(2,1)}, bf16[2,1,256,7168]{3,2,1,0:T(8,128)(2,1)}) custom-call(s32[16]{0:T(128)} %concatenate.9.table, bf16[2,1,256,7168]{3,2,1,0:T(8,128)(2,1)} %x_ref.9, bf16[128,7168]{1,0:T(8,128)(2,1)} %get-tuple-element.44.head_ref, bf16[2,1,256,512]{3,2,1,0:T(8,128)(2,1)} %ct_ref.5, ...), custom_call_target="tpu_custom_call" | custom-call | flops 3758096384 | bytes 16000000 | tf_op jit(solution)/shard_map/layer/pallas_call | solution.py:271
  132.7 0.8 add_bitcast_fusion.1
  133.5 1.3 collective-permute-start.28
  134.8 0.9 add_bitcast_fusion.2
  135.8 1.1 add.168
  137.0 0.8 slice_bitcast_fusion.6
  137.8 2.7 %collective-permute-start.30 = (bf16[224,512]{1,0:T(8,128)(2,1)}, bf16[224,512]{1,0:T(8,128)(2,1)}, u32[]{:S(2)}, u32[]{:S(2)}) collective-permute-start(bf16[224,512]{1,0:T(8,128)(2,1)} %get-tuple-element.80), channel_id=1, source_target_pairs={{0,6},{1,7},{2,0},{3,1},{4,2},{5,3},{6,4},{7,5},{8,14},{9,15},{10,... | collective-permute-start | bytes 688136 | tf_op jit(solution)/shard_map/ppermute | solution.py:38
  140.5 10.0 %layer.3 = (bf16[2,1,256,512]{3,2,1,0:T(8,128)(2,1)}, bf16[2,1,256,7168]{3,2,1,0:T(8,128)(2,1)}) custom-call(s32[16]{0:T(128)} %concatenate.9.table, bf16[2,1,256,7168]{3,2,1,0:T(8,128)(2,1)} %x_ref.9, bf16[128,7168]{1,0:T(8,128)(2,1)} %get-tuple-element.44.head_ref, ...), custom_call_target="tpu_custom_call", output_to_operand_aliasing={{0}: (23, {}), {1}: (24, {})} | custom-call | flops 3758096384 | bytes 16000000 | tf_op jit(solution)/shard_map/layer/pallas_call | solution.py:271
  150.4 2.1 %collective-permute-done.29 = bf16[224,512]{1,0:T(8,128)(2,1)} collective-permute-done((bf16[224,512]{1,0:T(8,128)(2,1)}, bf16[224,512]{1,0:T(8,128)(2,1)}, u32[]{:S(2)}, u32[]{:S(2)}) %collective-permute-start.29) | collective-permute-done | bytes 229408 | tf_op jit(solution)/shard_map/ppermute | solution.py:34
  152.5 6.1 %collective-permute-done.31 = bf16[3,448,512]{2,1,0:T(8,128)(2,1)S(1)} collective-permute-done((bf16[3,448,512]{2,1,0:T(8,128)(2,1)}, bf16[3,448,512]{2,1,0:T(8,128)(2,1)S(1)}, u32[]{:S(2)}, u32[]{:S(2)}) %collective-permute-start.31) | collective-permute-done | bytes 1376288 | tf_op jit(solution)/shard_map/ppermute | solution.py:42
  158.6 1.2 fusion.4
  159.8 2.7 %collective-permute-start.34 = (bf16[448,512]{1,0:T(8,128)(2,1)S(1)}, bf16[448,512]{1,0:T(8,128)(2,1)S(1)}, u32[]{:S(2)}, u32[]{:S(2)}) collective-permute-start(bf16[448,512]{1,0:T(8,128)(2,1)S(1)} %fusion.4), channel_id=1, source_target_pairs={{0,8},{1,9},{2,10},{3,11},{4,12},{5,13},{6,14},{7,15},{8,0},{9,1},... | collective-permute-start | bytes 1376264 | tf_op jit(solution)/shard_map/ppermute | solution.py:42
  162.7 1.1 fusion.9
  164.0 1.0 fusion.8
  165.0 2.7 %collective-permute-start.33 = (bf16[448,512]{1,0:T(8,128)(2,1)S(1)}, bf16[448,512]{1,0:T(8,128)(2,1)S(1)}, u32[]{:S(2)}, u32[]{:S(2)}) collective-permute-start(bf16[448,512]{1,0:T(8,128)(2,1)S(1)} %pad_maximum_fusion.2), channel_id=1, source_target_pairs={{0,6},{1,7},{2,0},{3,1},{4,2},{5,3},{6,4},{7,5},{8,14},{9,15},{10,... | collective-permute-start | bytes 1376264 | tf_op jit(solution)/shard_map/ppermute | solution.py:38
  167.7 3.8 %collective-permute-done.34 = bf16[448,512]{1,0:T(8,128)(2,1)S(1)} collective-permute-done((bf16[448,512]{1,0:T(8,128)(2,1)S(1)}, bf16[448,512]{1,0:T(8,128)(2,1)S(1)}, u32[]{:S(2)}, u32[]{:S(2)}) %collective-permute-start.34) | collective-permute-done | bytes 458784 | tf_op jit(solution)/shard_map/ppermute | solution.py:42
  171.6 1.5 fusion.1
  173.1 5.1 %collective-permute-start.35 = (bf16[448,512]{1,0:T(8,128)(2,1)S(1)}, bf16[448,512]{1,0:T(8,128)(2,1)S(1)}, u32[]{:S(2)}, u32[]{:S(2)}) collective-permute-start(bf16[448,512]{1,0:T(8,128)(2,1)S(1)} %get-tuple-element.75), channel_id=1, source_target_pairs={{0,112},{16,96},{32,80},{48,64},{64,48},{80,32},{96,16},{112,0},{1... | collective-permute-start | bytes 1376264 | tf_op jit(solution)/shard_map/ppermute | solution.py:51
  178.1 0.8 dynamic-slice_convert_fusion.1
  178.9 8.6 %collective-permute-done.35 = bf16[448,512]{1,0:T(8,128)(2,1)S(1)} collective-permute-done((bf16[448,512]{1,0:T(8,128)(2,1)S(1)}, bf16[448,512]{1,0:T(8,128)(2,1)S(1)}, u32[]{:S(2)}, u32[]{:S(2)}) %collective-permute-start.35) | collective-permute-done | bytes 458784 | tf_op jit(solution)/shard_map/ppermute | solution.py:51
  187.6 1.3 fusion.2
  188.9 0.6 convert_add_fusion.2
  (122 shorter events, 4.8 us)
Async XLA Ops:
  0.6 12.0 %copy-start = (bf16[2,64,7168]{2,1,0:T(8,128)(2,1)S(1)}, bf16[2,64,7168]{2,1,0:T(8,128)(2,1)}, u32[]{:S(2)}) copy-start(bf16[2,64,7168]{2,1,0:T(8,128)(2,1)} %param.15) | copy-start | bytes 5505028
  0.6 11.6 %copy-start.29 = (s32[2,16,16]{2,1,0:T(8,128)S(1)}, s32[2,16,16]{2,1,0:T(8,128)}, u32[]{:S(2)}) copy-start(s32[2,16,16]{2,1,0:T(8,128)} %param.16) | copy-start | bytes 6148
  0.7 61.3 %collective-permute-start.19 = (bf16[2,1,256,7168]{3,2,1,0:T(8,128)(2,1)}, bf16[2,1,256,7168]{3,2,1,0:T(8,128)(2,1)}, u32[]{:S(2)}, u32[]{:S(2)}) collective-permute-start(bf16[2,1,256,7168]{3,2,1,0:T(8,128)(2,1)} %x_ref.9), channel_id=1, source_target_pairs={{0,1},{1,0},{2,3},{3,2},{4,5},{5,4},{6,7},{7,6},{8,9},{9,8},{10,11... | collective-permute-start | bytes 22020104 | tf_op jit(solution)/shard_map/ppermute | solution.py:46
  5.8 23.7 %collective-permute-start.1 = (bf16[2,448,512]{2,1,0:T(8,128)(2,1)}, bf16[2,448,512]{2,1,0:T(8,128)(2,1)S(1)}, u32[]{:S(2)}, u32[]{:S(2)}) collective-permute-start(bf16[2,448,512]{2,1,0:T(8,128)(2,1)} %constant_dynamic-update-slice_fusion.refs_0_), channel_id=1, source_target_pairs={{0,2},{1,3},{2,4},{3,5},{4,6},{5,7},{6,0},{7,1},{8,10},{9,11},{10,... | collective-permute-start | bytes 2752520 | tf_op jit(solution)/shard_map/ppermute | solution.py:34
  7.2 22.3 %collective-permute-start.4 = (bf16[2,448,512]{2,1,0:T(8,128)(2,1)}, bf16[2,448,512]{2,1,0:T(8,128)(2,1)}, u32[]{:S(2)}, u32[]{:S(2)}) collective-permute-start(bf16[2,448,512]{2,1,0:T(8,128)(2,1)} %constant_dynamic-update-slice_fusion.refs_0_), channel_id=1, source_target_pairs={{0,6},{1,7},{2,0},{3,1},{4,2},{5,3},{6,4},{7,5},{8,14},{9,15},{10,... | collective-permute-start | bytes 2752520 | tf_op jit(solution)/shard_map/ppermute | solution.py:38
  8.6 26.5 %collective-permute-start = (bf16[2,448,512]{2,1,0:T(8,128)(2,1)}, bf16[2,448,512]{2,1,0:T(8,128)(2,1)}, u32[]{:S(2)}, u32[]{:S(2)}) collective-permute-start(bf16[2,448,512]{2,1,0:T(8,128)(2,1)} %constant_dynamic-update-slice_fusion.refs_0_), channel_id=1, source_target_pairs={{0,8},{1,9},{2,10},{3,11},{4,12},{5,13},{6,14},{7,15},{8,0},{9,1},... | collective-permute-start | bytes 2752520 | tf_op jit(solution)/shard_map/ppermute | solution.py:42
  11.4 30.2 %collective-permute-start.9 = (bf16[2,448,512]{2,1,0:T(8,128)(2,1)}, bf16[2,448,512]{2,1,0:T(8,128)(2,1)}, u32[]{:S(2)}, u32[]{:S(2)}) collective-permute-start(bf16[2,448,512]{2,1,0:T(8,128)(2,1)} %constant_dynamic-update-slice_fusion.refs_0_), channel_id=1, source_target_pairs={{0,1},{1,0},{2,3},{3,2},{4,5},{5,4},{6,7},{7,6},{8,9},{9,8},{10,11... | collective-permute-start | bytes 2752520 | tf_op jit(solution)/shard_map/ppermute | solution.py:46
  13.9 27.6 %all-to-all-start = ((bf16[16,8,2432]{2,1,0:T(8,128)(2,1)}), bf16[16,8,2432]{2,1,0:T(8,128)(2,1)S(1)}, u32[]{:S(2)}, u32[]{:S(2)}) async-start(bf16[16,8,2432]{2,1,0:T(8,128)(2,1)} %fusion), calls=%async_computation | async-start | bytes 1245184 | tf_op jit(solution)/shard_map/all_to_all | solution.py:333
  29.4 33.3 %copy-start.3 = (bf16[2,448,512]{2,1,0:T(8,128)(2,1)}, bf16[2,448,512]{2,1,0:T(8,128)(2,1)S(1)}, u32[]{:S(2)}) copy-start(bf16[2,448,512]{2,1,0:T(8,128)(2,1)S(1)} %collective-permute-done.1.refs_3_) | copy-start | bytes 2752516
  29.5 11.4 %copy-start.30 = (s32[3]{0:T(128)S(1)}, s32[3]{0:T(128)}, u32[]{:S(2)}) copy-start(s32[3]{0:T(128)} %constant.156.clone) | copy-start | bytes 40
  31.9 26.2 %collective-permute-start.5 = (bf16[2,448,512]{2,1,0:T(8,128)(2,1)}, bf16[2,448,512]{2,1,0:T(8,128)(2,1)}, u32[]{:S(2)}, u32[]{:S(2)}) collective-permute-start(bf16[2,448,512]{2,1,0:T(8,128)(2,1)} %pad_maximum_fusion), channel_id=1, source_target_pairs={{0,8},{1,9},{2,10},{3,11},{4,12},{5,13},{6,14},{7,15},{8,0},{9,1},... | collective-permute-start | bytes 2752520 | tf_op jit(solution)/shard_map/ppermute | solution.py:42
  34.4 25.0 %collective-permute-start.2 = (bf16[2,448,512]{2,1,0:T(8,128)(2,1)S(1)}, bf16[2,448,512]{2,1,0:T(8,128)(2,1)S(1)}, u32[]{:S(2)}, u32[]{:S(2)}) collective-permute-start(bf16[2,448,512]{2,1,0:T(8,128)(2,1)S(1)} %collective-permute-done.1.refs_3_), channel_id=1, source_target_pairs={{0,2},{1,3},{2,4},{3,5},{4,6},{5,7},{6,0},{7,1},{8,10},{9,11},{10,... | collective-permute-start | bytes 2752520 | tf_op jit(solution)/shard_map/ppermute | solution.py:34
  36.9 9.7 %collective-permute-start.3 = (bf16[448,512]{1,0:T(8,128)(2,1)}, bf16[448,512]{1,0:T(8,128)(2,1)S(1)}, u32[]{:S(2)}, u32[]{:S(2)}) collective-permute-start(bf16[448,512]{1,0:T(8,128)(2,1)} %slice_bitcast_fusion.1), channel_id=1, source_target_pairs={{0,6},{1,7},{2,0},{3,1},{4,2},{5,3},{6,4},{7,5},{8,14},{9,15},{10,... | collective-permute-start | bytes 1376264 | tf_op jit(solution)/shard_map/ppermute | solution.py:38
  41.5 29.6 %copy-start.9 = (bf16[16,8,2432]{2,1,0:T(8,128)(2,1)}, bf16[16,8,2432]{2,1,0:T(8,128)(2,1)S(1)}, u32[]{:S(2)}) copy-start(bf16[16,8,2432]{2,1,0:T(8,128)(2,1)S(1)} %all-to-all-done) | copy-start | bytes 1867780
  41.5 21.2 %collective-permute-start.20 = (bf16[128,2432]{1,0:T(8,128)(2,1)S(1)}, bf16[128,2432]{1,0:T(8,128)(2,1)S(1)}, u32[]{:S(2)}, u32[]{:S(2)}) collective-permute-start(bf16[128,2432]{1,0:T(8,128)(2,1)S(1)} %bitcast.77), channel_id=1, source_target_pairs={{16,0},{96,112},{17,1},{97,113},{18,2},{98,114},{19,3},{99,115},{2... | collective-permute-start | bytes 1867784 | tf_op jit(solution)/shard_map/ppermute | solution.py:337
  46.6 58.4 %copy-start.21 = (bf16[448,512]{1,0:T(8,128)(2,1)}, bf16[448,512]{1,0:T(8,128)(2,1)S(1)}, u32[]{:S(2)}) copy-start(bf16[448,512]{1,0:T(8,128)(2,1)S(1)} %collective-permute-done.3.refs_5_) | copy-start | bytes 1376260
  46.6 16.5 %collective-permute-start.21 = (bf16[128,2432]{1,0:T(8,128)(2,1)S(1)}, bf16[128,2432]{1,0:T(8,128)(2,1)S(1)}, u32[]{:S(2)}, u32[]{:S(2)}) collective-permute-start(bf16[128,2432]{1,0:T(8,128)(2,1)S(1)} %bitcast.78), channel_id=1, source_target_pairs={{48,0},{64,112},{49,1},{65,113},{50,2},{66,114},{51,3},{67,115},{5... | collective-permute-start | bytes 1867784 | tf_op jit(solution)/shard_map/ppermute | solution.py:338
  58.1 10.7 %collective-permute-start.7 = (bf16[448,512]{1,0:T(8,128)(2,1)S(1)}, bf16[448,512]{1,0:T(8,128)(2,1)}, u32[]{:S(2)}, u32[]{:S(2)}) collective-permute-start(bf16[448,512]{1,0:T(8,128)(2,1)S(1)} %collective-permute-done.3.refs_5_), channel_id=1, source_target_pairs={{0,6},{1,7},{2,0},{3,1},{4,2},{5,3},{6,4},{7,5},{8,14},{9,15},{10,... | collective-permute-start | bytes 1376264 | tf_op jit(solution)/shard_map/ppermute | solution.py:38
  59.4 21.0 %copy-start.4 = (bf16[2,448,512]{2,1,0:T(8,128)(2,1)}, bf16[2,448,512]{2,1,0:T(8,128)(2,1)S(1)}, u32[]{:S(2)}) copy-start(bf16[2,448,512]{2,1,0:T(8,128)(2,1)S(1)} %collective-permute-done.2.refs_2_) | copy-start | bytes 2752516
  59.4 21.0 %collective-permute-start.14 = (bf16[448,512]{1,0:T(8,128)(2,1)S(1)}, bf16[448,512]{1,0:T(8,128)(2,1)}, u32[]{:S(2)}, u32[]{:S(2)}) collective-permute-start(bf16[448,512]{1,0:T(8,128)(2,1)S(1)} %collective-permute-done.3.refs_5_), channel_id=1, source_target_pairs={{0,1},{1,0},{2,3},{3,2},{4,5},{5,4},{6,7},{7,6},{8,9},{9,8},{10,11... | collective-permute-start | bytes 1376264 | tf_op jit(solution)/shard_map/ppermute | solution.py:46
  61.9 18.6 %collective-permute-start.6 = (bf16[448,512]{1,0:T(8,128)(2,1)}, bf16[448,512]{1,0:T(8,128)(2,1)}, u32[]{:S(2)}, u32[]{:S(2)}) collective-permute-start(bf16[448,512]{1,0:T(8,128)(2,1)} %slice_bitcast_fusion.1), channel_id=1, source_target_pairs={{0,2},{1,3},{2,4},{3,5},{4,6},{5,7},{6,0},{7,1},{8,10},{9,11},{10,... | collective-permute-start | bytes 1376264 | tf_op jit(solution)/shard_map/ppermute | solution.py:34
  62.8 23.9 %collective-permute-start.11 = (bf16[2,448,512]{2,1,0:T(8,128)(2,1)S(1)}, bf16[2,448,512]{2,1,0:T(8,128)(2,1)S(1)}, u32[]{:S(2)}, u32[]{:S(2)}) collective-permute-start(bf16[2,448,512]{2,1,0:T(8,128)(2,1)S(1)} %collective-permute-done.1.refs_3_), channel_id=1, source_target_pairs={{0,1},{1,0},{2,3},{3,2},{4,5},{5,4},{6,7},{7,6},{8,9},{9,8},{10,11... | collective-permute-start | bytes 2752520 | tf_op jit(solution)/shard_map/ppermute | solution.py:46
  63.6 2.7 %copy-start.20 = (bf16[128,2432]{1,0:T(8,128)(2,1)}, bf16[128,2432]{1,0:T(8,128)(2,1)S(1)}, u32[]{:S(2)}) copy-start(bf16[128,2432]{1,0:T(8,128)(2,1)S(1)} %collective-permute-done.21.im2) | copy-start | bytes 1867780
  63.6 17.5 %collective-permute-start.8 = (bf16[448,512]{1,0:T(8,128)(2,1)}, bf16[448,512]{1,0:T(8,128)(2,1)}, u32[]{:S(2)}, u32[]{:S(2)}) collective-permute-start(bf16[448,512]{1,0:T(8,128)(2,1)} %slice_bitcast_fusion), channel_id=1, source_target_pairs={{0,8},{1,9},{2,10},{3,11},{4,12},{5,13},{6,14},{7,15},{8,0},{9,1},... | collective-permute-start | bytes 1376264 | tf_op jit(solution)/shard_map/ppermute | solution.py:42
  68.8 12.3 %collective-permute-start.17 = (bf16[448,512]{1,0:T(8,128)(2,1)}, bf16[448,512]{1,0:T(8,128)(2,1)}, u32[]{:S(2)}, u32[]{:S(2)}) collective-permute-start(bf16[448,512]{1,0:T(8,128)(2,1)} %collective-permute-done.7.refs_6_), channel_id=1, source_target_pairs={{0,1},{1,0},{2,3},{3,2},{4,5},{5,4},{6,7},{7,6},{8,9},{9,8},{10,11... | collective-permute-start | bytes 1376264 | tf_op jit(solution)/shard_map/ppermute | solution.py:46
  80.4 13.0 %collective-permute-start.22 = (bf16[128,7168]{1,0:T(8,128)(2,1)}, bf16[128,7168]{1,0:T(8,128)(2,1)S(1)}, u32[]{:S(2)}, u32[]{:S(2)}) collective-permute-start(bf16[128,7168]{1,0:T(8,128)(2,1)} %get-tuple-element.44.head_ref), channel_id=1, source_target_pairs={{0,1},{1,0},{2,3},{3,2},{4,5},{5,4},{6,7},{7,6},{8,9},{9,8},{10,11... | collective-permute-start | bytes 5505032 | tf_op jit(solution)/shard_map/ppermute | solution.py:46
  80.5 6.5 %collective-permute-start.12 = (bf16[2,448,512]{2,1,0:T(8,128)(2,1)}, bf16[2,448,512]{2,1,0:T(8,128)(2,1)S(1)}, u32[]{:S(2)}, u32[]{:S(2)}) collective-permute-start(bf16[2,448,512]{2,1,0:T(8,128)(2,1)} %collective-permute-done.refs_4_), channel_id=1, source_target_pairs={{0,1},{1,0},{2,3},{3,2},{4,5},{5,4},{6,7},{7,6},{8,9},{9,8},{10,11... | collective-permute-start | bytes 2752520 | tf_op jit(solution)/shard_map/ppermute | solution.py:46
  81.0 5.4 %collective-permute-start.16 = (bf16[448,512]{1,0:T(8,128)(2,1)}, bf16[448,512]{1,0:T(8,128)(2,1)S(1)}, u32[]{:S(2)}, u32[]{:S(2)}) collective-permute-start(bf16[448,512]{1,0:T(8,128)(2,1)} %collective-permute-done.6.refs_7_), channel_id=1, source_target_pairs={{0,1},{1,0},{2,3},{3,2},{4,5},{5,4},{6,7},{7,6},{8,9},{9,8},{10,11... | collective-permute-start | bytes 1376264 | tf_op jit(solution)/shard_map/ppermute | solution.py:46
  81.1 6.7 %collective-permute-start.10 = (bf16[2,448,512]{2,1,0:T(8,128)(2,1)}, bf16[2,448,512]{2,1,0:T(8,128)(2,1)S(1)}, u32[]{:S(2)}, u32[]{:S(2)}) collective-permute-start(bf16[2,448,512]{2,1,0:T(8,128)(2,1)} %collective-permute-done.4.refs_1_), channel_id=1, source_target_pairs={{0,1},{1,0},{2,3},{3,2},{4,5},{5,4},{6,7},{7,6},{8,9},{9,8},{10,11... | collective-permute-start | bytes 2752520 | tf_op jit(solution)/shard_map/ppermute | solution.py:46
  86.5 2.7 %collective-permute-start.15 = (bf16[2,448,512]{2,1,0:T(8,128)(2,1)}, bf16[2,448,512]{2,1,0:T(8,128)(2,1)S(1)}, u32[]{:S(2)}, u32[]{:S(2)}) collective-permute-start(bf16[2,448,512]{2,1,0:T(8,128)(2,1)} %collective-permute-done.5.refs_5_), channel_id=1, source_target_pairs={{0,1},{1,0},{2,3},{3,2},{4,5},{5,4},{6,7},{7,6},{8,9},{9,8},{10,11... | collective-permute-start | bytes 2752520 | tf_op jit(solution)/shard_map/ppermute | solution.py:46
  86.6 18.4 %copy-start.5 = (bf16[2,448,512]{2,1,0:T(8,128)(2,1)}, bf16[2,448,512]{2,1,0:T(8,128)(2,1)S(1)}, u32[]{:S(2)}) copy-start(bf16[2,448,512]{2,1,0:T(8,128)(2,1)S(1)} %collective-permute-done.11.refs_10_.refs_11_) | copy-start | bytes 2752516
  86.6 5.3 %collective-permute-start.13 = (bf16[2,448,512]{2,1,0:T(8,128)(2,1)}, bf16[2,448,512]{2,1,0:T(8,128)(2,1)S(1)}, u32[]{:S(2)}, u32[]{:S(2)}) collective-permute-start(bf16[2,448,512]{2,1,0:T(8,128)(2,1)} %copy-done.4), channel_id=1, source_target_pairs={{0,1},{1,0},{2,3},{3,2},{4,5},{5,4},{6,7},{7,6},{8,9},{9,8},{10,11... | collective-permute-start | bytes 2752520 | tf_op jit(solution)/shard_map/ppermute | solution.py:46
  87.3 4.6 %copy-start.6 = (bf16[2,448,512]{2,1,0:T(8,128)(2,1)}, bf16[2,448,512]{2,1,0:T(8,128)(2,1)S(1)}, u32[]{:S(2)}) copy-start(bf16[2,448,512]{2,1,0:T(8,128)(2,1)S(1)} %collective-permute-done.12.refs_11_.refs_12_) | copy-start | bytes 2752516
  87.3 4.6 %collective-permute-start.23 = (bf16[2,1,256,512]{3,2,1,0:T(8,128)(2,1)}, bf16[2,1,256,512]{3,2,1,0:T(8,128)(2,1)S(1)}, u32[]{:S(2)}, u32[]{:S(2)}) collective-permute-start(bf16[2,1,256,512]{3,2,1,0:T(8,128)(2,1)} %get-tuple-element.45.own_ct.scaled_ref), channel_id=1, source_target_pairs={{0,1},{1,0},{2,3},{3,2},{4,5},{5,4},{6,7},{7,6},{8,9},{9,8},{10,11... | collective-permute-start | bytes 1572872 | tf_op jit(solution)/shard_map/ppermute | solution.py:46
  87.8 4.1 %copy-start.7 = (bf16[2,448,512]{2,1,0:T(8,128)(2,1)}, bf16[2,448,512]{2,1,0:T(8,128)(2,1)S(1)}, u32[]{:S(2)}) copy-start(bf16[2,448,512]{2,1,0:T(8,128)(2,1)S(1)} %collective-permute-done.10.refs_8_.refs_9_) | copy-start | bytes 2752516
  87.8 4.1 %collective-permute-start.18 = (bf16[448,512]{1,0:T(8,128)(2,1)}, bf16[448,512]{1,0:T(8,128)(2,1)S(1)}, u32[]{:S(2)}, u32[]{:S(2)}) collective-permute-start(bf16[448,512]{1,0:T(8,128)(2,1)} %collective-permute-done.8.refs_6_), channel_id=1, source_target_pairs={{0,1},{1,0},{2,3},{3,2},{4,5},{5,4},{6,7},{7,6},{8,9},{9,8},{10,11... | collective-permute-start | bytes 1376264 | tf_op jit(solution)/shard_map/ppermute | solution.py:46
  89.2 2.8 %copy-start.18 = (bf16[2,448,512]{2,1,0:T(8,128)(2,1)}, bf16[2,448,512]{2,1,0:T(8,128)(2,1)S(1)}, u32[]{:S(2)}) copy-start(bf16[2,448,512]{2,1,0:T(8,128)(2,1)S(1)} %collective-permute-done.15.refs_12_) | copy-start | bytes 2752516
  91.9 13.1 %copy-start.8 = (bf16[2,448,512]{2,1,0:T(8,128)(2,1)}, bf16[2,448,512]{2,1,0:T(8,128)(2,1)S(1)}, u32[]{:S(2)}) copy-start(bf16[2,448,512]{2,1,0:T(8,128)(2,1)S(1)} %collective-permute-done.13.refs_9_.refs_10_) | copy-start | bytes 2752516
  105.0 27.6 %collective-permute-start.24 = (bf16[2,448,512]{2,1,0:T(8,128)(2,1)}, bf16[2,448,512]{2,1,0:T(8,128)(2,1)S(1)}, u32[]{:S(2)}, u32[]{:S(2)}) collective-permute-start(bf16[2,448,512]{2,1,0:T(8,128)(2,1)} %get-tuple-element.47), channel_id=1, source_target_pairs={{0,2},{1,3},{2,4},{3,5},{4,6},{5,7},{6,0},{7,1},{8,10},{9,11},{10,... | collective-permute-start | bytes 2752520 | tf_op jit(solution)/shard_map/ppermute | solution.py:34
  105.1 27.5 %collective-permute-start.25 = (bf16[2,448,512]{2,1,0:T(8,128)(2,1)}, bf16[2,448,512]{2,1,0:T(8,128)(2,1)S(1)}, u32[]{:S(2)}, u32[]{:S(2)}) collective-permute-start(bf16[2,448,512]{2,1,0:T(8,128)(2,1)} %get-tuple-element.48), channel_id=1, source_target_pairs={{0,6},{1,7},{2,0},{3,1},{4,2},{5,3},{6,4},{7,5},{8,14},{9,15},{10,... | collective-permute-start | bytes 2752520 | tf_op jit(solution)/shard_map/ppermute | solution.py:38
  118.2 14.4 %collective-permute-start.26 = (bf16[1,448,512]{2,1,0:T(8,128)(2,1)}, bf16[1,448,512]{2,1,0:T(8,128)(2,1)}, u32[]{:S(2)}, u32[]{:S(2)}) collective-permute-start(bf16[1,448,512]{2,1,0:T(8,128)(2,1)} %get-tuple-element.50), channel_id=1, source_target_pairs={{0,8},{1,9},{2,10},{3,11},{4,12},{5,13},{6,14},{7,15},{8,0},{9,1},... | collective-permute-start | bytes 1376264 | tf_op jit(solution)/shard_map/ppermute | solution.py:42
  122.4 36.2 %collective-permute-start.31 = (bf16[3,448,512]{2,1,0:T(8,128)(2,1)}, bf16[3,448,512]{2,1,0:T(8,128)(2,1)S(1)}, u32[]{:S(2)}, u32[]{:S(2)}) collective-permute-start(bf16[3,448,512]{2,1,0:T(8,128)(2,1)} %get-tuple-element.64), channel_id=1, source_target_pairs={{0,8},{1,9},{2,10},{3,11},{4,12},{5,13},{6,14},{7,15},{8,0},{9,1},... | collective-permute-start | bytes 4128776 | tf_op jit(solution)/shard_map/ppermute | solution.py:42
  122.6 10.0 %copy-start.26 = (bf16[1,448,512]{2,1,0:T(8,128)(2,1)S(1)}, bf16[1,448,512]{2,1,0:T(8,128)(2,1)}, u32[]{:S(2)}) copy-start(bf16[1,448,512]{2,1,0:T(8,128)(2,1)} %get-tuple-element.55) | copy-start | bytes 1376260
  122.6 12.2 %copy-start.24 = (bf16[1,448,512]{2,1,0:T(8,128)(2,1)S(1)}, bf16[1,448,512]{2,1,0:T(8,128)(2,1)}, u32[]{:S(2)}) copy-start(bf16[1,448,512]{2,1,0:T(8,128)(2,1)} %get-tuple-element.46) | copy-start | bytes 1376260
  132.6 3.2 %copy-start.27 = (bf16[1,448,512]{2,1,0:T(8,128)(2,1)S(1)}, bf16[1,448,512]{2,1,0:T(8,128)(2,1)}, u32[]{:S(2)}) copy-start(bf16[1,448,512]{2,1,0:T(8,128)(2,1)} %get-tuple-element.62) | copy-start | bytes 1376260
  132.6 3.2 %copy-start.15 = (bf16[2,448,512]{2,1,0:T(8,128)(2,1)}, bf16[2,448,512]{2,1,0:T(8,128)(2,1)S(1)}, u32[]{:S(2)}) copy-start(bf16[2,448,512]{2,1,0:T(8,128)(2,1)S(1)} %collective-permute-done.25) | copy-start | bytes 2752516
  133.5 19.0 %collective-permute-start.28 = (bf16[448,512]{1,0:T(8,128)(2,1)}, bf16[448,512]{1,0:T(8,128)(2,1)}, u32[]{:S(2)}, u32[]{:S(2)}) collective-permute-start(bf16[448,512]{1,0:T(8,128)(2,1)} %add_bitcast_fusion.1), channel_id=1, source_target_pairs={{0,6},{1,7},{2,0},{3,1},{4,2},{5,3},{6,4},{7,5},{8,14},{9,15},{10,... | collective-permute-start | bytes 1376264 | tf_op jit(solution)/shard_map/ppermute | solution.py:38
  135.7 16.8 %collective-permute-start.27 = (bf16[448,512]{1,0:T(8,128)(2,1)}, bf16[448,512]{1,0:T(8,128)(2,1)}, u32[]{:S(2)}, u32[]{:S(2)}) collective-permute-start(bf16[448,512]{1,0:T(8,128)(2,1)} %add_bitcast_fusion.2), channel_id=1, source_target_pairs={{0,2},{1,3},{2,4},{3,5},{4,6},{5,7},{6,0},{7,1},{8,10},{9,11},{10,... | collective-permute-start | bytes 1376264 | tf_op jit(solution)/shard_map/ppermute | solution.py:34
  137.8 14.7 %collective-permute-start.29 = (bf16[224,512]{1,0:T(8,128)(2,1)}, bf16[224,512]{1,0:T(8,128)(2,1)}, u32[]{:S(2)}, u32[]{:S(2)}) collective-permute-start(bf16[224,512]{1,0:T(8,128)(2,1)} %get-tuple-element.81), channel_id=1, source_target_pairs={{0,2},{1,3},{2,4},{3,5},{4,6},{5,7},{6,0},{7,1},{8,10},{9,11},{10,... | collective-permute-start | bytes 688136 | tf_op jit(solution)/shard_map/ppermute | solution.py:34
  137.8 14.7 %collective-permute-start.30 = (bf16[224,512]{1,0:T(8,128)(2,1)}, bf16[224,512]{1,0:T(8,128)(2,1)}, u32[]{:S(2)}, u32[]{:S(2)}) collective-permute-start(bf16[224,512]{1,0:T(8,128)(2,1)} %get-tuple-element.80), channel_id=1, source_target_pairs={{0,6},{1,7},{2,0},{3,1},{4,2},{5,3},{6,4},{7,5},{8,14},{9,15},{10,... | collective-permute-start | bytes 688136 | tf_op jit(solution)/shard_map/ppermute | solution.py:38
  140.4 18.2 %copy-start.13 = (bf16[2,448,512]{2,1,0:T(8,128)(2,1)S(1)}, bf16[2,448,512]{2,1,0:T(8,128)(2,1)}, u32[]{:S(2)}) copy-start(bf16[2,448,512]{2,1,0:T(8,128)(2,1)} %get-tuple-element.69) | copy-start | bytes 2752516
  150.4 12.1 %copy-start.17 = (bf16[2,448,512]{2,1,0:T(8,128)(2,1)S(1)}, bf16[2,448,512]{2,1,0:T(8,128)(2,1)}, u32[]{:S(2)}) copy-start(bf16[2,448,512]{2,1,0:T(8,128)(2,1)} %get-tuple-element.66) | copy-start | bytes 2752516
  159.8 11.8 %collective-permute-start.34 = (bf16[448,512]{1,0:T(8,128)(2,1)S(1)}, bf16[448,512]{1,0:T(8,128)(2,1)S(1)}, u32[]{:S(2)}, u32[]{:S(2)}) collective-permute-start(bf16[448,512]{1,0:T(8,128)(2,1)S(1)} %fusion.4), channel_id=1, source_target_pairs={{0,8},{1,9},{2,10},{3,11},{4,12},{5,13},{6,14},{7,15},{8,0},{9,1},... | collective-permute-start | bytes 1376264 | tf_op jit(solution)/shard_map/ppermute | solution.py:42
  162.7 8.9 %copy-start.11 = (bf16[1,448,512]{2,1,0:T(8,128)(2,1)S(1)}, bf16[1,448,512]{2,1,0:T(8,128)(2,1)}, u32[]{:S(2)}) copy-start(bf16[1,448,512]{2,1,0:T(8,128)(2,1)} %param.12) | copy-start | bytes 1376260
  162.7 8.9 %copy-start.14 = (bf16[2,448,512]{2,1,0:T(8,128)(2,1)S(1)}, bf16[2,448,512]{2,1,0:T(8,128)(2,1)}, u32[]{:S(2)}) copy-start(bf16[2,448,512]{2,1,0:T(8,128)(2,1)} %get-tuple-element.69) | copy-start | bytes 2752516
  162.7 8.9 %copy-start.16 = (bf16[2,448,512]{2,1,0:T(8,128)(2,1)S(1)}, bf16[2,448,512]{2,1,0:T(8,128)(2,1)}, u32[]{:S(2)}) copy-start(bf16[2,448,512]{2,1,0:T(8,128)(2,1)} %copy-done.15) | copy-start | bytes 2752516
  162.7 8.9 %copy-start.28 = (f32[1,448]{1,0:T(1,128)S(1)}, f32[1,448]{1,0:T(1,128)}, u32[]{:S(2)}) copy-start(f32[1,448]{1,0:T(1,128)} %dynamic-slice_convert_fusion) | copy-start | bytes 5380
  163.9 15.0 %collective-permute-start.32 = (bf16[448,512]{1,0:T(8,128)(2,1)S(1)}, bf16[448,512]{1,0:T(8,128)(2,1)S(1)}, u32[]{:S(2)}, u32[]{:S(2)}) collective-permute-start(bf16[448,512]{1,0:T(8,128)(2,1)S(1)} %pad_maximum_fusion.1), channel_id=1, source_target_pairs={{0,2},{1,3},{2,4},{3,5},{4,6},{5,7},{6,0},{7,1},{8,10},{9,11},{10,... | collective-permute-start | bytes 1376264 | tf_op jit(solution)/shard_map/ppermute | solution.py:34
  164.9 22.6 %copy-start.12 = (bf16[1,448,512]{2,1,0:T(8,128)(2,1)S(1)}, bf16[1,448,512]{2,1,0:T(8,128)(2,1)}, u32[]{:S(2)}) copy-start(bf16[1,448,512]{2,1,0:T(8,128)(2,1)} %param.11) | copy-start | bytes 1376260
  165.0 22.6 %copy-start.23 = (bf16[1,448,512]{2,1,0:T(8,128)(2,1)S(1)}, bf16[1,448,512]{2,1,0:T(8,128)(2,1)}, u32[]{:S(2)}) copy-start(bf16[1,448,512]{2,1,0:T(8,128)(2,1)} %get-tuple-element.61) | copy-start | bytes 1376260
  165.0 13.9 %collective-permute-start.33 = (bf16[448,512]{1,0:T(8,128)(2,1)S(1)}, bf16[448,512]{1,0:T(8,128)(2,1)S(1)}, u32[]{:S(2)}, u32[]{:S(2)}) collective-permute-start(bf16[448,512]{1,0:T(8,128)(2,1)S(1)} %pad_maximum_fusion.2), channel_id=1, source_target_pairs={{0,6},{1,7},{2,0},{3,1},{4,2},{5,3},{6,4},{7,5},{8,14},{9,15},{10,... | collective-permute-start | bytes 1376264 | tf_op jit(solution)/shard_map/ppermute | solution.py:38
  173.1 14.5 %collective-permute-start.35 = (bf16[448,512]{1,0:T(8,128)(2,1)S(1)}, bf16[448,512]{1,0:T(8,128)(2,1)S(1)}, u32[]{:S(2)}, u32[]{:S(2)}) collective-permute-start(bf16[448,512]{1,0:T(8,128)(2,1)S(1)} %get-tuple-element.75), channel_id=1, source_target_pairs={{0,112},{16,96},{32,80},{48,64},{64,48},{80,32},{96,16},{112,0},{1... | collective-permute-start | bytes 1376264 | tf_op jit(solution)/shard_map/ppermute | solution.py:51
  178.9 10.0 %collective-permute-start.36 = (bf16[448]{0:T(512)(128)(2,1)S(1)}, bf16[448]{0:T(512)(128)(2,1)S(1)}, u32[]{:S(2)}, u32[]{:S(2)}) collective-permute-start(bf16[448]{0:T(512)(128)(2,1)S(1)} %get-tuple-element.74), channel_id=1, source_target_pairs={{0,112},{16,96},{32,80},{48,64},{64,48},{80,32},{96,16},{112,0},{1... | collective-permute-start | bytes 2696 | tf_op jit(solution)/shard_map/ppermute | solution.py:51
  187.6 1.9 %copy-start.1 = (bf16[2,64,7168]{2,1,0:T(8,128)(2,1)S(1)}, bf16[2,64,7168]{2,1,0:T(8,128)(2,1)}, u32[]{:S(2)}) copy-start(bf16[2,64,7168]{2,1,0:T(8,128)(2,1)} %param.15) | copy-start | bytes 5505028
  (5 other events, 4.4 us)
where the time goes:
time: 190 us; the launch traced here: 189 us
  waiting for transfers between devices  58.6 us (31%)
  starting transfers between devices  50.6 us (27%)
  Pallas kernels  49.8 us (26%)
  other arithmetic  14.4 us (8%)
  local copies, waits for them, and re-layouts  13.2 us (7%)
    pallas_call x2, Pallas kernels, products(): pl.pallas_call(kernel, grid=(1,), in_specs=[pl.BlockSpec(memory_space=plt...  20.6 us
    ppermute x6, waiting for transfers between devices, to_across(): lax.ppermute(block, 'fsdp', fsdp_route(lambda x, y, core: (x + 1, y, core)))  20.2 us
    pallas_call x2, Pallas kernels, layer(): pl.pallas_call(kernel, grid=(1,), in_specs=[pl.BlockSpec(memory_space=plt...  19.9 us
    ppermute x7, starting transfers between devices, to_previous(): lax.ppermute(block, 'fsdp', fsdp_route(lambda x, y, core: (x, y - 1, core)))  14.3 us
    ppermute x7, waiting for transfers between devices, to_next(): lax.ppermute(block, 'fsdp', fsdp_route(lambda x, y, core: (x, y + 1, core)))  14.1 us
    ppermute x6, starting transfers between devices, to_across(): lax.ppermute(block, 'fsdp', fsdp_route(lambda x, y, core: (x + 1, y, core)))  13.8 us
    ppermute x13, waiting for transfers between devices, to_sibling(): lax.ppermute(block, 'fsdp', fsdp_route(lambda x, y, core: (x, y, core + 1)))  9.3 us
    pallas_call x1, Pallas kernels, prepare(): pl.pallas_call(prepare_kernel, grid=(pipes, tokens // tile), in_specs=[pl...  9.27 us
  transfers between devices with their start and end apart: 38, of which 12 were waited for; matrix products, arithmetic and copies ran while one was open for 12% of the time, Pallas kernels for 21%

commit v1 on v0

v1 whole, which is shorter than its diff:
```python
import jax
import jax.numpy as jnp
from jax import lax
from jax.experimental import pallas as pl
from jax.experimental.pallas import tpu as pltpu
from jax.sharding import PartitionSpec as P

BLOCK_ROWS = 4
CAP = 2
EPSILON = 1e-05
HEAD = 128
VMEM_BYTES = 60 * 1024 * 1024
SMALL = pl.CostEstimate(flops=1, bytes_accessed=1, transcendentals=0)
F32 = jnp.float32
BF16 = jnp.bfloat16

X_CHIPS, Y_CHIPS = 2, 4
CHIPS = X_CHIPS * Y_CHIPS
CORE, LIVE, FLAG, PART, PIPE, X_HALF = 8, 9, 10, 12, 15, 16


def fsdp_route(step):
    route = []
    for x in range(X_CHIPS):
        for y in range(Y_CHIPS):
            for core in range(2):
                to_x, to_y, to_core = step(x, y, core)
                target = (to_x % X_CHIPS * Y_CHIPS + to_y % Y_CHIPS) * 2 + to_core % 2
                route.append(((x * Y_CHIPS + y) * 2 + core, target))
    return route


def to_next(block):
    return lax.ppermute(block, "fsdp", fsdp_route(lambda x, y, core: (x, y + 1, core)))


def to_previous(block):
    return lax.ppermute(block, "fsdp", fsdp_route(lambda x, y, core: (x, y - 1, core)))


def to_across(block):
    return lax.ppermute(block, "fsdp", fsdp_route(lambda x, y, core: (x + 1, y, core)))


def to_sibling(block):
    return lax.ppermute(block, "fsdp", fsdp_route(lambda x, y, core: (x, y, core + 1)))


def to_mirror(block, flip):
    sections, fsdps = lax.axis_size("section"), lax.axis_size("fsdp")
    route = []
    for section in range(sections):
        for fsdp in range(fsdps):
            to_fsdp = (fsdp + flip * fsdps // X_CHIPS) % fsdps
            route.append((section * fsdps + fsdp, (sections - 1 - section) * fsdps + to_fsdp))
    return lax.ppermute(block, ("section", "fsdp"), route)


def columns(chip, size):
    return pl.ds(pl.multiple_of(chip * size, 128), size)


def inverse_rms(rows):
    tokens, width = rows.shape
    pair = width // CHIPS
    total = jnp.zeros((tokens, pair), F32)
    for chip in range(CHIPS):
        part = rows[:, chip * pair : (chip + 1) * pair].astype(F32)
        total = total + part * part
    return lax.rsqrt(jnp.sum(total, axis=1, keepdims=True) / width + EPSILON)


def scale_kernel(x_ref, ct_ref, ct_out, inverse_out):
    inverse = inverse_rms(x_ref.at[0, 0])
    ct_out[0, 0] = (ct_ref[0, 0].astype(F32) * inverse).astype(BF16)
    inverse_out[0] = jnp.broadcast_to(inverse, inverse_out.shape[1:])


def scale(section_inputs, cotangent):
    pipes, _, tokens, width = section_inputs.shape
    kv = cotangent.shape[3]
    tile = 64
    ct_spec = pl.BlockSpec((1, 1, tile, kv), lambda p, t: (p, 0, t, 0))
    return pl.pallas_call(
        scale_kernel,
        grid=(pipes, tokens // tile),
        in_specs=[pl.BlockSpec((1, 1, tile, width), lambda p, t: (p, 0, t, 0)), ct_spec],
        out_specs=[ct_spec, pl.BlockSpec((1, tile, 128), lambda p, t: (p, t, 0))],
        out_shape=[
            jax.ShapeDtypeStruct(cotangent.shape, BF16),
            jax.ShapeDtypeStruct((pipes, tokens, 128), F32),
        ],
        compiler_params=pltpu.CompilerParams(vmem_limit_bytes=VMEM_BYTES),
        cost_estimate=SMALL,
        name="scale",
    )(section_inputs, cotangent)


def patch_kernel(table, x_ref, ct_ref, perm_ref, im0, im1, im2, ct_in, inverse_in, head_ref, ct_out, inverse_out):
    pipe = table[PIPE]
    head_ref[...] = x_ref[0, 0]
    ct_out[...] = ct_in[...]
    inverse_out[...] = inverse_in[...]

    @pl.when(table[FLAG + pipe] == 1)
    def _():
        live = lax.broadcasted_iota(jnp.int32, (HEAD, 1), 0) < table[LIVE]
        for part, image in enumerate((im0, im1, im2)):
            where = pl.ds(pl.multiple_of(table[PART + part], 128), image.shape[1])
            arrived = jnp.dot(perm_ref[...], image[...], preferred_element_type=F32).astype(BF16)
            head_ref[:, where] = jnp.where(live, arrived, head_ref[:, where])
        inverse = inverse_rms(head_ref)
        ct_out[pipe, 0, :HEAD] = (ct_ref[0, 0].astype(F32) * inverse).astype(BF16)
        inverse_out[pipe, :HEAD] = jnp.broadcast_to(inverse, (HEAD, inverse_out.shape[2]))


def patch(table, section_inputs, cotangent, perm, images, scaled_ct, inverse):
    width = section_inputs.shape[3]
    kv = cotangent.shape[3]
    whole = pl.BlockSpec(memory_space=pltpu.VMEM)
    return pl.pallas_call(
        patch_kernel,
        grid_spec=pltpu.PrefetchScalarGridSpec(
            num_scalar_prefetch=1,
            grid=(1,),
            in_specs=[
                pl.BlockSpec((1, 1, HEAD, width), lambda i, table: (table[PIPE], 0, 0, 0)),
                pl.BlockSpec((1, 1, HEAD, kv), lambda i, table: (table[PIPE], 0, 0, 0)),
            ]
            + [whole] * 6,
            out_specs=[whole] * 3,
        ),
        out_shape=[
            jax.ShapeDtypeStruct((HEAD, width), BF16),
            jax.ShapeDtypeStruct(scaled_ct.shape, BF16),
            jax.ShapeDtypeStruct(inverse.shape, F32),
        ],
        compiler_params=pltpu.CompilerParams(vmem_limit_bytes=VMEM_BYTES),
        cost_estimate=SMALL,
        name="patch",
    )(table, section_inputs, cotangent, perm, *images, scaled_ct, inverse)


def pack(parts):
    count = len(parts)
    shape = parts[0][0].shape[-2:]

    def kernel(*refs):
        out, sems = refs[count:]
        copies = []
        for place, (ref, (_, at)) in enumerate(zip(refs, parts)):
            source = ref if at is None else ref.at[at]
            copies.append(pltpu.make_async_copy(source, out.at[place], sems.at[place]))
        for copy in copies:
            copy.start()
        for copy in copies:
            copy.wait()

    anywhere = pl.BlockSpec(memory_space=pl.ANY)
    return pl.pallas_call(
        kernel,
        in_specs=[anywhere] * count,
        out_specs=pl.BlockSpec(memory_space=pltpu.VMEM),
        out_shape=jax.ShapeDtypeStruct((count, *shape), BF16),
        scratch_shapes=[pltpu.SemaphoreType.DMA((count,))],
        compiler_params=pltpu.CompilerParams(vmem_limit_bytes=VMEM_BYTES),
        cost_estimate=SMALL,
        name="pack",
    )(*[array for array, _ in parts])


def start_columns(table, pipe, x_ref, head_ref, rows, sems, from_x, to_rows):
    flag = table[FLAG + pipe] == 1
    tail = pl.ds(HEAD, rows.shape[0] - HEAD)
    top = rows.at[pl.ds(0, HEAD), to_rows]
    plain = pltpu.make_async_copy(x_ref.at[pipe, 0, pl.ds(0, HEAD), from_x], top, sems.at[0])
    placed = pltpu.make_async_copy(head_ref.at[:, from_x], top, sems.at[0])
    rest = pltpu.make_async_copy(x_ref.at[pipe, 0, tail, from_x], rows.at[tail, to_rows], sems.at[1])
    pl.when(flag)(placed.start)
    pl.when(jnp.logical_not(flag))(plain.start)
    rest.start()
    return [plain, rest]


def products(table, x, sibling_x, head, sibling_head, ct, sibling_ct, groups):
    pipes, _, tokens, width = x.shape
    pair = width // CHIPS
    half = pair // 2
    window = -(-half // 128) * 128
    kv = ct.shape[3]
    order = [(g, i, *block) for g, group in enumerate(groups) for i, block in enumerate(group)]
    count = len(order)

    def kernel(table, x_ref, sibling_x_ref, head_ref, sibling_head_ref, own_ct, other_ct, *refs):
        outs = refs[: len(groups)]
        own, other, block, row_sems, out_sems = refs[len(groups) :]
        core = table[CORE]
        waits = []
        for n, (_, _, pipe, r) in enumerate(order):
            from_x = pl.ds(pl.multiple_of(table[r] * pair + core * (pair - window), 128), window)
            here = pl.ds(n * window, window)
            waits.append(
                start_columns(table, pipe, x_ref, head_ref, own, row_sems.at[n, 0], from_x, here)
                + start_columns(
                    table, pipe, sibling_x_ref, sibling_head_ref, other, row_sems.at[n, 1], from_x, here
                )
            )
        contract = (((0,), (0,)), ((), ()))
        written = []
        for n, (out, at, pipe, r) in enumerate(order):
            for copy in waits[n]:
                copy.wait()
            here = slice(n * window, (n + 1) * window)
            product = lax.dot_general(own[:, here], own_ct[pipe, 0], contract, preferred_element_type=F32)
            product += lax.dot_general(
                other[:, here], other_ct[pipe, 0], contract, preferred_element_type=F32
            )
            product = product.astype(BF16)

            @pl.when(core == 0)
            def _():
                block[n] = product[:half]

            @pl.when(core == 1)
            def _():
                block[n] = product[window - half :]

            copy = pltpu.make_async_copy(block.at[n], outs[out].at[at], out_sems.at[n])
            copy.start()
            written.append(copy)
        for copy in written:
            copy.wait()

    anywhere = pl.BlockSpec(memory_space=pl.ANY)
    whole = pl.BlockSpec(memory_space=pltpu.VMEM)
    return pl.pallas_call(
        kernel,
        in_specs=[pl.BlockSpec(memory_space=pltpu.SMEM)] + [anywhere] * 4 + [whole] * 2,
        out_specs=[anywhere for _ in groups],
        out_shape=[jax.ShapeDtypeStruct((len(g), half, kv), BF16) for g in groups],
        scratch_shapes=[
            pltpu.VMEM((tokens, count * window), BF16),
            pltpu.VMEM((tokens, count * window), BF16),
            pltpu.VMEM((count, half, kv), BF16),
            pltpu.SemaphoreType.DMA((count, 2, 2)),
            pltpu.SemaphoreType.DMA((count,)),
        ],
        compiler_params=pltpu.CompilerParams(vmem_limit_bytes=VMEM_BYTES),
        cost_estimate=SMALL,
        name="products",
    )(table, x, sibling_x, head, sibling_head, ct, sibling_ct)


def on_blocks(name, kernel, operands, outs):
    specs, arrays = [], []
    for operand in operands:
        array, at = operand if isinstance(operand, tuple) else (operand, None)
        shape = array.shape
        if len(shape) == 1:
            specs.append(pl.BlockSpec(memory_space=pltpu.SMEM))
        elif at is None:
            specs.append(pl.BlockSpec(shape, lambda i, n=len(shape): (0,) * n))
        else:
            specs.append(pl.BlockSpec((pl.squeezed, *shape[1:]), lambda i, at=at: (at, 0, 0)))
        arrays.append(array)
    return pl.pallas_call(
        kernel,
        grid=(1,),
        in_specs=specs,
        out_specs=[pl.BlockSpec(out.shape, lambda i, n=len(out.shape): (0,) * n) for out in outs],
        out_shape=outs,
        compiler_params=pltpu.CompilerParams(vmem_limit_bytes=VMEM_BYTES),
        cost_estimate=SMALL,
        name=name,
    )(*arrays)


def wide(*refs):
    total = refs[0][...].astype(F32)
    for ref in refs[1:]:
        total = total + ref[...].astype(F32)
    return total


def first_sums(near0, far0, near1, back1, far1, back0, keep2, came2, up, down):
    rows = near0.shape[0]
    half = rows // 2
    far = wide(keep2, came2).astype(BF16)
    up[:rows] = wide(near0, far0).astype(BF16)
    up[rows : 2 * rows] = near1[...]
    up[2 * rows :] = far[:half]
    down[:rows] = wide(back1, far1).astype(BF16)
    down[rows : 2 * rows] = back0[...]
    down[2 * rows :] = far[half:]


def gain_row(weight, share):
    products = weight[...].astype(F32) * share
    total = products[:, :128]
    for low in range(128, products.shape[1], 128):
        total = total + products[:, low : low + 128]
    return jnp.sum(jnp.transpose(total), axis=0, keepdims=True)


def gain_column(table, gain, chip):
    pair = gain.shape[1] // CHIPS
    both = gain[:, columns(chip, pair)].astype(F32)
    row = jnp.where(table[CORE] == 0, both[:, : pair // 2], both[:, pair // 2 :])
    return jnp.transpose(jnp.broadcast_to(row, (8, pair // 2)))[:, :1]


def mirror_sums(table, own0, own1, below, above, weight0, weight1, gain, here, there):
    rows = own0.shape[0]
    for out, own, low, high, weight, chip in (
        (here, own0, 0, rows, weight0, table[0]),
        (there, own1, rows, 0, weight1, table[Y_CHIPS]),
    ):
        share = wide(own, below.at[low : low + rows], above.at[high : high + rows])
        out[:rows] = (share * gain_column(table, gain, chip)).astype(BF16)
        out[rows:] = jnp.zeros((out.shape[0] - rows, out.shape[1]), BF16)
        out[rows : rows + 8, :rows] = jnp.broadcast_to(gain_row(weight, share), (8, rows)).astype(BF16)


def second_sums(keep1, came1, below, keep3, came3, above, ups, downs):
    rows = ups.shape[0]
    half = rows // 2
    ups[...] = wide(keep1, came1).astype(BF16)
    downs[...] = wide(keep3, came3).astype(BF16)
    ups[:half] = wide(ups.at[:half], below.at[2 * rows :]).astype(BF16)
    downs[half:] = wide(downs.at[half:], above.at[2 * rows :]).astype(BF16)


def last_sums(table, keep0, came0, below, above, weight, gain, mirrored0, mirrored1, weight_grad, gain_grad):
    share = wide(keep0, came0, below, above)
    rows = share.shape[0]
    moved = wide(mirrored0, mirrored1)
    weight_grad[0] = share * gain_column(table, gain, table[0]) + moved[:rows]
    gain_grad[...] = gain_row(weight, share) + moved[rows : rows + 1, :rows]


def layer(pipe, table, x, head, cotangent, scaled_ct, inverse, gain, own, sibling, carried):
    _, _, tokens, width = x.shape
    pair = width // CHIPS
    half = pair // 2
    kv = cotangent.shape[3]
    arrays = []
    for array, _ in [*own, *sibling]:
        if not any(array is known for known in arrays):
            arrays.append(array)
    position = [
        next(i for i, known in enumerate(arrays) if known is array) for array, _ in [*own, *sibling]
    ]
    index = [at for _, at in [*own, *sibling]]

    def kernel(table, x_ref, head_ref, ct_ref, scaled_ref, inverse_ref, gain_ref, *refs):
        pieces = refs[: len(arrays)]
        values_ref, grad_ref, rows, weight, grad, w_sems, x_sems, out_sems = refs[-8:]
        core = table[CORE]
        size = width // X_CHIPS
        row_waits = []
        for flip in range(X_CHIPS):
            half_x = table[X_HALF] if flip == 0 else 1 - table[X_HALF]
            where = columns(half_x, size)
            row_waits.append(start_columns(table, pipe, x_ref, head_ref, rows, x_sems.at[flip], where, where))
        waits = []
        for r in range(CHIPS):
            copies = []
            for side in range(2):
                piece = side * CHIPS + r
                source = pieces[position[piece]]
                if index[piece] is not None:
                    source = source.at[index[piece]]
                at = table[r] * pair + (core if side == 0 else 1 - core) * half
                copy = pltpu.make_async_copy(
                    source, weight.at[pl.ds(pl.multiple_of(at, 64), half)], w_sems.at[piece]
                )
                copy.start()
                copies.append(copy)
            waits.append(copies)
        values = jnp.zeros((tokens, kv), F32)
        for r in range(CHIPS):
            for copy in waits[r]:
                copy.wait()
            while row_waits[r // Y_CHIPS]:
                row_waits[r // Y_CHIPS].pop().wait()
            where = columns(table[r], pair)
            block = weight[pl.ds(pl.multiple_of(table[r] * pair, 128), pair)]
            values += jnp.dot(rows[:, where] * gain_ref[:, where], block, preferred_element_type=F32)
        inv = inverse_ref[0, :, :1]
        values = values * inv
        values_ref[0, 0] = values.astype(BF16)
        centre = jnp.sum(values * ct_ref[0, 0].astype(F32), axis=1, keepdims=True) / width
        pull = inv * inv * centre
        outs = []
        for chip in range(CHIPS):
            where = slice(chip * pair, (chip + 1) * pair)
            back = lax.dot_general(
                scaled_ref[0, 0], weight[where], (((1,), (1,)), ((), ())), preferred_element_type=F32
            )
            grad[:, where] = (
                back * gain_ref[:, where].astype(F32) - rows[:, where].astype(F32) * pull
            ).astype(BF16)
            if chip % 2 == 1:
                done = pl.ds((chip - 1) * pair, 2 * pair)
                copy = pltpu.make_async_copy(
                    grad.at[:, done], grad_ref.at[pipe, 0, :, done], out_sems.at[chip // 2]
                )
                copy.start()
                outs.append(copy)
        for copy in outs:
            copy.wait()

    anywhere = pl.BlockSpec(memory_space=pl.ANY)
    ct_spec = pl.BlockSpec((1, 1, tokens, kv), lambda i: (pipe, 0, 0, 0))
    operands = [table, x, head, cotangent, scaled_ct, inverse, gain, *arrays, *carried]
    return pl.pallas_call(
        kernel,
        grid=(1,),
        in_specs=[
            pl.BlockSpec(memory_space=pltpu.SMEM),
            anywhere,
            anywhere,
            ct_spec,
            ct_spec,
            pl.BlockSpec((1, tokens, 128), lambda i: (pipe, 0, 0)),
            pl.BlockSpec((1, width), lambda i: (0, 0)),
        ]
        + [anywhere] * (len(arrays) + len(carried)),
        out_specs=[ct_spec, anywhere],
        out_shape=[
            jax.ShapeDtypeStruct(cotangent.shape, BF16),
            jax.ShapeDtypeStruct(x.shape, BF16),
        ],
        scratch_shapes=[
            pltpu.VMEM((tokens, width), BF16),
            pltpu.VMEM((width, kv), BF16),
            pltpu.VMEM((tokens, width), BF16),
            pltpu.SemaphoreType.DMA((2 * CHIPS,)),
            pltpu.SemaphoreType.DMA((X_CHIPS, 2)),
            pltpu.SemaphoreType.DMA((CHIPS // 2,)),
        ],
        input_output_aliases={7 + len(arrays) + i: i for i in range(len(carried))},
        compiler_params=pltpu.CompilerParams(vmem_limit_bytes=VMEM_BYTES),
        cost_estimate=SMALL,
        name="layer",
    )(*operands)


def route_images(image_rows, image_route, section_place, fsdp_place):
    fsdp_count = lax.axis_size("fsdp")
    section_count = lax.axis_size("section")
    ring = section_count // 2
    width = image_rows.shape[2]
    size = -(-width // (3 * 128)) * 128
    pipe = section_place // ring
    z = section_place % ring
    enc_rows = image_rows.shape[1]
    enc_count = enc_rows // BLOCK_ROWS
    head = fsdp_count * CAP * BLOCK_ROWS
    routes = lax.dynamic_index_in_dim(image_route, pipe, 0, keepdims=False)
    own_route = lax.dynamic_index_in_dim(routes, fsdp_place, 0, keepdims=False)
    ids = jnp.arange(enc_count, dtype=jnp.int32)
    earlier = (own_route[:, None] == own_route[None, :]) & (ids[None, :] < ids[:, None])
    slot_of = own_route * CAP + jnp.sum(earlier.astype(jnp.int32), axis=1)
    goes_to = jnp.repeat(slot_of * BLOCK_ROWS, BLOCK_ROWS) + jnp.tile(
        jnp.arange(BLOCK_ROWS, dtype=jnp.int32), enc_count
    )
    row_ids = jnp.arange(head, dtype=jnp.int32)
    select = (row_ids[:, None] == goes_to[None, :]).astype(BF16)
    from_end = jnp.where(pipe == 0, z, ring - 1 - z)
    own_part = jnp.where(from_end == ring - 1, 2, jnp.minimum(from_end, 1))
    starts = jnp.array([0, size, width - size], jnp.int32)
    start = jnp.where(own_part == 0, 0, jnp.where(own_part == 1, size, width - size))
    part = lax.dynamic_slice(image_rows, (pipe, 0, start), (1, enc_rows, size))[0]
    outgoing = jnp.dot(select, part, preferred_element_type=F32).astype(BF16)
    incoming = lax.all_to_all(outgoing, "fsdp", split_axis=0, concat_axis=0, tiled=True)
    end = section_count - 1
    arrivals = jnp.sum((routes == fsdp_place).astype(jnp.int32), axis=1)
    offsets = jnp.cumsum(arrivals) - arrivals
    slot_rows = CAP * BLOCK_ROWS
    within = row_ids % slot_rows
    lands = jnp.repeat(offsets, slot_rows) * BLOCK_ROWS + within
    valid = within < jnp.repeat(arrivals, slot_rows) * BLOCK_ROWS
    lands = jnp.where(valid, lands, -1)
    perm = (jnp.arange(head, dtype=jnp.int32)[:, None] == lands[None, :]).astype(BF16)
    numbers = jnp.concatenate(
        [
            (jnp.sum(arrivals) * BLOCK_ROWS)[None],
            (section_place == 0).astype(jnp.int32)[None],
            (section_place == end).astype(jnp.int32)[None],
            starts,
            pipe[None],
        ]
    )
    return incoming, perm, numbers


def move_images(incoming):
    count = lax.axis_size("section")
    ring, end = count // 2, count - 1
    return [
        incoming,
        lax.ppermute(incoming, "section", [(1, 0), (end - 1, end)]),
        lax.ppermute(incoming, "section", [(ring - 1, 0), (end - ring + 1, end)]),
    ]


def hold(value, *before):
    return lax.optimization_barrier((value, before))[0]


def per_device(
    section_inputs,
    value_cotangent,
    down_weight,
    up_weight,
    down_gain,
    up_gain,
    image_rows,
    image_route,
):
    section_place = lax.axis_index("section")
    fsdp_place = lax.axis_index("fsdp")
    core = fsdp_place % 2
    y = fsdp_place // 2 % Y_CHIPS
    x = fsdp_place // (2 * Y_CHIPS)
    r = jnp.arange(CHIPS, dtype=jnp.int32)
    chips = (x ^ (r // Y_CHIPS)) * Y_CHIPS + (y + r % Y_CHIPS) % Y_CHIPS

    incoming, perm, numbers = route_images(image_rows, image_route, section_place, fsdp_place)
    table = jnp.concatenate([chips, core[None], numbers, x[None]]).astype(jnp.int32)

    shard, kv = down_weight.shape[1:]

    part = jax.ShapeDtypeStruct((shard, kv), BF16)

    sibling_x = to_sibling(section_inputs)
    w0 = pack([(down_weight, 0), (up_weight, 0)])
    w3, w1, w4 = to_next(w0), to_previous(w0), to_across(w0)
    scaled_ct, inverse = scale(section_inputs, value_cotangent)
    w3, w1, w4, incoming = hold((w3, w1, w4, incoming), scaled_ct, sibling_x)
    images = move_images(incoming)
    w2, w5, w7 = to_next(w3), to_previous(w4), to_across(w3)
    early = pack([(w0, 0), (w0, 1), (w1, 0), (w1, 1), (w3, 0), (w3, 1), (w4, 0), (w4, 1)])
    head, scaled_ct, inverse = patch(
        hold(table, early), section_inputs, value_cotangent, perm, images, scaled_ct, inverse
    )
    w2, w5, w7, head, scaled_ct = hold((w2, w5, w7, head, scaled_ct))
    sibling_head, sibling_ct = to_sibling(head), to_sibling(scaled_ct)
    down6, up6 = to_next(w7[0]), to_previous(w5[1])

    rows = (section_inputs, sibling_x, head, sibling_head, scaled_ct, sibling_ct)
    far0, far1, send2 = products(table, *rows, (((1, 2),), ((1, 6),), ((0, 6),)))
    middle = pack([(w2, 0), (w2, 1), (w5, 0), (w5, 1), (w7, 0), (hold(w7, far0), 1)])
    far0, far1, send2, down6, up6, middle = hold((far0, far1, send2, down6, up6, middle))
    from_below, from_above, came = to_next(far0[0]), to_previous(far1[0]), to_across(send2[0])
    sibling_early, sibling_middle = to_sibling(early), to_sibling(middle)
    near0, near1, back1, back0, keep2, send130, own01, keep13, keep0 = products(
        hold(table, middle),
        *rows,
        (
            ((1, 1),), ((1, 5),), ((1, 7),), ((1, 3),), ((0, 2),),
            ((0, 5), (0, 7), (0, 4)), ((1, 0), (1, 4)), ((0, 1), (0, 3)), ((0, 0),),
        ),
    )
    from_below, from_above, came = hold((from_below, from_above, came), keep0, sibling_early, sibling_middle)
    message = jax.ShapeDtypeStruct((2 * shard + shard // 2, kv), BF16)
    up, down = on_blocks(
        "first_sums",
        first_sums,
        [(near0, 0), from_below, (near1, 0), (back1, 0), from_above, (back0, 0), (keep2, 0), came],
        [message, message],
    )
    below, above = to_next(up), to_previous(down)
    came130 = to_across(hold(send130, up))

    down_places = ((0, 0), (0, 2), (1, 0), (0, 4), (0, 6), (1, 2), (2, None), (1, 4))
    up_places = ((0, 1), (0, 3), (1, 1), (0, 5), (0, 7), (1, 3), (3, None), (1, 5))
    own = (early, middle, down6, up6)
    sibling = (sibling_early, sibling_middle, to_sibling(hold(down6, up)), to_sibling(hold(up6, up)))

    def pieces(arrays, places):
        return [(arrays[array], at) for array, at in places]

    filled = layer(
        0,
        hold(table, up),
        section_inputs, head, value_cotangent, scaled_ct, inverse, down_gain,
        pieces(own, down_places), pieces(sibling, down_places), (),
    )
    below, above = hold((below, above), filled[0])
    payload = jax.ShapeDtypeStruct((shard + 16, kv), BF16)
    here, there = on_blocks(
        "mirror_sums",
        mirror_sums,
        [
            table, (own01, 0), (own01, 1), below, above, (up_weight, 0), (early, 7), up_gain,
        ],
        [payload, payload],
    )
    mirrored0, mirrored1 = to_mirror(here, 0), to_mirror(there, 1)
    ups, downs = on_blocks(
        "second_sums",
        second_sums,
        [(keep13, 0), (came130, 0), below, (keep13, 1), (came130, 1), above],
        [part, part],
    )
    last_below, last_above = to_next(ups), to_previous(downs)
    values, input_grad = layer(
        1,
        hold(table, ups),
        section_inputs, head, value_cotangent, scaled_ct, inverse, up_gain,
        pieces(own, up_places), pieces(sibling, up_places), tuple(filled),
    )
    mirrored0, mirrored1, last_below, last_above = hold((mirrored0, mirrored1, last_below, last_above), values)
    weight_grad, gain_grad = on_blocks(
        "last_sums",
        last_sums,
        [
            table, (keep0, 0), (came130, 2), last_below, last_above, (down_weight, 0), down_gain, mirrored0, mirrored1,
        ],
        [jax.ShapeDtypeStruct((1, shard, kv), F32), jax.ShapeDtypeStruct((1, shard), F32)],
    )
    return (values, input_grad, weight_grad, gain_grad)


def solution(mesh):
    return jax.shard_map(
        per_device,
        mesh=mesh,
        in_specs=(
            P(None, "section", "fsdp", None),
            P(None, "section", "fsdp", None),
            P("section", "fsdp", None),
            P("section", "fsdp", None),
            P("section", None),
            P("section", None),
            P(None, "fsdp", None),
            P(),
        ),
        out_specs=(
            P(None, "section", "fsdp", None),
            P(None, "section", "fsdp", None),
            P("section", "fsdp", None),
            P("section", "fsdp"),
        ),
        check_vma=False,
    )
```

time: 190 us -> 176 us (0.926)
  Pallas kernels: 49.8 us -> 74.4 us
  waiting for transfers between devices: 58.6 us -> 42.3 us
  other arithmetic: 14.4 us -> 1.7 us
  starting transfers between devices: 50.6 us -> 43.5 us
  local copies, waits for them, and re-layouts: 13.2 us -> 10.1 us
    pallas_call x3 -> x11, Pallas kernels: 29.8 us -> 52.4 us  [the longest x2 15.3 us: products(): pl.pallas_call(kernel, in_specs=[pl.BlockSpec(memory_space=pltpu.SMEM)] +...]
    ppermute x6 -> x4, waiting for transfers between devices: 20.2 us -> 0.3 us  [to_across(): lax.ppermute(block, 'fsdp', fsdp_route(lambda x, y, core: (x + 1, y, core)))]
    all_to_all x1, waiting for transfers between devices: 0.01 us -> 16.1 us  [route_images(): lax.all_to_all(outgoing, 'fsdp', split_axis=0, concat_axis=0, tiled=True)]
    ppermute x7 -> x6, waiting for transfers between devices: 14.1 us -> 6.32 us  [to_next(): lax.ppermute(block, 'fsdp', fsdp_route(lambda x, y, core: (x, y + 1, core)))]
    ppermute x13 -> x7, waiting for transfers between devices: 9.3 us -> 1.8 us  [to_sibling(): lax.ppermute(block, 'fsdp', fsdp_route(lambda x, y, core: (x, y, core + 1)))]
    add x7 -> x0, other arithmetic: 5.58 us -> none  [the longest x1 1.13 us: per_device(): down_far = keep2[0] + came2[0]]
    ppermute x6 -> x4, starting transfers between devices: 13.8 us -> 9.19 us  [to_across(): lax.ppermute(block, 'fsdp', fsdp_route(lambda x, y, core: (x + 1, y, core)))]
    ppermute x7 -> x6, starting transfers between devices: 14.3 us -> 10.8 us  [to_previous(): lax.ppermute(block, 'fsdp', fsdp_route(lambda x, y, core: (x, y - 1, core)))]
  transfers between devices with their start and end apart: 38 -> 28, of which waited for: 12 -> 9; matrix products, arithmetic and copies ran while one was open for 12% -> 4% of each run, Pallas kernels for 21% -> 39%
where the time goes in v1:
time: 176 us; the launch traced here: 175 us
  Pallas kernels  74.4 us (42%)
  starting transfers between devices  43.5 us (25%)
  waiting for transfers between devices  42.3 us (24%)
  local copies, waits for them, and re-layouts  10.1 us (6%)
    pallas_call x2, Pallas kernels, layer(): pl.pallas_call(kernel, grid=(1,), in_specs=[pl.BlockSpec(memory_space=plt...  22 us
    all_to_all x1, waiting for transfers between devices, route_images(): lax.all_to_all(outgoing, 'fsdp', split_axis=0, concat_axis=0, tiled=True)  16.1 us
    pallas_call x2, Pallas kernels, products(): pl.pallas_call(kernel, in_specs=[pl.BlockSpec(memory_space=pltpu.SMEM)] +...  15.3 us
    pallas_call x4, Pallas kernels, on_blocks(): pl.pallas_call(kernel, grid=(1,), in_specs=specs, out_specs=[pl.BlockSpec...  14.4 us
    ppermute x6, starting transfers between devices, to_previous(): lax.ppermute(block, 'fsdp', fsdp_route(lambda x, y, core: (x, y - 1, core)))  10.8 us
    ppermute x7, starting transfers between devices, to_sibling(): lax.ppermute(block, 'fsdp', fsdp_route(lambda x, y, core: (x, y, core + 1)))  9.94 us
    ppermute x1, waiting for transfers between devices, move_images(): lax.ppermute(incoming, 'section', [(ring - 1, 0), (end - ring + 1, end)])  9.34 us
    pallas_call x3, Pallas kernels, pack(): pl.pallas_call(kernel, in_specs=[anywhere] * count, out_specs=pl.BlockSpe...  9.32 us
  transfers between devices with their start and end apart: 28, of which 9 were waited for; matrix products, arithmetic and copies ran while one was open for 4% of the time, Pallas kernels for 39%

profile of v1, /device:TPU:1, one launch (start us, length us, event | category | flops | bytes accessed | tf_op | source)
XLA Modules:
  0.0 174.8 jit_solution(603424226381429766)
XLA Ops:
  0.7 1.5 collective-permute-start
  2.2 2.1 %pack.3.refs_0_.refs_1_ = bf16[2,448,512]{2,1,0:T(8,128)(2,1)} custom-call(bf16[1,448,512]{2,1,0:T(8,128)(2,1)} %weight.1, bf16[1,448,512]{2,1,0:T(8,128)(2,1)} %weight0.1), custom_call_target="tpu_custom_call" | custom-call | flops 1 | bytes 1 | tf_op jit(solution)/shard_map/pack/pallas_call | solution.py:160
  4.3 2.9 %collective-permute-start.3 = (bf16[2,448,512]{2,1,0:T(8,128)(2,1)}, bf16[2,448,512]{2,1,0:T(8,128)(2,1)}, u32[]{:S(2)}, u32[]{:S(2)}) collective-permute-start(bf16[2,448,512]{2,1,0:T(8,128)(2,1)} %pack.3.refs_0_.refs_1_), channel_id=1, source_target_pairs={{0,8},{1,9},{2,10},{3,11},{4,12},{5,13},{6,14},{7,15},{8,0},{9,1},... | collective-permute-start | bytes 2752520 | tf_op jit(solution)/shard_map/ppermute | solution.py:42
  7.2 2.7 %collective-permute-start.2 = (bf16[2,448,512]{2,1,0:T(8,128)(2,1)}, bf16[2,448,512]{2,1,0:T(8,128)(2,1)S(1)}, u32[]{:S(2)}, u32[]{:S(2)}) collective-permute-start(bf16[2,448,512]{2,1,0:T(8,128)(2,1)} %pack.3.refs_0_.refs_1_), channel_id=1, source_target_pairs={{0,6},{1,7},{2,0},{3,1},{4,2},{5,3},{6,4},{7,5},{8,14},{9,15},{10,... | collective-permute-start | bytes 2752520 | tf_op jit(solution)/shard_map/ppermute | solution.py:38
  9.9 0.2 convert_reduce_fusion.2
  10.2 0.1 add.89
  10.3 1.1 fusion
  11.4 5.2 %all-to-all-start = ((bf16[16,8,2432]{2,1,0:T(8,128)(2,1)}), bf16[16,8,2432]{2,1,0:T(8,128)(2,1)S(1)}, u32[]{:S(2)}, u32[]{:S(2)}) async-start(bf16[16,8,2432]{2,1,0:T(8,128)(2,1)} %fusion), calls=%async_computation | async-start | bytes 1245184 | tf_op jit(solution)/shard_map/all_to_all | solution.py:476
  16.7 7.3 %scale.1 = (bf16[2,1,256,512]{3,2,1,0:T(8,128)(2,1)}, f32[2,256,128]{2,1,0:T(8,128)}) custom-call(bf16[2,1,256,7168]{3,2,1,0:T(8,128)(2,1)} %x_ref.11, bf16[2,1,256,512]{3,2,1,0:T(8,128)(2,1)} %ct_ref.7), custom_call_target="tpu_custom_call" | custom-call | flops 1 | bytes 1 | tf_op jit(solution)/shard_map/scale/pallas_call | solution.py:84
  24.0 16.1 %all-to-all-done = bf16[16,8,2432]{2,1,0:T(8,128)(2,1)S(1)} async-done(((bf16[16,8,2432]{2,1,0:T(8,128)(2,1)}), bf16[16,8,2432]{2,1,0:T(8,128)(2,1)S(1)}, u32[]{:S(2)}, u32[]{:S(2)}) %all-to-all-start) | async-done | bytes 622624 | tf_op jit(solution)/shard_map/all_to_all | solution.py:476
  40.2 0.9 collective-permute-start.6
  41.1 0.8 collective-permute-start.4
  42.0 0.6 convert_reduce_fusion
  42.7 0.1 reduce.3
  42.8 1.3 collective-permute-start.8
  44.1 1.3 collective-permute-start.7
  46.2 0.1 mul.41
  46.4 0.1 mul.39
  46.5 0.6 concatenate.3.table
  47.1 0.6 fusion.3.perm_ref
  47.7 4.0 %pack.4.refs_0_.weight1 = bf16[8,448,512]{2,1,0:T(8,128)(2,1)} custom-call(bf16[2,448,512]{2,1,0:T(8,128)(2,1)} %pack.3.refs_0_.refs_1_, bf16[2,448,512]{2,1,0:T(8,128)(2,1)} %pack.3.refs_0_.refs_1_, bf16[2,448,512]{2,1,0:T(8,128)(2,1)} %copy-done.6, bf16[2,448,512]{2,1,0:T(8,128)(2,1)} %copy-done.6, ...), custom_call_target="tpu_custom_call" | custom-call | flops 1 | bytes 1 | tf_op jit(solution)/shard_map/pack/pallas_call | solution.py:160
  51.7 9.3 %collective-permute-done.8.im2 = bf16[128,2432]{1,0:T(8,128)(2,1)S(1)} collective-permute-done((bf16[128,2432]{1,0:T(8,128)(2,1)S(1)}, bf16[128,2432]{1,0:T(8,128)(2,1)S(1)}, u32[]{:S(2)}, u32[]{:S(2)}) %collective-permute-start.8) | collective-permute-done | bytes 622624 | tf_op jit(solution)/shard_map/ppermute | solution.py:504
  61.0 0.8 copy-done.8
  61.9 0.8 copy-done.9
  62.7 6.1 %patch.1 = (bf16[128,7168]{1,0:T(8,128)(2,1)}, bf16[2,1,256,512]{3,2,1,0:T(8,128)(2,1)}, f32[2,256,128]{2,1,0:T(8,128)}) custom-call(s32[17]{0:T(128)} %concatenate.3.table, bf16[2,1,256,7168]{3,2,1,0:T(8,128)(2,1)} %x_ref.11, bf16[2,1,256,512]{3,2,1,0:T(8,128)(2,1)} %ct_ref.7, bf16[128,128]{1,0:T(8,128)(2,1)} %fusion.3.perm_ref, ...), custom_call_target="tpu_custom_call" | custom-call | flops 1 | bytes 1 | tf_op jit(solution)/shard_map/patch/pallas_call | solution.py:121
  68.8 1.9 %collective-permute-start.9 = (bf16[128,7168]{1,0:T(8,128)(2,1)}, bf16[128,7168]{1,0:T(8,128)(2,1)}, u32[]{:S(2)}, u32[]{:S(2)}) collective-permute-start(bf16[128,7168]{1,0:T(8,128)(2,1)} %get-tuple-element.74.head_ref), channel_id=1, source_target_pairs={{0,1},{1,0},{2,3},{3,2},{4,5},{5,4},{6,7},{7,6},{8,9},{9,8},{10,11... | collective-permute-start | bytes 5505032 | tf_op jit(solution)/shard_map/ppermute | solution.py:46
  70.7 0.1 collective-permute-start.16
  70.8 0.4 collective-permute-start.10
  71.2 1.8 %slice_bitcast_fusion = bf16[448,512]{1,0:T(8,128)(2,1)} fusion(bf16[2,448,512]{2,1,0:T(8,128)(2,1)} %collective-permute-done.5.refs_2_.refs_3_), kind=kLoop, calls=%fused_computation.2 | loop fusion | bytes 917504 | tf_op jit(solution)/shard_map/squeeze | solution.py:550
  73.1 1.8 %slice_bitcast_fusion.1 = bf16[448,512]{1,0:T(8,128)(2,1)} fusion(bf16[2,448,512]{2,1,0:T(8,128)(2,1)} %collective-permute-done.6.refs_4_.refs_5_), kind=kLoop, calls=%fused_computation.3 | loop fusion | bytes 917504 | tf_op jit(solution)/shard_map/squeeze | solution.py:550
  74.9 2.7 %collective-permute-start.12 = (bf16[448,512]{1,0:T(8,128)(2,1)}, bf16[448,512]{1,0:T(8,128)(2,1)S(1)}, u32[]{:S(2)}, u32[]{:S(2)}) collective-permute-start(bf16[448,512]{1,0:T(8,128)(2,1)} %slice_bitcast_fusion), channel_id=1, source_target_pairs={{0,6},{1,7},{2,0},{3,1},{4,2},{5,3},{6,4},{7,5},{8,14},{9,15},{10,... | collective-permute-start | bytes 1376264 | tf_op jit(solution)/shard_map/ppermute | solution.py:38
  77.6 4.8 %products.2 = (bf16[1,448,512]{2,1,0:T(8,128)(2,1)}, bf16[1,448,512]{2,1,0:T(8,128)(2,1)}, bf16[1,448,512]{2,1,0:T(8,128)(2,1)}) custom-call(s32[17]{0:T(128)} %concatenate.3.table, bf16[2,1,256,7168]{3,2,1,0:T(8,128)(2,1)} %x_ref.11, bf16[2,1,256,7168]{3,2,1,0:T(8,128)(2,1)} %collective-permute-done.sibling_x_ref, ...), custom_call_target="tpu_custom_call" | custom-call | flops 1 | bytes 1 | tf_op jit(solution)/shard_map/products/pallas_call | solution.py:236
  82.3 3.3 %pack.5.refs_1_ = bf16[6,448,512]{2,1,0:T(8,128)(2,1)} custom-call(bf16[2,448,512]{2,1,0:T(8,128)(2,1)} %collective-permute-done.4.refs_0_.refs_1_, bf16[2,448,512]{2,1,0:T(8,128)(2,1)} %collective-permute-done.4.refs_0_.refs_1_, bf16[2,448,512]{2,1,0:T(8,128)(2,1)} %collective-permute-done.5.refs_2_.refs_3_, ...), custom_call_target="tpu_custom_call" | custom-call | flops 1 | bytes 1 | tf_op jit(solution)/shard_map/pack/pallas_call | solution.py:160
  85.6 2.9 %collective-permute-done.11.refs_2_ = bf16[448,512]{1,0:T(8,128)(2,1)} collective-permute-done((bf16[448,512]{1,0:T(8,128)(2,1)}, bf16[448,512]{1,0:T(8,128)(2,1)}, u32[]{:S(2)}, u32[]{:S(2)}) %collective-permute-start.11) | collective-permute-done | bytes 458784 | tf_op jit(solution)/shard_map/ppermute | solution.py:34
  88.5 0.9 collective-permute-start.17
  89.4 2.6 %collective-permute-start.14 = (bf16[448,512]{1,0:T(8,128)(2,1)}, bf16[448,512]{1,0:T(8,128)(2,1)}, u32[]{:S(2)}, u32[]{:S(2)}) collective-permute-start(bf16[448,512]{1,0:T(8,128)(2,1)} %bitcast.30), channel_id=1, source_target_pairs={{0,6},{1,7},{2,0},{3,1},{4,2},{5,3},{6,4},{7,5},{8,14},{9,15},{10,... | collective-permute-start | bytes 1376264 | tf_op jit(solution)/shard_map/ppermute | solution.py:38
  91.9 2.7 %collective-permute-start.15 = (bf16[448,512]{1,0:T(8,128)(2,1)}, bf16[448,512]{1,0:T(8,128)(2,1)}, u32[]{:S(2)}, u32[]{:S(2)}) collective-permute-start(bf16[448,512]{1,0:T(8,128)(2,1)} %bitcast.28), channel_id=1, source_target_pairs={{0,8},{1,9},{2,10},{3,11},{4,12},{5,13},{6,14},{7,15},{8,0},{9,1},... | collective-permute-start | bytes 1376264 | tf_op jit(solution)/shard_map/ppermute | solution.py:42
  94.6 10.5 %products.3 = (bf16[1,448,512]{2,1,0:T(8,128)(2,1)}, bf16[1,448,512]{2,1,0:T(8,128)(2,1)}, bf16[1,448,512]{2,1,0:T(8,128)(2,1)}, bf16[1,448,512]{2,1,0:T(8,128)(...) custom-call(s32[17]{0:T(128)} %concatenate.3.table, ...), custom_call_target="tpu_custom_call" | custom-call | flops 1 | bytes 1 | tf_op jit(solution)/shard_map/products/pallas_call | solution.py:236
  105.1 0.2 collective-permute-done.13.far0
  105.3 0.3 collective-permute-done.15.came2
  105.6 3.6 %first_sums.1 = (bf16[1120,512]{1,0:T(8,128)(2,1)}, bf16[1120,512]{1,0:T(8,128)(2,1)}) custom-call(bf16[1,448,512]{2,1,0:T(8,128)(2,1)} %get-tuple-element.87.near0, bf16[448,512]{1,0:T(8,128)(2,1)} %collective-permute-done.13.far0, bf16[1,448,512]{2,1,0:T(8,128)(2,1)} %get-tuple-element.93.near1, bf16[1,448,512]{2,1,0:T(8,128)(2,1)} %get-tuple-element.94.back1, ...), custom_call_target="tpu_custom_call" | custom-call | flops 1 | bytes 1 | tf_op jit(solution)/shard_map/first_sums/pallas_call | solution.py:266
  109.1 2.7 %collective-permute-start.18 = (bf16[3,448,512]{2,1,0:T(8,128)(2,1)}, bf16[3,448,512]{2,1,0:T(8,128)(2,1)S(1)}, u32[]{:S(2)}, u32[]{:S(2)}) collective-permute-start(bf16[3,448,512]{2,1,0:T(8,128)(2,1)} %get-tuple-element.100), channel_id=1, source_target_pairs={{0,8},{1,9},{2,10},{3,11},{4,12},{5,13},{6,14},{7,15},{8,0},{9,1},... | collective-permute-start | bytes 4128776 | tf_op jit(solution)/shard_map/ppermute | solution.py:42
  111.8 2.4 %collective-permute-start.20 = (bf16[1120,512]{1,0:T(8,128)(2,1)}, bf16[1120,512]{1,0:T(8,128)(2,1)S(1)}, u32[]{:S(2)}, u32[]{:S(2)}) collective-permute-start(bf16[1120,512]{1,0:T(8,128)(2,1)} %get-tuple-element.101), channel_id=1, source_target_pairs={{0,6},{1,7},{2,0},{3,1},{4,2},{5,3},{6,4},{7,5},{8,14},{9,15},{10,... | collective-permute-start | bytes 3440648 | tf_op jit(solution)/shard_map/ppermute | solution.py:38
  114.2 2.0 %collective-permute-start.21 = (bf16[448,512]{1,0:T(8,128)(2,1)}, bf16[448,512]{1,0:T(8,128)(2,1)}, u32[]{:S(2)}, u32[]{:S(2)}) collective-permute-start(bf16[448,512]{1,0:T(8,128)(2,1)} %collective-permute-done.11.refs_2_), channel_id=1, source_target_pairs={{0,1},{1,0},{2,3},{3,2},{4,5},{5,4},{6,7},{7,6},{8,9},{9,8},{10,11... | collective-permute-start | bytes 1376264 | tf_op jit(solution)/shard_map/ppermute | solution.py:46
  116.2 1.8 %collective-permute-done.21.refs_5_ = bf16[448,512]{1,0:T(8,128)(2,1)} collective-permute-done((bf16[448,512]{1,0:T(8,128)(2,1)}, bf16[448,512]{1,0:T(8,128)(2,1)}, u32[]{:S(2)}, u32[]{:S(2)}) %collective-permute-start.21) | collective-permute-done | bytes 458784 | tf_op jit(solution)/shard_map/ppermute | solution.py:46
  117.9 11.0 %layer.2 = (bf16[2,1,256,512]{3,2,1,0:T(8,128)(2,1)}, bf16[2,1,256,7168]{3,2,1,0:T(8,128)(2,1)}) custom-call(s32[17]{0:T(128)} %concatenate.3.table, bf16[2,1,256,7168]{3,2,1,0:T(8,128)(2,1)} %x_ref.11, bf16[128,7168]{1,0:T(8,128)(2,1)} %get-tuple-element.74.head_ref, bf16[2,1,256,512]{3,2,1,0:T(8,128)(2,1)} %ct_ref.7, ...), custom_call_target="tpu_custom_call" | custom-call | flops 1 | bytes 1 | tf_op jit(solution)/shard_map/layer/pallas_call | solution.py:416
  129.0 8.4 %collective-permute-done.20.above = bf16[1120,512]{1,0:T(8,128)(2,1)S(1)} collective-permute-done((bf16[1120,512]{1,0:T(8,128)(2,1)}, bf16[1120,512]{1,0:T(8,128)(2,1)S(1)}, u32[]{:S(2)}, u32[]{:S(2)}) %collective-permute-start.20) | collective-permute-done | bytes 1146912 | tf_op jit(solution)/shard_map/ppermute | solution.py:38
  137.4 3.0 %collective-permute-done.19.below = bf16[1120,512]{1,0:T(8,128)(2,1)S(1)} collective-permute-done((bf16[1120,512]{1,0:T(8,128)(2,1)}, bf16[1120,512]{1,0:T(8,128)(2,1)S(1)}, u32[]{:S(2)}, u32[]{:S(2)}) %collective-permute-start.19) | collective-permute-done | bytes 1146912 | tf_op jit(solution)/shard_map/ppermute | solution.py:34
  140.4 1.0 copy-done.5
  141.4 3.8 %mirror_sums.1 = (bf16[464,512]{1,0:T(8,128)(2,1)}, bf16[464,512]{1,0:T(8,128)(2,1)}) custom-call(s32[17]{0:T(128)} %concatenate.3.table, bf16[2,448,512]{2,1,0:T(8,128)(2,1)} %get-tuple-element.116.own0.own1, bf16[2,448,512]{2,1,0:T(8,128)(2,1)} %get-tuple-element.116.own0.own1, bf16[1120,512]{1,0:T(8,128)(2,1)} %copy-done.5, bf16[1120,512]{1,0:T(8,128)(2,1)} %copy-done.4, ...), custom_call_target="tpu_custom_call" | custom-call | flops 1 | bytes 1 | tf_op jit(solution)/shard_map/mirror_sums/pallas_call | solution.py:266
  145.2 3.3 %collective-permute-start.23 = (bf16[464,512]{1,0:T(8,128)(2,1)}, bf16[464,512]{1,0:T(8,128)(2,1)S(1)}, u32[]{:S(2)}, u32[]{:S(2)}) collective-permute-start(bf16[464,512]{1,0:T(8,128)(2,1)} %get-tuple-element.117), channel_id=1, source_target_pairs={{0,112},{1,113},{2,114},{3,115},{4,116},{5,117},{6,118},{7,119},{8... | collective-permute-start | bytes 1425416 | tf_op jit(solution)/shard_map/ppermute | solution.py:56
  148.5 0.5 collective-permute-start.24
  149.0 3.2 %collective-permute-start.22 = (bf16[448,512]{1,0:T(8,128)(2,1)}, bf16[448,512]{1,0:T(8,128)(2,1)S(1)}, u32[]{:S(2)}, u32[]{:S(2)}) collective-permute-start(bf16[448,512]{1,0:T(8,128)(2,1)} %copy-done.11), channel_id=1, source_target_pairs={{0,1},{1,0},{2,3},{3,2},{4,5},{5,4},{6,7},{7,6},{8,9},{9,8},{10,11... | collective-permute-start | bytes 1376264 | tf_op jit(solution)/shard_map/ppermute | solution.py:46
  152.2 1.1 copy-done.3
  153.4 3.6 %second_sums.1 = (bf16[448,512]{1,0:T(8,128)(2,1)}, bf16[448,512]{1,0:T(8,128)(2,1)}) custom-call(bf16[2,448,512]{2,1,0:T(8,128)(2,1)} %get-tuple-element.85.keep1.keep3, bf16[3,448,512]{2,1,0:T(8,128)(2,1)} %copy-done.3, bf16[1120,512]{1,0:T(8,128)(2,1)} %copy-done.5, bf16[2,448,512]{2,1,0:T(8,128)(2,1)} %get-tuple-element.85.keep1.keep3, ...), custom_call_target="tpu_custom_call" | custom-call | flops 1 | bytes 1 | tf_op jit(solution)/shard_map/second_sums/pallas_call | solution.py:266
  157.0 0.4 collective-permute-start.26
  157.4 1.1 collective-permute-start.25
  158.5 0.8 copy-done.12
  159.2 11.0 %layer.3 = (bf16[2,1,256,512]{3,2,1,0:T(8,128)(2,1)}, bf16[2,1,256,7168]{3,2,1,0:T(8,128)(2,1)}) custom-call(s32[17]{0:T(128)} %concatenate.3.table, bf16[2,1,256,7168]{3,2,1,0:T(8,128)(2,1)} %x_ref.11, bf16[128,7168]{1,0:T(8,128)(2,1)} %get-tuple-element.74.head_ref, ...), custom_call_target="tpu_custom_call", output_to_operand_aliasing={{0}: (13, {}), {1}: (14, {})} | custom-call | flops 1 | bytes 1 | tf_op jit(solution)/shard_map/layer/pallas_call | solution.py:416
  170.3 0.3 collective-permute-done.25.below
  170.6 0.4 copy-done.10
  171.0 0.2 copy-done.13
  171.2 0.2 copy-done.14
  171.4 3.4 %last_sums.1 = (f32[1,448,512]{2,1,0:T(8,128)}, f32[1,448]{1,0:T(1,128)}) custom-call(s32[17]{0:T(128)} %concatenate.3.table, bf16[1,448,512]{2,1,0:T(8,128)(2,1)} %get-tuple-element.91.keep0, bf16[3,448,512]{2,1,0:T(8,128)(2,1)} %copy-done.3, bf16[448,512]{1,0:T(8,128)(2,1)} %copy-done.14, bf16[448,512]{1,0:T(8,128)(2,1)} %copy-done.13, ...), custom_call_target="tpu_custom_call" | custom-call | flops 1 | bytes 1 | tf_op jit(solution)/shard_map/last_sums/pallas_call | solution.py:266
  (60 shorter events, 0.6 us)
Async XLA Ops:
  0.6 9.7 %copy-start = (bf16[2,64,7168]{2,1,0:T(8,128)(2,1)S(1)}, bf16[2,64,7168]{2,1,0:T(8,128)(2,1)}, u32[]{:S(2)}) copy-start(bf16[2,64,7168]{2,1,0:T(8,128)(2,1)} %param.15) | copy-start | bytes 5505028
  0.6 9.3 %copy-start.15 = (s32[2,16,16]{2,1,0:T(8,128)S(1)}, s32[2,16,16]{2,1,0:T(8,128)}, u32[]{:S(2)}) copy-start(s32[2,16,16]{2,1,0:T(8,128)} %param.16) | copy-start | bytes 6148
  0.7 39.5 %collective-permute-start = (bf16[2,1,256,7168]{3,2,1,0:T(8,128)(2,1)}, bf16[2,1,256,7168]{3,2,1,0:T(8,128)(2,1)}, u32[]{:S(2)}, u32[]{:S(2)}) collective-permute-start(bf16[2,1,256,7168]{3,2,1,0:T(8,128)(2,1)} %x_ref.11), channel_id=1, source_target_pairs={{0,1},{1,0},{2,3},{3,2},{4,5},{5,4},{6,7},{7,6},{8,9},{9,8},{10,11... | collective-permute-start | bytes 22020104 | tf_op jit(solution)/shard_map/ppermute | solution.py:46
  4.3 35.8 %collective-permute-start.3 = (bf16[2,448,512]{2,1,0:T(8,128)(2,1)}, bf16[2,448,512]{2,1,0:T(8,128)(2,1)}, u32[]{:S(2)}, u32[]{:S(2)}) collective-permute-start(bf16[2,448,512]{2,1,0:T(8,128)(2,1)} %pack.3.refs_0_.refs_1_), channel_id=1, source_target_pairs={{0,8},{1,9},{2,10},{3,11},{4,12},{5,13},{6,14},{7,15},{8,0},{9,1},... | collective-permute-start | bytes 2752520 | tf_op jit(solution)/shard_map/ppermute | solution.py:42
  7.2 32.9 %collective-permute-start.2 = (bf16[2,448,512]{2,1,0:T(8,128)(2,1)}, bf16[2,448,512]{2,1,0:T(8,128)(2,1)S(1)}, u32[]{:S(2)}, u32[]{:S(2)}) collective-permute-start(bf16[2,448,512]{2,1,0:T(8,128)(2,1)} %pack.3.refs_0_.refs_1_), channel_id=1, source_target_pairs={{0,6},{1,7},{2,0},{3,1},{4,2},{5,3},{6,4},{7,5},{8,14},{9,15},{10,... | collective-permute-start | bytes 2752520 | tf_op jit(solution)/shard_map/ppermute | solution.py:38
  9.9 30.2 %collective-permute-start.1 = (bf16[2,448,512]{2,1,0:T(8,128)(2,1)}, bf16[2,448,512]{2,1,0:T(8,128)(2,1)}, u32[]{:S(2)}, u32[]{:S(2)}) collective-permute-start(bf16[2,448,512]{2,1,0:T(8,128)(2,1)} %pack.3.refs_0_.refs_1_), channel_id=1, source_target_pairs={{0,2},{1,3},{2,4},{3,5},{4,6},{5,7},{6,0},{7,1},{8,10},{9,11},{10,... | collective-permute-start | bytes 2752520 | tf_op jit(solution)/shard_map/ppermute | solution.py:34
  11.4 28.6 %all-to-all-start = ((bf16[16,8,2432]{2,1,0:T(8,128)(2,1)}), bf16[16,8,2432]{2,1,0:T(8,128)(2,1)S(1)}, u32[]{:S(2)}, u32[]{:S(2)}) async-start(bf16[16,8,2432]{2,1,0:T(8,128)(2,1)} %fusion), calls=%async_computation | async-start | bytes 1245184 | tf_op jit(solution)/shard_map/all_to_all | solution.py:476
  16.7 29.8 %copy-start.16 = (s32[3]{0:T(128)S(1)}, s32[3]{0:T(128)}, u32[]{:S(2)}) copy-start(s32[3]{0:T(128)} %constant.149.clone) | copy-start | bytes 40
  40.1 11.6 %copy-start.7 = (bf16[16,8,2432]{2,1,0:T(8,128)(2,1)}, bf16[16,8,2432]{2,1,0:T(8,128)(2,1)S(1)}, u32[]{:S(2)}) copy-start(bf16[16,8,2432]{2,1,0:T(8,128)(2,1)S(1)} %all-to-all-done) | copy-start | bytes 1867780
  40.1 7.6 %copy-start.6 = (bf16[2,448,512]{2,1,0:T(8,128)(2,1)}, bf16[2,448,512]{2,1,0:T(8,128)(2,1)S(1)}, u32[]{:S(2)}) copy-start(bf16[2,448,512]{2,1,0:T(8,128)(2,1)S(1)} %collective-permute-done.2.refs_2_.refs_3_) | copy-start | bytes 2752516
  40.1 28.7 %collective-permute-start.5 = (bf16[2,448,512]{2,1,0:T(8,128)(2,1)}, bf16[2,448,512]{2,1,0:T(8,128)(2,1)}, u32[]{:S(2)}, u32[]{:S(2)}) collective-permute-start(bf16[2,448,512]{2,1,0:T(8,128)(2,1)} %collective-permute-done.3.refs_6_.refs_7_), channel_id=1, source_target_pairs={{0,6},{1,7},{2,0},{3,1},{4,2},{5,3},{6,4},{7,5},{8,14},{9,15},{10,... | collective-permute-start | bytes 2752520 | tf_op jit(solution)/shard_map/ppermute | solution.py:38
  40.2 28.6 %collective-permute-start.6 = (bf16[2,448,512]{2,1,0:T(8,128)(2,1)}, bf16[2,448,512]{2,1,0:T(8,128)(2,1)}, u32[]{:S(2)}, u32[]{:S(2)}) collective-permute-start(bf16[2,448,512]{2,1,0:T(8,128)(2,1)} %collective-permute-done.1.refs_4_.refs_5_), channel_id=1, source_target_pairs={{0,8},{1,9},{2,10},{3,11},{4,12},{5,13},{6,14},{7,15},{8,0},{9,1},... | collective-permute-start | bytes 2752520 | tf_op jit(solution)/shard_map/ppermute | solution.py:42
  41.1 27.7 %collective-permute-start.4 = (bf16[2,448,512]{2,1,0:T(8,128)(2,1)}, bf16[2,448,512]{2,1,0:T(8,128)(2,1)}, u32[]{:S(2)}, u32[]{:S(2)}) collective-permute-start(bf16[2,448,512]{2,1,0:T(8,128)(2,1)} %collective-permute-done.1.refs_4_.refs_5_), channel_id=1, source_target_pairs={{0,2},{1,3},{2,4},{3,5},{4,6},{5,7},{6,0},{7,1},{8,10},{9,11},{10,... | collective-permute-start | bytes 2752520 | tf_op jit(solution)/shard_map/ppermute | solution.py:34
  42.8 18.2 %collective-permute-start.8 = (bf16[128,2432]{1,0:T(8,128)(2,1)S(1)}, bf16[128,2432]{1,0:T(8,128)(2,1)S(1)}, u32[]{:S(2)}, u32[]{:S(2)}) collective-permute-start(bf16[128,2432]{1,0:T(8,128)(2,1)S(1)} %bitcast.24), channel_id=1, source_target_pairs={{48,0},{64,112},{49,1},{65,113},{50,2},{66,114},{51,3},{67,115},{5... | collective-permute-start | bytes 1867784 | tf_op jit(solution)/shard_map/ppermute | solution.py:504
  44.1 16.9 %collective-permute-start.7 = (bf16[128,2432]{1,0:T(8,128)(2,1)S(1)}, bf16[128,2432]{1,0:T(8,128)(2,1)S(1)}, u32[]{:S(2)}, u32[]{:S(2)}) collective-permute-start(bf16[128,2432]{1,0:T(8,128)(2,1)S(1)} %bitcast.25), channel_id=1, source_target_pairs={{16,0},{96,112},{17,1},{97,113},{18,2},{98,114},{19,3},{99,115},{2... | collective-permute-start | bytes 1867784 | tf_op jit(solution)/shard_map/ppermute | solution.py:503
  61.0 0.8 copy-start.8
  61.9 0.8 copy-start.9
  62.7 8.1 %copy-start.2 = (bf16[8,448,512]{2,1,0:T(8,128)(2,1)S(1)}, bf16[8,448,512]{2,1,0:T(8,128)(2,1)}, u32[]{:S(2)}) copy-start(bf16[8,448,512]{2,1,0:T(8,128)(2,1)} %pack.4.refs_0_.weight1) | copy-start | bytes 11010052
  68.8 8.7 %collective-permute-start.9 = (bf16[128,7168]{1,0:T(8,128)(2,1)}, bf16[128,7168]{1,0:T(8,128)(2,1)}, u32[]{:S(2)}, u32[]{:S(2)}) collective-permute-start(bf16[128,7168]{1,0:T(8,128)(2,1)} %get-tuple-element.74.head_ref), channel_id=1, source_target_pairs={{0,1},{1,0},{2,3},{3,2},{4,5},{5,4},{6,7},{7,6},{8,9},{9,8},{10,11... | collective-permute-start | bytes 5505032 | tf_op jit(solution)/shard_map/ppermute | solution.py:46
  70.7 34.9 %collective-permute-start.16 = (bf16[8,448,512]{2,1,0:T(8,128)(2,1)S(1)}, bf16[8,448,512]{2,1,0:T(8,128)(2,1)}, u32[]{:S(2)}, u32[]{:S(2)}) collective-permute-start(bf16[8,448,512]{2,1,0:T(8,128)(2,1)S(1)} %copy-done.2), channel_id=1, source_target_pairs={{0,1},{1,0},{2,3},{3,2},{4,5},{5,4},{6,7},{7,6},{8,9},{9,8},{10,11... | collective-permute-start | bytes 11010056 | tf_op jit(solution)/shard_map/ppermute | solution.py:46
  70.8 6.7 %collective-permute-start.10 = (bf16[2,1,256,512]{3,2,1,0:T(8,128)(2,1)}, bf16[2,1,256,512]{3,2,1,0:T(8,128)(2,1)}, u32[]{:S(2)}, u32[]{:S(2)}) collective-permute-start(bf16[2,1,256,512]{3,2,1,0:T(8,128)(2,1)} %get-tuple-element.75.own_ct.scaled_ref), channel_id=1, source_target_pairs={{0,1},{1,0},{2,3},{3,2},{4,5},{5,4},{6,7},{7,6},{8,9},{9,8},{10,11... | collective-permute-start | bytes 1572872 | tf_op jit(solution)/shard_map/ppermute | solution.py:46
  74.9 13.6 %collective-permute-start.11 = (bf16[448,512]{1,0:T(8,128)(2,1)}, bf16[448,512]{1,0:T(8,128)(2,1)}, u32[]{:S(2)}, u32[]{:S(2)}) collective-permute-start(bf16[448,512]{1,0:T(8,128)(2,1)} %slice_bitcast_fusion.1), channel_id=1, source_target_pairs={{0,2},{1,3},{2,4},{3,5},{4,6},{5,7},{6,0},{7,1},{8,10},{9,11},{10,... | collective-permute-start | bytes 1376264 | tf_op jit(solution)/shard_map/ppermute | solution.py:34
  74.9 13.6 %collective-permute-start.12 = (bf16[448,512]{1,0:T(8,128)(2,1)}, bf16[448,512]{1,0:T(8,128)(2,1)S(1)}, u32[]{:S(2)}, u32[]{:S(2)}) collective-permute-start(bf16[448,512]{1,0:T(8,128)(2,1)} %slice_bitcast_fusion), channel_id=1, source_target_pairs={{0,6},{1,7},{2,0},{3,1},{4,2},{5,3},{6,4},{7,5},{8,14},{9,15},{10,... | collective-permute-start | bytes 1376264 | tf_op jit(solution)/shard_map/ppermute | solution.py:38
  88.5 16.6 %copy-start.11 = (bf16[448,512]{1,0:T(8,128)(2,1)}, bf16[448,512]{1,0:T(8,128)(2,1)S(1)}, u32[]{:S(2)}) copy-start(bf16[448,512]{1,0:T(8,128)(2,1)S(1)} %collective-permute-done.12.refs_2_) | copy-start | bytes 1376260
  88.5 17.1 %collective-permute-start.17 = (bf16[6,448,512]{2,1,0:T(8,128)(2,1)}, bf16[6,448,512]{2,1,0:T(8,128)(2,1)}, u32[]{:S(2)}, u32[]{:S(2)}) collective-permute-start(bf16[6,448,512]{2,1,0:T(8,128)(2,1)} %pack.5.refs_1_), channel_id=1, source_target_pairs={{0,1},{1,0},{2,3},{3,2},{4,5},{5,4},{6,7},{7,6},{8,9},{9,8},{10,11... | collective-permute-start | bytes 8257544 | tf_op jit(solution)/shard_map/ppermute | solution.py:46
  89.4 15.8 %collective-permute-start.14 = (bf16[448,512]{1,0:T(8,128)(2,1)}, bf16[448,512]{1,0:T(8,128)(2,1)}, u32[]{:S(2)}, u32[]{:S(2)}) collective-permute-start(bf16[448,512]{1,0:T(8,128)(2,1)} %bitcast.30), channel_id=1, source_target_pairs={{0,6},{1,7},{2,0},{3,1},{4,2},{5,3},{6,4},{7,5},{8,14},{9,15},{10,... | collective-permute-start | bytes 1376264 | tf_op jit(solution)/shard_map/ppermute | solution.py:38
  91.9 13.4 %collective-permute-start.13 = (bf16[448,512]{1,0:T(8,128)(2,1)}, bf16[448,512]{1,0:T(8,128)(2,1)}, u32[]{:S(2)}, u32[]{:S(2)}) collective-permute-start(bf16[448,512]{1,0:T(8,128)(2,1)} %bitcast.29), channel_id=1, source_target_pairs={{0,2},{1,3},{2,4},{3,5},{4,6},{5,7},{6,0},{7,1},{8,10},{9,11},{10,... | collective-permute-start | bytes 1376264 | tf_op jit(solution)/shard_map/ppermute | solution.py:34
  91.9 13.7 %collective-permute-start.15 = (bf16[448,512]{1,0:T(8,128)(2,1)}, bf16[448,512]{1,0:T(8,128)(2,1)}, u32[]{:S(2)}, u32[]{:S(2)}) collective-permute-start(bf16[448,512]{1,0:T(8,128)(2,1)} %bitcast.28), channel_id=1, source_target_pairs={{0,8},{1,9},{2,10},{3,11},{4,12},{5,13},{6,14},{7,15},{8,0},{9,1},... | collective-permute-start | bytes 1376264 | tf_op jit(solution)/shard_map/ppermute | solution.py:42
  109.1 43.1 %collective-permute-start.18 = (bf16[3,448,512]{2,1,0:T(8,128)(2,1)}, bf16[3,448,512]{2,1,0:T(8,128)(2,1)S(1)}, u32[]{:S(2)}, u32[]{:S(2)}) collective-permute-start(bf16[3,448,512]{2,1,0:T(8,128)(2,1)} %get-tuple-element.100), channel_id=1, source_target_pairs={{0,8},{1,9},{2,10},{3,11},{4,12},{5,13},{6,14},{7,15},{8,0},{9,1},... | collective-permute-start | bytes 4128776 | tf_op jit(solution)/shard_map/ppermute | solution.py:42
  111.8 25.6 %collective-permute-start.20 = (bf16[1120,512]{1,0:T(8,128)(2,1)}, bf16[1120,512]{1,0:T(8,128)(2,1)S(1)}, u32[]{:S(2)}, u32[]{:S(2)}) collective-permute-start(bf16[1120,512]{1,0:T(8,128)(2,1)} %get-tuple-element.101), channel_id=1, source_target_pairs={{0,6},{1,7},{2,0},{3,1},{4,2},{5,3},{6,4},{7,5},{8,14},{9,15},{10,... | collective-permute-start | bytes 3440648 | tf_op jit(solution)/shard_map/ppermute | solution.py:38
  114.2 26.2 %collective-permute-start.19 = (bf16[1120,512]{1,0:T(8,128)(2,1)}, bf16[1120,512]{1,0:T(8,128)(2,1)S(1)}, u32[]{:S(2)}, u32[]{:S(2)}) collective-permute-start(bf16[1120,512]{1,0:T(8,128)(2,1)} %get-tuple-element.99), channel_id=1, source_target_pairs={{0,2},{1,3},{2,4},{3,5},{4,6},{5,7},{6,0},{7,1},{8,10},{9,11},{10,... | collective-permute-start | bytes 3440648 | tf_op jit(solution)/shard_map/ppermute | solution.py:34
  114.2 3.8 %collective-permute-start.21 = (bf16[448,512]{1,0:T(8,128)(2,1)}, bf16[448,512]{1,0:T(8,128)(2,1)}, u32[]{:S(2)}, u32[]{:S(2)}) collective-permute-start(bf16[448,512]{1,0:T(8,128)(2,1)} %collective-permute-done.11.refs_2_), channel_id=1, source_target_pairs={{0,1},{1,0},{2,3},{3,2},{4,5},{5,4},{6,7},{7,6},{8,9},{9,8},{10,11... | collective-permute-start | bytes 1376264 | tf_op jit(solution)/shard_map/ppermute | solution.py:46
  137.4 3.0 %copy-start.4 = (bf16[1120,512]{1,0:T(8,128)(2,1)}, bf16[1120,512]{1,0:T(8,128)(2,1)S(1)}, u32[]{:S(2)}) copy-start(bf16[1120,512]{1,0:T(8,128)(2,1)S(1)} %collective-permute-done.20.above) | copy-start | bytes 3440644
  140.4 1.0 copy-start.5
  145.2 25.1 %collective-permute-start.23 = (bf16[464,512]{1,0:T(8,128)(2,1)}, bf16[464,512]{1,0:T(8,128)(2,1)S(1)}, u32[]{:S(2)}, u32[]{:S(2)}) collective-permute-start(bf16[464,512]{1,0:T(8,128)(2,1)} %get-tuple-element.117), channel_id=1, source_target_pairs={{0,112},{1,113},{2,114},{3,115},{4,116},{5,117},{6,118},{7,119},{8... | collective-permute-start | bytes 1425416 | tf_op jit(solution)/shard_map/ppermute | solution.py:56
  148.5 21.8 %collective-permute-start.24 = (bf16[464,512]{1,0:T(8,128)(2,1)}, bf16[464,512]{1,0:T(8,128)(2,1)}, u32[]{:S(2)}, u32[]{:S(2)}) collective-permute-start(bf16[464,512]{1,0:T(8,128)(2,1)} %get-tuple-element.118), channel_id=1, source_target_pairs={{0,120},{1,121},{2,122},{3,123},{4,124},{5,125},{6,126},{7,127},{8... | collective-permute-start | bytes 1425416 | tf_op jit(solution)/shard_map/ppermute | solution.py:56
  149.0 9.4 %collective-permute-start.22 = (bf16[448,512]{1,0:T(8,128)(2,1)}, bf16[448,512]{1,0:T(8,128)(2,1)S(1)}, u32[]{:S(2)}, u32[]{:S(2)}) collective-permute-start(bf16[448,512]{1,0:T(8,128)(2,1)} %copy-done.11), channel_id=1, source_target_pairs={{0,1},{1,0},{2,3},{3,2},{4,5},{5,4},{6,7},{7,6},{8,9},{9,8},{10,11... | collective-permute-start | bytes 1376264 | tf_op jit(solution)/shard_map/ppermute | solution.py:46
  152.2 1.1 copy-start.3
  157.0 13.3 %collective-permute-start.26 = (bf16[448,512]{1,0:T(8,128)(2,1)}, bf16[448,512]{1,0:T(8,128)(2,1)S(1)}, u32[]{:S(2)}, u32[]{:S(2)}) collective-permute-start(bf16[448,512]{1,0:T(8,128)(2,1)} %get-tuple-element.119), channel_id=1, source_target_pairs={{0,6},{1,7},{2,0},{3,1},{4,2},{5,3},{6,4},{7,5},{8,14},{9,15},{10,... | collective-permute-start | bytes 1376264 | tf_op jit(solution)/shard_map/ppermute | solution.py:38
  157.4 13.3 %collective-permute-start.25 = (bf16[448,512]{1,0:T(8,128)(2,1)}, bf16[448,512]{1,0:T(8,128)(2,1)S(1)}, u32[]{:S(2)}, u32[]{:S(2)}) collective-permute-start(bf16[448,512]{1,0:T(8,128)(2,1)} %get-tuple-element.109), channel_id=1, source_target_pairs={{0,2},{1,3},{2,4},{3,5},{4,6},{5,7},{6,0},{7,1},{8,10},{9,11},{10,... | collective-permute-start | bytes 1376264 | tf_op jit(solution)/shard_map/ppermute | solution.py:34
  158.5 0.8 copy-start.12
  170.3 0.8 copy-start.10
  170.3 0.9 copy-start.13
  170.6 0.8 copy-start.14
  170.6 4.2 %copy-start.1 = (bf16[2,64,7168]{2,1,0:T(8,128)(2,1)S(1)}, bf16[2,64,7168]{2,1,0:T(8,128)(2,1)}, u32[]{:S(2)}) copy-start(bf16[2,64,7168]{2,1,0:T(8,128)(2,1)} %param.15) | copy-start | bytes 5505028

commit v2 on v1

--- a/solution.py
+++ b/solution.py
@@ -9,7 +9,8 @@
 CAP = 2
 EPSILON = 1e-05
 HEAD = 128
-VMEM_BYTES = 60 * 1024 * 1024
+VMEM_BYTES = 63 * 1024 * 1024 + 512 * 1024
+PATCH_VMEM_BYTES = VMEM_BYTES
 SMALL = pl.CostEstimate(flops=1, bytes_accessed=1, transcendentals=0)
 F32 = jnp.float32
 BF16 = jnp.bfloat16
@@ -58,6 +59,10 @@
 
 def columns(chip, size):
     return pl.ds(pl.multiple_of(chip * size, 128), size)
+
+
+def core_window(width):
+    return -(-(width // CHIPS // 2) // 128) * 128
 
 
 def inverse_rms(rows):
@@ -96,7 +101,9 @@
     )(section_inputs, cotangent)
 
 
-def patch_kernel(table, x_ref, ct_ref, perm_ref, im0, im1, im2, ct_in, inverse_in, head_ref, ct_out, inverse_out):
+def patch_kernel(
+    table, x_ref, ct_ref, perm_ref, ct_in, inverse_in, im0, im1, im2, head_ref, other_ref, ct_out, inverse_out, images, sems
+):
     pipe = table[PIPE]
     head_ref[...] = x_ref[0, 0]
     ct_out[...] = ct_in[...]
@@ -105,13 +112,28 @@
     @pl.when(table[FLAG + pipe] == 1)
     def _():
         live = lax.broadcasted_iota(jnp.int32, (HEAD, 1), 0) < table[LIVE]
-        for part, image in enumerate((im0, im1, im2)):
-            where = pl.ds(pl.multiple_of(table[PART + part], 128), image.shape[1])
-            arrived = jnp.dot(perm_ref[...], image[...], preferred_element_type=F32).astype(BF16)
+        copies = [
+            pltpu.make_async_copy(image, images.at[part], sems.at[part])
+            for part, image in enumerate((im0, im1, im2))
+        ]
+        for copy in copies:
+            copy.start()
+        for part, copy in enumerate(copies):
+            copy.wait()
+            where = pl.ds(pl.multiple_of(table[PART + part], 128), images.shape[2])
+            arrived = jnp.dot(perm_ref[...], images[part], preferred_element_type=F32).astype(BF16)
             head_ref[:, where] = jnp.where(live, arrived, head_ref[:, where])
         inverse = inverse_rms(head_ref)
         ct_out[pipe, 0, :HEAD] = (ct_ref[0, 0].astype(F32) * inverse).astype(BF16)
         inverse_out[pipe, :HEAD] = jnp.broadcast_to(inverse, (HEAD, inverse_out.shape[2]))
+
+    pair = head_ref.shape[1] // CHIPS
+    window = other_ref.shape[1] // CHIPS
+    for chip in range(CHIPS):
+        start = chip * pair + (1 - table[CORE]) * (pair - window)
+        other_ref[:, chip * window : (chip + 1) * window] = head_ref[
+            :, pl.ds(pl.multiple_of(start, 128), window)
+        ]
 
 
 def patch(table, section_inputs, cotangent, perm, images, scaled_ct, inverse):
@@ -127,18 +149,24 @@
                 pl.BlockSpec((1, 1, HEAD, width), lambda i, table: (table[PIPE], 0, 0, 0)),
                 pl.BlockSpec((1, 1, HEAD, kv), lambda i, table: (table[PIPE], 0, 0, 0)),
             ]
-            + [whole] * 6,
-            out_specs=[whole] * 3,
+            + [whole] * 3
+            + [pl.BlockSpec(memory_space=pl.ANY)] * 3,
+            out_specs=[whole] * 4,
+            scratch_shapes=[
+                pltpu.VMEM((3, *images[0].shape), BF16),
+                pltpu.SemaphoreType.DMA((3,)),
+            ],
         ),
         out_shape=[
             jax.ShapeDtypeStruct((HEAD, width), BF16),
+            jax.ShapeDtypeStruct((HEAD, CHIPS * core_window(width)), BF16),
             jax.ShapeDtypeStruct(scaled_ct.shape, BF16),
             jax.ShapeDtypeStruct(inverse.shape, F32),
         ],
-        compiler_params=pltpu.CompilerParams(vmem_limit_bytes=VMEM_BYTES),
+        compiler_params=pltpu.CompilerParams(vmem_limit_bytes=PATCH_VMEM_BYTES),
         cost_estimate=SMALL,
         name="patch",
-    )(table, section_inputs, cotangent, perm, *images, scaled_ct, inverse)
+    )(table, section_inputs, cotangent, perm, scaled_ct, inverse, *images)
 
 
 def pack(parts):
@@ -169,12 +197,13 @@
     )(*[array for array, _ in parts])
 
 
-def start_columns(table, pipe, x_ref, head_ref, rows, sems, from_x, to_rows):
+def start_columns(table, pipe, x_ref, head_ref, rows, sems, from_x, to_rows, from_head=None):
+    from_head = from_x if from_head is None else from_head
     flag = table[FLAG + pipe] == 1
     tail = pl.ds(HEAD, rows.shape[0] - HEAD)
     top = rows.at[pl.ds(0, HEAD), to_rows]
     plain = pltpu.make_async_copy(x_ref.at[pipe, 0, pl.ds(0, HEAD), from_x], top, sems.at[0])
-    placed = pltpu.make_async_copy(head_ref.at[:, from_x], top, sems.at[0])
+    placed = pltpu.make_async_copy(head_ref.at[:, from_head], top, sems.at[0])
     rest = pltpu.make_async_copy(x_ref.at[pipe, 0, tail, from_x], rows.at[tail, to_rows], sems.at[1])
     pl.when(flag)(placed.start)
     pl.when(jnp.logical_not(flag))(plain.start)
@@ -186,7 +215,7 @@
     pipes, _, tokens, width = x.shape
     pair = width // CHIPS
     half = pair // 2
-    window = -(-half // 128) * 128
+    window = core_window(width)
     kv = ct.shape[3]
     order = [(g, i, *block) for g, group in enumerate(groups) for i, block in enumerate(group)]
     count = len(order)
@@ -202,7 +231,8 @@
             waits.append(
                 start_columns(table, pipe, x_ref, head_ref, own, row_sems.at[n, 0], from_x, here)
                 + start_columns(
-                    table, pipe, sibling_x_ref, sibling_head_ref, other, row_sems.at[n, 1], from_x, here
+                    table, pipe, sibling_x_ref, sibling_head_ref, other, row_sems.at[n, 1], from_x, here,
+                    columns(table[r], window),
                 )
             )
         contract = (((0,), (0,)), ((), ()))
@@ -282,16 +312,19 @@
     return total
 
 
-def first_sums(near0, far0, near1, back1, far1, back0, keep2, came2, up, down):
+def halves(first, second, first_out, second_out):
+    first_out[...] = first[...]
+    second_out[...] = second[...]
+
+
+def first_sums(near0, far0, back1, far1, keep2, came2, up, down):
     rows = near0.shape[0]
     half = rows // 2
     far = wide(keep2, came2).astype(BF16)
     up[:rows] = wide(near0, far0).astype(BF16)
-    up[rows : 2 * rows] = near1[...]
-    up[2 * rows :] = far[:half]
+    up[rows:] = far[:half]
     down[:rows] = wide(back1, far1).astype(BF16)
-    down[rows : 2 * rows] = back0[...]
-    down[2 * rows :] = far[half:]
+    down[rows:] = far[half:]
 
 
 def gain_row(weight, share):
@@ -309,13 +342,13 @@
     return jnp.transpose(jnp.broadcast_to(row, (8, pair // 2)))[:, :1]
 
 
-def mirror_sums(table, own0, own1, below, above, weight0, weight1, gain, here, there):
+def mirror_sums(table, own0, below0, above0, own1, below1, above1, weight0, weight1, gain, here, there):
     rows = own0.shape[0]
-    for out, own, low, high, weight, chip in (
-        (here, own0, 0, rows, weight0, table[0]),
-        (there, own1, rows, 0, weight1, table[Y_CHIPS]),
+    for out, sums, weight, chip in (
+        (here, (own0, below0.at[:rows], above0), weight0, table[0]),
+        (there, (own1, below1, above1.at[:rows]), weight1, table[Y_CHIPS]),
     ):
-        share = wide(own, below.at[low : low + rows], above.at[high : high + rows])
+        share = wide(*sums)
         out[:rows] = (share * gain_column(table, gain, chip)).astype(BF16)
         out[rows:] = jnp.zeros((out.shape[0] - rows, out.shape[1]), BF16)
         out[rows : rows + 8, :rows] = jnp.broadcast_to(gain_row(weight, share), (8, rows)).astype(BF16)
@@ -326,16 +359,21 @@
     half = rows // 2
     ups[...] = wide(keep1, came1).astype(BF16)
     downs[...] = wide(keep3, came3).astype(BF16)
-    ups[:half] = wide(ups.at[:half], below.at[2 * rows :]).astype(BF16)
-    downs[half:] = wide(downs.at[half:], above.at[2 * rows :]).astype(BF16)
-
-
-def last_sums(table, keep0, came0, below, above, weight, gain, mirrored0, mirrored1, weight_grad, gain_grad):
+    ups[:half] = wide(ups.at[:half], below.at[rows:]).astype(BF16)
+    downs[half:] = wide(downs.at[half:], above.at[rows:]).astype(BF16)
+
+
+def down_sums(table, keep0, came0, below, above, weight, gain, weight_part, gain_part):
     share = wide(keep0, came0, below, above)
-    rows = share.shape[0]
+    weight_part[...] = share * gain_column(table, gain, table[0])
+    gain_part[...] = gain_row(weight, share)
+
+
+def last_sums(weight_part, gain_part, mirrored0, mirrored1, weight_grad, gain_grad):
+    rows = weight_part.shape[0]
     moved = wide(mirrored0, mirrored1)
-    weight_grad[0] = share * gain_column(table, gain, table[0]) + moved[:rows]
-    gain_grad[...] = gain_row(weight, share) + moved[rows : rows + 1, :rows]
+    weight_grad[0] = weight_part[...] + moved[:rows]
+    gain_grad[...] = gain_part[...] + moved[rows : rows + 1, :rows]
 
 
 def layer(pipe, table, x, head, cotangent, scaled_ct, inverse, gain, own, sibling, carried):
@@ -542,46 +580,49 @@
     images = move_images(incoming)
     w2, w5, w7 = to_next(w3), to_previous(w4), to_across(w3)
     early = pack([(w0, 0), (w0, 1), (w1, 0), (w1, 1), (w3, 0), (w3, 1), (w4, 0), (w4, 1)])
-    head, scaled_ct, inverse = patch(
+    head, other_head, scaled_ct, inverse = patch(
         hold(table, early), section_inputs, value_cotangent, perm, images, scaled_ct, inverse
     )
-    w2, w5, w7, head, scaled_ct = hold((w2, w5, w7, head, scaled_ct))
-    sibling_head, sibling_ct = to_sibling(head), to_sibling(scaled_ct)
-    down6, up6 = to_next(w7[0]), to_previous(w5[1])
+    w2, w5, w7, other_head, scaled_ct, early = hold((w2, w5, w7, other_head, scaled_ct, early))
+    sibling_head, sibling_ct = to_sibling(other_head), to_sibling(scaled_ct)
+    down7, up5 = on_blocks("halves", halves, [(w7, 0), (w5, 1)], [part, part])
+    down6, up6 = to_next(down7), to_previous(up5)
 
     rows = (section_inputs, sibling_x, head, sibling_head, scaled_ct, sibling_ct)
-    far0, far1, send2 = products(table, *rows, (((1, 2),), ((1, 6),), ((0, 6),)))
-    middle = pack([(w2, 0), (w2, 1), (w5, 0), (w5, 1), (w7, 0), (hold(w7, far0), 1)])
-    far0, far1, send2, down6, up6, middle = hold((far0, far1, send2, down6, up6, middle))
-    from_below, from_above, came = to_next(far0[0]), to_previous(far1[0]), to_across(send2[0])
-    sibling_early, sibling_middle = to_sibling(early), to_sibling(middle)
-    near0, near1, back1, back0, keep2, send130, own01, keep13, keep0 = products(
-        hold(table, middle),
+    far0_near1, far1_back0, send20 = products(
+        table, *rows, (((1, 2), (1, 5)), ((1, 6), (1, 3)), ((0, 6), (0, 4)))
+    )
+    far0_near1, far1_back0, send20, down6, up6, w7, early = hold(
+        (far0_near1, far1_back0, send20, down6, up6, w7, early)
+    )
+    sibling_early = to_sibling(early)
+    from_below, from_above, came20 = to_next(far0_near1), to_previous(far1_back0), to_across(send20)
+    down_places = ((0, 0), (0, 2), (1, 0), (0, 4), (0, 6), (1, 2), (2, None), (1, 4))
+    up_places = ((0, 1), (0, 3), (1, 1), (0, 5), (0, 7), (1, 3), (3, None), (1, 5))
+    near0, back1, keep2, send13, own01, keep13, keep0 = products(
+        hold(table, up6),
         *rows,
-        (
-            ((1, 1),), ((1, 5),), ((1, 7),), ((1, 3),), ((0, 2),),
-            ((0, 5), (0, 7), (0, 4)), ((1, 0), (1, 4)), ((0, 1), (0, 3)), ((0, 0),),
-        ),
-    )
-    from_below, from_above, came = hold((from_below, from_above, came), keep0, sibling_early, sibling_middle)
-    message = jax.ShapeDtypeStruct((2 * shard + shard // 2, kv), BF16)
+        (((1, 1),), ((1, 7),), ((0, 2),), ((0, 5), (0, 7)), ((1, 0), (1, 4)), ((0, 1), (0, 3)), ((0, 0),)),
+    )
+
+    def pieces(arrays, places):
+        return [(arrays[array], at) for array, at in places]
+
+    middle = pack([(w2, 0), (w2, 1), (w5, 0), (w5, 1), (w7, 0), (w7, 1)])
+    from_below, from_above, came20, send13 = hold(
+        (from_below, from_above, came20, send13), keep0, middle, sibling_early
+    )
+    message = jax.ShapeDtypeStruct((shard + shard // 2, kv), BF16)
     up, down = on_blocks(
         "first_sums",
         first_sums,
-        [(near0, 0), from_below, (near1, 0), (back1, 0), from_above, (back0, 0), (keep2, 0), came],
+        [(near0, 0), (from_below, 0), (back1, 0), (from_above, 0), (keep2, 0), (came20, 0)],
         [message, message],
     )
     below, above = to_next(up), to_previous(down)
-    came130 = to_across(hold(send130, up))
-
-    down_places = ((0, 0), (0, 2), (1, 0), (0, 4), (0, 6), (1, 2), (2, None), (1, 4))
-    up_places = ((0, 1), (0, 3), (1, 1), (0, 5), (0, 7), (1, 3), (3, None), (1, 5))
+    came13 = to_across(hold(send13, up))
     own = (early, middle, down6, up6)
-    sibling = (sibling_early, sibling_middle, to_sibling(hold(down6, up)), to_sibling(hold(up6, up)))
-
-    def pieces(arrays, places):
-        return [(arrays[array], at) for array, at in places]
-
+    sibling = [sibling_early, *[to_sibling(hold(array, up)) for array in (middle, down6, up6)]]
     filled = layer(
         0,
         hold(table, up),
@@ -594,7 +635,8 @@
         "mirror_sums",
         mirror_sums,
         [
-            table, (own01, 0), (own01, 1), below, above, (up_weight, 0), (early, 7), up_gain,
+            table, (own01, 0), below, (from_above, 1), (own01, 1), (from_below, 1), above,
+            (up_weight, 0), (early, 7), up_gain,
         ],
         [payload, payload],
     )
@@ -602,7 +644,7 @@
     ups, downs = on_blocks(
         "second_sums",
         second_sums,
-        [(keep13, 0), (came130, 0), below, (keep13, 1), (came130, 1), above],
+        [(keep13, 0), (came13, 0), below, (keep13, 1), (came13, 1), above],
         [part, part],
     )
     last_below, last_above = to_next(ups), to_previous(downs)
@@ -612,13 +654,18 @@
         section_inputs, head, value_cotangent, scaled_ct, inverse, up_gain,
         pieces(own, up_places), pieces(sibling, up_places), tuple(filled),
     )
-    mirrored0, mirrored1, last_below, last_above = hold((mirrored0, mirrored1, last_below, last_above), values)
+    last_below, last_above = hold((last_below, last_above), values)
+    weight_part, gain_part = on_blocks(
+        "down_sums",
+        down_sums,
+        [table, (keep0, 0), (came20, 1), last_below, last_above, (down_weight, 0), down_gain],
+        [jax.ShapeDtypeStruct((shard, kv), F32), jax.ShapeDtypeStruct((1, shard), F32)],
+    )
+    mirrored0, mirrored1 = hold((mirrored0, mirrored1), weight_part)
     weight_grad, gain_grad = on_blocks(
         "last_sums",
         last_sums,
-        [
-            table, (keep0, 0), (came130, 2), last_below, last_above, (down_weight, 0), down_gain, mirrored0, mirrored1,
-        ],
+        [weight_part, gain_part, mirrored0, mirrored1],
         [jax.ShapeDtypeStruct((1, shard, kv), F32), jax.ShapeDtypeStruct((1, shard), F32)],
     )
     return (values, input_grad, weight_grad, gain_grad)

time: 176 us -> 171 us (0.972)
  local copies, waits for them, and re-layouts: 10.1 us -> 1.82 us
  Pallas kernels: 74.4 us -> 78.6 us
  starting transfers between devices: 43.5 us -> 41.6 us
    ppermute x6, waiting for transfers between devices: 6.32 us -> 12.9 us  [to_next(): lax.ppermute(block, 'fsdp', fsdp_route(lambda x, y, core: (x, y + 1, core)))]
    ppermute x6, waiting for transfers between devices: 8.46 us -> 1.96 us  [to_previous(): lax.ppermute(block, 'fsdp', fsdp_route(lambda x, y, core: (x, y - 1, core)))]
    unnamed x34 -> x6, local copies, waits for them, and re-layouts: 5.37 us -> 0.01 us
    squeeze x2 -> x0, local copies, waits for them, and re-layouts: 3.63 us -> none  [per_device(): down6, up6 = (to_next(w7[0]), to_previous(w5[1]))]
    pallas_call x4 -> x6, Pallas kernels: 14.4 us -> 17.7 us  [on_blocks(): pl.pallas_call(kernel, grid=(1,), in_specs=specs, out_specs=[pl.BlockSpec...]
    all_to_all x1, waiting for transfers between devices: 16.1 us -> 14 us  [route_images(): lax.all_to_all(outgoing, 'fsdp', split_axis=0, concat_axis=0, tiled=True)]
    ppermute x4, waiting for transfers between devices: 0.3 us -> 2.34 us  [to_across(): lax.ppermute(block, 'fsdp', fsdp_route(lambda x, y, core: (x + 1, y, core)))]
  transfers between devices with their start and end apart: 28 -> 28, of which waited for: 9 -> 9; matrix products, arithmetic and copies ran while one was open for 4% -> 4% of each run, Pallas kernels for 39% -> 43%
where the time goes in v2:
time: 171 us
  Pallas kernels  78.6 us (46%)
  waiting for transfers between devices  42.5 us (25%)
  starting transfers between devices  41.6 us (24%)
  other arithmetic  2.38 us (1%)
  matrix products  2.11 us (1%)
  local copies, waits for them, and re-layouts  1.82 us (1%)
    pallas_call x2, Pallas kernels, layer(): pl.pallas_call(kernel, grid=(1,), in_specs=[pl.BlockSpec(memory_space=plt...  22 us
    pallas_call x6, Pallas kernels, on_blocks(): pl.pallas_call(kernel, grid=(1,), in_specs=specs, out_specs=[pl.BlockSpec...  17.7 us
    pallas_call x2, Pallas kernels, products(): pl.pallas_call(kernel, in_specs=[pl.BlockSpec(memory_space=pltpu.SMEM)] +...  15.5 us
    all_to_all x1, waiting for transfers between devices, route_images(): lax.all_to_all(outgoing, 'fsdp', split_axis=0, concat_axis=0, tiled=True)  14 us
    ppermute x6, waiting for transfers between devices, to_next(): lax.ppermute(block, 'fsdp', fsdp_route(lambda x, y, core: (x, y + 1, core)))  12.9 us
    ppermute x6, starting transfers between devices, to_previous(): lax.ppermute(block, 'fsdp', fsdp_route(lambda x, y, core: (x, y - 1, core)))  9.52 us
    ppermute x1, waiting for transfers between devices, move_images(): lax.ppermute(incoming, 'section', [(ring - 1, 0), (end - ring + 1, end)])  9.5 us
    pallas_call x3, Pallas kernels, pack(): pl.pallas_call(kernel, in_specs=[anywhere] * count, out_specs=pl.BlockSpe...  9.34 us
  transfers between devices with their start and end apart: 28, of which 9 were waited for; matrix products, arithmetic and copies ran while one was open for 4% of the time, Pallas kernels for 43%

profile of v2, /device:TPU:1, one launch (start us, length us, event | category | flops | bytes accessed | tf_op | source)
XLA Modules:
  0.0 170.6 jit_solution(16824133337355283986)
XLA Ops:
  0.6 1.5 collective-permute-start
  2.1 2.1 %pack.3.refs_0_.refs_1_ = bf16[2,448,512]{2,1,0:T(8,128)(2,1)} custom-call(bf16[1,448,512]{2,1,0:T(8,128)(2,1)} %weight.1, bf16[1,448,512]{2,1,0:T(8,128)(2,1)} %weight0.1), custom_call_target="tpu_custom_call" | custom-call | flops 1 | bytes 1 | tf_op jit(solution)/shard_map/pack/pallas_call | solution.py:188
  4.2 2.9 %collective-permute-start.3 = (bf16[2,448,512]{2,1,0:T(8,128)(2,1)}, bf16[2,448,512]{2,1,0:T(8,128)(2,1)}, u32[]{:S(2)}, u32[]{:S(2)}) collective-permute-start(bf16[2,448,512]{2,1,0:T(8,128)(2,1)} %pack.3.refs_0_.refs_1_), channel_id=1, source_target_pairs={{0,8},{1,9},{2,10},{3,11},{4,12},{5,13},{6,14},{7,15},{8,0},{9,1},... | collective-permute-start | bytes 2752520 | tf_op jit(solution)/shard_map/ppermute | solution.py:43
  7.1 2.7 %collective-permute-start.2 = (bf16[2,448,512]{2,1,0:T(8,128)(2,1)}, bf16[2,448,512]{2,1,0:T(8,128)(2,1)}, u32[]{:S(2)}, u32[]{:S(2)}) collective-permute-start(bf16[2,448,512]{2,1,0:T(8,128)(2,1)} %pack.3.refs_0_.refs_1_), channel_id=1, source_target_pairs={{0,6},{1,7},{2,0},{3,1},{4,2},{5,3},{6,4},{7,5},{8,14},{9,15},{10,... | collective-permute-start | bytes 2752520 | tf_op jit(solution)/shard_map/ppermute | solution.py:39
  9.9 0.7 fusion.9
  10.6 0.2 convert_reduce_fusion.2
  10.8 0.7 add_multiply_fusion
  11.5 0.1 iota_add_fusion
  11.5 0.1 add.89
  11.6 2.1 %fusion = bf16[16,8,2432]{2,1,0:T(8,128)(2,1)} fusion(bf16[2,64,7168]{2,1,0:T(8,128)(2,1)} %param.15, s32[]{:T(128)S(6)} %select_n.97, s32[]{:T(128)S(6)} %select_n.105, s32[64]{0:T(128)S(1)} %add.89), kind=kOutput, calls=%fused_computation.1 | convolution fusion | flops 40165376 | bytes 934152 | tf_op jit(solution)/shard_map/dot_general | solution.py:513
  13.7 5.1 %all-to-all-start = ((bf16[16,8,2432]{2,1,0:T(8,128)(2,1)}), bf16[16,8,2432]{2,1,0:T(8,128)(2,1)}, u32[]{:S(2)}, u32[]{:S(2)}) async-start(bf16[16,8,2432]{2,1,0:T(8,128)(2,1)} %fusion), calls=%async_computation | async-start | bytes 1245184 | tf_op jit(solution)/shard_map/all_to_all | solution.py:514
  18.9 7.3 %scale.1 = (bf16[2,1,256,512]{3,2,1,0:T(8,128)(2,1)}, f32[2,256,128]{2,1,0:T(8,128)}) custom-call(bf16[2,1,256,7168]{3,2,1,0:T(8,128)(2,1)} %x_ref.11, bf16[2,1,256,512]{3,2,1,0:T(8,128)(2,1)} %ct_ref.7), custom_call_target="tpu_custom_call" | custom-call | flops 1 | bytes 1 | tf_op jit(solution)/shard_map/scale/pallas_call | solution.py:89
  26.2 14.0 %all-to-all-done = bf16[16,8,2432]{2,1,0:T(8,128)(2,1)} async-done(((bf16[16,8,2432]{2,1,0:T(8,128)(2,1)}), bf16[16,8,2432]{2,1,0:T(8,128)(2,1)}, u32[]{:S(2)}, u32[]{:S(2)}) %all-to-all-start) | async-done | bytes 622624 | tf_op jit(solution)/shard_map/all_to_all | solution.py:514
  40.2 0.1 collective-permute-start.7
  40.3 0.9 collective-permute-start.8
  41.2 0.8 collective-permute-start.6
  42.0 0.6 convert_reduce_fusion
  42.7 0.1 copy.17
  42.8 0.1 reduce.3
  42.9 1.3 collective-permute-start.5
  44.2 1.3 collective-permute-start.4
  46.2 0.1 broadcast_in_dim.55
  46.3 0.1 mul.41
  46.4 0.1 broadcast_in_dim.54
  46.4 0.1 mul.39
  46.6 0.6 concatenate.3.table
  47.2 0.6 fusion.3.perm_ref
  47.8 4.0 %pack.4.refs_0_.weight1 = bf16[8,448,512]{2,1,0:T(8,128)(2,1)} custom-call(bf16[2,448,512]{2,1,0:T(8,128)(2,1)} %pack.3.refs_0_.refs_1_, bf16[2,448,512]{2,1,0:T(8,128)(2,1)} %pack.3.refs_0_.refs_1_, bf16[2,448,512]{2,1,0:T(8,128)(2,1)} %collective-permute-done.2.refs_2_.refs_3_, bf16[2,448,512]{2,1,0:T(8,128)(2,1)} %collective-permute-done.2.refs_2_.refs_3_, ...), custom_call_target="tpu_custom_call" | custom-call | flops 1 | bytes 1 | tf_op jit(solution)/shard_map/pack/pallas_call | solution.py:188
  51.8 9.5 %collective-permute-done.5.im2 = bf16[128,2432]{1,0:T(8,128)(2,1)} collective-permute-done((bf16[128,2432]{1,0:T(8,128)(2,1)}, bf16[128,2432]{1,0:T(8,128)(2,1)}, u32[]{:S(2)}, u32[]{:S(2)}) %collective-permute-start.5) | collective-permute-done | bytes 622624 | tf_op jit(solution)/shard_map/ppermute | solution.py:542
  61.3 6.7 %patch.1 = (bf16[128,7168]{1,0:T(8,128)(2,1)}, bf16[128,4096]{1,0:T(8,128)(2,1)}, bf16[2,1,256,512]{3,2,1,0:T(8,128)(2,1)}, f32[2,256,128]{2,1,0:T(8,128)}) custom-call(s32[17]{0:T(128)} %concatenate.3.table, bf16[2,1,256,7168]{3,2,1,0:T(8,128)(2,1)} %x_ref.11, bf16[2,1,256,512]{3,2,1,0:T(8,128)(2,1)} %ct_ref.7, bf16[128,128]{1,0:T(8,128)(2,1)} %fusion.3.perm_ref, ...), custom_call_target="tpu_custom_call" | custom-call | flops 1 | bytes 1 | tf_op jit(solution)/shard_map/patch/pallas_call | solution.py:143
  68.0 2.0 %collective-permute-start.9 = (bf16[128,4096]{1,0:T(8,128)(2,1)}, bf16[128,4096]{1,0:T(8,128)(2,1)}, u32[]{:S(2)}, u32[]{:S(2)}) collective-permute-start(bf16[128,4096]{1,0:T(8,128)(2,1)} %get-tuple-element.81), channel_id=1, source_target_pairs={{0,1},{1,0},{2,3},{3,2},{4,5},{5,4},{6,7},{7,6},{8,9},{9,8},{10,11... | collective-permute-start | bytes 3145736 | tf_op jit(solution)/shard_map/ppermute | solution.py:47
  70.0 0.1 collective-permute-start.10
  70.1 2.1 %halves.1 = (bf16[448,512]{1,0:T(8,128)(2,1)}, bf16[448,512]{1,0:T(8,128)(2,1)}) custom-call(bf16[2,448,512]{2,1,0:T(8,128)(2,1)} %collective-permute-done.8.first.refs_4_.refs_5_, bf16[2,448,512]{2,1,0:T(8,128)(2,1)} %collective-permute-done.7.second.refs_2_.refs_3_), custom_call_target="tpu_custom_call" | custom-call | flops 1 | bytes 1 | tf_op jit(solution)/shard_map/halves/pallas_call | solution.py:296
  72.2 0.0 collective-permute-start.11
  72.3 2.7 %collective-permute-start.12 = (bf16[448,512]{1,0:T(8,128)(2,1)}, bf16[448,512]{1,0:T(8,128)(2,1)S(1)}, u32[]{:S(2)}, u32[]{:S(2)}) collective-permute-start(bf16[448,512]{1,0:T(8,128)(2,1)} %get-tuple-element.89), channel_id=1, source_target_pairs={{0,6},{1,7},{2,0},{3,1},{4,2},{5,3},{6,4},{7,5},{8,14},{9,15},{10,... | collective-permute-start | bytes 1376264 | tf_op jit(solution)/shard_map/ppermute | solution.py:39
  74.9 6.5 %products.2 = (bf16[2,448,512]{2,1,0:T(8,128)(2,1)}, bf16[2,448,512]{2,1,0:T(8,128)(2,1)}, bf16[2,448,512]{2,1,0:T(8,128)(2,1)}) custom-call(s32[17]{0:T(128)} %concatenate.3.table, bf16[2,1,256,7168]{3,2,1,0:T(8,128)(2,1)} %x_ref.11, bf16[2,1,256,7168]{3,2,1,0:T(8,128)(2,1)} %collective-permute-done.sibling_x_ref, ...), custom_call_target="tpu_custom_call" | custom-call | flops 1 | bytes 1 | tf_op jit(solution)/shard_map/products/pallas_call | solution.py:266
  81.4 4.0 %collective-permute-done.11.refs_2_ = bf16[448,512]{1,0:T(8,128)(2,1)} collective-permute-done((bf16[448,512]{1,0:T(8,128)(2,1)}, bf16[448,512]{1,0:T(8,128)(2,1)}, u32[]{:S(2)}, u32[]{:S(2)}) %collective-permute-start.11) | collective-permute-done | bytes 458784 | tf_op jit(solution)/shard_map/ppermute | solution.py:35
  85.5 1.3 collective-permute-start.16
  86.7 2.7 %collective-permute-start.14 = (bf16[2,448,512]{2,1,0:T(8,128)(2,1)}, bf16[2,448,512]{2,1,0:T(8,128)(2,1)}, u32[]{:S(2)}, u32[]{:S(2)}) collective-permute-start(bf16[2,448,512]{2,1,0:T(8,128)(2,1)} %get-tuple-element.95), channel_id=1, source_target_pairs={{0,6},{1,7},{2,0},{3,1},{4,2},{5,3},{6,4},{7,5},{8,14},{9,15},{10,... | collective-permute-start | bytes 2752520 | tf_op jit(solution)/shard_map/ppermute | solution.py:39
  89.4 2.7 %collective-permute-start.15 = (bf16[2,448,512]{2,1,0:T(8,128)(2,1)}, bf16[2,448,512]{2,1,0:T(8,128)(2,1)}, u32[]{:S(2)}, u32[]{:S(2)}) collective-permute-start(bf16[2,448,512]{2,1,0:T(8,128)(2,1)} %get-tuple-element.96), channel_id=1, source_target_pairs={{0,8},{1,9},{2,10},{3,11},{4,12},{5,13},{6,14},{7,15},{8,0},{9,1},... | collective-permute-start | bytes 2752520 | tf_op jit(solution)/shard_map/ppermute | solution.py:43
  92.1 3.3 %pack.5.refs_1_ = bf16[6,448,512]{2,1,0:T(8,128)(2,1)} custom-call(bf16[2,448,512]{2,1,0:T(8,128)(2,1)} %collective-permute-done.6.refs_0_.refs_1_, bf16[2,448,512]{2,1,0:T(8,128)(2,1)} %collective-permute-done.6.refs_0_.refs_1_, bf16[2,448,512]{2,1,0:T(8,128)(2,1)} %collective-permute-done.7.second.refs_2_.refs_3_, ...), custom_call_target="tpu_custom_call" | custom-call | flops 1 | bytes 1 | tf_op jit(solution)/shard_map/pack/pallas_call | solution.py:188
  95.3 9.0 %products.3 = (bf16[1,448,512]{2,1,0:T(8,128)(2,1)}, bf16[1,448,512]{2,1,0:T(8,128)(2,1)}, bf16[1,448,512]{2,1,0:T(8,128)(2,1)}, bf16[2,448,512]{2,1,0:T(8,128)(...) custom-call(s32[17]{0:T(128)} %concatenate.3.table, ...), custom_call_target="tpu_custom_call" | custom-call | flops 1 | bytes 1 | tf_op jit(solution)/shard_map/products/pallas_call | solution.py:266
  104.3 5.8 %collective-permute-done.13.far0.below1 = bf16[2,448,512]{2,1,0:T(8,128)(2,1)} collective-permute-done((bf16[2,448,512]{2,1,0:T(8,128)(2,1)}, bf16[2,448,512]{2,1,0:T(8,128)(2,1)}, u32[]{:S(2)}, u32[]{:S(2)}) %collective-permute-start.13) | collective-permute-done | bytes 917536 | tf_op jit(solution)/shard_map/ppermute | solution.py:35
  110.1 2.3 %collective-permute-done.15.came2.came0 = bf16[2,448,512]{2,1,0:T(8,128)(2,1)} collective-permute-done((bf16[2,448,512]{2,1,0:T(8,128)(2,1)}, bf16[2,448,512]{2,1,0:T(8,128)(2,1)}, u32[]{:S(2)}, u32[]{:S(2)}) %collective-permute-start.15) | collective-permute-done | bytes 917536 | tf_op jit(solution)/shard_map/ppermute | solution.py:43
  112.5 3.0 %first_sums.1 = (bf16[672,512]{1,0:T(8,128)(2,1)}, bf16[672,512]{1,0:T(8,128)(2,1)}) custom-call(bf16[1,448,512]{2,1,0:T(8,128)(2,1)} %get-tuple-element.103.near0, bf16[2,448,512]{2,1,0:T(8,128)(2,1)} %collective-permute-done.13.far0.below1, bf16[1,448,512]{2,1,0:T(8,128)(2,1)} %get-tuple-element.105.back1, ...), custom_call_target="tpu_custom_call" | custom-call | flops 1 | bytes 1 | tf_op jit(solution)/shard_map/first_sums/pallas_call | solution.py:296
  115.4 1.5 collective-permute-start.20
  116.9 2.7 %collective-permute-start.17 = (bf16[2,448,512]{2,1,0:T(8,128)(2,1)}, bf16[2,448,512]{2,1,0:T(8,128)(2,1)}, u32[]{:S(2)}, u32[]{:S(2)}) collective-permute-start(bf16[2,448,512]{2,1,0:T(8,128)(2,1)} %get-tuple-element.110), channel_id=1, source_target_pairs={{0,8},{1,9},{2,10},{3,11},{4,12},{5,13},{6,14},{7,15},{8,0},{9,1},... | collective-permute-start | bytes 2752520 | tf_op jit(solution)/shard_map/ppermute | solution.py:43
  119.6 1.4 collective-permute-start.19
  121.0 0.1 collective-permute-start.18
  121.1 0.8 collective-permute-start.21
  121.9 1.8 %collective-permute-done.21.refs_5_ = bf16[448,512]{1,0:T(8,128)(2,1)} collective-permute-done((bf16[448,512]{1,0:T(8,128)(2,1)}, bf16[448,512]{1,0:T(8,128)(2,1)}, u32[]{:S(2)}, u32[]{:S(2)}) %collective-permute-start.21) | collective-permute-done | bytes 458784 | tf_op jit(solution)/shard_map/ppermute | solution.py:47
  123.7 11.0 %layer.2 = (bf16[2,1,256,512]{3,2,1,0:T(8,128)(2,1)}, bf16[2,1,256,7168]{3,2,1,0:T(8,128)(2,1)}) custom-call(s32[17]{0:T(128)} %concatenate.3.table, bf16[2,1,256,7168]{3,2,1,0:T(8,128)(2,1)} %x_ref.11, bf16[128,7168]{1,0:T(8,128)(2,1)} %get-tuple-element.78.head_ref, bf16[2,1,256,512]{3,2,1,0:T(8,128)(2,1)} %ct_ref.7, ...), custom_call_target="tpu_custom_call" | custom-call | flops 1 | bytes 1 | tf_op jit(solution)/shard_map/layer/pallas_call | solution.py:454
  134.7 1.9 %collective-permute-done.19.above.above1 = bf16[672,512]{1,0:T(8,128)(2,1)} collective-permute-done((bf16[672,512]{1,0:T(8,128)(2,1)}, bf16[672,512]{1,0:T(8,128)(2,1)}, u32[]{:S(2)}, u32[]{:S(2)}) %collective-permute-start.19) | collective-permute-done | bytes 688160 | tf_op jit(solution)/shard_map/ppermute | solution.py:39
  136.7 2.2 %collective-permute-done.18.below.below0 = bf16[672,512]{1,0:T(8,128)(2,1)} collective-permute-done((bf16[672,512]{1,0:T(8,128)(2,1)}, bf16[672,512]{1,0:T(8,128)(2,1)}, u32[]{:S(2)}, u32[]{:S(2)}) %collective-permute-start.18) | collective-permute-done | bytes 688160 | tf_op jit(solution)/shard_map/ppermute | solution.py:35
  138.9 3.8 %mirror_sums.1 = (bf16[464,512]{1,0:T(8,128)(2,1)}, bf16[464,512]{1,0:T(8,128)(2,1)}) custom-call(s32[17]{0:T(128)} %concatenate.3.table, bf16[2,448,512]{2,1,0:T(8,128)(2,1)} %get-tuple-element.131.own0.own1, bf16[672,512]{1,0:T(8,128)(2,1)} %collective-permute-done.18.below.below0, bf16[2,448,512]{2,1,0:T(8,128)(2,1)} %collective-permute-done.14.far1.above0, ...), custom_call_target="tpu_custom_call" | custom-call | flops 1 | bytes 1 | tf_op jit(solution)/shard_map/mirror_sums/pallas_call | solution.py:296
  142.7 3.4 %collective-permute-start.25 = (bf16[464,512]{1,0:T(8,128)(2,1)}, bf16[464,512]{1,0:T(8,128)(2,1)}, u32[]{:S(2)}, u32[]{:S(2)}) collective-permute-start(bf16[464,512]{1,0:T(8,128)(2,1)} %get-tuple-element.132), channel_id=1, source_target_pairs={{0,112},{1,113},{2,114},{3,115},{4,116},{5,117},{6,118},{7,119},{8... | collective-permute-start | bytes 1425416 | tf_op jit(solution)/shard_map/ppermute | solution.py:57
  146.1 0.5 collective-permute-start.26
  146.6 1.7 collective-permute-start.22
  148.3 3.4 %second_sums.1 = (bf16[448,512]{1,0:T(8,128)(2,1)}, bf16[448,512]{1,0:T(8,128)(2,1)}) custom-call(bf16[2,448,512]{2,1,0:T(8,128)(2,1)} %get-tuple-element.93.keep1.keep3, bf16[2,448,512]{2,1,0:T(8,128)(2,1)} %collective-permute-done.17.came1.came3, bf16[672,512]{1,0:T(8,128)(2,1)} %collective-permute-done.18.below.below0, ...), custom_call_target="tpu_custom_call" | custom-call | flops 1 | bytes 1 | tf_op jit(solution)/shard_map/second_sums/pallas_call | solution.py:296
  151.7 1.5 collective-permute-start.23
  153.2 11.0 %layer.3 = (bf16[2,1,256,512]{3,2,1,0:T(8,128)(2,1)}, bf16[2,1,256,7168]{3,2,1,0:T(8,128)(2,1)}) custom-call(s32[17]{0:T(128)} %concatenate.3.table, bf16[2,1,256,7168]{3,2,1,0:T(8,128)(2,1)} %x_ref.11, bf16[128,7168]{1,0:T(8,128)(2,1)} %get-tuple-element.78.head_ref, ...), custom_call_target="tpu_custom_call", output_to_operand_aliasing={{0}: (13, {}), {1}: (14, {})} | custom-call | flops 1 | bytes 1 | tf_op jit(solution)/shard_map/layer/pallas_call | solution.py:454
  164.2 0.8 collective-permute-done.23.below
  165.1 3.0 %down_sums.1 = (f32[448,512]{1,0:T(8,128)}, f32[1,448]{1,0:T(1,128)}) custom-call(s32[17]{0:T(128)} %concatenate.3.table, bf16[1,448,512]{2,1,0:T(8,128)(2,1)} %get-tuple-element.98.keep0, bf16[2,448,512]{2,1,0:T(8,128)(2,1)} %collective-permute-done.15.came2.came0, bf16[448,512]{1,0:T(8,128)(2,1)} %collective-permute-done.23.below, ...), custom_call_target="tpu_custom_call" | custom-call | flops 1 | bytes 1 | tf_op jit(solution)/shard_map/down_sums/pallas_call | solution.py:296
  168.1 2.5 %last_sums.1 = (f32[1,448,512]{2,1,0:T(8,128)}, f32[1,448]{1,0:T(1,128)}) custom-call(f32[448,512]{1,0:T(8,128)} %get-tuple-element.129.weight_part, f32[1,448]{1,0:T(1,128)} %get-tuple-element.130.gain_part, bf16[464,512]{1,0:T(8,128)(2,1)} %collective-permute-done.25.mirrored0, bf16[464,512]{1,0:T(8,128)(2,1)} %collective-permute-done.26.mirrored1), custom_call_target="tpu_custom_call" | custom-call | flops 1 | bytes 1 | tf_op jit(solution)/shard_map/last_sums/pallas_call | solution.py:296
  (32 shorter events, 0.1 us)
Async XLA Ops:
  0.6 39.5 %collective-permute-start = (bf16[2,1,256,7168]{3,2,1,0:T(8,128)(2,1)}, bf16[2,1,256,7168]{3,2,1,0:T(8,128)(2,1)}, u32[]{:S(2)}, u32[]{:S(2)}) collective-permute-start(bf16[2,1,256,7168]{3,2,1,0:T(8,128)(2,1)} %x_ref.11), channel_id=1, source_target_pairs={{0,1},{1,0},{2,3},{3,2},{4,5},{5,4},{6,7},{7,6},{8,9},{9,8},{10,11... | collective-permute-start | bytes 22020104 | tf_op jit(solution)/shard_map/ppermute | solution.py:47
  4.2 35.9 %collective-permute-start.3 = (bf16[2,448,512]{2,1,0:T(8,128)(2,1)}, bf16[2,448,512]{2,1,0:T(8,128)(2,1)}, u32[]{:S(2)}, u32[]{:S(2)}) collective-permute-start(bf16[2,448,512]{2,1,0:T(8,128)(2,1)} %pack.3.refs_0_.refs_1_), channel_id=1, source_target_pairs={{0,8},{1,9},{2,10},{3,11},{4,12},{5,13},{6,14},{7,15},{8,0},{9,1},... | collective-permute-start | bytes 2752520 | tf_op jit(solution)/shard_map/ppermute | solution.py:43
  7.1 33.0 %collective-permute-start.2 = (bf16[2,448,512]{2,1,0:T(8,128)(2,1)}, bf16[2,448,512]{2,1,0:T(8,128)(2,1)}, u32[]{:S(2)}, u32[]{:S(2)}) collective-permute-start(bf16[2,448,512]{2,1,0:T(8,128)(2,1)} %pack.3.refs_0_.refs_1_), channel_id=1, source_target_pairs={{0,6},{1,7},{2,0},{3,1},{4,2},{5,3},{6,4},{7,5},{8,14},{9,15},{10,... | collective-permute-start | bytes 2752520 | tf_op jit(solution)/shard_map/ppermute | solution.py:39
  9.9 30.3 %collective-permute-start.1 = (bf16[2,448,512]{2,1,0:T(8,128)(2,1)}, bf16[2,448,512]{2,1,0:T(8,128)(2,1)}, u32[]{:S(2)}, u32[]{:S(2)}) collective-permute-start(bf16[2,448,512]{2,1,0:T(8,128)(2,1)} %pack.3.refs_0_.refs_1_), channel_id=1, source_target_pairs={{0,2},{1,3},{2,4},{3,5},{4,6},{5,7},{6,0},{7,1},{8,10},{9,11},{10,... | collective-permute-start | bytes 2752520 | tf_op jit(solution)/shard_map/ppermute | solution.py:35
  13.7 26.4 %all-to-all-start = ((bf16[16,8,2432]{2,1,0:T(8,128)(2,1)}), bf16[16,8,2432]{2,1,0:T(8,128)(2,1)}, u32[]{:S(2)}, u32[]{:S(2)}) async-start(bf16[16,8,2432]{2,1,0:T(8,128)(2,1)} %fusion), calls=%async_computation | async-start | bytes 1245184 | tf_op jit(solution)/shard_map/all_to_all | solution.py:514
  18.8 23.2 %copy-start.1 = (s32[2,16,16]{2,1,0:T(8,128)S(1)}, s32[2,16,16]{2,1,0:T(8,128)}, u32[]{:S(2)}) copy-start(s32[2,16,16]{2,1,0:T(8,128)} %param.16) | copy-start | bytes 6148
  18.8 27.7 %copy-start.2 = (s32[3]{0:T(128)S(1)}, s32[3]{0:T(128)}, u32[]{:S(2)}) copy-start(s32[3]{0:T(128)} %constant.149.clone) | copy-start | bytes 40
  40.2 27.8 %collective-permute-start.7 = (bf16[2,448,512]{2,1,0:T(8,128)(2,1)}, bf16[2,448,512]{2,1,0:T(8,128)(2,1)}, u32[]{:S(2)}, u32[]{:S(2)}) collective-permute-start(bf16[2,448,512]{2,1,0:T(8,128)(2,1)} %collective-permute-done.3.refs_6_.refs_7_), channel_id=1, source_target_pairs={{0,6},{1,7},{2,0},{3,1},{4,2},{5,3},{6,4},{7,5},{8,14},{9,15},{10,... | collective-permute-start | bytes 2752520 | tf_op jit(solution)/shard_map/ppermute | solution.py:39
  40.3 27.8 %collective-permute-start.8 = (bf16[2,448,512]{2,1,0:T(8,128)(2,1)}, bf16[2,448,512]{2,1,0:T(8,128)(2,1)}, u32[]{:S(2)}, u32[]{:S(2)}) collective-permute-start(bf16[2,448,512]{2,1,0:T(8,128)(2,1)} %collective-permute-done.1.refs_4_.refs_5_), channel_id=1, source_target_pairs={{0,8},{1,9},{2,10},{3,11},{4,12},{5,13},{6,14},{7,15},{8,0},{9,1},... | collective-permute-start | bytes 2752520 | tf_op jit(solution)/shard_map/ppermute | solution.py:43
  41.2 26.8 %collective-permute-start.6 = (bf16[2,448,512]{2,1,0:T(8,128)(2,1)}, bf16[2,448,512]{2,1,0:T(8,128)(2,1)}, u32[]{:S(2)}, u32[]{:S(2)}) collective-permute-start(bf16[2,448,512]{2,1,0:T(8,128)(2,1)} %collective-permute-done.1.refs_4_.refs_5_), channel_id=1, source_target_pairs={{0,2},{1,3},{2,4},{3,5},{4,6},{5,7},{6,0},{7,1},{8,10},{9,11},{10,... | collective-permute-start | bytes 2752520 | tf_op jit(solution)/shard_map/ppermute | solution.py:35
  42.9 18.4 %collective-permute-start.5 = (bf16[128,2432]{1,0:T(8,128)(2,1)}, bf16[128,2432]{1,0:T(8,128)(2,1)}, u32[]{:S(2)}, u32[]{:S(2)}) collective-permute-start(bf16[128,2432]{1,0:T(8,128)(2,1)} %bitcast.9.im0), channel_id=1, source_target_pairs={{48,0},{64,112},{49,1},{65,113},{50,2},{66,114},{51,3},{67,115},{5... | collective-permute-start | bytes 1867784 | tf_op jit(solution)/shard_map/ppermute | solution.py:542
  44.2 17.1 %collective-permute-start.4 = (bf16[128,2432]{1,0:T(8,128)(2,1)}, bf16[128,2432]{1,0:T(8,128)(2,1)}, u32[]{:S(2)}, u32[]{:S(2)}) collective-permute-start(bf16[128,2432]{1,0:T(8,128)(2,1)} %bitcast.9.im0), channel_id=1, source_target_pairs={{16,0},{96,112},{17,1},{97,113},{18,2},{98,114},{19,3},{99,115},{2... | collective-permute-start | bytes 1867784 | tf_op jit(solution)/shard_map/ppermute | solution.py:541
  68.0 6.9 %collective-permute-start.9 = (bf16[128,4096]{1,0:T(8,128)(2,1)}, bf16[128,4096]{1,0:T(8,128)(2,1)}, u32[]{:S(2)}, u32[]{:S(2)}) collective-permute-start(bf16[128,4096]{1,0:T(8,128)(2,1)} %get-tuple-element.81), channel_id=1, source_target_pairs={{0,1},{1,0},{2,3},{3,2},{4,5},{5,4},{6,7},{7,6},{8,9},{9,8},{10,11... | collective-permute-start | bytes 3145736 | tf_op jit(solution)/shard_map/ppermute | solution.py:47
  70.0 4.9 %collective-permute-start.10 = (bf16[2,1,256,512]{3,2,1,0:T(8,128)(2,1)}, bf16[2,1,256,512]{3,2,1,0:T(8,128)(2,1)}, u32[]{:S(2)}, u32[]{:S(2)}) collective-permute-start(bf16[2,1,256,512]{3,2,1,0:T(8,128)(2,1)} %get-tuple-element.82.own_ct.scaled_ref), channel_id=1, source_target_pairs={{0,1},{1,0},{2,3},{3,2},{4,5},{5,4},{6,7},{7,6},{8,9},{9,8},{10,11... | collective-permute-start | bytes 1572872 | tf_op jit(solution)/shard_map/ppermute | solution.py:47
  72.2 13.2 %collective-permute-start.11 = (bf16[448,512]{1,0:T(8,128)(2,1)}, bf16[448,512]{1,0:T(8,128)(2,1)}, u32[]{:S(2)}, u32[]{:S(2)}) collective-permute-start(bf16[448,512]{1,0:T(8,128)(2,1)} %get-tuple-element.88), channel_id=1, source_target_pairs={{0,2},{1,3},{2,4},{3,5},{4,6},{5,7},{6,0},{7,1},{8,10},{9,11},{10,... | collective-permute-start | bytes 1376264 | tf_op jit(solution)/shard_map/ppermute | solution.py:35
  72.3 13.2 %collective-permute-start.12 = (bf16[448,512]{1,0:T(8,128)(2,1)}, bf16[448,512]{1,0:T(8,128)(2,1)S(1)}, u32[]{:S(2)}, u32[]{:S(2)}) collective-permute-start(bf16[448,512]{1,0:T(8,128)(2,1)} %get-tuple-element.89), channel_id=1, source_target_pairs={{0,6},{1,7},{2,0},{3,1},{4,2},{5,3},{6,4},{7,5},{8,14},{9,15},{10,... | collective-permute-start | bytes 1376264 | tf_op jit(solution)/shard_map/ppermute | solution.py:39
  85.5 61.2 %copy-start = (bf16[448,512]{1,0:T(8,128)(2,1)}, bf16[448,512]{1,0:T(8,128)(2,1)S(1)}, u32[]{:S(2)}) copy-start(bf16[448,512]{1,0:T(8,128)(2,1)S(1)} %collective-permute-done.12.refs_2_) | copy-start | bytes 1376260
  85.5 27.0 %collective-permute-start.16 = (bf16[8,448,512]{2,1,0:T(8,128)(2,1)}, bf16[8,448,512]{2,1,0:T(8,128)(2,1)}, u32[]{:S(2)}, u32[]{:S(2)}) collective-permute-start(bf16[8,448,512]{2,1,0:T(8,128)(2,1)} %pack.4.refs_0_.weight1), channel_id=1, source_target_pairs={{0,1},{1,0},{2,3},{3,2},{4,5},{5,4},{6,7},{7,6},{8,9},{9,8},{10,11... | collective-permute-start | bytes 11010056 | tf_op jit(solution)/shard_map/ppermute | solution.py:47
  86.7 23.4 %collective-permute-start.13 = (bf16[2,448,512]{2,1,0:T(8,128)(2,1)}, bf16[2,448,512]{2,1,0:T(8,128)(2,1)}, u32[]{:S(2)}, u32[]{:S(2)}) collective-permute-start(bf16[2,448,512]{2,1,0:T(8,128)(2,1)} %get-tuple-element.94), channel_id=1, source_target_pairs={{0,2},{1,3},{2,4},{3,5},{4,6},{5,7},{6,0},{7,1},{8,10},{9,11},{10,... | collective-permute-start | bytes 2752520 | tf_op jit(solution)/shard_map/ppermute | solution.py:35
  86.7 23.4 %collective-permute-start.14 = (bf16[2,448,512]{2,1,0:T(8,128)(2,1)}, bf16[2,448,512]{2,1,0:T(8,128)(2,1)}, u32[]{:S(2)}, u32[]{:S(2)}) collective-permute-start(bf16[2,448,512]{2,1,0:T(8,128)(2,1)} %get-tuple-element.95), channel_id=1, source_target_pairs={{0,6},{1,7},{2,0},{3,1},{4,2},{5,3},{6,4},{7,5},{8,14},{9,15},{10,... | collective-permute-start | bytes 2752520 | tf_op jit(solution)/shard_map/ppermute | solution.py:39
  89.4 23.1 %collective-permute-start.15 = (bf16[2,448,512]{2,1,0:T(8,128)(2,1)}, bf16[2,448,512]{2,1,0:T(8,128)(2,1)}, u32[]{:S(2)}, u32[]{:S(2)}) collective-permute-start(bf16[2,448,512]{2,1,0:T(8,128)(2,1)} %get-tuple-element.96), channel_id=1, source_target_pairs={{0,8},{1,9},{2,10},{3,11},{4,12},{5,13},{6,14},{7,15},{8,0},{9,1},... | collective-permute-start | bytes 2752520 | tf_op jit(solution)/shard_map/ppermute | solution.py:43
  115.4 8.3 %collective-permute-start.20 = (bf16[6,448,512]{2,1,0:T(8,128)(2,1)}, bf16[6,448,512]{2,1,0:T(8,128)(2,1)}, u32[]{:S(2)}, u32[]{:S(2)}) collective-permute-start(bf16[6,448,512]{2,1,0:T(8,128)(2,1)} %pack.5.refs_1_), channel_id=1, source_target_pairs={{0,1},{1,0},{2,3},{3,2},{4,5},{5,4},{6,7},{7,6},{8,9},{9,8},{10,11... | collective-permute-start | bytes 8257544 | tf_op jit(solution)/shard_map/ppermute | solution.py:47
  116.9 31.4 %collective-permute-start.17 = (bf16[2,448,512]{2,1,0:T(8,128)(2,1)}, bf16[2,448,512]{2,1,0:T(8,128)(2,1)}, u32[]{:S(2)}, u32[]{:S(2)}) collective-permute-start(bf16[2,448,512]{2,1,0:T(8,128)(2,1)} %get-tuple-element.110), channel_id=1, source_target_pairs={{0,8},{1,9},{2,10},{3,11},{4,12},{5,13},{6,14},{7,15},{8,0},{9,1},... | collective-permute-start | bytes 2752520 | tf_op jit(solution)/shard_map/ppermute | solution.py:43
  119.6 17.1 %collective-permute-start.19 = (bf16[672,512]{1,0:T(8,128)(2,1)}, bf16[672,512]{1,0:T(8,128)(2,1)}, u32[]{:S(2)}, u32[]{:S(2)}) collective-permute-start(bf16[672,512]{1,0:T(8,128)(2,1)} %get-tuple-element.111), channel_id=1, source_target_pairs={{0,6},{1,7},{2,0},{3,1},{4,2},{5,3},{6,4},{7,5},{8,14},{9,15},{10,... | collective-permute-start | bytes 2064392 | tf_op jit(solution)/shard_map/ppermute | solution.py:39
  121.0 18.0 %collective-permute-start.18 = (bf16[672,512]{1,0:T(8,128)(2,1)}, bf16[672,512]{1,0:T(8,128)(2,1)}, u32[]{:S(2)}, u32[]{:S(2)}) collective-permute-start(bf16[672,512]{1,0:T(8,128)(2,1)} %get-tuple-element.109), channel_id=1, source_target_pairs={{0,2},{1,3},{2,4},{3,5},{4,6},{5,7},{6,0},{7,1},{8,10},{9,11},{10,... | collective-permute-start | bytes 2064392 | tf_op jit(solution)/shard_map/ppermute | solution.py:35
  121.1 2.6 %collective-permute-start.21 = (bf16[448,512]{1,0:T(8,128)(2,1)}, bf16[448,512]{1,0:T(8,128)(2,1)}, u32[]{:S(2)}, u32[]{:S(2)}) collective-permute-start(bf16[448,512]{1,0:T(8,128)(2,1)} %collective-permute-done.11.refs_2_), channel_id=1, source_target_pairs={{0,1},{1,0},{2,3},{3,2},{4,5},{5,4},{6,7},{7,6},{8,9},{9,8},{10,11... | collective-permute-start | bytes 1376264 | tf_op jit(solution)/shard_map/ppermute | solution.py:47
  142.7 25.4 %collective-permute-start.25 = (bf16[464,512]{1,0:T(8,128)(2,1)}, bf16[464,512]{1,0:T(8,128)(2,1)}, u32[]{:S(2)}, u32[]{:S(2)}) collective-permute-start(bf16[464,512]{1,0:T(8,128)(2,1)} %get-tuple-element.132), channel_id=1, source_target_pairs={{0,112},{1,113},{2,114},{3,115},{4,116},{5,117},{6,118},{7,119},{8... | collective-permute-start | bytes 1425416 | tf_op jit(solution)/shard_map/ppermute | solution.py:57
  146.1 22.0 %collective-permute-start.26 = (bf16[464,512]{1,0:T(8,128)(2,1)}, bf16[464,512]{1,0:T(8,128)(2,1)}, u32[]{:S(2)}, u32[]{:S(2)}) collective-permute-start(bf16[464,512]{1,0:T(8,128)(2,1)} %get-tuple-element.133), channel_id=1, source_target_pairs={{0,120},{1,121},{2,122},{3,123},{4,124},{5,125},{6,126},{7,127},{8... | collective-permute-start | bytes 1425416 | tf_op jit(solution)/shard_map/ppermute | solution.py:57
  146.6 6.5 %collective-permute-start.22 = (bf16[448,512]{1,0:T(8,128)(2,1)S(1)}, bf16[448,512]{1,0:T(8,128)(2,1)}, u32[]{:S(2)}, u32[]{:S(2)}) collective-permute-start(bf16[448,512]{1,0:T(8,128)(2,1)S(1)} %collective-permute-done.12.refs_2_), channel_id=1, source_target_pairs={{0,1},{1,0},{2,3},{3,2},{4,5},{5,4},{6,7},{7,6},{8,9},{9,8},{10,11... | collective-permute-start | bytes 1376264 | tf_op jit(solution)/shard_map/ppermute | solution.py:47
  151.7 12.5 %collective-permute-start.24 = (bf16[448,512]{1,0:T(8,128)(2,1)}, bf16[448,512]{1,0:T(8,128)(2,1)}, u32[]{:S(2)}, u32[]{:S(2)}) collective-permute-start(bf16[448,512]{1,0:T(8,128)(2,1)} %get-tuple-element.126), channel_id=1, source_target_pairs={{0,6},{1,7},{2,0},{3,1},{4,2},{5,3},{6,4},{7,5},{8,14},{9,15},{10,... | collective-permute-start | bytes 1376264 | tf_op jit(solution)/shard_map/ppermute | solution.py:39
  151.7 13.4 %collective-permute-start.23 = (bf16[448,512]{1,0:T(8,128)(2,1)}, bf16[448,512]{1,0:T(8,128)(2,1)}, u32[]{:S(2)}, u32[]{:S(2)}) collective-permute-start(bf16[448,512]{1,0:T(8,128)(2,1)} %get-tuple-element.120), channel_id=1, source_target_pairs={{0,2},{1,3},{2,4},{3,5},{4,6},{5,7},{6,0},{7,1},{8,10},{9,11},{10,... | collective-permute-start | bytes 1376264 | tf_op jit(solution)/shard_map/ppermute | solution.py:35

commit v3 on v2

--- a/solution.py
+++ b/solution.py
@@ -10,7 +10,6 @@
 EPSILON = 1e-05
 HEAD = 128
 VMEM_BYTES = 63 * 1024 * 1024 + 512 * 1024
-PATCH_VMEM_BYTES = VMEM_BYTES
 SMALL = pl.CostEstimate(flops=1, bytes_accessed=1, transcendentals=0)
 F32 = jnp.float32
 BF16 = jnp.bfloat16
@@ -102,71 +101,94 @@
 
 
 def patch_kernel(
-    table, x_ref, ct_ref, perm_ref, ct_in, inverse_in, im0, im1, im2, head_ref, other_ref, ct_out, inverse_out, images, sems
+    table, ct_ref, perm_ref, x_ref, im0, im1, im2, ct_in, inverse_in, head_ref, other_ref, ct_out, inverse_out,
+    rows, others, images, new_ct, new_inverse, in_sems, out_sems,
 ):
     pipe = table[PIPE]
-    head_ref[...] = x_ref[0, 0]
-    ct_out[...] = ct_in[...]
-    inverse_out[...] = inverse_in[...]
+    width = rows.shape[1]
+    pair = width // CHIPS
+    window = others.shape[1] // CHIPS
 
     @pl.when(table[FLAG + pipe] == 1)
     def _():
+        coming = [pltpu.make_async_copy(x_ref.at[pipe, 0, pl.ds(0, HEAD)], rows, in_sems.at[0])]
+        for part, image in enumerate((im0, im1, im2)):
+            coming.append(pltpu.make_async_copy(image, images.at[part], in_sems.at[1 + part]))
+        for copy in coming:
+            copy.start()
+        for copy in coming:
+            copy.wait()
         live = lax.broadcasted_iota(jnp.int32, (HEAD, 1), 0) < table[LIVE]
-        copies = [
-            pltpu.make_async_copy(image, images.at[part], sems.at[part])
-            for part, image in enumerate((im0, im1, im2))
-        ]
-        for copy in copies:
-            copy.start()
-        for part, copy in enumerate(copies):
-            copy.wait()
+        for part in range(3):
             where = pl.ds(pl.multiple_of(table[PART + part], 128), images.shape[2])
             arrived = jnp.dot(perm_ref[...], images[part], preferred_element_type=F32).astype(BF16)
-            head_ref[:, where] = jnp.where(live, arrived, head_ref[:, where])
-        inverse = inverse_rms(head_ref)
-        ct_out[pipe, 0, :HEAD] = (ct_ref[0, 0].astype(F32) * inverse).astype(BF16)
-        inverse_out[pipe, :HEAD] = jnp.broadcast_to(inverse, (HEAD, inverse_out.shape[2]))
-
-    pair = head_ref.shape[1] // CHIPS
-    window = other_ref.shape[1] // CHIPS
-    for chip in range(CHIPS):
-        start = chip * pair + (1 - table[CORE]) * (pair - window)
-        other_ref[:, chip * window : (chip + 1) * window] = head_ref[
-            :, pl.ds(pl.multiple_of(start, 128), window)
-        ]
+            rows[:, where] = jnp.where(live, arrived, rows[:, where])
+        going = []
+        total = jnp.zeros((HEAD, pair), F32)
+        for chip in range(CHIPS):
+            start = chip * pair + (1 - table[CORE]) * (pair - window)
+            others[:, chip * window : (chip + 1) * window] = rows[
+                :, pl.ds(pl.multiple_of(start, 128), window)
+            ]
+            part = rows[:, chip * pair : (chip + 1) * pair].astype(F32)
+            total = total + part * part
+            if chip % 4 == 3:
+                for n, (source, target, size) in enumerate(((rows, head_ref, pair), (others, other_ref, window))):
+                    done = pl.ds((chip - 3) * size, 4 * size)
+                    going.append(
+                        pltpu.make_async_copy(source.at[:, done], target.at[:, done], out_sems.at[n, chip // 4])
+                    )
+                    going[-1].start()
+        inverse = lax.rsqrt(jnp.sum(total, axis=1, keepdims=True) / width + EPSILON)
+        new_ct[...] = (ct_ref[0, 0].astype(F32) * inverse).astype(BF16)
+        new_inverse[...] = jnp.broadcast_to(inverse, new_inverse.shape)
+        top = pl.ds(0, HEAD)
+        for n, (source, target) in enumerate(
+            ((new_ct, ct_out.at[pipe, 0, top]), (new_inverse, inverse_out.at[pipe, top]))
+        ):
+            going.append(pltpu.make_async_copy(source, target, out_sems.at[2, n]))
+            going[-1].start()
+        for copy in going:
+            copy.wait()
 
 
 def patch(table, section_inputs, cotangent, perm, images, scaled_ct, inverse):
     width = section_inputs.shape[3]
     kv = cotangent.shape[3]
-    whole = pl.BlockSpec(memory_space=pltpu.VMEM)
+    window = core_window(width)
+    anywhere = pl.BlockSpec(memory_space=pl.ANY)
     return pl.pallas_call(
         patch_kernel,
         grid_spec=pltpu.PrefetchScalarGridSpec(
             num_scalar_prefetch=1,
             grid=(1,),
             in_specs=[
-                pl.BlockSpec((1, 1, HEAD, width), lambda i, table: (table[PIPE], 0, 0, 0)),
                 pl.BlockSpec((1, 1, HEAD, kv), lambda i, table: (table[PIPE], 0, 0, 0)),
+                pl.BlockSpec(memory_space=pltpu.VMEM),
             ]
-            + [whole] * 3
-            + [pl.BlockSpec(memory_space=pl.ANY)] * 3,
-            out_specs=[whole] * 4,
+            + [anywhere] * 6,
+            out_specs=[anywhere] * 4,
             scratch_shapes=[
+                pltpu.VMEM((HEAD, width), BF16),
+                pltpu.VMEM((HEAD, CHIPS * window), BF16),
                 pltpu.VMEM((3, *images[0].shape), BF16),
-                pltpu.SemaphoreType.DMA((3,)),
+                pltpu.VMEM((HEAD, kv), BF16),
+                pltpu.VMEM((HEAD, inverse.shape[2]), F32),
+                pltpu.SemaphoreType.DMA((4,)),
+                pltpu.SemaphoreType.DMA((3, 2)),
             ],
         ),
         out_shape=[
             jax.ShapeDtypeStruct((HEAD, width), BF16),
-            jax.ShapeDtypeStruct((HEAD, CHIPS * core_window(width)), BF16),
+            jax.ShapeDtypeStruct((HEAD, CHIPS * window), BF16),
             jax.ShapeDtypeStruct(scaled_ct.shape, BF16),
             jax.ShapeDtypeStruct(inverse.shape, F32),
         ],
-        compiler_params=pltpu.CompilerParams(vmem_limit_bytes=PATCH_VMEM_BYTES),
+        input_output_aliases={7: 2, 8: 3},
+        compiler_params=pltpu.CompilerParams(vmem_limit_bytes=VMEM_BYTES),
         cost_estimate=SMALL,
         name="patch",
-    )(table, section_inputs, cotangent, perm, scaled_ct, inverse, *images)
+    )(table, cotangent, perm, section_inputs, *images, scaled_ct, inverse)
 
 
 def pack(parts):
@@ -217,7 +239,12 @@
     half = pair // 2
     window = core_window(width)
     kv = ct.shape[3]
-    order = [(g, i, *block) for g, group in enumerate(groups) for i, block in enumerate(group)]
+    order, sizes = [], []
+    for g, group in enumerate(groups):
+        sizes.append(0)
+        for pipe, r, low, high in group:
+            order.append((g, sizes[g], pipe, r, low, high))
+            sizes[g] += high - low
     count = len(order)
 
     def kernel(table, x_ref, sibling_x_ref, head_ref, sibling_head_ref, own_ct, other_ct, *refs):
@@ -225,7 +252,7 @@
         own, other, block, row_sems, out_sems = refs[len(groups) :]
         core = table[CORE]
         waits = []
-        for n, (_, _, pipe, r) in enumerate(order):
+        for n, (_, _, pipe, r, _, _) in enumerate(order):
             from_x = pl.ds(pl.multiple_of(table[r] * pair + core * (pair - window), 128), window)
             here = pl.ds(n * window, window)
             waits.append(
@@ -237,7 +264,7 @@
             )
         contract = (((0,), (0,)), ((), ()))
         written = []
-        for n, (out, at, pipe, r) in enumerate(order):
+        for n, (out, at, pipe, r, low, high) in enumerate(order):
             for copy in waits[n]:
                 copy.wait()
             here = slice(n * window, (n + 1) * window)
@@ -255,7 +282,9 @@
             def _():
                 block[n] = product[window - half :]
 
-            copy = pltpu.make_async_copy(block.at[n], outs[out].at[at], out_sems.at[n])
+            copy = pltpu.make_async_copy(
+                block.at[n, pl.ds(low, high - low)], outs[out].at[pl.ds(at, high - low)], out_sems.at[n]
+            )
             copy.start()
             written.append(copy)
         for copy in written:
@@ -267,7 +296,7 @@
         kernel,
         in_specs=[pl.BlockSpec(memory_space=pltpu.SMEM)] + [anywhere] * 4 + [whole] * 2,
         out_specs=[anywhere for _ in groups],
-        out_shape=[jax.ShapeDtypeStruct((len(g), half, kv), BF16) for g in groups],
+        out_shape=[jax.ShapeDtypeStruct((size, kv), BF16) for size in sizes],
         scratch_shapes=[
             pltpu.VMEM((tokens, count * window), BF16),
             pltpu.VMEM((tokens, count * window), BF16),
@@ -317,8 +346,9 @@
     second_out[...] = second[...]
 
 
-def first_sums(near0, far0, back1, far1, keep2, came2, up, down):
+def first_sums(near0, from_below, back1, from_above, keep2, came20, up, down):
     rows = near0.shape[0]
+    far0, far1, came2 = from_below.at[:rows], from_above.at[:rows], came20.at[:rows]
     half = rows // 2
     far = wide(keep2, came2).astype(BF16)
     up[:rows] = wide(near0, far0).astype(BF16)
@@ -342,8 +372,10 @@
     return jnp.transpose(jnp.broadcast_to(row, (8, pair // 2)))[:, :1]
 
 
-def mirror_sums(table, own0, below0, above0, own1, below1, above1, weight0, weight1, gain, here, there):
-    rows = own0.shape[0]
+def mirror_sums(table, own, below0, from_above, from_below, above1, weight0, weight1, gain, here, there):
+    rows = own.shape[0] // 2
+    own0, own1 = own.at[:rows], own.at[rows:]
+    above0, below1 = from_above.at[rows:], from_below.at[rows:]
     for out, sums, weight, chip in (
         (here, (own0, below0.at[:rows], above0), weight0, table[0]),
         (there, (own1, below1, above1.at[:rows]), weight1, table[Y_CHIPS]),
@@ -354,8 +386,10 @@
         out[rows : rows + 8, :rows] = jnp.broadcast_to(gain_row(weight, share), (8, rows)).astype(BF16)
 
 
-def second_sums(keep1, came1, below, keep3, came3, above, ups, downs):
+def second_sums(keep13, came130, below, above, ups, downs):
     rows = ups.shape[0]
+    keep1, keep3 = keep13.at[:rows], keep13.at[rows:]
+    came1, came3 = came130.at[:rows], came130.at[rows : 2 * rows]
     half = rows // 2
     ups[...] = wide(keep1, came1).astype(BF16)
     downs[...] = wide(keep3, came3).astype(BF16)
@@ -363,8 +397,10 @@
     downs[half:] = wide(downs.at[half:], above.at[rows:]).astype(BF16)
 
 
-def down_sums(table, keep0, came0, below, above, weight, gain, weight_part, gain_part):
-    share = wide(keep0, came0, below, above)
+def down_sums(table, keep0, came20, came130, below, above, weight, gain, weight_part, gain_part):
+    rows = keep0.shape[0]
+    came0 = jnp.concatenate([came20[rows:], came130[2 * rows :]]).astype(F32)
+    share = wide(keep0, below, above) + came0
     weight_part[...] = share * gain_column(table, gain, table[0])
     gain_part[...] = gain_row(weight, share)
 
@@ -589,38 +625,48 @@
     down6, up6 = to_next(down7), to_previous(up5)
 
     rows = (section_inputs, sibling_x, head, sibling_head, scaled_ct, sibling_ct)
+    half = shard // 2
+
+    def blocks(*parts):
+        return tuple((pipe, r, 0, shard) for pipe, r in parts)
+
     far0_near1, far1_back0, send20 = products(
-        table, *rows, (((1, 2), (1, 5)), ((1, 6), (1, 3)), ((0, 6), (0, 4)))
+        table,
+        *rows,
+        (blocks((1, 2), (1, 5)), blocks((1, 6), (1, 3)), (*blocks((0, 6)), (0, 4, 0, half))),
     )
     far0_near1, far1_back0, send20, down6, up6, w7, early = hold(
         (far0_near1, far1_back0, send20, down6, up6, w7, early)
     )
+    from_below, from_above, came20 = to_next(far0_near1), to_previous(far1_back0), to_across(send20)
     sibling_early = to_sibling(early)
-    from_below, from_above, came20 = to_next(far0_near1), to_previous(far1_back0), to_across(send20)
     down_places = ((0, 0), (0, 2), (1, 0), (0, 4), (0, 6), (1, 2), (2, None), (1, 4))
     up_places = ((0, 1), (0, 3), (1, 1), (0, 5), (0, 7), (1, 3), (3, None), (1, 5))
-    near0, back1, keep2, send13, own01, keep13, keep0 = products(
+    near0, back1, keep2, send130, own01, keep13, keep0 = products(
         hold(table, up6),
         *rows,
-        (((1, 1),), ((1, 7),), ((0, 2),), ((0, 5), (0, 7)), ((1, 0), (1, 4)), ((0, 1), (0, 3)), ((0, 0),)),
+        (
+            blocks((1, 1)), blocks((1, 7)), blocks((0, 2)), (*blocks((0, 5), (0, 7)), (0, 4, half, shard)),
+            blocks((1, 0), (1, 4)), blocks((0, 1), (0, 3)), blocks((0, 0)),
+        ),
     )
 
     def pieces(arrays, places):
         return [(arrays[array], at) for array, at in places]
 
     middle = pack([(w2, 0), (w2, 1), (w5, 0), (w5, 1), (w7, 0), (w7, 1)])
-    from_below, from_above, came20, send13 = hold(
-        (from_below, from_above, came20, send13), keep0, middle, sibling_early
+    from_below, from_above, came20, send130 = hold(
+        (from_below, from_above, came20, send130), keep0, middle, sibling_early
     )
     message = jax.ShapeDtypeStruct((shard + shard // 2, kv), BF16)
     up, down = on_blocks(
         "first_sums",
         first_sums,
-        [(near0, 0), (from_below, 0), (back1, 0), (from_above, 0), (keep2, 0), (came20, 0)],
+        [near0, from_below, back1, from_above, keep2, came20],
         [message, message],
     )
     below, above = to_next(up), to_previous(down)
-    came13 = to_across(hold(send13, up))
+    came130 = to_across(hold(send130, up))
     own = (early, middle, down6, up6)
     sibling = [sibling_early, *[to_sibling(hold(array, up)) for array in (middle, down6, up6)]]
     filled = layer(
@@ -635,8 +681,7 @@
         "mirror_sums",
         mirror_sums,
         [
-            table, (own01, 0), below, (from_above, 1), (own01, 1), (from_below, 1), above,
-            (up_weight, 0), (early, 7), up_gain,
+            table, own01, below, from_above, from_below, above, (up_weight, 0), (early, 7), up_gain,
         ],
         [payload, payload],
     )
@@ -644,7 +689,7 @@
     ups, downs = on_blocks(
         "second_sums",
         second_sums,
-        [(keep13, 0), (came13, 0), below, (keep13, 1), (came13, 1), above],
+        [keep13, came130, below, above],
         [part, part],
     )
     last_below, last_above = to_next(ups), to_previous(downs)
@@ -658,7 +703,7 @@
     weight_part, gain_part = on_blocks(
         "down_sums",
         down_sums,
-        [table, (keep0, 0), (came20, 1), last_below, last_above, (down_weight, 0), down_gain],
+        [table, keep0, came20, came130, last_below, last_above, (down_weight, 0), down_gain],
         [jax.ShapeDtypeStruct((shard, kv), F32), jax.ShapeDtypeStruct((1, shard), F32)],
     )
     mirrored0, mirrored1 = hold((mirrored0, mirrored1), weight_part)

time: 171 us -> 170 us (level)
  waiting for transfers between devices: 42.5 us -> 40.1 us
    ppermute x6, waiting for transfers between devices: 12.9 us -> 10.6 us  [to_next(): lax.ppermute(block, 'fsdp', fsdp_route(lambda x, y, core: (x, y + 1, core)))]
where the time goes in v3:
time: 170 us; the launch traced here: 169 us
  Pallas kernels  79.3 us (47%)
  starting transfers between devices  41.9 us (25%)
  waiting for transfers between devices  40.1 us (24%)
  other arithmetic  2.4 us (1%)
  matrix products  2.11 us (1%)
  local copies, waits for them, and re-layouts  1.88 us (1%)
    pallas_call x2, Pallas kernels, layer(): pl.pallas_call(kernel, grid=(1,), in_specs=[pl.BlockSpec(memory_space=plt...  22 us
    pallas_call x6, Pallas kernels, on_blocks(): pl.pallas_call(kernel, grid=(1,), in_specs=specs, out_specs=[pl.BlockSpec...  18.8 us
    pallas_call x2, Pallas kernels, products(): pl.pallas_call(kernel, in_specs=[pl.BlockSpec(memory_space=pltpu.SMEM)] +...  15.8 us
    all_to_all x1, waiting for transfers between devices, route_images(): lax.all_to_all(outgoing, 'fsdp', split_axis=0, concat_axis=0, tiled=True)  14 us
    ppermute x6, starting transfers between devices, to_previous(): lax.ppermute(block, 'fsdp', fsdp_route(lambda x, y, core: (x, y - 1, core)))  10.8 us
    ppermute x6, waiting for transfers between devices, to_next(): lax.ppermute(block, 'fsdp', fsdp_route(lambda x, y, core: (x, y + 1, core)))  10.6 us
    ppermute x1, waiting for transfers between devices, move_images(): lax.ppermute(incoming, 'section', [(ring - 1, 0), (end - ring + 1, end)])  9.42 us
    pallas_call x3, Pallas kernels, pack(): pl.pallas_call(kernel, in_specs=[anywhere] * count, out_specs=pl.BlockSpe...  9.34 us
  transfers between devices with their start and end apart: 28, of which 9 were waited for; matrix products, arithmetic and copies ran while one was open for 4% of the time, Pallas kernels for 43%

profile of v3, /device:TPU:1, one launch (start us, length us, event | category | flops | bytes accessed | tf_op | source)
XLA Modules:
  0.0 169.3 jit_solution(7333889798769364447)
XLA Ops:
  0.6 1.5 collective-permute-start
  2.1 2.1 %pack.3.refs_0_.refs_1_ = bf16[2,448,512]{2,1,0:T(8,128)(2,1)} custom-call(bf16[1,448,512]{2,1,0:T(8,128)(2,1)} %weight.1, bf16[1,448,512]{2,1,0:T(8,128)(2,1)} %weight0.1), custom_call_target="tpu_custom_call" | custom-call | flops 1 | bytes 1 | tf_op jit(solution)/shard_map/pack/pallas_call | solution.py:210
  4.2 2.9 %collective-permute-start.3 = (bf16[2,448,512]{2,1,0:T(8,128)(2,1)}, bf16[2,448,512]{2,1,0:T(8,128)(2,1)}, u32[]{:S(2)}, u32[]{:S(2)}) collective-permute-start(bf16[2,448,512]{2,1,0:T(8,128)(2,1)} %pack.3.refs_0_.refs_1_), channel_id=1, source_target_pairs={{0,8},{1,9},{2,10},{3,11},{4,12},{5,13},{6,14},{7,15},{8,0},{9,1},... | collective-permute-start | bytes 2752520 | tf_op jit(solution)/shard_map/ppermute | solution.py:42
  7.1 2.7 %collective-permute-start.2 = (bf16[2,448,512]{2,1,0:T(8,128)(2,1)}, bf16[2,448,512]{2,1,0:T(8,128)(2,1)}, u32[]{:S(2)}, u32[]{:S(2)}) collective-permute-start(bf16[2,448,512]{2,1,0:T(8,128)(2,1)} %pack.3.refs_0_.refs_1_), channel_id=1, source_target_pairs={{0,6},{1,7},{2,0},{3,1},{4,2},{5,3},{6,4},{7,5},{8,14},{9,15},{10,... | collective-permute-start | bytes 2752520 | tf_op jit(solution)/shard_map/ppermute | solution.py:38
  9.9 0.7 fusion.9
  10.6 0.2 convert_reduce_fusion.2
  10.8 0.7 add_multiply_fusion
  11.5 0.1 iota_add_fusion
  11.5 0.1 add.89
  11.6 2.1 %fusion = bf16[16,8,2432]{2,1,0:T(8,128)(2,1)} fusion(bf16[2,64,7168]{2,1,0:T(8,128)(2,1)} %param.15, s32[]{:T(128)S(6)} %select_n.97, s32[]{:T(128)S(6)} %select_n.105, s32[64]{0:T(128)S(1)} %add.89), kind=kOutput, calls=%fused_computation.1 | convolution fusion | flops 40165376 | bytes 934152 | tf_op jit(solution)/shard_map/dot_general | solution.py:549
  13.7 5.1 %all-to-all-start = ((bf16[16,8,2432]{2,1,0:T(8,128)(2,1)}), bf16[16,8,2432]{2,1,0:T(8,128)(2,1)}, u32[]{:S(2)}, u32[]{:S(2)}) async-start(bf16[16,8,2432]{2,1,0:T(8,128)(2,1)} %fusion), calls=%async_computation | async-start | bytes 1245184 | tf_op jit(solution)/shard_map/all_to_all | solution.py:550
  18.8 0.0 copy-start.2
  18.9 7.3 %scale.1 = (bf16[2,1,256,512]{3,2,1,0:T(8,128)(2,1)}, f32[2,256,128]{2,1,0:T(8,128)}) custom-call(bf16[2,1,256,7168]{3,2,1,0:T(8,128)(2,1)} %x_ref.11, bf16[2,1,256,512]{3,2,1,0:T(8,128)(2,1)} %ct_ref.7), custom_call_target="tpu_custom_call" | custom-call | flops 1 | bytes 1 | tf_op jit(solution)/shard_map/scale/pallas_call | solution.py:88
  26.2 14.0 %all-to-all-done = bf16[16,8,2432]{2,1,0:T(8,128)(2,1)} async-done(((bf16[16,8,2432]{2,1,0:T(8,128)(2,1)}), bf16[16,8,2432]{2,1,0:T(8,128)(2,1)}, u32[]{:S(2)}, u32[]{:S(2)}) %all-to-all-start) | async-done | bytes 622624 | tf_op jit(solution)/shard_map/all_to_all | solution.py:550
  40.2 0.1 collective-permute-start.7
  40.3 0.9 collective-permute-start.8
  41.2 0.8 collective-permute-start.6
  42.0 0.6 convert_reduce_fusion
  42.7 0.1 copy.19
  42.8 0.1 reduce.3
  42.9 1.3 collective-permute-start.5
  44.2 1.3 collective-permute-start.4
  46.2 0.1 broadcast_in_dim.55
  46.3 0.1 mul.41
  46.4 0.1 broadcast_in_dim.54
  46.4 0.1 mul.39
  46.6 0.7 concatenate.3.table
  47.3 0.6 fusion.3.perm_ref
  47.9 4.0 %pack.4.refs_0_.weight1 = bf16[8,448,512]{2,1,0:T(8,128)(2,1)} custom-call(bf16[2,448,512]{2,1,0:T(8,128)(2,1)} %pack.3.refs_0_.refs_1_, bf16[2,448,512]{2,1,0:T(8,128)(2,1)} %pack.3.refs_0_.refs_1_, bf16[2,448,512]{2,1,0:T(8,128)(2,1)} %collective-permute-done.2.refs_2_.refs_3_, bf16[2,448,512]{2,1,0:T(8,128)(2,1)} %collective-permute-done.2.refs_2_.refs_3_, ...), custom_call_target="tpu_custom_call" | custom-call | flops 1 | bytes 1 | tf_op jit(solution)/shard_map/pack/pallas_call | solution.py:210
  51.9 9.4 %collective-permute-done.5.im2 = bf16[128,2432]{1,0:T(8,128)(2,1)} collective-permute-done((bf16[128,2432]{1,0:T(8,128)(2,1)}, bf16[128,2432]{1,0:T(8,128)(2,1)}, u32[]{:S(2)}, u32[]{:S(2)}) %collective-permute-start.5) | collective-permute-done | bytes 622624 | tf_op jit(solution)/shard_map/ppermute | solution.py:578
  61.3 6.0 %patch.1 = (bf16[128,7168]{1,0:T(8,128)(2,1)}, bf16[128,4096]{1,0:T(8,128)(2,1)}, bf16[2,1,256,512]{3,2,1,0:T(8,128)(2,1)}, f32[2,256,128]{2,1,0:T(8,128)}) custom-call(s32[17]{0:T(128)} %concatenate.3.table, bf16[2,1,256,512]{3,2,1,0:T(8,128)(2,1)} %ct_ref.7, bf16[128,128]{1,0:T(8,128)(2,1)} %fusion.3.perm_ref, ...), custom_call_target="tpu_custom_call", output_to_operand_aliasing={{2}: (7, {}), {3}: (8, {})} | custom-call | flops 1 | bytes 1 | tf_op jit(solution)/shard_map/patch/pallas_call | solution.py:160
  67.3 2.0 %collective-permute-start.9 = (bf16[128,4096]{1,0:T(8,128)(2,1)}, bf16[128,4096]{1,0:T(8,128)(2,1)}, u32[]{:S(2)}, u32[]{:S(2)}) collective-permute-start(bf16[128,4096]{1,0:T(8,128)(2,1)} %get-tuple-element.81), channel_id=1, source_target_pairs={{0,1},{1,0},{2,3},{3,2},{4,5},{5,4},{6,7},{7,6},{8,9},{9,8},{10,11... | collective-permute-start | bytes 3145736 | tf_op jit(solution)/shard_map/ppermute | solution.py:46
  69.3 0.1 collective-permute-start.10
  69.4 2.1 %halves.1 = (bf16[448,512]{1,0:T(8,128)(2,1)}, bf16[448,512]{1,0:T(8,128)(2,1)}) custom-call(bf16[2,448,512]{2,1,0:T(8,128)(2,1)} %collective-permute-done.8.first.refs_4_.refs_5_, bf16[2,448,512]{2,1,0:T(8,128)(2,1)} %collective-permute-done.7.second.refs_2_.refs_3_), custom_call_target="tpu_custom_call" | custom-call | flops 1 | bytes 1 | tf_op jit(solution)/shard_map/halves/pallas_call | solution.py:325
  71.5 2.7 %collective-permute-start.12 = (bf16[448,512]{1,0:T(8,128)(2,1)}, bf16[448,512]{1,0:T(8,128)(2,1)S(1)}, u32[]{:S(2)}, u32[]{:S(2)}) collective-permute-start(bf16[448,512]{1,0:T(8,128)(2,1)} %get-tuple-element.89), channel_id=1, source_target_pairs={{0,6},{1,7},{2,0},{3,1},{4,2},{5,3},{6,4},{7,5},{8,14},{9,15},{10,... | collective-permute-start | bytes 1376264 | tf_op jit(solution)/shard_map/ppermute | solution.py:38
  74.2 6.4 %products.2 = (bf16[896,512]{1,0:T(8,128)(2,1)}, bf16[896,512]{1,0:T(8,128)(2,1)}, bf16[672,512]{1,0:T(8,128)(2,1)}) custom-call(s32[17]{0:T(128)} %concatenate.3.table, bf16[2,1,256,7168]{3,2,1,0:T(8,128)(2,1)} %x_ref.11, bf16[2,1,256,7168]{3,2,1,0:T(8,128)(2,1)} %collective-permute-done.sibling_x_ref, bf16[128,7168]{1,0:T(8,128)(2,1)} %get-tuple-element.78.head_ref, ...), custom_call_target="tpu_custom_call" | custom-call | flops 1 | bytes 1 | tf_op jit(solution)/shard_map/products/pallas_call | solution.py:295
  80.6 4.1 %collective-permute-done.11.refs_2_ = bf16[448,512]{1,0:T(8,128)(2,1)} collective-permute-done((bf16[448,512]{1,0:T(8,128)(2,1)}, bf16[448,512]{1,0:T(8,128)(2,1)}, u32[]{:S(2)}, u32[]{:S(2)}) %collective-permute-start.11) | collective-permute-done | bytes 458784 | tf_op jit(solution)/shard_map/ppermute | solution.py:34
  84.7 1.3 collective-permute-start.16
  86.0 2.7 %collective-permute-start.14 = (bf16[896,512]{1,0:T(8,128)(2,1)}, bf16[896,512]{1,0:T(8,128)(2,1)}, u32[]{:S(2)}, u32[]{:S(2)}) collective-permute-start(bf16[896,512]{1,0:T(8,128)(2,1)} %get-tuple-element.95), channel_id=1, source_target_pairs={{0,6},{1,7},{2,0},{3,1},{4,2},{5,3},{6,4},{7,5},{8,14},{9,15},{10,... | collective-permute-start | bytes 2752520 | tf_op jit(solution)/shard_map/ppermute | solution.py:38
  88.6 2.7 %collective-permute-start.15 = (bf16[672,512]{1,0:T(8,128)(2,1)}, bf16[672,512]{1,0:T(8,128)(2,1)}, u32[]{:S(2)}, u32[]{:S(2)}) collective-permute-start(bf16[672,512]{1,0:T(8,128)(2,1)} %get-tuple-element.96), channel_id=1, source_target_pairs={{0,8},{1,9},{2,10},{3,11},{4,12},{5,13},{6,14},{7,15},{8,0},{9,1},... | collective-permute-start | bytes 2064392 | tf_op jit(solution)/shard_map/ppermute | solution.py:42
  91.3 3.3 %pack.5.refs_1_ = bf16[6,448,512]{2,1,0:T(8,128)(2,1)} custom-call(bf16[2,448,512]{2,1,0:T(8,128)(2,1)} %collective-permute-done.6.refs_0_.refs_1_, bf16[2,448,512]{2,1,0:T(8,128)(2,1)} %collective-permute-done.6.refs_0_.refs_1_, bf16[2,448,512]{2,1,0:T(8,128)(2,1)} %collective-permute-done.7.second.refs_2_.refs_3_, ...), custom_call_target="tpu_custom_call" | custom-call | flops 1 | bytes 1 | tf_op jit(solution)/shard_map/pack/pallas_call | solution.py:210
  94.6 9.4 %products.3 = (bf16[448,512]{1,0:T(8,128)(2,1)}, bf16[448,512]{1,0:T(8,128)(2,1)}, bf16[448,512]{1,0:T(8,128)(2,1)}, bf16[1120,512]{1,0:T(8,128)(2,1)}, bf16[896...) custom-call(s32[17]{0:T(128)} %concatenate.3.table, bf16[2,1,256,7168]{3,2,1,0:T(8,128)(2,1)} %x_ref.11, ...), custom_call_target="tpu_custom_call" | custom-call | flops 1 | bytes 1 | tf_op jit(solution)/shard_map/products/pallas_call | solution.py:295
  104.0 2.8 %collective-permute-done.15.came20 = bf16[672,512]{1,0:T(8,128)(2,1)} collective-permute-done((bf16[672,512]{1,0:T(8,128)(2,1)}, bf16[672,512]{1,0:T(8,128)(2,1)}, u32[]{:S(2)}, u32[]{:S(2)}) %collective-permute-start.15) | collective-permute-done | bytes 688160 | tf_op jit(solution)/shard_map/ppermute | solution.py:42
  106.8 2.6 %collective-permute-done.13.from_below = bf16[896,512]{1,0:T(8,128)(2,1)} collective-permute-done((bf16[896,512]{1,0:T(8,128)(2,1)}, bf16[896,512]{1,0:T(8,128)(2,1)}, u32[]{:S(2)}, u32[]{:S(2)}) %collective-permute-start.13) | collective-permute-done | bytes 917536 | tf_op jit(solution)/shard_map/ppermute | solution.py:34
  109.4 3.4 %first_sums.1 = (bf16[672,512]{1,0:T(8,128)(2,1)}, bf16[672,512]{1,0:T(8,128)(2,1)}) custom-call(bf16[448,512]{1,0:T(8,128)(2,1)} %get-tuple-element.103.near0, bf16[896,512]{1,0:T(8,128)(2,1)} %collective-permute-done.13.from_below, bf16[448,512]{1,0:T(8,128)(2,1)} %get-tuple-element.105.back1, bf16[896,512]{1,0:T(8,128)(2,1)} %collective-permute-done.14.from_above, ...), custom_call_target="tpu_custom_call" | custom-call | flops 1 | bytes 1 | tf_op jit(solution)/shard_map/first_sums/pallas_call | solution.py:325
  112.7 0.9 collective-permute-start.20
  113.6 2.7 %collective-permute-start.17 = (bf16[1120,512]{1,0:T(8,128)(2,1)}, bf16[1120,512]{1,0:T(8,128)(2,1)}, u32[]{:S(2)}, u32[]{:S(2)}) collective-permute-start(bf16[1120,512]{1,0:T(8,128)(2,1)} %get-tuple-element.110), channel_id=1, source_target_pairs={{0,8},{1,9},{2,10},{3,11},{4,12},{5,13},{6,14},{7,15},{8,0},{9,1},... | collective-permute-start | bytes 3440648 | tf_op jit(solution)/shard_map/ppermute | solution.py:42
  116.3 2.7 %collective-permute-start.19 = (bf16[672,512]{1,0:T(8,128)(2,1)}, bf16[672,512]{1,0:T(8,128)(2,1)}, u32[]{:S(2)}, u32[]{:S(2)}) collective-permute-start(bf16[672,512]{1,0:T(8,128)(2,1)} %get-tuple-element.111), channel_id=1, source_target_pairs={{0,6},{1,7},{2,0},{3,1},{4,2},{5,3},{6,4},{7,5},{8,14},{9,15},{10,... | collective-permute-start | bytes 2064392 | tf_op jit(solution)/shard_map/ppermute | solution.py:38
  119.0 0.6 collective-permute-start.21
  119.5 1.8 %collective-permute-done.21.refs_5_ = bf16[448,512]{1,0:T(8,128)(2,1)} collective-permute-done((bf16[448,512]{1,0:T(8,128)(2,1)}, bf16[448,512]{1,0:T(8,128)(2,1)}, u32[]{:S(2)}, u32[]{:S(2)}) %collective-permute-start.21) | collective-permute-done | bytes 458784 | tf_op jit(solution)/shard_map/ppermute | solution.py:46
  121.3 11.0 %layer.2 = (bf16[2,1,256,512]{3,2,1,0:T(8,128)(2,1)}, bf16[2,1,256,7168]{3,2,1,0:T(8,128)(2,1)}) custom-call(s32[17]{0:T(128)} %concatenate.3.table, bf16[2,1,256,7168]{3,2,1,0:T(8,128)(2,1)} %x_ref.11, bf16[128,7168]{1,0:T(8,128)(2,1)} %get-tuple-element.78.head_ref, bf16[2,1,256,512]{3,2,1,0:T(8,128)(2,1)} %ct_ref.7, ...), custom_call_target="tpu_custom_call" | custom-call | flops 1 | bytes 1 | tf_op jit(solution)/shard_map/layer/pallas_call | solution.py:490
  132.3 1.5 collective-permute-done.19.above.above1
  133.8 3.1 %collective-permute-done.18.below.below0 = bf16[672,512]{1,0:T(8,128)(2,1)} collective-permute-done((bf16[672,512]{1,0:T(8,128)(2,1)}, bf16[672,512]{1,0:T(8,128)(2,1)}, u32[]{:S(2)}, u32[]{:S(2)}) %collective-permute-start.18) | collective-permute-done | bytes 688160 | tf_op jit(solution)/shard_map/ppermute | solution.py:34
  136.9 4.1 %mirror_sums.1 = (bf16[464,512]{1,0:T(8,128)(2,1)}, bf16[464,512]{1,0:T(8,128)(2,1)}) custom-call(s32[17]{0:T(128)} %concatenate.3.table, bf16[896,512]{1,0:T(8,128)(2,1)} %get-tuple-element.131.own, bf16[672,512]{1,0:T(8,128)(2,1)} %collective-permute-done.18.below.below0, bf16[896,512]{1,0:T(8,128)(2,1)} %collective-permute-done.14.from_above, ...), custom_call_target="tpu_custom_call" | custom-call | flops 1 | bytes 1 | tf_op jit(solution)/shard_map/mirror_sums/pallas_call | solution.py:325
  141.0 3.4 %collective-permute-start.25 = (bf16[464,512]{1,0:T(8,128)(2,1)}, bf16[464,512]{1,0:T(8,128)(2,1)}, u32[]{:S(2)}, u32[]{:S(2)}) collective-permute-start(bf16[464,512]{1,0:T(8,128)(2,1)} %get-tuple-element.132), channel_id=1, source_target_pairs={{0,112},{1,113},{2,114},{3,115},{4,116},{5,117},{6,118},{7,119},{8... | collective-permute-start | bytes 1425416 | tf_op jit(solution)/shard_map/ppermute | solution.py:56
  144.4 0.6 collective-permute-start.26
  144.9 1.7 %collective-permute-start.22 = (bf16[448,512]{1,0:T(8,128)(2,1)S(1)}, bf16[448,512]{1,0:T(8,128)(2,1)}, u32[]{:S(2)}, u32[]{:S(2)}) collective-permute-start(bf16[448,512]{1,0:T(8,128)(2,1)S(1)} %collective-permute-done.12.refs_2_), channel_id=1, source_target_pairs={{0,1},{1,0},{2,3},{3,2},{4,5},{5,4},{6,7},{7,6},{8,9},{9,8},{10,11... | collective-permute-start | bytes 1376264 | tf_op jit(solution)/shard_map/ppermute | solution.py:46
  146.6 3.4 %second_sums.1 = (bf16[448,512]{1,0:T(8,128)(2,1)}, bf16[448,512]{1,0:T(8,128)(2,1)}) custom-call(bf16[896,512]{1,0:T(8,128)(2,1)} %get-tuple-element.93.keep13, bf16[1120,512]{1,0:T(8,128)(2,1)} %collective-permute-done.17.came130, bf16[672,512]{1,0:T(8,128)(2,1)} %collective-permute-done.18.below.below0, bf16[672,512]{1,0:T(8,128)(2,1)} %collective-permute-done.19.above.above1), custom_call_target="tpu_custom_call" | custom-call | flops 1 | bytes 1 | tf_op jit(solution)/shard_map/second_sums/pallas_call | solution.py:325
  150.0 0.0 collective-permute-start.24
  150.0 1.5 collective-permute-start.23
  151.5 11.0 %layer.3 = (bf16[2,1,256,512]{3,2,1,0:T(8,128)(2,1)}, bf16[2,1,256,7168]{3,2,1,0:T(8,128)(2,1)}) custom-call(s32[17]{0:T(128)} %concatenate.3.table, bf16[2,1,256,7168]{3,2,1,0:T(8,128)(2,1)} %x_ref.11, bf16[128,7168]{1,0:T(8,128)(2,1)} %get-tuple-element.78.head_ref, ...), custom_call_target="tpu_custom_call", output_to_operand_aliasing={{0}: (13, {}), {1}: (14, {})} | custom-call | flops 1 | bytes 1 | tf_op jit(solution)/shard_map/layer/pallas_call | solution.py:490
  162.5 0.8 collective-permute-done.23.below
  163.4 3.4 %down_sums.1 = (f32[448,512]{1,0:T(8,128)}, f32[1,448]{1,0:T(1,128)}) custom-call(s32[17]{0:T(128)} %concatenate.3.table, bf16[448,512]{1,0:T(8,128)(2,1)} %get-tuple-element.98.keep0, bf16[672,512]{1,0:T(8,128)(2,1)} %collective-permute-done.15.came20, bf16[1120,512]{1,0:T(8,128)(2,1)} %collective-permute-done.17.came130, ...), custom_call_target="tpu_custom_call" | custom-call | flops 1 | bytes 1 | tf_op jit(solution)/shard_map/down_sums/pallas_call | solution.py:325
  166.8 2.5 %last_sums.1 = (f32[1,448,512]{2,1,0:T(8,128)}, f32[1,448]{1,0:T(1,128)}) custom-call(f32[448,512]{1,0:T(8,128)} %get-tuple-element.129.weight_part, f32[1,448]{1,0:T(1,128)} %get-tuple-element.130.gain_part, bf16[464,512]{1,0:T(8,128)(2,1)} %collective-permute-done.25.mirrored0, bf16[464,512]{1,0:T(8,128)(2,1)} %collective-permute-done.26.mirrored1), custom_call_target="tpu_custom_call" | custom-call | flops 1 | bytes 1 | tf_op jit(solution)/shard_map/last_sums/pallas_call | solution.py:325
  (32 shorter events, 0.1 us)
Async XLA Ops:
  0.6 39.5 %collective-permute-start = (bf16[2,1,256,7168]{3,2,1,0:T(8,128)(2,1)}, bf16[2,1,256,7168]{3,2,1,0:T(8,128)(2,1)}, u32[]{:S(2)}, u32[]{:S(2)}) collective-permute-start(bf16[2,1,256,7168]{3,2,1,0:T(8,128)(2,1)} %x_ref.11), channel_id=1, source_target_pairs={{0,1},{1,0},{2,3},{3,2},{4,5},{5,4},{6,7},{7,6},{8,9},{9,8},{10,11... | collective-permute-start | bytes 22020104 | tf_op jit(solution)/shard_map/ppermute | solution.py:46
  4.2 35.9 %collective-permute-start.3 = (bf16[2,448,512]{2,1,0:T(8,128)(2,1)}, bf16[2,448,512]{2,1,0:T(8,128)(2,1)}, u32[]{:S(2)}, u32[]{:S(2)}) collective-permute-start(bf16[2,448,512]{2,1,0:T(8,128)(2,1)} %pack.3.refs_0_.refs_1_), channel_id=1, source_target_pairs={{0,8},{1,9},{2,10},{3,11},{4,12},{5,13},{6,14},{7,15},{8,0},{9,1},... | collective-permute-start | bytes 2752520 | tf_op jit(solution)/shard_map/ppermute | solution.py:42
  7.1 33.0 %collective-permute-start.2 = (bf16[2,448,512]{2,1,0:T(8,128)(2,1)}, bf16[2,448,512]{2,1,0:T(8,128)(2,1)}, u32[]{:S(2)}, u32[]{:S(2)}) collective-permute-start(bf16[2,448,512]{2,1,0:T(8,128)(2,1)} %pack.3.refs_0_.refs_1_), channel_id=1, source_target_pairs={{0,6},{1,7},{2,0},{3,1},{4,2},{5,3},{6,4},{7,5},{8,14},{9,15},{10,... | collective-permute-start | bytes 2752520 | tf_op jit(solution)/shard_map/ppermute | solution.py:38
  9.9 30.3 %collective-permute-start.1 = (bf16[2,448,512]{2,1,0:T(8,128)(2,1)}, bf16[2,448,512]{2,1,0:T(8,128)(2,1)}, u32[]{:S(2)}, u32[]{:S(2)}) collective-permute-start(bf16[2,448,512]{2,1,0:T(8,128)(2,1)} %pack.3.refs_0_.refs_1_), channel_id=1, source_target_pairs={{0,2},{1,3},{2,4},{3,5},{4,6},{5,7},{6,0},{7,1},{8,10},{9,11},{10,... | collective-permute-start | bytes 2752520 | tf_op jit(solution)/shard_map/ppermute | solution.py:34
  13.7 26.4 %all-to-all-start = ((bf16[16,8,2432]{2,1,0:T(8,128)(2,1)}), bf16[16,8,2432]{2,1,0:T(8,128)(2,1)}, u32[]{:S(2)}, u32[]{:S(2)}) async-start(bf16[16,8,2432]{2,1,0:T(8,128)(2,1)} %fusion), calls=%async_computation | async-start | bytes 1245184 | tf_op jit(solution)/shard_map/all_to_all | solution.py:550
  18.8 23.2 %copy-start.1 = (s32[2,16,16]{2,1,0:T(8,128)S(1)}, s32[2,16,16]{2,1,0:T(8,128)}, u32[]{:S(2)}) copy-start(s32[2,16,16]{2,1,0:T(8,128)} %param.16) | copy-start | bytes 6148
  18.8 27.7 %copy-start.2 = (s32[3]{0:T(128)S(1)}, s32[3]{0:T(128)}, u32[]{:S(2)}) copy-start(s32[3]{0:T(128)} %constant.149.clone) | copy-start | bytes 40
  40.2 27.1 %collective-permute-start.7 = (bf16[2,448,512]{2,1,0:T(8,128)(2,1)}, bf16[2,448,512]{2,1,0:T(8,128)(2,1)}, u32[]{:S(2)}, u32[]{:S(2)}) collective-permute-start(bf16[2,448,512]{2,1,0:T(8,128)(2,1)} %collective-permute-done.3.refs_6_.refs_7_), channel_id=1, source_target_pairs={{0,6},{1,7},{2,0},{3,1},{4,2},{5,3},{6,4},{7,5},{8,14},{9,15},{10,... | collective-permute-start | bytes 2752520 | tf_op jit(solution)/shard_map/ppermute | solution.py:38
  40.3 27.0 %collective-permute-start.8 = (bf16[2,448,512]{2,1,0:T(8,128)(2,1)}, bf16[2,448,512]{2,1,0:T(8,128)(2,1)}, u32[]{:S(2)}, u32[]{:S(2)}) collective-permute-start(bf16[2,448,512]{2,1,0:T(8,128)(2,1)} %collective-permute-done.1.refs_4_.refs_5_), channel_id=1, source_target_pairs={{0,8},{1,9},{2,10},{3,11},{4,12},{5,13},{6,14},{7,15},{8,0},{9,1},... | collective-permute-start | bytes 2752520 | tf_op jit(solution)/shard_map/ppermute | solution.py:42
  41.2 26.1 %collective-permute-start.6 = (bf16[2,448,512]{2,1,0:T(8,128)(2,1)}, bf16[2,448,512]{2,1,0:T(8,128)(2,1)}, u32[]{:S(2)}, u32[]{:S(2)}) collective-permute-start(bf16[2,448,512]{2,1,0:T(8,128)(2,1)} %collective-permute-done.1.refs_4_.refs_5_), channel_id=1, source_target_pairs={{0,2},{1,3},{2,4},{3,5},{4,6},{5,7},{6,0},{7,1},{8,10},{9,11},{10,... | collective-permute-start | bytes 2752520 | tf_op jit(solution)/shard_map/ppermute | solution.py:34
  42.9 18.4 %collective-permute-start.5 = (bf16[128,2432]{1,0:T(8,128)(2,1)}, bf16[128,2432]{1,0:T(8,128)(2,1)}, u32[]{:S(2)}, u32[]{:S(2)}) collective-permute-start(bf16[128,2432]{1,0:T(8,128)(2,1)} %bitcast.9.im0), channel_id=1, source_target_pairs={{48,0},{64,112},{49,1},{65,113},{50,2},{66,114},{51,3},{67,115},{5... | collective-permute-start | bytes 1867784 | tf_op jit(solution)/shard_map/ppermute | solution.py:578
  44.2 17.1 %collective-permute-start.4 = (bf16[128,2432]{1,0:T(8,128)(2,1)}, bf16[128,2432]{1,0:T(8,128)(2,1)}, u32[]{:S(2)}, u32[]{:S(2)}) collective-permute-start(bf16[128,2432]{1,0:T(8,128)(2,1)} %bitcast.9.im0), channel_id=1, source_target_pairs={{16,0},{96,112},{17,1},{97,113},{18,2},{98,114},{19,3},{99,115},{2... | collective-permute-start | bytes 1867784 | tf_op jit(solution)/shard_map/ppermute | solution.py:577
  67.3 6.9 %collective-permute-start.9 = (bf16[128,4096]{1,0:T(8,128)(2,1)}, bf16[128,4096]{1,0:T(8,128)(2,1)}, u32[]{:S(2)}, u32[]{:S(2)}) collective-permute-start(bf16[128,4096]{1,0:T(8,128)(2,1)} %get-tuple-element.81), channel_id=1, source_target_pairs={{0,1},{1,0},{2,3},{3,2},{4,5},{5,4},{6,7},{7,6},{8,9},{9,8},{10,11... | collective-permute-start | bytes 3145736 | tf_op jit(solution)/shard_map/ppermute | solution.py:46
  69.3 4.9 %collective-permute-start.10 = (bf16[2,1,256,512]{3,2,1,0:T(8,128)(2,1)}, bf16[2,1,256,512]{3,2,1,0:T(8,128)(2,1)}, u32[]{:S(2)}, u32[]{:S(2)}) collective-permute-start(bf16[2,1,256,512]{3,2,1,0:T(8,128)(2,1)} %get-tuple-element.82.own_ct.scaled_ref), channel_id=1, source_target_pairs={{0,1},{1,0},{2,3},{3,2},{4,5},{5,4},{6,7},{7,6},{8,9},{9,8},{10,11... | collective-permute-start | bytes 1572872 | tf_op jit(solution)/shard_map/ppermute | solution.py:46
  71.5 13.2 %collective-permute-start.11 = (bf16[448,512]{1,0:T(8,128)(2,1)}, bf16[448,512]{1,0:T(8,128)(2,1)}, u32[]{:S(2)}, u32[]{:S(2)}) collective-permute-start(bf16[448,512]{1,0:T(8,128)(2,1)} %get-tuple-element.88), channel_id=1, source_target_pairs={{0,2},{1,3},{2,4},{3,5},{4,6},{5,7},{6,0},{7,1},{8,10},{9,11},{10,... | collective-permute-start | bytes 1376264 | tf_op jit(solution)/shard_map/ppermute | solution.py:34
  71.5 13.2 %collective-permute-start.12 = (bf16[448,512]{1,0:T(8,128)(2,1)}, bf16[448,512]{1,0:T(8,128)(2,1)S(1)}, u32[]{:S(2)}, u32[]{:S(2)}) collective-permute-start(bf16[448,512]{1,0:T(8,128)(2,1)} %get-tuple-element.89), channel_id=1, source_target_pairs={{0,6},{1,7},{2,0},{3,1},{4,2},{5,3},{6,4},{7,5},{8,14},{9,15},{10,... | collective-permute-start | bytes 1376264 | tf_op jit(solution)/shard_map/ppermute | solution.py:38
  84.7 60.2 %copy-start = (bf16[448,512]{1,0:T(8,128)(2,1)}, bf16[448,512]{1,0:T(8,128)(2,1)S(1)}, u32[]{:S(2)}) copy-start(bf16[448,512]{1,0:T(8,128)(2,1)S(1)} %collective-permute-done.12.refs_2_) | copy-start | bytes 1376260
  84.7 24.7 %collective-permute-start.16 = (bf16[8,448,512]{2,1,0:T(8,128)(2,1)}, bf16[8,448,512]{2,1,0:T(8,128)(2,1)}, u32[]{:S(2)}, u32[]{:S(2)}) collective-permute-start(bf16[8,448,512]{2,1,0:T(8,128)(2,1)} %pack.4.refs_0_.weight1), channel_id=1, source_target_pairs={{0,1},{1,0},{2,3},{3,2},{4,5},{5,4},{6,7},{7,6},{8,9},{9,8},{10,11... | collective-permute-start | bytes 11010056 | tf_op jit(solution)/shard_map/ppermute | solution.py:46
  86.0 23.4 %collective-permute-start.13 = (bf16[896,512]{1,0:T(8,128)(2,1)}, bf16[896,512]{1,0:T(8,128)(2,1)}, u32[]{:S(2)}, u32[]{:S(2)}) collective-permute-start(bf16[896,512]{1,0:T(8,128)(2,1)} %get-tuple-element.94), channel_id=1, source_target_pairs={{0,2},{1,3},{2,4},{3,5},{4,6},{5,7},{6,0},{7,1},{8,10},{9,11},{10,... | collective-permute-start | bytes 2752520 | tf_op jit(solution)/shard_map/ppermute | solution.py:34
  86.0 23.4 %collective-permute-start.14 = (bf16[896,512]{1,0:T(8,128)(2,1)}, bf16[896,512]{1,0:T(8,128)(2,1)}, u32[]{:S(2)}, u32[]{:S(2)}) collective-permute-start(bf16[896,512]{1,0:T(8,128)(2,1)} %get-tuple-element.95), channel_id=1, source_target_pairs={{0,6},{1,7},{2,0},{3,1},{4,2},{5,3},{6,4},{7,5},{8,14},{9,15},{10,... | collective-permute-start | bytes 2752520 | tf_op jit(solution)/shard_map/ppermute | solution.py:38
  88.6 18.2 %collective-permute-start.15 = (bf16[672,512]{1,0:T(8,128)(2,1)}, bf16[672,512]{1,0:T(8,128)(2,1)}, u32[]{:S(2)}, u32[]{:S(2)}) collective-permute-start(bf16[672,512]{1,0:T(8,128)(2,1)} %get-tuple-element.96), channel_id=1, source_target_pairs={{0,8},{1,9},{2,10},{3,11},{4,12},{5,13},{6,14},{7,15},{8,0},{9,1},... | collective-permute-start | bytes 2064392 | tf_op jit(solution)/shard_map/ppermute | solution.py:42
  112.7 8.6 %collective-permute-start.20 = (bf16[6,448,512]{2,1,0:T(8,128)(2,1)}, bf16[6,448,512]{2,1,0:T(8,128)(2,1)}, u32[]{:S(2)}, u32[]{:S(2)}) collective-permute-start(bf16[6,448,512]{2,1,0:T(8,128)(2,1)} %pack.5.refs_1_), channel_id=1, source_target_pairs={{0,1},{1,0},{2,3},{3,2},{4,5},{5,4},{6,7},{7,6},{8,9},{9,8},{10,11... | collective-permute-start | bytes 8257544 | tf_op jit(solution)/shard_map/ppermute | solution.py:46
  113.6 33.0 %collective-permute-start.17 = (bf16[1120,512]{1,0:T(8,128)(2,1)}, bf16[1120,512]{1,0:T(8,128)(2,1)}, u32[]{:S(2)}, u32[]{:S(2)}) collective-permute-start(bf16[1120,512]{1,0:T(8,128)(2,1)} %get-tuple-element.110), channel_id=1, source_target_pairs={{0,8},{1,9},{2,10},{3,11},{4,12},{5,13},{6,14},{7,15},{8,0},{9,1},... | collective-permute-start | bytes 3440648 | tf_op jit(solution)/shard_map/ppermute | solution.py:42
  116.3 17.5 %collective-permute-start.19 = (bf16[672,512]{1,0:T(8,128)(2,1)}, bf16[672,512]{1,0:T(8,128)(2,1)}, u32[]{:S(2)}, u32[]{:S(2)}) collective-permute-start(bf16[672,512]{1,0:T(8,128)(2,1)} %get-tuple-element.111), channel_id=1, source_target_pairs={{0,6},{1,7},{2,0},{3,1},{4,2},{5,3},{6,4},{7,5},{8,14},{9,15},{10,... | collective-permute-start | bytes 2064392 | tf_op jit(solution)/shard_map/ppermute | solution.py:38
  119.0 18.0 %collective-permute-start.18 = (bf16[672,512]{1,0:T(8,128)(2,1)}, bf16[672,512]{1,0:T(8,128)(2,1)}, u32[]{:S(2)}, u32[]{:S(2)}) collective-permute-start(bf16[672,512]{1,0:T(8,128)(2,1)} %get-tuple-element.109), channel_id=1, source_target_pairs={{0,2},{1,3},{2,4},{3,5},{4,6},{5,7},{6,0},{7,1},{8,10},{9,11},{10,... | collective-permute-start | bytes 2064392 | tf_op jit(solution)/shard_map/ppermute | solution.py:34
  119.0 2.3 %collective-permute-start.21 = (bf16[448,512]{1,0:T(8,128)(2,1)}, bf16[448,512]{1,0:T(8,128)(2,1)}, u32[]{:S(2)}, u32[]{:S(2)}) collective-permute-start(bf16[448,512]{1,0:T(8,128)(2,1)} %collective-permute-done.11.refs_2_), channel_id=1, source_target_pairs={{0,1},{1,0},{2,3},{3,2},{4,5},{5,4},{6,7},{7,6},{8,9},{9,8},{10,11... | collective-permute-start | bytes 1376264 | tf_op jit(solution)/shard_map/ppermute | solution.py:46
  141.0 25.8 %collective-permute-start.25 = (bf16[464,512]{1,0:T(8,128)(2,1)}, bf16[464,512]{1,0:T(8,128)(2,1)}, u32[]{:S(2)}, u32[]{:S(2)}) collective-permute-start(bf16[464,512]{1,0:T(8,128)(2,1)} %get-tuple-element.132), channel_id=1, source_target_pairs={{0,112},{1,113},{2,114},{3,115},{4,116},{5,117},{6,118},{7,119},{8... | collective-permute-start | bytes 1425416 | tf_op jit(solution)/shard_map/ppermute | solution.py:56
  144.4 22.4 %collective-permute-start.26 = (bf16[464,512]{1,0:T(8,128)(2,1)}, bf16[464,512]{1,0:T(8,128)(2,1)}, u32[]{:S(2)}, u32[]{:S(2)}) collective-permute-start(bf16[464,512]{1,0:T(8,128)(2,1)} %get-tuple-element.133), channel_id=1, source_target_pairs={{0,120},{1,121},{2,122},{3,123},{4,124},{5,125},{6,126},{7,127},{8... | collective-permute-start | bytes 1425416 | tf_op jit(solution)/shard_map/ppermute | solution.py:56
  144.9 6.6 %collective-permute-start.22 = (bf16[448,512]{1,0:T(8,128)(2,1)S(1)}, bf16[448,512]{1,0:T(8,128)(2,1)}, u32[]{:S(2)}, u32[]{:S(2)}) collective-permute-start(bf16[448,512]{1,0:T(8,128)(2,1)S(1)} %collective-permute-done.12.refs_2_), channel_id=1, source_target_pairs={{0,1},{1,0},{2,3},{3,2},{4,5},{5,4},{6,7},{7,6},{8,9},{9,8},{10,11... | collective-permute-start | bytes 1376264 | tf_op jit(solution)/shard_map/ppermute | solution.py:46
  150.0 12.5 %collective-permute-start.24 = (bf16[448,512]{1,0:T(8,128)(2,1)}, bf16[448,512]{1,0:T(8,128)(2,1)}, u32[]{:S(2)}, u32[]{:S(2)}) collective-permute-start(bf16[448,512]{1,0:T(8,128)(2,1)} %get-tuple-element.126), channel_id=1, source_target_pairs={{0,6},{1,7},{2,0},{3,1},{4,2},{5,3},{6,4},{7,5},{8,14},{9,15},{10,... | collective-permute-start | bytes 1376264 | tf_op jit(solution)/shard_map/ppermute | solution.py:38
  150.0 13.4 %collective-permute-start.23 = (bf16[448,512]{1,0:T(8,128)(2,1)}, bf16[448,512]{1,0:T(8,128)(2,1)}, u32[]{:S(2)}, u32[]{:S(2)}) collective-permute-start(bf16[448,512]{1,0:T(8,128)(2,1)} %get-tuple-element.120), channel_id=1, source_target_pairs={{0,2},{1,3},{2,4},{3,5},{4,6},{5,7},{6,0},{7,1},{8,10},{9,11},{10,... | collective-permute-start | bytes 1376264 | tf_op jit(solution)/shard_map/ppermute | solution.py:34

commit v4 on v3

--- a/solution.py
+++ b/solution.py
@@ -313,14 +313,16 @@
 def on_blocks(name, kernel, operands, outs):
     specs, arrays = [], []
     for operand in operands:
-        array, at = operand if isinstance(operand, tuple) else (operand, None)
+        array, *which = operand if isinstance(operand, tuple) else (operand,)
         shape = array.shape
         if len(shape) == 1:
             specs.append(pl.BlockSpec(memory_space=pltpu.SMEM))
-        elif at is None:
+        elif not which:
             specs.append(pl.BlockSpec(shape, lambda i, n=len(shape): (0,) * n))
+        elif len(which) == 1:
+            specs.append(pl.BlockSpec((pl.squeezed, *shape[1:]), lambda i, at=which[0]: (at, 0, 0)))
         else:
-            specs.append(pl.BlockSpec((pl.squeezed, *shape[1:]), lambda i, at=at: (at, 0, 0)))
+            specs.append(pl.BlockSpec((which[0], shape[1]), lambda i, at=which[1]: (at, 0)))
         arrays.append(array)
     return pl.pallas_call(
         kernel,
@@ -346,9 +348,8 @@
     second_out[...] = second[...]
 
 
-def first_sums(near0, from_below, back1, from_above, keep2, came20, up, down):
+def first_sums(near0, far0, back1, far1, keep2, came2, up, down):
     rows = near0.shape[0]
-    far0, far1, came2 = from_below.at[:rows], from_above.at[:rows], came20.at[:rows]
     half = rows // 2
     far = wide(keep2, came2).astype(BF16)
     up[:rows] = wide(near0, far0).astype(BF16)
@@ -372,13 +373,11 @@
     return jnp.transpose(jnp.broadcast_to(row, (8, pair // 2)))[:, :1]
 
 
-def mirror_sums(table, own, below0, from_above, from_below, above1, weight0, weight1, gain, here, there):
-    rows = own.shape[0] // 2
-    own0, own1 = own.at[:rows], own.at[rows:]
-    above0, below1 = from_above.at[rows:], from_below.at[rows:]
+def mirror_sums(table, own0, below0, above0, own1, below1, above1, weight0, weight1, gain, here, there):
+    rows = own0.shape[0]
     for out, sums, weight, chip in (
-        (here, (own0, below0.at[:rows], above0), weight0, table[0]),
-        (there, (own1, below1, above1.at[:rows]), weight1, table[Y_CHIPS]),
+        (here, (own0, below0, above0), weight0, table[0]),
+        (there, (own1, below1, above1), weight1, table[Y_CHIPS]),
     ):
         share = wide(*sums)
         out[:rows] = (share * gain_column(table, gain, chip)).astype(BF16)
@@ -386,21 +385,17 @@
         out[rows : rows + 8, :rows] = jnp.broadcast_to(gain_row(weight, share), (8, rows)).astype(BF16)
 
 
-def second_sums(keep13, came130, below, above, ups, downs):
-    rows = ups.shape[0]
-    keep1, keep3 = keep13.at[:rows], keep13.at[rows:]
-    came1, came3 = came130.at[:rows], came130.at[rows : 2 * rows]
-    half = rows // 2
-    ups[...] = wide(keep1, came1).astype(BF16)
-    downs[...] = wide(keep3, came3).astype(BF16)
-    ups[:half] = wide(ups.at[:half], below.at[rows:]).astype(BF16)
-    downs[half:] = wide(downs.at[half:], above.at[rows:]).astype(BF16)
-
-
-def down_sums(table, keep0, came20, came130, below, above, weight, gain, weight_part, gain_part):
-    rows = keep0.shape[0]
-    came0 = jnp.concatenate([came20[rows:], came130[2 * rows :]]).astype(F32)
-    share = wide(keep0, below, above) + came0
+def second_sums(keep1, came1, below, keep3, came3, above, ups, downs):
+    half = ups.shape[0] // 2
+    up, down = wide(keep1, came1), wide(keep3, came3)
+    ups[:half] = (up[:half] + below[...].astype(F32)).astype(BF16)
+    ups[half:] = up[half:].astype(BF16)
+    downs[:half] = down[:half].astype(BF16)
+    downs[half:] = (down[half:] + above[...].astype(F32)).astype(BF16)
+
+
+def down_sums(table, keep0, came_low, came_high, below, above, weight, gain, weight_part, gain_part):
+    share = wide(keep0, below, above) + jnp.concatenate([came_low[...], came_high[...]]).astype(F32)
     weight_part[...] = share * gain_column(table, gain, table[0])
     gain_part[...] = gain_row(weight, share)
 
@@ -662,7 +657,7 @@
     up, down = on_blocks(
         "first_sums",
         first_sums,
-        [near0, from_below, back1, from_above, keep2, came20],
+        [near0, (from_below, shard, 0), back1, (from_above, shard, 0), keep2, (came20, shard, 0)],
         [message, message],
     )
     below, above = to_next(up), to_previous(down)
@@ -681,7 +676,8 @@
         "mirror_sums",
         mirror_sums,
         [
-            table, own01, below, from_above, from_below, above, (up_weight, 0), (early, 7), up_gain,
+            table, (own01, shard, 0), (below, shard, 0), (from_above, shard, 1),
+            (own01, shard, 1), (from_below, shard, 1), (above, shard, 0), (up_weight, 0), (early, 7), up_gain,
         ],
         [payload, payload],
     )
@@ -689,7 +685,10 @@
     ups, downs = on_blocks(
         "second_sums",
         second_sums,
-        [keep13, came130, below, above],
+        [
+            (keep13, shard, 0), (came130, shard, 0), (below, half, 2),
+            (keep13, shard, 1), (came130, shard, 1), (above, half, 2),
+        ],
         [part, part],
     )
     last_below, last_above = to_next(ups), to_previous(downs)
@@ -703,7 +702,9 @@
     weight_part, gain_part = on_blocks(
         "down_sums",
         down_sums,
-        [table, keep0, came20, came130, last_below, last_above, (down_weight, 0), down_gain],
+        [
+            table, keep0, (came20, half, 2), (came130, half, 4), last_below, last_above, (down_weight, 0), down_gain,
+        ],
         [jax.ShapeDtypeStruct((shard, kv), F32), jax.ShapeDtypeStruct((1, shard), F32)],
     )
     mirrored0, mirrored1 = hold((mirrored0, mirrored1), weight_part)

time: 170 us -> 168 us (0.988)
  Pallas kernels: 79.3 us -> 77.4 us
    pallas_call x6, Pallas kernels: 18.8 us -> 16.9 us  [on_blocks(): pl.pallas_call(kernel, grid=(1,), in_specs=specs, out_specs=[pl.BlockSpec...]
where the time goes in v4:
time: 168 us; the launch traced here: 167 us
  Pallas kernels  77.4 us (46%)
  starting transfers between devices  41.9 us (25%)
  waiting for transfers between devices  40.1 us (24%)
  other arithmetic  2.4 us (1%)
  matrix products  2.11 us (1%)
  local copies, waits for them, and re-layouts  1.88 us (1%)
    pallas_call x2, Pallas kernels, layer(): pl.pallas_call(kernel, grid=(1,), in_specs=[pl.BlockSpec(memory_space=plt...  22 us
    pallas_call x6, Pallas kernels, on_blocks(): pl.pallas_call(kernel, grid=(1,), in_specs=specs, out_specs=[pl.BlockSpec...  16.9 us
    pallas_call x2, Pallas kernels, products(): pl.pallas_call(kernel, in_specs=[pl.BlockSpec(memory_space=pltpu.SMEM)] +...  15.8 us
    all_to_all x1, waiting for transfers between devices, route_images(): lax.all_to_all(outgoing, 'fsdp', split_axis=0, concat_axis=0, tiled=True)  14 us
    ppermute x6, starting transfers between devices, to_previous(): lax.ppermute(block, 'fsdp', fsdp_route(lambda x, y, core: (x, y - 1, core)))  10.8 us
    ppermute x6, waiting for transfers between devices, to_next(): lax.ppermute(block, 'fsdp', fsdp_route(lambda x, y, core: (x, y + 1, core)))  10.6 us
    ppermute x1, waiting for transfers between devices, move_images(): lax.ppermute(incoming, 'section', [(ring - 1, 0), (end - ring + 1, end)])  9.42 us
    pallas_call x3, Pallas kernels, pack(): pl.pallas_call(kernel, in_specs=[anywhere] * count, out_specs=pl.BlockSpe...  9.34 us
  transfers between devices with their start and end apart: 28, of which 9 were waited for; matrix products, arithmetic and copies ran while one was open for 4% of the time, Pallas kernels for 43%

profile of v4, /device:TPU:1, one launch (start us, length us, event | category | flops | bytes accessed | tf_op | source)
XLA Modules:
  0.0 167.4 jit_solution(10450453263094404739)
XLA Ops:
  0.6 1.5 collective-permute-start
  2.1 2.1 %pack.3.refs_0_.refs_1_ = bf16[2,448,512]{2,1,0:T(8,128)(2,1)} custom-call(bf16[1,448,512]{2,1,0:T(8,128)(2,1)} %weight.1, bf16[1,448,512]{2,1,0:T(8,128)(2,1)} %weight0.1), custom_call_target="tpu_custom_call" | custom-call | flops 1 | bytes 1 | tf_op jit(solution)/shard_map/pack/pallas_call | solution.py:210
  4.2 2.9 %collective-permute-start.3 = (bf16[2,448,512]{2,1,0:T(8,128)(2,1)}, bf16[2,448,512]{2,1,0:T(8,128)(2,1)}, u32[]{:S(2)}, u32[]{:S(2)}) collective-permute-start(bf16[2,448,512]{2,1,0:T(8,128)(2,1)} %pack.3.refs_0_.refs_1_), channel_id=1, source_target_pairs={{0,8},{1,9},{2,10},{3,11},{4,12},{5,13},{6,14},{7,15},{8,0},{9,1},... | collective-permute-start | bytes 2752520 | tf_op jit(solution)/shard_map/ppermute | solution.py:42
  7.1 2.7 %collective-permute-start.2 = (bf16[2,448,512]{2,1,0:T(8,128)(2,1)}, bf16[2,448,512]{2,1,0:T(8,128)(2,1)}, u32[]{:S(2)}, u32[]{:S(2)}) collective-permute-start(bf16[2,448,512]{2,1,0:T(8,128)(2,1)} %pack.3.refs_0_.refs_1_), channel_id=1, source_target_pairs={{0,6},{1,7},{2,0},{3,1},{4,2},{5,3},{6,4},{7,5},{8,14},{9,15},{10,... | collective-permute-start | bytes 2752520 | tf_op jit(solution)/shard_map/ppermute | solution.py:38
  9.9 0.7 fusion.9
  10.6 0.2 convert_reduce_fusion.2
  10.8 0.7 add_multiply_fusion
  11.5 0.1 iota_add_fusion
  11.5 0.1 add.89
  11.6 2.1 %fusion = bf16[16,8,2432]{2,1,0:T(8,128)(2,1)} fusion(bf16[2,64,7168]{2,1,0:T(8,128)(2,1)} %param.15, s32[]{:T(128)S(6)} %select_n.97, s32[]{:T(128)S(6)} %select_n.105, s32[64]{0:T(128)S(1)} %add.89), kind=kOutput, calls=%fused_computation.1 | convolution fusion | flops 40165376 | bytes 934152 | tf_op jit(solution)/shard_map/dot_general | solution.py:544
  13.7 5.1 %all-to-all-start = ((bf16[16,8,2432]{2,1,0:T(8,128)(2,1)}), bf16[16,8,2432]{2,1,0:T(8,128)(2,1)}, u32[]{:S(2)}, u32[]{:S(2)}) async-start(bf16[16,8,2432]{2,1,0:T(8,128)(2,1)} %fusion), calls=%async_computation | async-start | bytes 1245184 | tf_op jit(solution)/shard_map/all_to_all | solution.py:545
  18.8 0.0 copy-start.2
  18.9 7.3 %scale.1 = (bf16[2,1,256,512]{3,2,1,0:T(8,128)(2,1)}, f32[2,256,128]{2,1,0:T(8,128)}) custom-call(bf16[2,1,256,7168]{3,2,1,0:T(8,128)(2,1)} %x_ref.11, bf16[2,1,256,512]{3,2,1,0:T(8,128)(2,1)} %ct_ref.7), custom_call_target="tpu_custom_call" | custom-call | flops 1 | bytes 1 | tf_op jit(solution)/shard_map/scale/pallas_call | solution.py:88
  26.2 14.0 %all-to-all-done = bf16[16,8,2432]{2,1,0:T(8,128)(2,1)} async-done(((bf16[16,8,2432]{2,1,0:T(8,128)(2,1)}), bf16[16,8,2432]{2,1,0:T(8,128)(2,1)}, u32[]{:S(2)}, u32[]{:S(2)}) %all-to-all-start) | async-done | bytes 622624 | tf_op jit(solution)/shard_map/all_to_all | solution.py:545
  40.2 0.1 collective-permute-start.7
  40.3 0.9 collective-permute-start.8
  41.2 0.8 collective-permute-start.6
  42.0 0.6 convert_reduce_fusion
  42.7 0.1 copy.19
  42.8 0.1 reduce.3
  42.9 1.3 collective-permute-start.5
  44.2 1.3 collective-permute-start.4
  46.2 0.1 broadcast_in_dim.55
  46.3 0.1 mul.41
  46.4 0.1 broadcast_in_dim.54
  46.4 0.1 mul.39
  46.6 0.7 concatenate.3.table
  47.3 0.6 fusion.3.perm_ref
  47.9 4.0 %pack.4.refs_0_.weight1 = bf16[8,448,512]{2,1,0:T(8,128)(2,1)} custom-call(bf16[2,448,512]{2,1,0:T(8,128)(2,1)} %pack.3.refs_0_.refs_1_, bf16[2,448,512]{2,1,0:T(8,128)(2,1)} %pack.3.refs_0_.refs_1_, bf16[2,448,512]{2,1,0:T(8,128)(2,1)} %collective-permute-done.2.refs_2_.refs_3_, bf16[2,448,512]{2,1,0:T(8,128)(2,1)} %collective-permute-done.2.refs_2_.refs_3_, ...), custom_call_target="tpu_custom_call" | custom-call | flops 1 | bytes 1 | tf_op jit(solution)/shard_map/pack/pallas_call | solution.py:210
  51.9 9.4 %collective-permute-done.5.im2 = bf16[128,2432]{1,0:T(8,128)(2,1)} collective-permute-done((bf16[128,2432]{1,0:T(8,128)(2,1)}, bf16[128,2432]{1,0:T(8,128)(2,1)}, u32[]{:S(2)}, u32[]{:S(2)}) %collective-permute-start.5) | collective-permute-done | bytes 622624 | tf_op jit(solution)/shard_map/ppermute | solution.py:573
  61.3 6.0 %patch.1 = (bf16[128,7168]{1,0:T(8,128)(2,1)}, bf16[128,4096]{1,0:T(8,128)(2,1)}, bf16[2,1,256,512]{3,2,1,0:T(8,128)(2,1)}, f32[2,256,128]{2,1,0:T(8,128)}) custom-call(s32[17]{0:T(128)} %concatenate.3.table, bf16[2,1,256,512]{3,2,1,0:T(8,128)(2,1)} %ct_ref.7, bf16[128,128]{1,0:T(8,128)(2,1)} %fusion.3.perm_ref, ...), custom_call_target="tpu_custom_call", output_to_operand_aliasing={{2}: (7, {}), {3}: (8, {})} | custom-call | flops 1 | bytes 1 | tf_op jit(solution)/shard_map/patch/pallas_call | solution.py:160
  67.3 2.0 %collective-permute-start.9 = (bf16[128,4096]{1,0:T(8,128)(2,1)}, bf16[128,4096]{1,0:T(8,128)(2,1)}, u32[]{:S(2)}, u32[]{:S(2)}) collective-permute-start(bf16[128,4096]{1,0:T(8,128)(2,1)} %get-tuple-element.81), channel_id=1, source_target_pairs={{0,1},{1,0},{2,3},{3,2},{4,5},{5,4},{6,7},{7,6},{8,9},{9,8},{10,11... | collective-permute-start | bytes 3145736 | tf_op jit(solution)/shard_map/ppermute | solution.py:46
  69.3 0.1 collective-permute-start.10
  69.4 2.1 %halves.1 = (bf16[448,512]{1,0:T(8,128)(2,1)}, bf16[448,512]{1,0:T(8,128)(2,1)}) custom-call(bf16[2,448,512]{2,1,0:T(8,128)(2,1)} %collective-permute-done.8.first.refs_4_.refs_5_, bf16[2,448,512]{2,1,0:T(8,128)(2,1)} %collective-permute-done.7.second.refs_2_.refs_3_), custom_call_target="tpu_custom_call" | custom-call | flops 1 | bytes 1 | tf_op jit(solution)/shard_map/halves/pallas_call | solution.py:327
  71.5 2.7 %collective-permute-start.12 = (bf16[448,512]{1,0:T(8,128)(2,1)}, bf16[448,512]{1,0:T(8,128)(2,1)S(1)}, u32[]{:S(2)}, u32[]{:S(2)}) collective-permute-start(bf16[448,512]{1,0:T(8,128)(2,1)} %get-tuple-element.89), channel_id=1, source_target_pairs={{0,6},{1,7},{2,0},{3,1},{4,2},{5,3},{6,4},{7,5},{8,14},{9,15},{10,... | collective-permute-start | bytes 1376264 | tf_op jit(solution)/shard_map/ppermute | solution.py:38
  74.2 6.4 %products.2 = (bf16[896,512]{1,0:T(8,128)(2,1)}, bf16[896,512]{1,0:T(8,128)(2,1)}, bf16[672,512]{1,0:T(8,128)(2,1)}) custom-call(s32[17]{0:T(128)} %concatenate.3.table, bf16[2,1,256,7168]{3,2,1,0:T(8,128)(2,1)} %x_ref.11, bf16[2,1,256,7168]{3,2,1,0:T(8,128)(2,1)} %collective-permute-done.sibling_x_ref, bf16[128,7168]{1,0:T(8,128)(2,1)} %get-tuple-element.78.head_ref, ...), custom_call_target="tpu_custom_call" | custom-call | flops 1 | bytes 1 | tf_op jit(solution)/shard_map/products/pallas_call | solution.py:295
  80.6 4.1 %collective-permute-done.11.refs_2_ = bf16[448,512]{1,0:T(8,128)(2,1)} collective-permute-done((bf16[448,512]{1,0:T(8,128)(2,1)}, bf16[448,512]{1,0:T(8,128)(2,1)}, u32[]{:S(2)}, u32[]{:S(2)}) %collective-permute-start.11) | collective-permute-done | bytes 458784 | tf_op jit(solution)/shard_map/ppermute | solution.py:34
  84.7 1.3 collective-permute-start.16
  86.0 2.7 %collective-permute-start.14 = (bf16[896,512]{1,0:T(8,128)(2,1)}, bf16[896,512]{1,0:T(8,128)(2,1)}, u32[]{:S(2)}, u32[]{:S(2)}) collective-permute-start(bf16[896,512]{1,0:T(8,128)(2,1)} %get-tuple-element.95), channel_id=1, source_target_pairs={{0,6},{1,7},{2,0},{3,1},{4,2},{5,3},{6,4},{7,5},{8,14},{9,15},{10,... | collective-permute-start | bytes 2752520 | tf_op jit(solution)/shard_map/ppermute | solution.py:38
  88.6 2.7 %collective-permute-start.15 = (bf16[672,512]{1,0:T(8,128)(2,1)}, bf16[672,512]{1,0:T(8,128)(2,1)}, u32[]{:S(2)}, u32[]{:S(2)}) collective-permute-start(bf16[672,512]{1,0:T(8,128)(2,1)} %get-tuple-element.96), channel_id=1, source_target_pairs={{0,8},{1,9},{2,10},{3,11},{4,12},{5,13},{6,14},{7,15},{8,0},{9,1},... | collective-permute-start | bytes 2064392 | tf_op jit(solution)/shard_map/ppermute | solution.py:42
  91.3 3.3 %pack.5.refs_1_ = bf16[6,448,512]{2,1,0:T(8,128)(2,1)} custom-call(bf16[2,448,512]{2,1,0:T(8,128)(2,1)} %collective-permute-done.6.refs_0_.refs_1_, bf16[2,448,512]{2,1,0:T(8,128)(2,1)} %collective-permute-done.6.refs_0_.refs_1_, bf16[2,448,512]{2,1,0:T(8,128)(2,1)} %collective-permute-done.7.second.refs_2_.refs_3_, ...), custom_call_target="tpu_custom_call" | custom-call | flops 1 | bytes 1 | tf_op jit(solution)/shard_map/pack/pallas_call | solution.py:210
  94.6 9.4 %products.3 = (bf16[448,512]{1,0:T(8,128)(2,1)}, bf16[448,512]{1,0:T(8,128)(2,1)}, bf16[448,512]{1,0:T(8,128)(2,1)}, bf16[1120,512]{1,0:T(8,128)(2,1)}, bf16[896...) custom-call(s32[17]{0:T(128)} %concatenate.3.table, bf16[2,1,256,7168]{3,2,1,0:T(8,128)(2,1)} %x_ref.11, ...), custom_call_target="tpu_custom_call" | custom-call | flops 1 | bytes 1 | tf_op jit(solution)/shard_map/products/pallas_call | solution.py:295
  104.0 2.8 %collective-permute-done.15.came2.came_low = bf16[672,512]{1,0:T(8,128)(2,1)} collective-permute-done((bf16[672,512]{1,0:T(8,128)(2,1)}, bf16[672,512]{1,0:T(8,128)(2,1)}, u32[]{:S(2)}, u32[]{:S(2)}) %collective-permute-start.15) | collective-permute-done | bytes 688160 | tf_op jit(solution)/shard_map/ppermute | solution.py:42
  106.8 2.6 %collective-permute-done.13.far0.below1 = bf16[896,512]{1,0:T(8,128)(2,1)} collective-permute-done((bf16[896,512]{1,0:T(8,128)(2,1)}, bf16[896,512]{1,0:T(8,128)(2,1)}, u32[]{:S(2)}, u32[]{:S(2)}) %collective-permute-start.13) | collective-permute-done | bytes 917536 | tf_op jit(solution)/shard_map/ppermute | solution.py:34
  109.4 3.0 %first_sums.1 = (bf16[672,512]{1,0:T(8,128)(2,1)}, bf16[672,512]{1,0:T(8,128)(2,1)}) custom-call(bf16[448,512]{1,0:T(8,128)(2,1)} %get-tuple-element.103.near0, bf16[896,512]{1,0:T(8,128)(2,1)} %collective-permute-done.13.far0.below1, bf16[448,512]{1,0:T(8,128)(2,1)} %get-tuple-element.105.back1, bf16[896,512]{1,0:T(8,128)(2,1)} %collective-permute-done.14.far1.above0, ...), custom_call_target="tpu_custom_call" | custom-call | flops 1 | bytes 1 | tf_op jit(solution)/shard_map/first_sums/pallas_call | solution.py:327
  112.4 0.9 collective-permute-start.20
  113.3 2.7 %collective-permute-start.17 = (bf16[1120,512]{1,0:T(8,128)(2,1)}, bf16[1120,512]{1,0:T(8,128)(2,1)}, u32[]{:S(2)}, u32[]{:S(2)}) collective-permute-start(bf16[1120,512]{1,0:T(8,128)(2,1)} %get-tuple-element.110), channel_id=1, source_target_pairs={{0,8},{1,9},{2,10},{3,11},{4,12},{5,13},{6,14},{7,15},{8,0},{9,1},... | collective-permute-start | bytes 3440648 | tf_op jit(solution)/shard_map/ppermute | solution.py:42
  115.9 2.7 %collective-permute-start.19 = (bf16[672,512]{1,0:T(8,128)(2,1)}, bf16[672,512]{1,0:T(8,128)(2,1)}, u32[]{:S(2)}, u32[]{:S(2)}) collective-permute-start(bf16[672,512]{1,0:T(8,128)(2,1)} %get-tuple-element.111), channel_id=1, source_target_pairs={{0,6},{1,7},{2,0},{3,1},{4,2},{5,3},{6,4},{7,5},{8,14},{9,15},{10,... | collective-permute-start | bytes 2064392 | tf_op jit(solution)/shard_map/ppermute | solution.py:38
  118.6 0.6 collective-permute-start.21
  119.2 1.8 %collective-permute-done.21.refs_5_ = bf16[448,512]{1,0:T(8,128)(2,1)} collective-permute-done((bf16[448,512]{1,0:T(8,128)(2,1)}, bf16[448,512]{1,0:T(8,128)(2,1)}, u32[]{:S(2)}, u32[]{:S(2)}) %collective-permute-start.21) | collective-permute-done | bytes 458784 | tf_op jit(solution)/shard_map/ppermute | solution.py:46
  121.0 11.0 %layer.2 = (bf16[2,1,256,512]{3,2,1,0:T(8,128)(2,1)}, bf16[2,1,256,7168]{3,2,1,0:T(8,128)(2,1)}) custom-call(s32[17]{0:T(128)} %concatenate.3.table, bf16[2,1,256,7168]{3,2,1,0:T(8,128)(2,1)} %x_ref.11, bf16[128,7168]{1,0:T(8,128)(2,1)} %get-tuple-element.78.head_ref, bf16[2,1,256,512]{3,2,1,0:T(8,128)(2,1)} %ct_ref.7, ...), custom_call_target="tpu_custom_call" | custom-call | flops 1 | bytes 1 | tf_op jit(solution)/shard_map/layer/pallas_call | solution.py:485
  132.0 1.5 collective-permute-done.19.above.above1
  133.5 3.1 %collective-permute-done.18.below.below0 = bf16[672,512]{1,0:T(8,128)(2,1)} collective-permute-done((bf16[672,512]{1,0:T(8,128)(2,1)}, bf16[672,512]{1,0:T(8,128)(2,1)}, u32[]{:S(2)}, u32[]{:S(2)}) %collective-permute-start.18) | collective-permute-done | bytes 688160 | tf_op jit(solution)/shard_map/ppermute | solution.py:34
  136.6 3.7 %mirror_sums.1 = (bf16[464,512]{1,0:T(8,128)(2,1)}, bf16[464,512]{1,0:T(8,128)(2,1)}) custom-call(s32[17]{0:T(128)} %concatenate.3.table, bf16[896,512]{1,0:T(8,128)(2,1)} %get-tuple-element.131.own0.own1, bf16[672,512]{1,0:T(8,128)(2,1)} %collective-permute-done.18.below.below0, bf16[896,512]{1,0:T(8,128)(2,1)} %collective-permute-done.14.far1.above0, ...), custom_call_target="tpu_custom_call" | custom-call | flops 1 | bytes 1 | tf_op jit(solution)/shard_map/mirror_sums/pallas_call | solution.py:327
  140.2 3.4 %collective-permute-start.25 = (bf16[464,512]{1,0:T(8,128)(2,1)}, bf16[464,512]{1,0:T(8,128)(2,1)}, u32[]{:S(2)}, u32[]{:S(2)}) collective-permute-start(bf16[464,512]{1,0:T(8,128)(2,1)} %get-tuple-element.132), channel_id=1, source_target_pairs={{0,112},{1,113},{2,114},{3,115},{4,116},{5,117},{6,118},{7,119},{8... | collective-permute-start | bytes 1425416 | tf_op jit(solution)/shard_map/ppermute | solution.py:56
  143.6 0.6 collective-permute-start.26
  144.2 1.7 %collective-permute-start.22 = (bf16[448,512]{1,0:T(8,128)(2,1)S(1)}, bf16[448,512]{1,0:T(8,128)(2,1)}, u32[]{:S(2)}, u32[]{:S(2)}) collective-permute-start(bf16[448,512]{1,0:T(8,128)(2,1)S(1)} %collective-permute-done.12.refs_2_), channel_id=1, source_target_pairs={{0,1},{1,0},{2,3},{3,2},{4,5},{5,4},{6,7},{7,6},{8,9},{9,8},{10,11... | collective-permute-start | bytes 1376264 | tf_op jit(solution)/shard_map/ppermute | solution.py:46
  145.9 2.6 %second_sums.1 = (bf16[448,512]{1,0:T(8,128)(2,1)}, bf16[448,512]{1,0:T(8,128)(2,1)}) custom-call(bf16[896,512]{1,0:T(8,128)(2,1)} %get-tuple-element.93.keep1.keep3, bf16[1120,512]{1,0:T(8,128)(2,1)} %collective-permute-done.17.came1.came3.came_high, bf16[672,512]{1,0:T(8,128)(2,1)} %collective-permute-done.18.below.below0, ...), custom_call_target="tpu_custom_call" | custom-call | flops 1 | bytes 1 | tf_op jit(solution)/shard_map/second_sums/pallas_call | solution.py:327
  148.5 0.0 collective-permute-start.24
  148.5 1.5 collective-permute-start.23
  150.0 11.0 %layer.3 = (bf16[2,1,256,512]{3,2,1,0:T(8,128)(2,1)}, bf16[2,1,256,7168]{3,2,1,0:T(8,128)(2,1)}) custom-call(s32[17]{0:T(128)} %concatenate.3.table, bf16[2,1,256,7168]{3,2,1,0:T(8,128)(2,1)} %x_ref.11, bf16[128,7168]{1,0:T(8,128)(2,1)} %get-tuple-element.78.head_ref, ...), custom_call_target="tpu_custom_call", output_to_operand_aliasing={{0}: (13, {}), {1}: (14, {})} | custom-call | flops 1 | bytes 1 | tf_op jit(solution)/shard_map/layer/pallas_call | solution.py:485
  161.0 0.8 collective-permute-done.23.below
  161.9 3.1 %down_sums.1 = (f32[448,512]{1,0:T(8,128)}, f32[1,448]{1,0:T(1,128)}) custom-call(s32[17]{0:T(128)} %concatenate.3.table, bf16[448,512]{1,0:T(8,128)(2,1)} %get-tuple-element.98.keep0, bf16[672,512]{1,0:T(8,128)(2,1)} %collective-permute-done.15.came2.came_low, bf16[1120,512]{1,0:T(8,128)(2,1)} %collective-permute-done.17.came1.came3.came_high, ...), custom_call_target="tpu_custom_call" | custom-call | flops 1 | bytes 1 | tf_op jit(solution)/shard_map/down_sums/pallas_call | solution.py:327
  164.9 2.5 %last_sums.1 = (f32[1,448,512]{2,1,0:T(8,128)}, f32[1,448]{1,0:T(1,128)}) custom-call(f32[448,512]{1,0:T(8,128)} %get-tuple-element.129.weight_part, f32[1,448]{1,0:T(1,128)} %get-tuple-element.130.gain_part, bf16[464,512]{1,0:T(8,128)(2,1)} %collective-permute-done.25.mirrored0, bf16[464,512]{1,0:T(8,128)(2,1)} %collective-permute-done.26.mirrored1), custom_call_target="tpu_custom_call" | custom-call | flops 1 | bytes 1 | tf_op jit(solution)/shard_map/last_sums/pallas_call | solution.py:327
  (32 shorter events, 0.1 us)
Async XLA Ops:
  0.6 39.5 %collective-permute-start = (bf16[2,1,256,7168]{3,2,1,0:T(8,128)(2,1)}, bf16[2,1,256,7168]{3,2,1,0:T(8,128)(2,1)}, u32[]{:S(2)}, u32[]{:S(2)}) collective-permute-start(bf16[2,1,256,7168]{3,2,1,0:T(8,128)(2,1)} %x_ref.11), channel_id=1, source_target_pairs={{0,1},{1,0},{2,3},{3,2},{4,5},{5,4},{6,7},{7,6},{8,9},{9,8},{10,11... | collective-permute-start | bytes 22020104 | tf_op jit(solution)/shard_map/ppermute | solution.py:46
  4.2 35.9 %collective-permute-start.3 = (bf16[2,448,512]{2,1,0:T(8,128)(2,1)}, bf16[2,448,512]{2,1,0:T(8,128)(2,1)}, u32[]{:S(2)}, u32[]{:S(2)}) collective-permute-start(bf16[2,448,512]{2,1,0:T(8,128)(2,1)} %pack.3.refs_0_.refs_1_), channel_id=1, source_target_pairs={{0,8},{1,9},{2,10},{3,11},{4,12},{5,13},{6,14},{7,15},{8,0},{9,1},... | collective-permute-start | bytes 2752520 | tf_op jit(solution)/shard_map/ppermute | solution.py:42
  7.1 33.0 %collective-permute-start.2 = (bf16[2,448,512]{2,1,0:T(8,128)(2,1)}, bf16[2,448,512]{2,1,0:T(8,128)(2,1)}, u32[]{:S(2)}, u32[]{:S(2)}) collective-permute-start(bf16[2,448,512]{2,1,0:T(8,128)(2,1)} %pack.3.refs_0_.refs_1_), channel_id=1, source_target_pairs={{0,6},{1,7},{2,0},{3,1},{4,2},{5,3},{6,4},{7,5},{8,14},{9,15},{10,... | collective-permute-start | bytes 2752520 | tf_op jit(solution)/shard_map/ppermute | solution.py:38
  9.9 30.3 %collective-permute-start.1 = (bf16[2,448,512]{2,1,0:T(8,128)(2,1)}, bf16[2,448,512]{2,1,0:T(8,128)(2,1)}, u32[]{:S(2)}, u32[]{:S(2)}) collective-permute-start(bf16[2,448,512]{2,1,0:T(8,128)(2,1)} %pack.3.refs_0_.refs_1_), channel_id=1, source_target_pairs={{0,2},{1,3},{2,4},{3,5},{4,6},{5,7},{6,0},{7,1},{8,10},{9,11},{10,... | collective-permute-start | bytes 2752520 | tf_op jit(solution)/shard_map/ppermute | solution.py:34
  13.7 26.4 %all-to-all-start = ((bf16[16,8,2432]{2,1,0:T(8,128)(2,1)}), bf16[16,8,2432]{2,1,0:T(8,128)(2,1)}, u32[]{:S(2)}, u32[]{:S(2)}) async-start(bf16[16,8,2432]{2,1,0:T(8,128)(2,1)} %fusion), calls=%async_computation | async-start | bytes 1245184 | tf_op jit(solution)/shard_map/all_to_all | solution.py:545
  18.8 23.2 %copy-start.1 = (s32[2,16,16]{2,1,0:T(8,128)S(1)}, s32[2,16,16]{2,1,0:T(8,128)}, u32[]{:S(2)}) copy-start(s32[2,16,16]{2,1,0:T(8,128)} %param.16) | copy-start | bytes 6148
  18.8 27.7 %copy-start.2 = (s32[3]{0:T(128)S(1)}, s32[3]{0:T(128)}, u32[]{:S(2)}) copy-start(s32[3]{0:T(128)} %constant.149.clone) | copy-start | bytes 40
  40.2 27.1 %collective-permute-start.7 = (bf16[2,448,512]{2,1,0:T(8,128)(2,1)}, bf16[2,448,512]{2,1,0:T(8,128)(2,1)}, u32[]{:S(2)}, u32[]{:S(2)}) collective-permute-start(bf16[2,448,512]{2,1,0:T(8,128)(2,1)} %collective-permute-done.3.refs_6_.refs_7_), channel_id=1, source_target_pairs={{0,6},{1,7},{2,0},{3,1},{4,2},{5,3},{6,4},{7,5},{8,14},{9,15},{10,... | collective-permute-start | bytes 2752520 | tf_op jit(solution)/shard_map/ppermute | solution.py:38
  40.3 27.0 %collective-permute-start.8 = (bf16[2,448,512]{2,1,0:T(8,128)(2,1)}, bf16[2,448,512]{2,1,0:T(8,128)(2,1)}, u32[]{:S(2)}, u32[]{:S(2)}) collective-permute-start(bf16[2,448,512]{2,1,0:T(8,128)(2,1)} %collective-permute-done.1.refs_4_.refs_5_), channel_id=1, source_target_pairs={{0,8},{1,9},{2,10},{3,11},{4,12},{5,13},{6,14},{7,15},{8,0},{9,1},... | collective-permute-start | bytes 2752520 | tf_op jit(solution)/shard_map/ppermute | solution.py:42
  41.2 26.1 %collective-permute-start.6 = (bf16[2,448,512]{2,1,0:T(8,128)(2,1)}, bf16[2,448,512]{2,1,0:T(8,128)(2,1)}, u32[]{:S(2)}, u32[]{:S(2)}) collective-permute-start(bf16[2,448,512]{2,1,0:T(8,128)(2,1)} %collective-permute-done.1.refs_4_.refs_5_), channel_id=1, source_target_pairs={{0,2},{1,3},{2,4},{3,5},{4,6},{5,7},{6,0},{7,1},{8,10},{9,11},{10,... | collective-permute-start | bytes 2752520 | tf_op jit(solution)/shard_map/ppermute | solution.py:34
  42.9 18.4 %collective-permute-start.5 = (bf16[128,2432]{1,0:T(8,128)(2,1)}, bf16[128,2432]{1,0:T(8,128)(2,1)}, u32[]{:S(2)}, u32[]{:S(2)}) collective-permute-start(bf16[128,2432]{1,0:T(8,128)(2,1)} %bitcast.9.im0), channel_id=1, source_target_pairs={{48,0},{64,112},{49,1},{65,113},{50,2},{66,114},{51,3},{67,115},{5... | collective-permute-start | bytes 1867784 | tf_op jit(solution)/shard_map/ppermute | solution.py:573
  44.2 17.1 %collective-permute-start.4 = (bf16[128,2432]{1,0:T(8,128)(2,1)}, bf16[128,2432]{1,0:T(8,128)(2,1)}, u32[]{:S(2)}, u32[]{:S(2)}) collective-permute-start(bf16[128,2432]{1,0:T(8,128)(2,1)} %bitcast.9.im0), channel_id=1, source_target_pairs={{16,0},{96,112},{17,1},{97,113},{18,2},{98,114},{19,3},{99,115},{2... | collective-permute-start | bytes 1867784 | tf_op jit(solution)/shard_map/ppermute | solution.py:572
  67.3 6.9 %collective-permute-start.9 = (bf16[128,4096]{1,0:T(8,128)(2,1)}, bf16[128,4096]{1,0:T(8,128)(2,1)}, u32[]{:S(2)}, u32[]{:S(2)}) collective-permute-start(bf16[128,4096]{1,0:T(8,128)(2,1)} %get-tuple-element.81), channel_id=1, source_target_pairs={{0,1},{1,0},{2,3},{3,2},{4,5},{5,4},{6,7},{7,6},{8,9},{9,8},{10,11... | collective-permute-start | bytes 3145736 | tf_op jit(solution)/shard_map/ppermute | solution.py:46
  69.3 4.9 %collective-permute-start.10 = (bf16[2,1,256,512]{3,2,1,0:T(8,128)(2,1)}, bf16[2,1,256,512]{3,2,1,0:T(8,128)(2,1)}, u32[]{:S(2)}, u32[]{:S(2)}) collective-permute-start(bf16[2,1,256,512]{3,2,1,0:T(8,128)(2,1)} %get-tuple-element.82.own_ct.scaled_ref), channel_id=1, source_target_pairs={{0,1},{1,0},{2,3},{3,2},{4,5},{5,4},{6,7},{7,6},{8,9},{9,8},{10,11... | collective-permute-start | bytes 1572872 | tf_op jit(solution)/shard_map/ppermute | solution.py:46
  71.5 13.2 %collective-permute-start.11 = (bf16[448,512]{1,0:T(8,128)(2,1)}, bf16[448,512]{1,0:T(8,128)(2,1)}, u32[]{:S(2)}, u32[]{:S(2)}) collective-permute-start(bf16[448,512]{1,0:T(8,128)(2,1)} %get-tuple-element.88), channel_id=1, source_target_pairs={{0,2},{1,3},{2,4},{3,5},{4,6},{5,7},{6,0},{7,1},{8,10},{9,11},{10,... | collective-permute-start | bytes 1376264 | tf_op jit(solution)/shard_map/ppermute | solution.py:34
  71.5 13.2 %collective-permute-start.12 = (bf16[448,512]{1,0:T(8,128)(2,1)}, bf16[448,512]{1,0:T(8,128)(2,1)S(1)}, u32[]{:S(2)}, u32[]{:S(2)}) collective-permute-start(bf16[448,512]{1,0:T(8,128)(2,1)} %get-tuple-element.89), channel_id=1, source_target_pairs={{0,6},{1,7},{2,0},{3,1},{4,2},{5,3},{6,4},{7,5},{8,14},{9,15},{10,... | collective-permute-start | bytes 1376264 | tf_op jit(solution)/shard_map/ppermute | solution.py:38
  84.7 59.5 %copy-start = (bf16[448,512]{1,0:T(8,128)(2,1)}, bf16[448,512]{1,0:T(8,128)(2,1)S(1)}, u32[]{:S(2)}) copy-start(bf16[448,512]{1,0:T(8,128)(2,1)S(1)} %collective-permute-done.12.refs_2_) | copy-start | bytes 1376260
  84.7 24.7 %collective-permute-start.16 = (bf16[8,448,512]{2,1,0:T(8,128)(2,1)}, bf16[8,448,512]{2,1,0:T(8,128)(2,1)}, u32[]{:S(2)}, u32[]{:S(2)}) collective-permute-start(bf16[8,448,512]{2,1,0:T(8,128)(2,1)} %pack.4.refs_0_.weight1), channel_id=1, source_target_pairs={{0,1},{1,0},{2,3},{3,2},{4,5},{5,4},{6,7},{7,6},{8,9},{9,8},{10,11... | collective-permute-start | bytes 11010056 | tf_op jit(solution)/shard_map/ppermute | solution.py:46
  86.0 23.4 %collective-permute-start.13 = (bf16[896,512]{1,0:T(8,128)(2,1)}, bf16[896,512]{1,0:T(8,128)(2,1)}, u32[]{:S(2)}, u32[]{:S(2)}) collective-permute-start(bf16[896,512]{1,0:T(8,128)(2,1)} %get-tuple-element.94), channel_id=1, source_target_pairs={{0,2},{1,3},{2,4},{3,5},{4,6},{5,7},{6,0},{7,1},{8,10},{9,11},{10,... | collective-permute-start | bytes 2752520 | tf_op jit(solution)/shard_map/ppermute | solution.py:34
  86.0 23.4 %collective-permute-start.14 = (bf16[896,512]{1,0:T(8,128)(2,1)}, bf16[896,512]{1,0:T(8,128)(2,1)}, u32[]{:S(2)}, u32[]{:S(2)}) collective-permute-start(bf16[896,512]{1,0:T(8,128)(2,1)} %get-tuple-element.95), channel_id=1, source_target_pairs={{0,6},{1,7},{2,0},{3,1},{4,2},{5,3},{6,4},{7,5},{8,14},{9,15},{10,... | collective-permute-start | bytes 2752520 | tf_op jit(solution)/shard_map/ppermute | solution.py:38
  88.6 18.2 %collective-permute-start.15 = (bf16[672,512]{1,0:T(8,128)(2,1)}, bf16[672,512]{1,0:T(8,128)(2,1)}, u32[]{:S(2)}, u32[]{:S(2)}) collective-permute-start(bf16[672,512]{1,0:T(8,128)(2,1)} %get-tuple-element.96), channel_id=1, source_target_pairs={{0,8},{1,9},{2,10},{3,11},{4,12},{5,13},{6,14},{7,15},{8,0},{9,1},... | collective-permute-start | bytes 2064392 | tf_op jit(solution)/shard_map/ppermute | solution.py:42
  112.4 8.6 %collective-permute-start.20 = (bf16[6,448,512]{2,1,0:T(8,128)(2,1)}, bf16[6,448,512]{2,1,0:T(8,128)(2,1)}, u32[]{:S(2)}, u32[]{:S(2)}) collective-permute-start(bf16[6,448,512]{2,1,0:T(8,128)(2,1)} %pack.5.refs_1_), channel_id=1, source_target_pairs={{0,1},{1,0},{2,3},{3,2},{4,5},{5,4},{6,7},{7,6},{8,9},{9,8},{10,11... | collective-permute-start | bytes 8257544 | tf_op jit(solution)/shard_map/ppermute | solution.py:46
  113.3 32.6 %collective-permute-start.17 = (bf16[1120,512]{1,0:T(8,128)(2,1)}, bf16[1120,512]{1,0:T(8,128)(2,1)}, u32[]{:S(2)}, u32[]{:S(2)}) collective-permute-start(bf16[1120,512]{1,0:T(8,128)(2,1)} %get-tuple-element.110), channel_id=1, source_target_pairs={{0,8},{1,9},{2,10},{3,11},{4,12},{5,13},{6,14},{7,15},{8,0},{9,1},... | collective-permute-start | bytes 3440648 | tf_op jit(solution)/shard_map/ppermute | solution.py:42
  115.9 17.5 %collective-permute-start.19 = (bf16[672,512]{1,0:T(8,128)(2,1)}, bf16[672,512]{1,0:T(8,128)(2,1)}, u32[]{:S(2)}, u32[]{:S(2)}) collective-permute-start(bf16[672,512]{1,0:T(8,128)(2,1)} %get-tuple-element.111), channel_id=1, source_target_pairs={{0,6},{1,7},{2,0},{3,1},{4,2},{5,3},{6,4},{7,5},{8,14},{9,15},{10,... | collective-permute-start | bytes 2064392 | tf_op jit(solution)/shard_map/ppermute | solution.py:38
  118.6 18.0 %collective-permute-start.18 = (bf16[672,512]{1,0:T(8,128)(2,1)}, bf16[672,512]{1,0:T(8,128)(2,1)}, u32[]{:S(2)}, u32[]{:S(2)}) collective-permute-start(bf16[672,512]{1,0:T(8,128)(2,1)} %get-tuple-element.109), channel_id=1, source_target_pairs={{0,2},{1,3},{2,4},{3,5},{4,6},{5,7},{6,0},{7,1},{8,10},{9,11},{10,... | collective-permute-start | bytes 2064392 | tf_op jit(solution)/shard_map/ppermute | solution.py:34
  118.6 2.3 %collective-permute-start.21 = (bf16[448,512]{1,0:T(8,128)(2,1)}, bf16[448,512]{1,0:T(8,128)(2,1)}, u32[]{:S(2)}, u32[]{:S(2)}) collective-permute-start(bf16[448,512]{1,0:T(8,128)(2,1)} %collective-permute-done.11.refs_2_), channel_id=1, source_target_pairs={{0,1},{1,0},{2,3},{3,2},{4,5},{5,4},{6,7},{7,6},{8,9},{9,8},{10,11... | collective-permute-start | bytes 1376264 | tf_op jit(solution)/shard_map/ppermute | solution.py:46
  140.2 24.7 %collective-permute-start.25 = (bf16[464,512]{1,0:T(8,128)(2,1)}, bf16[464,512]{1,0:T(8,128)(2,1)}, u32[]{:S(2)}, u32[]{:S(2)}) collective-permute-start(bf16[464,512]{1,0:T(8,128)(2,1)} %get-tuple-element.132), channel_id=1, source_target_pairs={{0,112},{1,113},{2,114},{3,115},{4,116},{5,117},{6,118},{7,119},{8... | collective-permute-start | bytes 1425416 | tf_op jit(solution)/shard_map/ppermute | solution.py:56
  143.6 21.3 %collective-permute-start.26 = (bf16[464,512]{1,0:T(8,128)(2,1)}, bf16[464,512]{1,0:T(8,128)(2,1)}, u32[]{:S(2)}, u32[]{:S(2)}) collective-permute-start(bf16[464,512]{1,0:T(8,128)(2,1)} %get-tuple-element.133), channel_id=1, source_target_pairs={{0,120},{1,121},{2,122},{3,123},{4,124},{5,125},{6,126},{7,127},{8... | collective-permute-start | bytes 1425416 | tf_op jit(solution)/shard_map/ppermute | solution.py:56
  144.2 5.8 %collective-permute-start.22 = (bf16[448,512]{1,0:T(8,128)(2,1)S(1)}, bf16[448,512]{1,0:T(8,128)(2,1)}, u32[]{:S(2)}, u32[]{:S(2)}) collective-permute-start(bf16[448,512]{1,0:T(8,128)(2,1)S(1)} %collective-permute-done.12.refs_2_), channel_id=1, source_target_pairs={{0,1},{1,0},{2,3},{3,2},{4,5},{5,4},{6,7},{7,6},{8,9},{9,8},{10,11... | collective-permute-start | bytes 1376264 | tf_op jit(solution)/shard_map/ppermute | solution.py:46
  148.5 12.5 %collective-permute-start.24 = (bf16[448,512]{1,0:T(8,128)(2,1)}, bf16[448,512]{1,0:T(8,128)(2,1)}, u32[]{:S(2)}, u32[]{:S(2)}) collective-permute-start(bf16[448,512]{1,0:T(8,128)(2,1)} %get-tuple-element.126), channel_id=1, source_target_pairs={{0,6},{1,7},{2,0},{3,1},{4,2},{5,3},{6,4},{7,5},{8,14},{9,15},{10,... | collective-permute-start | bytes 1376264 | tf_op jit(solution)/shard_map/ppermute | solution.py:38
  148.5 13.4 %collective-permute-start.23 = (bf16[448,512]{1,0:T(8,128)(2,1)}, bf16[448,512]{1,0:T(8,128)(2,1)}, u32[]{:S(2)}, u32[]{:S(2)}) collective-permute-start(bf16[448,512]{1,0:T(8,128)(2,1)} %get-tuple-element.120), channel_id=1, source_target_pairs={{0,2},{1,3},{2,4},{3,5},{4,6},{5,7},{6,0},{7,1},{8,10},{9,11},{10,... | collective-permute-start | bytes 1376264 | tf_op jit(solution)/shard_map/ppermute | solution.py:34

commit v5 on v4

--- a/solution.py
+++ b/solution.py
@@ -607,7 +607,7 @@
     w0 = pack([(down_weight, 0), (up_weight, 0)])
     w3, w1, w4 = to_next(w0), to_previous(w0), to_across(w0)
     scaled_ct, inverse = scale(section_inputs, value_cotangent)
-    w3, w1, w4, incoming = hold((w3, w1, w4, incoming), scaled_ct, sibling_x)
+    w3, w1, w4, incoming, perm, table = hold((w3, w1, w4, incoming, perm, table), scaled_ct, sibling_x)
     images = move_images(incoming)
     w2, w5, w7 = to_next(w3), to_previous(w4), to_across(w3)
     early = pack([(w0, 0), (w0, 1), (w1, 0), (w1, 1), (w3, 0), (w3, 1), (w4, 0), (w4, 1)])

time: 168 us -> 167 us (level)
    all_to_all x1, waiting for transfers between devices: 14 us -> 10.7 us  [route_images(): lax.all_to_all(outgoing, 'fsdp', split_axis=0, concat_axis=0, tiled=True)]
    ppermute x1, waiting for transfers between devices: 9.42 us -> 11.9 us  [move_images(): lax.ppermute(incoming, 'section', [(ring - 1, 0), (end - ring + 1, end)])]
where the time goes in v5:
time: 167 us
  Pallas kernels  77.3 us (46%)
  starting transfers between devices  41.9 us (25%)
  waiting for transfers between devices  39.4 us (24%)
  other arithmetic  2.41 us (1%)
  matrix products  2.11 us (1%)
  local copies, waits for them, and re-layouts  1.89 us (1%)
    pallas_call x2, Pallas kernels, layer(): pl.pallas_call(kernel, grid=(1,), in_specs=[pl.BlockSpec(memory_space=plt...  22 us
    pallas_call x6, Pallas kernels, on_blocks(): pl.pallas_call(kernel, grid=(1,), in_specs=specs, out_specs=[pl.BlockSpec...  16.9 us
    pallas_call x2, Pallas kernels, products(): pl.pallas_call(kernel, in_specs=[pl.BlockSpec(memory_space=pltpu.SMEM)] +...  15.8 us
    ppermute x1, waiting for transfers between devices, move_images(): lax.ppermute(incoming, 'section', [(ring - 1, 0), (end - ring + 1, end)])  11.9 us
    ppermute x6, starting transfers between devices, to_previous(): lax.ppermute(block, 'fsdp', fsdp_route(lambda x, y, core: (x, y - 1, core)))  10.8 us
    all_to_all x1, waiting for transfers between devices, route_images(): lax.all_to_all(outgoing, 'fsdp', split_axis=0, concat_axis=0, tiled=True)  10.7 us
    ppermute x6, waiting for transfers between devices, to_next(): lax.ppermute(block, 'fsdp', fsdp_route(lambda x, y, core: (x, y + 1, core)))  10.6 us
    pallas_call x3, Pallas kernels, pack(): pl.pallas_call(kernel, in_specs=[anywhere] * count, out_specs=pl.BlockSpe...  9.25 us
  transfers between devices with their start and end apart: 28, of which 9 were waited for; matrix products, arithmetic and copies ran while one was open for 4% of the time, Pallas kernels for 43%

profile of v5, /device:TPU:1, one launch (start us, length us, event | category | flops | bytes accessed | tf_op | source)
XLA Modules:
  0.0 166.5 jit_solution(6296990893327423699)
XLA Ops:
  0.6 1.5 collective-permute-start.3
  2.1 2.1 %pack.3.refs_0_.refs_1_ = bf16[2,448,512]{2,1,0:T(8,128)(2,1)} custom-call(bf16[1,448,512]{2,1,0:T(8,128)(2,1)} %weight.1, bf16[1,448,512]{2,1,0:T(8,128)(2,1)} %weight0.1), custom_call_target="tpu_custom_call" | custom-call | flops 1 | bytes 1 | tf_op jit(solution)/shard_map/pack/pallas_call | solution.py:210
  4.2 2.9 %collective-permute-start.2 = (bf16[2,448,512]{2,1,0:T(8,128)(2,1)}, bf16[2,448,512]{2,1,0:T(8,128)(2,1)}, u32[]{:S(2)}, u32[]{:S(2)}) collective-permute-start(bf16[2,448,512]{2,1,0:T(8,128)(2,1)} %pack.3.refs_0_.refs_1_), channel_id=1, source_target_pairs={{0,8},{1,9},{2,10},{3,11},{4,12},{5,13},{6,14},{7,15},{8,0},{9,1},... | collective-permute-start | bytes 2752520 | tf_op jit(solution)/shard_map/ppermute | solution.py:42
  7.2 2.7 %collective-permute-start.1 = (bf16[2,448,512]{2,1,0:T(8,128)(2,1)}, bf16[2,448,512]{2,1,0:T(8,128)(2,1)}, u32[]{:S(2)}, u32[]{:S(2)}) collective-permute-start(bf16[2,448,512]{2,1,0:T(8,128)(2,1)} %pack.3.refs_0_.refs_1_), channel_id=1, source_target_pairs={{0,6},{1,7},{2,0},{3,1},{4,2},{5,3},{6,4},{7,5},{8,14},{9,15},{10,... | collective-permute-start | bytes 2752520 | tf_op jit(solution)/shard_map/ppermute | solution.py:38
  9.9 0.7 fusion.9
  10.6 0.2 convert_reduce_fusion.2
  10.8 0.7 add_multiply_fusion
  11.5 0.1 iota_add_fusion
  11.5 0.1 add.82
  11.6 2.1 %fusion = bf16[16,8,2432]{2,1,0:T(8,128)(2,1)} fusion(bf16[2,64,7168]{2,1,0:T(8,128)(2,1)} %param.15, s32[]{:T(128)S(6)} %select_n.90, s32[]{:T(128)S(6)} %select_n.98, s32[64]{0:T(128)S(1)} %add.82), kind=kOutput, calls=%fused_computation.1 | convolution fusion | flops 40165376 | bytes 934152 | tf_op jit(solution)/shard_map/dot_general | solution.py:544
  13.7 5.1 %all-to-all-start = ((bf16[16,8,2432]{2,1,0:T(8,128)(2,1)}), bf16[16,8,2432]{2,1,0:T(8,128)(2,1)}, u32[]{:S(2)}, u32[]{:S(2)}) async-start(bf16[16,8,2432]{2,1,0:T(8,128)(2,1)} %fusion), calls=%async_computation | async-start | bytes 1245184 | tf_op jit(solution)/shard_map/all_to_all | solution.py:545
  18.9 0.6 convert_reduce_fusion
  19.5 0.1 copy.19
  19.6 0.1 reduce.3
  19.8 7.4 %scale.1 = (bf16[2,1,256,512]{3,2,1,0:T(8,128)(2,1)}, f32[2,256,128]{2,1,0:T(8,128)}) custom-call(bf16[2,1,256,7168]{3,2,1,0:T(8,128)(2,1)} %x_ref.11, bf16[2,1,256,512]{3,2,1,0:T(8,128)(2,1)} %ct_ref.7), custom_call_target="tpu_custom_call" | custom-call | flops 1 | bytes 1 | tf_op jit(solution)/shard_map/scale/pallas_call | solution.py:88
  27.8 0.1 broadcast_in_dim.47
  27.8 0.1 mul.39
  27.9 0.1 broadcast_in_dim.46
  28.0 0.1 mul.37
  28.1 0.7 concatenate.3.table
  28.8 0.6 fusion.3.perm_ref
  29.5 10.7 %all-to-all-done = bf16[16,8,2432]{2,1,0:T(8,128)(2,1)} async-done(((bf16[16,8,2432]{2,1,0:T(8,128)(2,1)}), bf16[16,8,2432]{2,1,0:T(8,128)(2,1)}, u32[]{:S(2)}, u32[]{:S(2)}) %all-to-all-start) | async-done | bytes 622624 | tf_op jit(solution)/shard_map/all_to_all | solution.py:545
  40.2 0.1 collective-permute-start.7
  40.3 0.9 collective-permute-start.8
  41.2 0.8 collective-permute-start.6
  42.0 1.3 collective-permute-start.5
  43.3 1.3 collective-permute-start.4
  44.6 3.9 %pack.4.refs_0_.weight1 = bf16[8,448,512]{2,1,0:T(8,128)(2,1)} custom-call(bf16[2,448,512]{2,1,0:T(8,128)(2,1)} %pack.3.refs_0_.refs_1_, bf16[2,448,512]{2,1,0:T(8,128)(2,1)} %pack.3.refs_0_.refs_1_, bf16[2,448,512]{2,1,0:T(8,128)(2,1)} %collective-permute-done.1.refs_2_.refs_3_, bf16[2,448,512]{2,1,0:T(8,128)(2,1)} %collective-permute-done.1.refs_2_.refs_3_, ...), custom_call_target="tpu_custom_call" | custom-call | flops 1 | bytes 1 | tf_op jit(solution)/shard_map/pack/pallas_call | solution.py:210
  48.5 11.9 %collective-permute-done.5.im2 = bf16[128,2432]{1,0:T(8,128)(2,1)} collective-permute-done((bf16[128,2432]{1,0:T(8,128)(2,1)}, bf16[128,2432]{1,0:T(8,128)(2,1)}, u32[]{:S(2)}, u32[]{:S(2)}) %collective-permute-start.5) | collective-permute-done | bytes 622624 | tf_op jit(solution)/shard_map/ppermute | solution.py:573
  60.4 6.0 %patch.1 = (bf16[128,7168]{1,0:T(8,128)(2,1)}, bf16[128,4096]{1,0:T(8,128)(2,1)}, bf16[2,1,256,512]{3,2,1,0:T(8,128)(2,1)}, f32[2,256,128]{2,1,0:T(8,128)}) custom-call(s32[17]{0:T(128)} %concatenate.3.table, bf16[2,1,256,512]{3,2,1,0:T(8,128)(2,1)} %ct_ref.7, bf16[128,128]{1,0:T(8,128)(2,1)} %fusion.3.perm_ref, ...), custom_call_target="tpu_custom_call", output_to_operand_aliasing={{2}: (7, {}), {3}: (8, {})} | custom-call | flops 1 | bytes 1 | tf_op jit(solution)/shard_map/patch/pallas_call | solution.py:160
  66.4 2.0 %collective-permute-start.9 = (bf16[128,4096]{1,0:T(8,128)(2,1)}, bf16[128,4096]{1,0:T(8,128)(2,1)}, u32[]{:S(2)}, u32[]{:S(2)}) collective-permute-start(bf16[128,4096]{1,0:T(8,128)(2,1)} %get-tuple-element.85), channel_id=1, source_target_pairs={{0,1},{1,0},{2,3},{3,2},{4,5},{5,4},{6,7},{7,6},{8,9},{9,8},{10,11... | collective-permute-start | bytes 3145736 | tf_op jit(solution)/shard_map/ppermute | solution.py:46
  68.4 0.1 collective-permute-start.10
  68.5 2.1 %halves.1 = (bf16[448,512]{1,0:T(8,128)(2,1)}, bf16[448,512]{1,0:T(8,128)(2,1)}) custom-call(bf16[2,448,512]{2,1,0:T(8,128)(2,1)} %collective-permute-done.8.first.refs_4_.refs_5_, bf16[2,448,512]{2,1,0:T(8,128)(2,1)} %collective-permute-done.7.second.refs_2_.refs_3_), custom_call_target="tpu_custom_call" | custom-call | flops 1 | bytes 1 | tf_op jit(solution)/shard_map/halves/pallas_call | solution.py:327
  70.6 0.0 collective-permute-start.11
  70.6 2.7 %collective-permute-start.12 = (bf16[448,512]{1,0:T(8,128)(2,1)}, bf16[448,512]{1,0:T(8,128)(2,1)S(1)}, u32[]{:S(2)}, u32[]{:S(2)}) collective-permute-start(bf16[448,512]{1,0:T(8,128)(2,1)} %get-tuple-element.93), channel_id=1, source_target_pairs={{0,6},{1,7},{2,0},{3,1},{4,2},{5,3},{6,4},{7,5},{8,14},{9,15},{10,... | collective-permute-start | bytes 1376264 | tf_op jit(solution)/shard_map/ppermute | solution.py:38
  73.3 6.4 %products.2 = (bf16[896,512]{1,0:T(8,128)(2,1)}, bf16[896,512]{1,0:T(8,128)(2,1)}, bf16[672,512]{1,0:T(8,128)(2,1)}) custom-call(s32[17]{0:T(128)} %concatenate.3.table, bf16[2,1,256,7168]{3,2,1,0:T(8,128)(2,1)} %x_ref.11, bf16[2,1,256,7168]{3,2,1,0:T(8,128)(2,1)} %collective-permute-done.3.sibling_x_ref, bf16[128,7168]{1,0:T(8,128)(2,1)} %get-tuple-element.82.head_ref, ...), custom_call_target="tpu_custom_call" | custom-call | flops 1 | bytes 1 | tf_op jit(solution)/shard_map/products/pallas_call | solution.py:295
  79.7 4.1 %collective-permute-done.11.refs_2_ = bf16[448,512]{1,0:T(8,128)(2,1)} collective-permute-done((bf16[448,512]{1,0:T(8,128)(2,1)}, bf16[448,512]{1,0:T(8,128)(2,1)}, u32[]{:S(2)}, u32[]{:S(2)}) %collective-permute-start.11) | collective-permute-done | bytes 458784 | tf_op jit(solution)/shard_map/ppermute | solution.py:34
  83.8 1.3 collective-permute-start.16
  85.1 2.7 %collective-permute-start.14 = (bf16[896,512]{1,0:T(8,128)(2,1)}, bf16[896,512]{1,0:T(8,128)(2,1)}, u32[]{:S(2)}, u32[]{:S(2)}) collective-permute-start(bf16[896,512]{1,0:T(8,128)(2,1)} %get-tuple-element.99), channel_id=1, source_target_pairs={{0,6},{1,7},{2,0},{3,1},{4,2},{5,3},{6,4},{7,5},{8,14},{9,15},{10,... | collective-permute-start | bytes 2752520 | tf_op jit(solution)/shard_map/ppermute | solution.py:38
  87.8 2.7 %collective-permute-start.15 = (bf16[672,512]{1,0:T(8,128)(2,1)}, bf16[672,512]{1,0:T(8,128)(2,1)}, u32[]{:S(2)}, u32[]{:S(2)}) collective-permute-start(bf16[672,512]{1,0:T(8,128)(2,1)} %get-tuple-element.100), channel_id=1, source_target_pairs={{0,8},{1,9},{2,10},{3,11},{4,12},{5,13},{6,14},{7,15},{8,0},{9,1},... | collective-permute-start | bytes 2064392 | tf_op jit(solution)/shard_map/ppermute | solution.py:42
  90.4 3.3 %pack.5.refs_1_ = bf16[6,448,512]{2,1,0:T(8,128)(2,1)} custom-call(bf16[2,448,512]{2,1,0:T(8,128)(2,1)} %collective-permute-done.6.refs_0_.refs_1_, bf16[2,448,512]{2,1,0:T(8,128)(2,1)} %collective-permute-done.6.refs_0_.refs_1_, bf16[2,448,512]{2,1,0:T(8,128)(2,1)} %collective-permute-done.7.second.refs_2_.refs_3_, ...), custom_call_target="tpu_custom_call" | custom-call | flops 1 | bytes 1 | tf_op jit(solution)/shard_map/pack/pallas_call | solution.py:210
  93.7 9.4 %products.3 = (bf16[448,512]{1,0:T(8,128)(2,1)}, bf16[448,512]{1,0:T(8,128)(2,1)}, bf16[448,512]{1,0:T(8,128)(2,1)}, bf16[1120,512]{1,0:T(8,128)(2,1)}, bf16[896...) custom-call(s32[17]{0:T(128)} %concatenate.3.table, bf16[2,1,256,7168]{3,2,1,0:T(8,128)(2,1)} %x_ref.11, ...), custom_call_target="tpu_custom_call" | custom-call | flops 1 | bytes 1 | tf_op jit(solution)/shard_map/products/pallas_call | solution.py:295
  103.1 2.8 %collective-permute-done.15.came2.came_low = bf16[672,512]{1,0:T(8,128)(2,1)} collective-permute-done((bf16[672,512]{1,0:T(8,128)(2,1)}, bf16[672,512]{1,0:T(8,128)(2,1)}, u32[]{:S(2)}, u32[]{:S(2)}) %collective-permute-start.15) | collective-permute-done | bytes 688160 | tf_op jit(solution)/shard_map/ppermute | solution.py:42
  105.9 2.6 %collective-permute-done.13.far0.below1 = bf16[896,512]{1,0:T(8,128)(2,1)} collective-permute-done((bf16[896,512]{1,0:T(8,128)(2,1)}, bf16[896,512]{1,0:T(8,128)(2,1)}, u32[]{:S(2)}, u32[]{:S(2)}) %collective-permute-start.13) | collective-permute-done | bytes 917536 | tf_op jit(solution)/shard_map/ppermute | solution.py:34
  108.5 3.0 %first_sums.1 = (bf16[672,512]{1,0:T(8,128)(2,1)}, bf16[672,512]{1,0:T(8,128)(2,1)}) custom-call(bf16[448,512]{1,0:T(8,128)(2,1)} %get-tuple-element.107.near0, bf16[896,512]{1,0:T(8,128)(2,1)} %collective-permute-done.13.far0.below1, bf16[448,512]{1,0:T(8,128)(2,1)} %get-tuple-element.109.back1, bf16[896,512]{1,0:T(8,128)(2,1)} %collective-permute-done.14.far1.above0, ...), custom_call_target="tpu_custom_call" | custom-call | flops 1 | bytes 1 | tf_op jit(solution)/shard_map/first_sums/pallas_call | solution.py:327
  111.5 0.9 collective-permute-start.20
  112.3 2.7 %collective-permute-start.17 = (bf16[1120,512]{1,0:T(8,128)(2,1)}, bf16[1120,512]{1,0:T(8,128)(2,1)}, u32[]{:S(2)}, u32[]{:S(2)}) collective-permute-start(bf16[1120,512]{1,0:T(8,128)(2,1)} %get-tuple-element.114), channel_id=1, source_target_pairs={{0,8},{1,9},{2,10},{3,11},{4,12},{5,13},{6,14},{7,15},{8,0},{9,1},... | collective-permute-start | bytes 3440648 | tf_op jit(solution)/shard_map/ppermute | solution.py:42
  115.0 2.7 %collective-permute-start.19 = (bf16[672,512]{1,0:T(8,128)(2,1)}, bf16[672,512]{1,0:T(8,128)(2,1)}, u32[]{:S(2)}, u32[]{:S(2)}) collective-permute-start(bf16[672,512]{1,0:T(8,128)(2,1)} %get-tuple-element.115), channel_id=1, source_target_pairs={{0,6},{1,7},{2,0},{3,1},{4,2},{5,3},{6,4},{7,5},{8,14},{9,15},{10,... | collective-permute-start | bytes 2064392 | tf_op jit(solution)/shard_map/ppermute | solution.py:38
  117.7 0.6 collective-permute-start.21
  118.3 1.8 %collective-permute-done.21.refs_5_ = bf16[448,512]{1,0:T(8,128)(2,1)} collective-permute-done((bf16[448,512]{1,0:T(8,128)(2,1)}, bf16[448,512]{1,0:T(8,128)(2,1)}, u32[]{:S(2)}, u32[]{:S(2)}) %collective-permute-start.21) | collective-permute-done | bytes 458784 | tf_op jit(solution)/shard_map/ppermute | solution.py:46
  120.0 11.0 %layer.2 = (bf16[2,1,256,512]{3,2,1,0:T(8,128)(2,1)}, bf16[2,1,256,7168]{3,2,1,0:T(8,128)(2,1)}) custom-call(s32[17]{0:T(128)} %concatenate.3.table, bf16[2,1,256,7168]{3,2,1,0:T(8,128)(2,1)} %x_ref.11, bf16[128,7168]{1,0:T(8,128)(2,1)} %get-tuple-element.82.head_ref, bf16[2,1,256,512]{3,2,1,0:T(8,128)(2,1)} %ct_ref.7, ...), custom_call_target="tpu_custom_call" | custom-call | flops 1 | bytes 1 | tf_op jit(solution)/shard_map/layer/pallas_call | solution.py:485
  131.1 1.5 collective-permute-done.19.above.above1
  132.6 3.1 %collective-permute-done.18.below.below0 = bf16[672,512]{1,0:T(8,128)(2,1)} collective-permute-done((bf16[672,512]{1,0:T(8,128)(2,1)}, bf16[672,512]{1,0:T(8,128)(2,1)}, u32[]{:S(2)}, u32[]{:S(2)}) %collective-permute-start.18) | collective-permute-done | bytes 688160 | tf_op jit(solution)/shard_map/ppermute | solution.py:34
  135.6 3.7 %mirror_sums.1 = (bf16[464,512]{1,0:T(8,128)(2,1)}, bf16[464,512]{1,0:T(8,128)(2,1)}) custom-call(s32[17]{0:T(128)} %concatenate.3.table, bf16[896,512]{1,0:T(8,128)(2,1)} %get-tuple-element.135.own0.own1, bf16[672,512]{1,0:T(8,128)(2,1)} %collective-permute-done.18.below.below0, bf16[896,512]{1,0:T(8,128)(2,1)} %collective-permute-done.14.far1.above0, ...), custom_call_target="tpu_custom_call" | custom-call | flops 1 | bytes 1 | tf_op jit(solution)/shard_map/mirror_sums/pallas_call | solution.py:327
  139.3 3.4 %collective-permute-start.25 = (bf16[464,512]{1,0:T(8,128)(2,1)}, bf16[464,512]{1,0:T(8,128)(2,1)}, u32[]{:S(2)}, u32[]{:S(2)}) collective-permute-start(bf16[464,512]{1,0:T(8,128)(2,1)} %get-tuple-element.136), channel_id=1, source_target_pairs={{0,112},{1,113},{2,114},{3,115},{4,116},{5,117},{6,118},{7,119},{8... | collective-permute-start | bytes 1425416 | tf_op jit(solution)/shard_map/ppermute | solution.py:56
  142.7 0.5 collective-permute-start.26
  143.3 1.7 %collective-permute-start.22 = (bf16[448,512]{1,0:T(8,128)(2,1)S(1)}, bf16[448,512]{1,0:T(8,128)(2,1)}, u32[]{:S(2)}, u32[]{:S(2)}) collective-permute-start(bf16[448,512]{1,0:T(8,128)(2,1)S(1)} %collective-permute-done.12.refs_2_), channel_id=1, source_target_pairs={{0,1},{1,0},{2,3},{3,2},{4,5},{5,4},{6,7},{7,6},{8,9},{9,8},{10,11... | collective-permute-start | bytes 1376264 | tf_op jit(solution)/shard_map/ppermute | solution.py:46
  145.0 2.6 %second_sums.1 = (bf16[448,512]{1,0:T(8,128)(2,1)}, bf16[448,512]{1,0:T(8,128)(2,1)}) custom-call(bf16[896,512]{1,0:T(8,128)(2,1)} %get-tuple-element.97.keep1.keep3, bf16[1120,512]{1,0:T(8,128)(2,1)} %collective-permute-done.17.came1.came3.came_high, bf16[672,512]{1,0:T(8,128)(2,1)} %collective-permute-done.18.below.below0, ...), custom_call_target="tpu_custom_call" | custom-call | flops 1 | bytes 1 | tf_op jit(solution)/shard_map/second_sums/pallas_call | solution.py:327
  147.6 0.0 collective-permute-start.24
  147.6 1.5 collective-permute-start.23
  149.1 11.0 %layer.3 = (bf16[2,1,256,512]{3,2,1,0:T(8,128)(2,1)}, bf16[2,1,256,7168]{3,2,1,0:T(8,128)(2,1)}) custom-call(s32[17]{0:T(128)} %concatenate.3.table, bf16[2,1,256,7168]{3,2,1,0:T(8,128)(2,1)} %x_ref.11, bf16[128,7168]{1,0:T(8,128)(2,1)} %get-tuple-element.82.head_ref, ...), custom_call_target="tpu_custom_call", output_to_operand_aliasing={{0}: (13, {}), {1}: (14, {})} | custom-call | flops 1 | bytes 1 | tf_op jit(solution)/shard_map/layer/pallas_call | solution.py:485
  160.1 0.9 collective-permute-done.23.below
  161.0 3.0 %down_sums.1 = (f32[448,512]{1,0:T(8,128)}, f32[1,448]{1,0:T(1,128)}) custom-call(s32[17]{0:T(128)} %concatenate.3.table, bf16[448,512]{1,0:T(8,128)(2,1)} %get-tuple-element.102.keep0, bf16[672,512]{1,0:T(8,128)(2,1)} %collective-permute-done.15.came2.came_low, bf16[1120,512]{1,0:T(8,128)(2,1)} %collective-permute-done.17.came1.came3.came_high, ...), custom_call_target="tpu_custom_call" | custom-call | flops 1 | bytes 1 | tf_op jit(solution)/shard_map/down_sums/pallas_call | solution.py:327
  164.0 2.5 %last_sums.1 = (f32[1,448,512]{2,1,0:T(8,128)}, f32[1,448]{1,0:T(1,128)}) custom-call(f32[448,512]{1,0:T(8,128)} %get-tuple-element.133.weight_part, f32[1,448]{1,0:T(1,128)} %get-tuple-element.134.gain_part, bf16[464,512]{1,0:T(8,128)(2,1)} %collective-permute-done.25.mirrored0, bf16[464,512]{1,0:T(8,128)(2,1)} %collective-permute-done.26.mirrored1), custom_call_target="tpu_custom_call" | custom-call | flops 1 | bytes 1 | tf_op jit(solution)/shard_map/last_sums/pallas_call | solution.py:327
  (32 shorter events, 0.1 us)
Async XLA Ops:
  0.6 18.2 %copy-start.1 = (s32[2,16,16]{2,1,0:T(8,128)S(1)}, s32[2,16,16]{2,1,0:T(8,128)}, u32[]{:S(2)}) copy-start(s32[2,16,16]{2,1,0:T(8,128)} %param.16) | copy-start | bytes 6148
  0.6 39.5 %collective-permute-start.3 = (bf16[2,1,256,7168]{3,2,1,0:T(8,128)(2,1)}, bf16[2,1,256,7168]{3,2,1,0:T(8,128)(2,1)}, u32[]{:S(2)}, u32[]{:S(2)}) collective-permute-start(bf16[2,1,256,7168]{3,2,1,0:T(8,128)(2,1)} %x_ref.11), channel_id=1, source_target_pairs={{0,1},{1,0},{2,3},{3,2},{4,5},{5,4},{6,7},{7,6},{8,9},{9,8},{10,11... | collective-permute-start | bytes 22020104 | tf_op jit(solution)/shard_map/ppermute | solution.py:46
  4.2 35.9 %collective-permute-start.2 = (bf16[2,448,512]{2,1,0:T(8,128)(2,1)}, bf16[2,448,512]{2,1,0:T(8,128)(2,1)}, u32[]{:S(2)}, u32[]{:S(2)}) collective-permute-start(bf16[2,448,512]{2,1,0:T(8,128)(2,1)} %pack.3.refs_0_.refs_1_), channel_id=1, source_target_pairs={{0,8},{1,9},{2,10},{3,11},{4,12},{5,13},{6,14},{7,15},{8,0},{9,1},... | collective-permute-start | bytes 2752520 | tf_op jit(solution)/shard_map/ppermute | solution.py:42
  7.2 33.0 %collective-permute-start.1 = (bf16[2,448,512]{2,1,0:T(8,128)(2,1)}, bf16[2,448,512]{2,1,0:T(8,128)(2,1)}, u32[]{:S(2)}, u32[]{:S(2)}) collective-permute-start(bf16[2,448,512]{2,1,0:T(8,128)(2,1)} %pack.3.refs_0_.refs_1_), channel_id=1, source_target_pairs={{0,6},{1,7},{2,0},{3,1},{4,2},{5,3},{6,4},{7,5},{8,14},{9,15},{10,... | collective-permute-start | bytes 2752520 | tf_op jit(solution)/shard_map/ppermute | solution.py:38
  9.9 30.3 %collective-permute-start = (bf16[2,448,512]{2,1,0:T(8,128)(2,1)}, bf16[2,448,512]{2,1,0:T(8,128)(2,1)}, u32[]{:S(2)}, u32[]{:S(2)}) collective-permute-start(bf16[2,448,512]{2,1,0:T(8,128)(2,1)} %pack.3.refs_0_.refs_1_), channel_id=1, source_target_pairs={{0,2},{1,3},{2,4},{3,5},{4,6},{5,7},{6,0},{7,1},{8,10},{9,11},{10,... | collective-permute-start | bytes 2752520 | tf_op jit(solution)/shard_map/ppermute | solution.py:34
  13.7 26.4 %all-to-all-start = ((bf16[16,8,2432]{2,1,0:T(8,128)(2,1)}), bf16[16,8,2432]{2,1,0:T(8,128)(2,1)}, u32[]{:S(2)}, u32[]{:S(2)}) async-start(bf16[16,8,2432]{2,1,0:T(8,128)(2,1)} %fusion), calls=%async_computation | async-start | bytes 1245184 | tf_op jit(solution)/shard_map/all_to_all | solution.py:545
  19.7 8.4 %copy-start.2 = (s32[3]{0:T(128)S(1)}, s32[3]{0:T(128)}, u32[]{:S(2)}) copy-start(s32[3]{0:T(128)} %constant.149.clone) | copy-start | bytes 40
  40.2 26.2 %collective-permute-start.7 = (bf16[2,448,512]{2,1,0:T(8,128)(2,1)}, bf16[2,448,512]{2,1,0:T(8,128)(2,1)}, u32[]{:S(2)}, u32[]{:S(2)}) collective-permute-start(bf16[2,448,512]{2,1,0:T(8,128)(2,1)} %collective-permute-done.2.refs_6_.refs_7_), channel_id=1, source_target_pairs={{0,6},{1,7},{2,0},{3,1},{4,2},{5,3},{6,4},{7,5},{8,14},{9,15},{10,... | collective-permute-start | bytes 2752520 | tf_op jit(solution)/shard_map/ppermute | solution.py:38
  40.3 26.1 %collective-permute-start.8 = (bf16[2,448,512]{2,1,0:T(8,128)(2,1)}, bf16[2,448,512]{2,1,0:T(8,128)(2,1)}, u32[]{:S(2)}, u32[]{:S(2)}) collective-permute-start(bf16[2,448,512]{2,1,0:T(8,128)(2,1)} %collective-permute-done.refs_4_.refs_5_), channel_id=1, source_target_pairs={{0,8},{1,9},{2,10},{3,11},{4,12},{5,13},{6,14},{7,15},{8,0},{9,1},... | collective-permute-start | bytes 2752520 | tf_op jit(solution)/shard_map/ppermute | solution.py:42
  41.2 25.2 %collective-permute-start.6 = (bf16[2,448,512]{2,1,0:T(8,128)(2,1)}, bf16[2,448,512]{2,1,0:T(8,128)(2,1)}, u32[]{:S(2)}, u32[]{:S(2)}) collective-permute-start(bf16[2,448,512]{2,1,0:T(8,128)(2,1)} %collective-permute-done.refs_4_.refs_5_), channel_id=1, source_target_pairs={{0,2},{1,3},{2,4},{3,5},{4,6},{5,7},{6,0},{7,1},{8,10},{9,11},{10,... | collective-permute-start | bytes 2752520 | tf_op jit(solution)/shard_map/ppermute | solution.py:34
  42.0 18.4 %collective-permute-start.5 = (bf16[128,2432]{1,0:T(8,128)(2,1)}, bf16[128,2432]{1,0:T(8,128)(2,1)}, u32[]{:S(2)}, u32[]{:S(2)}) collective-permute-start(bf16[128,2432]{1,0:T(8,128)(2,1)} %bitcast.3.im0), channel_id=1, source_target_pairs={{48,0},{64,112},{49,1},{65,113},{50,2},{66,114},{51,3},{67,115},{5... | collective-permute-start | bytes 1867784 | tf_op jit(solution)/shard_map/ppermute | solution.py:573
  43.3 17.1 %collective-permute-start.4 = (bf16[128,2432]{1,0:T(8,128)(2,1)}, bf16[128,2432]{1,0:T(8,128)(2,1)}, u32[]{:S(2)}, u32[]{:S(2)}) collective-permute-start(bf16[128,2432]{1,0:T(8,128)(2,1)} %bitcast.3.im0), channel_id=1, source_target_pairs={{16,0},{96,112},{17,1},{97,113},{18,2},{98,114},{19,3},{99,115},{2... | collective-permute-start | bytes 1867784 | tf_op jit(solution)/shard_map/ppermute | solution.py:572
  66.4 6.9 %collective-permute-start.9 = (bf16[128,4096]{1,0:T(8,128)(2,1)}, bf16[128,4096]{1,0:T(8,128)(2,1)}, u32[]{:S(2)}, u32[]{:S(2)}) collective-permute-start(bf16[128,4096]{1,0:T(8,128)(2,1)} %get-tuple-element.85), channel_id=1, source_target_pairs={{0,1},{1,0},{2,3},{3,2},{4,5},{5,4},{6,7},{7,6},{8,9},{9,8},{10,11... | collective-permute-start | bytes 3145736 | tf_op jit(solution)/shard_map/ppermute | solution.py:46
  68.4 4.9 %collective-permute-start.10 = (bf16[2,1,256,512]{3,2,1,0:T(8,128)(2,1)}, bf16[2,1,256,512]{3,2,1,0:T(8,128)(2,1)}, u32[]{:S(2)}, u32[]{:S(2)}) collective-permute-start(bf16[2,1,256,512]{3,2,1,0:T(8,128)(2,1)} %get-tuple-element.86.own_ct.scaled_ref), channel_id=1, source_target_pairs={{0,1},{1,0},{2,3},{3,2},{4,5},{5,4},{6,7},{7,6},{8,9},{9,8},{10,11... | collective-permute-start | bytes 1572872 | tf_op jit(solution)/shard_map/ppermute | solution.py:46
  70.6 13.2 %collective-permute-start.11 = (bf16[448,512]{1,0:T(8,128)(2,1)}, bf16[448,512]{1,0:T(8,128)(2,1)}, u32[]{:S(2)}, u32[]{:S(2)}) collective-permute-start(bf16[448,512]{1,0:T(8,128)(2,1)} %get-tuple-element.92), channel_id=1, source_target_pairs={{0,2},{1,3},{2,4},{3,5},{4,6},{5,7},{6,0},{7,1},{8,10},{9,11},{10,... | collective-permute-start | bytes 1376264 | tf_op jit(solution)/shard_map/ppermute | solution.py:34
  70.6 13.2 %collective-permute-start.12 = (bf16[448,512]{1,0:T(8,128)(2,1)}, bf16[448,512]{1,0:T(8,128)(2,1)S(1)}, u32[]{:S(2)}, u32[]{:S(2)}) collective-permute-start(bf16[448,512]{1,0:T(8,128)(2,1)} %get-tuple-element.93), channel_id=1, source_target_pairs={{0,6},{1,7},{2,0},{3,1},{4,2},{5,3},{6,4},{7,5},{8,14},{9,15},{10,... | collective-permute-start | bytes 1376264 | tf_op jit(solution)/shard_map/ppermute | solution.py:38
  83.8 59.4 %copy-start = (bf16[448,512]{1,0:T(8,128)(2,1)}, bf16[448,512]{1,0:T(8,128)(2,1)S(1)}, u32[]{:S(2)}) copy-start(bf16[448,512]{1,0:T(8,128)(2,1)S(1)} %collective-permute-done.12.refs_2_) | copy-start | bytes 1376260
  83.8 24.7 %collective-permute-start.16 = (bf16[8,448,512]{2,1,0:T(8,128)(2,1)}, bf16[8,448,512]{2,1,0:T(8,128)(2,1)}, u32[]{:S(2)}, u32[]{:S(2)}) collective-permute-start(bf16[8,448,512]{2,1,0:T(8,128)(2,1)} %pack.4.refs_0_.weight1), channel_id=1, source_target_pairs={{0,1},{1,0},{2,3},{3,2},{4,5},{5,4},{6,7},{7,6},{8,9},{9,8},{10,11... | collective-permute-start | bytes 11010056 | tf_op jit(solution)/shard_map/ppermute | solution.py:46
  85.1 23.4 %collective-permute-start.13 = (bf16[896,512]{1,0:T(8,128)(2,1)}, bf16[896,512]{1,0:T(8,128)(2,1)}, u32[]{:S(2)}, u32[]{:S(2)}) collective-permute-start(bf16[896,512]{1,0:T(8,128)(2,1)} %get-tuple-element.98), channel_id=1, source_target_pairs={{0,2},{1,3},{2,4},{3,5},{4,6},{5,7},{6,0},{7,1},{8,10},{9,11},{10,... | collective-permute-start | bytes 2752520 | tf_op jit(solution)/shard_map/ppermute | solution.py:34
  85.1 23.4 %collective-permute-start.14 = (bf16[896,512]{1,0:T(8,128)(2,1)}, bf16[896,512]{1,0:T(8,128)(2,1)}, u32[]{:S(2)}, u32[]{:S(2)}) collective-permute-start(bf16[896,512]{1,0:T(8,128)(2,1)} %get-tuple-element.99), channel_id=1, source_target_pairs={{0,6},{1,7},{2,0},{3,1},{4,2},{5,3},{6,4},{7,5},{8,14},{9,15},{10,... | collective-permute-start | bytes 2752520 | tf_op jit(solution)/shard_map/ppermute | solution.py:38
  87.8 18.2 %collective-permute-start.15 = (bf16[672,512]{1,0:T(8,128)(2,1)}, bf16[672,512]{1,0:T(8,128)(2,1)}, u32[]{:S(2)}, u32[]{:S(2)}) collective-permute-start(bf16[672,512]{1,0:T(8,128)(2,1)} %get-tuple-element.100), channel_id=1, source_target_pairs={{0,8},{1,9},{2,10},{3,11},{4,12},{5,13},{6,14},{7,15},{8,0},{9,1},... | collective-permute-start | bytes 2064392 | tf_op jit(solution)/shard_map/ppermute | solution.py:42
  111.5 8.6 %collective-permute-start.20 = (bf16[6,448,512]{2,1,0:T(8,128)(2,1)}, bf16[6,448,512]{2,1,0:T(8,128)(2,1)}, u32[]{:S(2)}, u32[]{:S(2)}) collective-permute-start(bf16[6,448,512]{2,1,0:T(8,128)(2,1)} %pack.5.refs_1_), channel_id=1, source_target_pairs={{0,1},{1,0},{2,3},{3,2},{4,5},{5,4},{6,7},{7,6},{8,9},{9,8},{10,11... | collective-permute-start | bytes 8257544 | tf_op jit(solution)/shard_map/ppermute | solution.py:46
  112.3 32.6 %collective-permute-start.17 = (bf16[1120,512]{1,0:T(8,128)(2,1)}, bf16[1120,512]{1,0:T(8,128)(2,1)}, u32[]{:S(2)}, u32[]{:S(2)}) collective-permute-start(bf16[1120,512]{1,0:T(8,128)(2,1)} %get-tuple-element.114), channel_id=1, source_target_pairs={{0,8},{1,9},{2,10},{3,11},{4,12},{5,13},{6,14},{7,15},{8,0},{9,1},... | collective-permute-start | bytes 3440648 | tf_op jit(solution)/shard_map/ppermute | solution.py:42
  115.0 17.5 %collective-permute-start.19 = (bf16[672,512]{1,0:T(8,128)(2,1)}, bf16[672,512]{1,0:T(8,128)(2,1)}, u32[]{:S(2)}, u32[]{:S(2)}) collective-permute-start(bf16[672,512]{1,0:T(8,128)(2,1)} %get-tuple-element.115), channel_id=1, source_target_pairs={{0,6},{1,7},{2,0},{3,1},{4,2},{5,3},{6,4},{7,5},{8,14},{9,15},{10,... | collective-permute-start | bytes 2064392 | tf_op jit(solution)/shard_map/ppermute | solution.py:38
  117.7 18.0 %collective-permute-start.18 = (bf16[672,512]{1,0:T(8,128)(2,1)}, bf16[672,512]{1,0:T(8,128)(2,1)}, u32[]{:S(2)}, u32[]{:S(2)}) collective-permute-start(bf16[672,512]{1,0:T(8,128)(2,1)} %get-tuple-element.113), channel_id=1, source_target_pairs={{0,2},{1,3},{2,4},{3,5},{4,6},{5,7},{6,0},{7,1},{8,10},{9,11},{10,... | collective-permute-start | bytes 2064392 | tf_op jit(solution)/shard_map/ppermute | solution.py:34
  117.7 2.3 %collective-permute-start.21 = (bf16[448,512]{1,0:T(8,128)(2,1)}, bf16[448,512]{1,0:T(8,128)(2,1)}, u32[]{:S(2)}, u32[]{:S(2)}) collective-permute-start(bf16[448,512]{1,0:T(8,128)(2,1)} %collective-permute-done.11.refs_2_), channel_id=1, source_target_pairs={{0,1},{1,0},{2,3},{3,2},{4,5},{5,4},{6,7},{7,6},{8,9},{9,8},{10,11... | collective-permute-start | bytes 1376264 | tf_op jit(solution)/shard_map/ppermute | solution.py:46
  139.3 24.7 %collective-permute-start.25 = (bf16[464,512]{1,0:T(8,128)(2,1)}, bf16[464,512]{1,0:T(8,128)(2,1)}, u32[]{:S(2)}, u32[]{:S(2)}) collective-permute-start(bf16[464,512]{1,0:T(8,128)(2,1)} %get-tuple-element.136), channel_id=1, source_target_pairs={{0,112},{1,113},{2,114},{3,115},{4,116},{5,117},{6,118},{7,119},{8... | collective-permute-start | bytes 1425416 | tf_op jit(solution)/shard_map/ppermute | solution.py:56
  142.7 21.3 %collective-permute-start.26 = (bf16[464,512]{1,0:T(8,128)(2,1)}, bf16[464,512]{1,0:T(8,128)(2,1)}, u32[]{:S(2)}, u32[]{:S(2)}) collective-permute-start(bf16[464,512]{1,0:T(8,128)(2,1)} %get-tuple-element.137), channel_id=1, source_target_pairs={{0,120},{1,121},{2,122},{3,123},{4,124},{5,125},{6,126},{7,127},{8... | collective-permute-start | bytes 1425416 | tf_op jit(solution)/shard_map/ppermute | solution.py:56
  143.3 5.8 %collective-permute-start.22 = (bf16[448,512]{1,0:T(8,128)(2,1)S(1)}, bf16[448,512]{1,0:T(8,128)(2,1)}, u32[]{:S(2)}, u32[]{:S(2)}) collective-permute-start(bf16[448,512]{1,0:T(8,128)(2,1)S(1)} %collective-permute-done.12.refs_2_), channel_id=1, source_target_pairs={{0,1},{1,0},{2,3},{3,2},{4,5},{5,4},{6,7},{7,6},{8,9},{9,8},{10,11... | collective-permute-start | bytes 1376264 | tf_op jit(solution)/shard_map/ppermute | solution.py:46
  147.6 12.5 %collective-permute-start.24 = (bf16[448,512]{1,0:T(8,128)(2,1)}, bf16[448,512]{1,0:T(8,128)(2,1)}, u32[]{:S(2)}, u32[]{:S(2)}) collective-permute-start(bf16[448,512]{1,0:T(8,128)(2,1)} %get-tuple-element.130), channel_id=1, source_target_pairs={{0,6},{1,7},{2,0},{3,1},{4,2},{5,3},{6,4},{7,5},{8,14},{9,15},{10,... | collective-permute-start | bytes 1376264 | tf_op jit(solution)/shard_map/ppermute | solution.py:38
  147.6 13.4 %collective-permute-start.23 = (bf16[448,512]{1,0:T(8,128)(2,1)}, bf16[448,512]{1,0:T(8,128)(2,1)}, u32[]{:S(2)}, u32[]{:S(2)}) collective-permute-start(bf16[448,512]{1,0:T(8,128)(2,1)} %get-tuple-element.124), channel_id=1, source_target_pairs={{0,2},{1,3},{2,4},{3,5},{4,6},{5,7},{6,0},{7,1},{8,10},{9,11},{10,... | collective-permute-start | bytes 1376264 | tf_op jit(solution)/shard_map/ppermute | solution.py:34

commit v6 on v5

--- a/solution.py
+++ b/solution.py
@@ -381,8 +381,9 @@
     ):
         share = wide(*sums)
         out[:rows] = (share * gain_column(table, gain, chip)).astype(BF16)
-        out[rows:] = jnp.zeros((out.shape[0] - rows, out.shape[1]), BF16)
-        out[rows : rows + 8, :rows] = jnp.broadcast_to(gain_row(weight, share), (8, rows)).astype(BF16)
+        below = out.shape[0] - rows
+        out[rows:] = jnp.zeros((below, out.shape[1]), BF16)
+        out[rows:, :rows] = jnp.broadcast_to(gain_row(weight, share), (below, rows)).astype(BF16)
 
 
 def second_sums(keep1, came1, below, keep3, came3, above, ups, downs):

time: 167 us -> 167 us (level)
  no operation moved by 1% of the time
where the time goes in v6:
time: 167 us
  Pallas kernels  77.3 us (46%)
  starting transfers between devices  41.9 us (25%)
  waiting for transfers between devices  39.4 us (24%)
  other arithmetic  2.41 us (1%)
  matrix products  2.11 us (1%)
  local copies, waits for them, and re-layouts  1.89 us (1%)
    pallas_call x2, Pallas kernels, layer(): pl.pallas_call(kernel, grid=(1,), in_specs=[pl.BlockSpec(memory_space=plt...  22 us
    pallas_call x6, Pallas kernels, on_blocks(): pl.pallas_call(kernel, grid=(1,), in_specs=specs, out_specs=[pl.BlockSpec...  16.9 us
    pallas_call x2, Pallas kernels, products(): pl.pallas_call(kernel, in_specs=[pl.BlockSpec(memory_space=pltpu.SMEM)] +...  15.8 us
    ppermute x1, waiting for transfers between devices, move_images(): lax.ppermute(incoming, 'section', [(ring - 1, 0), (end - ring + 1, end)])  11.9 us
    ppermute x6, starting transfers between devices, to_previous(): lax.ppermute(block, 'fsdp', fsdp_route(lambda x, y, core: (x, y - 1, core)))  10.8 us
    all_to_all x1, waiting for transfers between devices, route_images(): lax.all_to_all(outgoing, 'fsdp', split_axis=0, concat_axis=0, tiled=True)  10.7 us
    ppermute x6, waiting for transfers between devices, to_next(): lax.ppermute(block, 'fsdp', fsdp_route(lambda x, y, core: (x, y + 1, core)))  10.6 us
    pallas_call x3, Pallas kernels, pack(): pl.pallas_call(kernel, in_specs=[anywhere] * count, out_specs=pl.BlockSpe...  9.25 us
  transfers between devices with their start and end apart: 28, of which 9 were waited for; matrix products, arithmetic and copies ran while one was open for 4% of the time, Pallas kernels for 43%

profile of v6, /device:TPU:1, one launch (start us, length us, event | category | flops | bytes accessed | tf_op | source)
XLA Modules:
  0.0 166.5 jit_solution(17206700441726344939)
XLA Ops:
  0.6 1.5 collective-permute-start.3
  2.1 2.1 %pack.3.refs_0_.refs_1_ = bf16[2,448,512]{2,1,0:T(8,128)(2,1)} custom-call(bf16[1,448,512]{2,1,0:T(8,128)(2,1)} %weight.1, bf16[1,448,512]{2,1,0:T(8,128)(2,1)} %weight0.1), custom_call_target="tpu_custom_call" | custom-call | flops 1 | bytes 1 | tf_op jit(solution)/shard_map/pack/pallas_call | solution.py:210
  4.2 2.9 %collective-permute-start.2 = (bf16[2,448,512]{2,1,0:T(8,128)(2,1)}, bf16[2,448,512]{2,1,0:T(8,128)(2,1)}, u32[]{:S(2)}, u32[]{:S(2)}) collective-permute-start(bf16[2,448,512]{2,1,0:T(8,128)(2,1)} %pack.3.refs_0_.refs_1_), channel_id=1, source_target_pairs={{0,8},{1,9},{2,10},{3,11},{4,12},{5,13},{6,14},{7,15},{8,0},{9,1},... | collective-permute-start | bytes 2752520 | tf_op jit(solution)/shard_map/ppermute | solution.py:42
  7.2 2.7 %collective-permute-start.1 = (bf16[2,448,512]{2,1,0:T(8,128)(2,1)}, bf16[2,448,512]{2,1,0:T(8,128)(2,1)}, u32[]{:S(2)}, u32[]{:S(2)}) collective-permute-start(bf16[2,448,512]{2,1,0:T(8,128)(2,1)} %pack.3.refs_0_.refs_1_), channel_id=1, source_target_pairs={{0,6},{1,7},{2,0},{3,1},{4,2},{5,3},{6,4},{7,5},{8,14},{9,15},{10,... | collective-permute-start | bytes 2752520 | tf_op jit(solution)/shard_map/ppermute | solution.py:38
  9.9 0.7 fusion.9
  10.6 0.2 convert_reduce_fusion.2
  10.8 0.7 add_multiply_fusion
  11.5 0.1 iota_add_fusion
  11.5 0.1 add.82
  11.6 2.1 %fusion = bf16[16,8,2432]{2,1,0:T(8,128)(2,1)} fusion(bf16[2,64,7168]{2,1,0:T(8,128)(2,1)} %param.15, s32[]{:T(128)S(6)} %select_n.90, s32[]{:T(128)S(6)} %select_n.98, s32[64]{0:T(128)S(1)} %add.82), kind=kOutput, calls=%fused_computation.1 | convolution fusion | flops 40165376 | bytes 934152 | tf_op jit(solution)/shard_map/dot_general | solution.py:545
  13.7 5.1 %all-to-all-start = ((bf16[16,8,2432]{2,1,0:T(8,128)(2,1)}), bf16[16,8,2432]{2,1,0:T(8,128)(2,1)}, u32[]{:S(2)}, u32[]{:S(2)}) async-start(bf16[16,8,2432]{2,1,0:T(8,128)(2,1)} %fusion), calls=%async_computation | async-start | bytes 1245184 | tf_op jit(solution)/shard_map/all_to_all | solution.py:546
  18.9 0.6 convert_reduce_fusion
  19.5 0.1 copy.19
  19.6 0.1 reduce.3
  19.8 7.4 %scale.1 = (bf16[2,1,256,512]{3,2,1,0:T(8,128)(2,1)}, f32[2,256,128]{2,1,0:T(8,128)}) custom-call(bf16[2,1,256,7168]{3,2,1,0:T(8,128)(2,1)} %x_ref.11, bf16[2,1,256,512]{3,2,1,0:T(8,128)(2,1)} %ct_ref.7), custom_call_target="tpu_custom_call" | custom-call | flops 1 | bytes 1 | tf_op jit(solution)/shard_map/scale/pallas_call | solution.py:88
  27.8 0.1 broadcast_in_dim.47
  27.8 0.1 mul.39
  27.9 0.1 broadcast_in_dim.46
  28.0 0.1 mul.37
  28.1 0.7 concatenate.3.table
  28.8 0.6 fusion.3.perm_ref
  29.5 10.7 %all-to-all-done = bf16[16,8,2432]{2,1,0:T(8,128)(2,1)} async-done(((bf16[16,8,2432]{2,1,0:T(8,128)(2,1)}), bf16[16,8,2432]{2,1,0:T(8,128)(2,1)}, u32[]{:S(2)}, u32[]{:S(2)}) %all-to-all-start) | async-done | bytes 622624 | tf_op jit(solution)/shard_map/all_to_all | solution.py:546
  40.2 0.1 collective-permute-start.7
  40.3 0.9 collective-permute-start.8
  41.2 0.8 collective-permute-start.6
  42.0 1.3 collective-permute-start.5
  43.3 1.3 collective-permute-start.4
  44.6 3.9 %pack.4.refs_0_.weight1 = bf16[8,448,512]{2,1,0:T(8,128)(2,1)} custom-call(bf16[2,448,512]{2,1,0:T(8,128)(2,1)} %pack.3.refs_0_.refs_1_, bf16[2,448,512]{2,1,0:T(8,128)(2,1)} %pack.3.refs_0_.refs_1_, bf16[2,448,512]{2,1,0:T(8,128)(2,1)} %collective-permute-done.1.refs_2_.refs_3_, bf16[2,448,512]{2,1,0:T(8,128)(2,1)} %collective-permute-done.1.refs_2_.refs_3_, ...), custom_call_target="tpu_custom_call" | custom-call | flops 1 | bytes 1 | tf_op jit(solution)/shard_map/pack/pallas_call | solution.py:210
  48.5 11.9 %collective-permute-done.5.im2 = bf16[128,2432]{1,0:T(8,128)(2,1)} collective-permute-done((bf16[128,2432]{1,0:T(8,128)(2,1)}, bf16[128,2432]{1,0:T(8,128)(2,1)}, u32[]{:S(2)}, u32[]{:S(2)}) %collective-permute-start.5) | collective-permute-done | bytes 622624 | tf_op jit(solution)/shard_map/ppermute | solution.py:574
  60.4 6.0 %patch.1 = (bf16[128,7168]{1,0:T(8,128)(2,1)}, bf16[128,4096]{1,0:T(8,128)(2,1)}, bf16[2,1,256,512]{3,2,1,0:T(8,128)(2,1)}, f32[2,256,128]{2,1,0:T(8,128)}) custom-call(s32[17]{0:T(128)} %concatenate.3.table, bf16[2,1,256,512]{3,2,1,0:T(8,128)(2,1)} %ct_ref.7, bf16[128,128]{1,0:T(8,128)(2,1)} %fusion.3.perm_ref, ...), custom_call_target="tpu_custom_call", output_to_operand_aliasing={{2}: (7, {}), {3}: (8, {})} | custom-call | flops 1 | bytes 1 | tf_op jit(solution)/shard_map/patch/pallas_call | solution.py:160
  66.4 2.0 %collective-permute-start.9 = (bf16[128,4096]{1,0:T(8,128)(2,1)}, bf16[128,4096]{1,0:T(8,128)(2,1)}, u32[]{:S(2)}, u32[]{:S(2)}) collective-permute-start(bf16[128,4096]{1,0:T(8,128)(2,1)} %get-tuple-element.85), channel_id=1, source_target_pairs={{0,1},{1,0},{2,3},{3,2},{4,5},{5,4},{6,7},{7,6},{8,9},{9,8},{10,11... | collective-permute-start | bytes 3145736 | tf_op jit(solution)/shard_map/ppermute | solution.py:46
  68.4 0.1 collective-permute-start.10
  68.5 2.1 %halves.1 = (bf16[448,512]{1,0:T(8,128)(2,1)}, bf16[448,512]{1,0:T(8,128)(2,1)}) custom-call(bf16[2,448,512]{2,1,0:T(8,128)(2,1)} %collective-permute-done.8.first.refs_4_.refs_5_, bf16[2,448,512]{2,1,0:T(8,128)(2,1)} %collective-permute-done.7.second.refs_2_.refs_3_), custom_call_target="tpu_custom_call" | custom-call | flops 1 | bytes 1 | tf_op jit(solution)/shard_map/halves/pallas_call | solution.py:327
  70.6 0.0 collective-permute-start.11
  70.6 2.7 %collective-permute-start.12 = (bf16[448,512]{1,0:T(8,128)(2,1)}, bf16[448,512]{1,0:T(8,128)(2,1)S(1)}, u32[]{:S(2)}, u32[]{:S(2)}) collective-permute-start(bf16[448,512]{1,0:T(8,128)(2,1)} %get-tuple-element.93), channel_id=1, source_target_pairs={{0,6},{1,7},{2,0},{3,1},{4,2},{5,3},{6,4},{7,5},{8,14},{9,15},{10,... | collective-permute-start | bytes 1376264 | tf_op jit(solution)/shard_map/ppermute | solution.py:38
  73.3 6.4 %products.2 = (bf16[896,512]{1,0:T(8,128)(2,1)}, bf16[896,512]{1,0:T(8,128)(2,1)}, bf16[672,512]{1,0:T(8,128)(2,1)}) custom-call(s32[17]{0:T(128)} %concatenate.3.table, bf16[2,1,256,7168]{3,2,1,0:T(8,128)(2,1)} %x_ref.11, bf16[2,1,256,7168]{3,2,1,0:T(8,128)(2,1)} %collective-permute-done.3.sibling_x_ref, bf16[128,7168]{1,0:T(8,128)(2,1)} %get-tuple-element.82.head_ref, ...), custom_call_target="tpu_custom_call" | custom-call | flops 1 | bytes 1 | tf_op jit(solution)/shard_map/products/pallas_call | solution.py:295
  79.7 4.1 %collective-permute-done.11.refs_2_ = bf16[448,512]{1,0:T(8,128)(2,1)} collective-permute-done((bf16[448,512]{1,0:T(8,128)(2,1)}, bf16[448,512]{1,0:T(8,128)(2,1)}, u32[]{:S(2)}, u32[]{:S(2)}) %collective-permute-start.11) | collective-permute-done | bytes 458784 | tf_op jit(solution)/shard_map/ppermute | solution.py:34
  83.8 1.3 collective-permute-start.16
  85.1 2.7 %collective-permute-start.14 = (bf16[896,512]{1,0:T(8,128)(2,1)}, bf16[896,512]{1,0:T(8,128)(2,1)}, u32[]{:S(2)}, u32[]{:S(2)}) collective-permute-start(bf16[896,512]{1,0:T(8,128)(2,1)} %get-tuple-element.99), channel_id=1, source_target_pairs={{0,6},{1,7},{2,0},{3,1},{4,2},{5,3},{6,4},{7,5},{8,14},{9,15},{10,... | collective-permute-start | bytes 2752520 | tf_op jit(solution)/shard_map/ppermute | solution.py:38
  87.8 2.7 %collective-permute-start.15 = (bf16[672,512]{1,0:T(8,128)(2,1)}, bf16[672,512]{1,0:T(8,128)(2,1)}, u32[]{:S(2)}, u32[]{:S(2)}) collective-permute-start(bf16[672,512]{1,0:T(8,128)(2,1)} %get-tuple-element.100), channel_id=1, source_target_pairs={{0,8},{1,9},{2,10},{3,11},{4,12},{5,13},{6,14},{7,15},{8,0},{9,1},... | collective-permute-start | bytes 2064392 | tf_op jit(solution)/shard_map/ppermute | solution.py:42
  90.4 3.3 %pack.5.refs_1_ = bf16[6,448,512]{2,1,0:T(8,128)(2,1)} custom-call(bf16[2,448,512]{2,1,0:T(8,128)(2,1)} %collective-permute-done.6.refs_0_.refs_1_, bf16[2,448,512]{2,1,0:T(8,128)(2,1)} %collective-permute-done.6.refs_0_.refs_1_, bf16[2,448,512]{2,1,0:T(8,128)(2,1)} %collective-permute-done.7.second.refs_2_.refs_3_, ...), custom_call_target="tpu_custom_call" | custom-call | flops 1 | bytes 1 | tf_op jit(solution)/shard_map/pack/pallas_call | solution.py:210
  93.7 9.4 %products.3 = (bf16[448,512]{1,0:T(8,128)(2,1)}, bf16[448,512]{1,0:T(8,128)(2,1)}, bf16[448,512]{1,0:T(8,128)(2,1)}, bf16[1120,512]{1,0:T(8,128)(2,1)}, bf16[896...) custom-call(s32[17]{0:T(128)} %concatenate.3.table, bf16[2,1,256,7168]{3,2,1,0:T(8,128)(2,1)} %x_ref.11, ...), custom_call_target="tpu_custom_call" | custom-call | flops 1 | bytes 1 | tf_op jit(solution)/shard_map/products/pallas_call | solution.py:295
  103.1 2.8 %collective-permute-done.15.came2.came_low = bf16[672,512]{1,0:T(8,128)(2,1)} collective-permute-done((bf16[672,512]{1,0:T(8,128)(2,1)}, bf16[672,512]{1,0:T(8,128)(2,1)}, u32[]{:S(2)}, u32[]{:S(2)}) %collective-permute-start.15) | collective-permute-done | bytes 688160 | tf_op jit(solution)/shard_map/ppermute | solution.py:42
  105.9 2.6 %collective-permute-done.13.far0.below1 = bf16[896,512]{1,0:T(8,128)(2,1)} collective-permute-done((bf16[896,512]{1,0:T(8,128)(2,1)}, bf16[896,512]{1,0:T(8,128)(2,1)}, u32[]{:S(2)}, u32[]{:S(2)}) %collective-permute-start.13) | collective-permute-done | bytes 917536 | tf_op jit(solution)/shard_map/ppermute | solution.py:34
  108.5 3.0 %first_sums.1 = (bf16[672,512]{1,0:T(8,128)(2,1)}, bf16[672,512]{1,0:T(8,128)(2,1)}) custom-call(bf16[448,512]{1,0:T(8,128)(2,1)} %get-tuple-element.107.near0, bf16[896,512]{1,0:T(8,128)(2,1)} %collective-permute-done.13.far0.below1, bf16[448,512]{1,0:T(8,128)(2,1)} %get-tuple-element.109.back1, bf16[896,512]{1,0:T(8,128)(2,1)} %collective-permute-done.14.far1.above0, ...), custom_call_target="tpu_custom_call" | custom-call | flops 1 | bytes 1 | tf_op jit(solution)/shard_map/first_sums/pallas_call | solution.py:327
  111.5 0.9 collective-permute-start.20
  112.3 2.7 %collective-permute-start.17 = (bf16[1120,512]{1,0:T(8,128)(2,1)}, bf16[1120,512]{1,0:T(8,128)(2,1)}, u32[]{:S(2)}, u32[]{:S(2)}) collective-permute-start(bf16[1120,512]{1,0:T(8,128)(2,1)} %get-tuple-element.114), channel_id=1, source_target_pairs={{0,8},{1,9},{2,10},{3,11},{4,12},{5,13},{6,14},{7,15},{8,0},{9,1},... | collective-permute-start | bytes 3440648 | tf_op jit(solution)/shard_map/ppermute | solution.py:42
  115.0 2.7 %collective-permute-start.19 = (bf16[672,512]{1,0:T(8,128)(2,1)}, bf16[672,512]{1,0:T(8,128)(2,1)}, u32[]{:S(2)}, u32[]{:S(2)}) collective-permute-start(bf16[672,512]{1,0:T(8,128)(2,1)} %get-tuple-element.115), channel_id=1, source_target_pairs={{0,6},{1,7},{2,0},{3,1},{4,2},{5,3},{6,4},{7,5},{8,14},{9,15},{10,... | collective-permute-start | bytes 2064392 | tf_op jit(solution)/shard_map/ppermute | solution.py:38
  117.7 0.6 collective-permute-start.21
  118.3 1.8 %collective-permute-done.21.refs_5_ = bf16[448,512]{1,0:T(8,128)(2,1)} collective-permute-done((bf16[448,512]{1,0:T(8,128)(2,1)}, bf16[448,512]{1,0:T(8,128)(2,1)}, u32[]{:S(2)}, u32[]{:S(2)}) %collective-permute-start.21) | collective-permute-done | bytes 458784 | tf_op jit(solution)/shard_map/ppermute | solution.py:46
  120.0 11.0 %layer.2 = (bf16[2,1,256,512]{3,2,1,0:T(8,128)(2,1)}, bf16[2,1,256,7168]{3,2,1,0:T(8,128)(2,1)}) custom-call(s32[17]{0:T(128)} %concatenate.3.table, bf16[2,1,256,7168]{3,2,1,0:T(8,128)(2,1)} %x_ref.11, bf16[128,7168]{1,0:T(8,128)(2,1)} %get-tuple-element.82.head_ref, bf16[2,1,256,512]{3,2,1,0:T(8,128)(2,1)} %ct_ref.7, ...), custom_call_target="tpu_custom_call" | custom-call | flops 1 | bytes 1 | tf_op jit(solution)/shard_map/layer/pallas_call | solution.py:486
  131.1 1.5 collective-permute-done.19.above.above1
  132.6 3.1 %collective-permute-done.18.below.below0 = bf16[672,512]{1,0:T(8,128)(2,1)} collective-permute-done((bf16[672,512]{1,0:T(8,128)(2,1)}, bf16[672,512]{1,0:T(8,128)(2,1)}, u32[]{:S(2)}, u32[]{:S(2)}) %collective-permute-start.18) | collective-permute-done | bytes 688160 | tf_op jit(solution)/shard_map/ppermute | solution.py:34
  135.6 3.7 %mirror_sums.1 = (bf16[464,512]{1,0:T(8,128)(2,1)}, bf16[464,512]{1,0:T(8,128)(2,1)}) custom-call(s32[17]{0:T(128)} %concatenate.3.table, bf16[896,512]{1,0:T(8,128)(2,1)} %get-tuple-element.135.own0.own1, bf16[672,512]{1,0:T(8,128)(2,1)} %collective-permute-done.18.below.below0, bf16[896,512]{1,0:T(8,128)(2,1)} %collective-permute-done.14.far1.above0, ...), custom_call_target="tpu_custom_call" | custom-call | flops 1 | bytes 1 | tf_op jit(solution)/shard_map/mirror_sums/pallas_call | solution.py:327
  139.3 3.4 %collective-permute-start.25 = (bf16[464,512]{1,0:T(8,128)(2,1)}, bf16[464,512]{1,0:T(8,128)(2,1)}, u32[]{:S(2)}, u32[]{:S(2)}) collective-permute-start(bf16[464,512]{1,0:T(8,128)(2,1)} %get-tuple-element.136), channel_id=1, source_target_pairs={{0,112},{1,113},{2,114},{3,115},{4,116},{5,117},{6,118},{7,119},{8... | collective-permute-start | bytes 1425416 | tf_op jit(solution)/shard_map/ppermute | solution.py:56
  142.7 0.5 collective-permute-start.26
  143.3 1.7 %collective-permute-start.22 = (bf16[448,512]{1,0:T(8,128)(2,1)S(1)}, bf16[448,512]{1,0:T(8,128)(2,1)}, u32[]{:S(2)}, u32[]{:S(2)}) collective-permute-start(bf16[448,512]{1,0:T(8,128)(2,1)S(1)} %collective-permute-done.12.refs_2_), channel_id=1, source_target_pairs={{0,1},{1,0},{2,3},{3,2},{4,5},{5,4},{6,7},{7,6},{8,9},{9,8},{10,11... | collective-permute-start | bytes 1376264 | tf_op jit(solution)/shard_map/ppermute | solution.py:46
  145.0 2.6 %second_sums.1 = (bf16[448,512]{1,0:T(8,128)(2,1)}, bf16[448,512]{1,0:T(8,128)(2,1)}) custom-call(bf16[896,512]{1,0:T(8,128)(2,1)} %get-tuple-element.97.keep1.keep3, bf16[1120,512]{1,0:T(8,128)(2,1)} %collective-permute-done.17.came1.came3.came_high, bf16[672,512]{1,0:T(8,128)(2,1)} %collective-permute-done.18.below.below0, ...), custom_call_target="tpu_custom_call" | custom-call | flops 1 | bytes 1 | tf_op jit(solution)/shard_map/second_sums/pallas_call | solution.py:327
  147.6 0.0 collective-permute-start.24
  147.6 1.5 collective-permute-start.23
  149.1 11.0 %layer.3 = (bf16[2,1,256,512]{3,2,1,0:T(8,128)(2,1)}, bf16[2,1,256,7168]{3,2,1,0:T(8,128)(2,1)}) custom-call(s32[17]{0:T(128)} %concatenate.3.table, bf16[2,1,256,7168]{3,2,1,0:T(8,128)(2,1)} %x_ref.11, bf16[128,7168]{1,0:T(8,128)(2,1)} %get-tuple-element.82.head_ref, ...), custom_call_target="tpu_custom_call", output_to_operand_aliasing={{0}: (13, {}), {1}: (14, {})} | custom-call | flops 1 | bytes 1 | tf_op jit(solution)/shard_map/layer/pallas_call | solution.py:486
  160.1 0.9 collective-permute-done.23.below
  161.0 3.0 %down_sums.1 = (f32[448,512]{1,0:T(8,128)}, f32[1,448]{1,0:T(1,128)}) custom-call(s32[17]{0:T(128)} %concatenate.3.table, bf16[448,512]{1,0:T(8,128)(2,1)} %get-tuple-element.102.keep0, bf16[672,512]{1,0:T(8,128)(2,1)} %collective-permute-done.15.came2.came_low, bf16[1120,512]{1,0:T(8,128)(2,1)} %collective-permute-done.17.came1.came3.came_high, ...), custom_call_target="tpu_custom_call" | custom-call | flops 1 | bytes 1 | tf_op jit(solution)/shard_map/down_sums/pallas_call | solution.py:327
  164.0 2.5 %last_sums.1 = (f32[1,448,512]{2,1,0:T(8,128)}, f32[1,448]{1,0:T(1,128)}) custom-call(f32[448,512]{1,0:T(8,128)} %get-tuple-element.133.weight_part, f32[1,448]{1,0:T(1,128)} %get-tuple-element.134.gain_part, bf16[464,512]{1,0:T(8,128)(2,1)} %collective-permute-done.25.mirrored0, bf16[464,512]{1,0:T(8,128)(2,1)} %collective-permute-done.26.mirrored1), custom_call_target="tpu_custom_call" | custom-call | flops 1 | bytes 1 | tf_op jit(solution)/shard_map/last_sums/pallas_call | solution.py:327
  (32 shorter events, 0.1 us)
Async XLA Ops:
  0.6 18.2 %copy-start.1 = (s32[2,16,16]{2,1,0:T(8,128)S(1)}, s32[2,16,16]{2,1,0:T(8,128)}, u32[]{:S(2)}) copy-start(s32[2,16,16]{2,1,0:T(8,128)} %param.16) | copy-start | bytes 6148
  0.6 39.5 %collective-permute-start.3 = (bf16[2,1,256,7168]{3,2,1,0:T(8,128)(2,1)}, bf16[2,1,256,7168]{3,2,1,0:T(8,128)(2,1)}, u32[]{:S(2)}, u32[]{:S(2)}) collective-permute-start(bf16[2,1,256,7168]{3,2,1,0:T(8,128)(2,1)} %x_ref.11), channel_id=1, source_target_pairs={{0,1},{1,0},{2,3},{3,2},{4,5},{5,4},{6,7},{7,6},{8,9},{9,8},{10,11... | collective-permute-start | bytes 22020104 | tf_op jit(solution)/shard_map/ppermute | solution.py:46
  4.2 35.9 %collective-permute-start.2 = (bf16[2,448,512]{2,1,0:T(8,128)(2,1)}, bf16[2,448,512]{2,1,0:T(8,128)(2,1)}, u32[]{:S(2)}, u32[]{:S(2)}) collective-permute-start(bf16[2,448,512]{2,1,0:T(8,128)(2,1)} %pack.3.refs_0_.refs_1_), channel_id=1, source_target_pairs={{0,8},{1,9},{2,10},{3,11},{4,12},{5,13},{6,14},{7,15},{8,0},{9,1},... | collective-permute-start | bytes 2752520 | tf_op jit(solution)/shard_map/ppermute | solution.py:42
  7.2 33.0 %collective-permute-start.1 = (bf16[2,448,512]{2,1,0:T(8,128)(2,1)}, bf16[2,448,512]{2,1,0:T(8,128)(2,1)}, u32[]{:S(2)}, u32[]{:S(2)}) collective-permute-start(bf16[2,448,512]{2,1,0:T(8,128)(2,1)} %pack.3.refs_0_.refs_1_), channel_id=1, source_target_pairs={{0,6},{1,7},{2,0},{3,1},{4,2},{5,3},{6,4},{7,5},{8,14},{9,15},{10,... | collective-permute-start | bytes 2752520 | tf_op jit(solution)/shard_map/ppermute | solution.py:38
  9.9 30.3 %collective-permute-start = (bf16[2,448,512]{2,1,0:T(8,128)(2,1)}, bf16[2,448,512]{2,1,0:T(8,128)(2,1)}, u32[]{:S(2)}, u32[]{:S(2)}) collective-permute-start(bf16[2,448,512]{2,1,0:T(8,128)(2,1)} %pack.3.refs_0_.refs_1_), channel_id=1, source_target_pairs={{0,2},{1,3},{2,4},{3,5},{4,6},{5,7},{6,0},{7,1},{8,10},{9,11},{10,... | collective-permute-start | bytes 2752520 | tf_op jit(solution)/shard_map/ppermute | solution.py:34
  13.7 26.4 %all-to-all-start = ((bf16[16,8,2432]{2,1,0:T(8,128)(2,1)}), bf16[16,8,2432]{2,1,0:T(8,128)(2,1)}, u32[]{:S(2)}, u32[]{:S(2)}) async-start(bf16[16,8,2432]{2,1,0:T(8,128)(2,1)} %fusion), calls=%async_computation | async-start | bytes 1245184 | tf_op jit(solution)/shard_map/all_to_all | solution.py:546
  19.7 8.4 %copy-start.2 = (s32[3]{0:T(128)S(1)}, s32[3]{0:T(128)}, u32[]{:S(2)}) copy-start(s32[3]{0:T(128)} %constant.149.clone) | copy-start | bytes 40
  40.2 26.2 %collective-permute-start.7 = (bf16[2,448,512]{2,1,0:T(8,128)(2,1)}, bf16[2,448,512]{2,1,0:T(8,128)(2,1)}, u32[]{:S(2)}, u32[]{:S(2)}) collective-permute-start(bf16[2,448,512]{2,1,0:T(8,128)(2,1)} %collective-permute-done.2.refs_6_.refs_7_), channel_id=1, source_target_pairs={{0,6},{1,7},{2,0},{3,1},{4,2},{5,3},{6,4},{7,5},{8,14},{9,15},{10,... | collective-permute-start | bytes 2752520 | tf_op jit(solution)/shard_map/ppermute | solution.py:38
  40.3 26.1 %collective-permute-start.8 = (bf16[2,448,512]{2,1,0:T(8,128)(2,1)}, bf16[2,448,512]{2,1,0:T(8,128)(2,1)}, u32[]{:S(2)}, u32[]{:S(2)}) collective-permute-start(bf16[2,448,512]{2,1,0:T(8,128)(2,1)} %collective-permute-done.refs_4_.refs_5_), channel_id=1, source_target_pairs={{0,8},{1,9},{2,10},{3,11},{4,12},{5,13},{6,14},{7,15},{8,0},{9,1},... | collective-permute-start | bytes 2752520 | tf_op jit(solution)/shard_map/ppermute | solution.py:42
  41.2 25.2 %collective-permute-start.6 = (bf16[2,448,512]{2,1,0:T(8,128)(2,1)}, bf16[2,448,512]{2,1,0:T(8,128)(2,1)}, u32[]{:S(2)}, u32[]{:S(2)}) collective-permute-start(bf16[2,448,512]{2,1,0:T(8,128)(2,1)} %collective-permute-done.refs_4_.refs_5_), channel_id=1, source_target_pairs={{0,2},{1,3},{2,4},{3,5},{4,6},{5,7},{6,0},{7,1},{8,10},{9,11},{10,... | collective-permute-start | bytes 2752520 | tf_op jit(solution)/shard_map/ppermute | solution.py:34
  42.0 18.4 %collective-permute-start.5 = (bf16[128,2432]{1,0:T(8,128)(2,1)}, bf16[128,2432]{1,0:T(8,128)(2,1)}, u32[]{:S(2)}, u32[]{:S(2)}) collective-permute-start(bf16[128,2432]{1,0:T(8,128)(2,1)} %bitcast.3.im0), channel_id=1, source_target_pairs={{48,0},{64,112},{49,1},{65,113},{50,2},{66,114},{51,3},{67,115},{5... | collective-permute-start | bytes 1867784 | tf_op jit(solution)/shard_map/ppermute | solution.py:574
  43.3 17.1 %collective-permute-start.4 = (bf16[128,2432]{1,0:T(8,128)(2,1)}, bf16[128,2432]{1,0:T(8,128)(2,1)}, u32[]{:S(2)}, u32[]{:S(2)}) collective-permute-start(bf16[128,2432]{1,0:T(8,128)(2,1)} %bitcast.3.im0), channel_id=1, source_target_pairs={{16,0},{96,112},{17,1},{97,113},{18,2},{98,114},{19,3},{99,115},{2... | collective-permute-start | bytes 1867784 | tf_op jit(solution)/shard_map/ppermute | solution.py:573
  66.4 6.9 %collective-permute-start.9 = (bf16[128,4096]{1,0:T(8,128)(2,1)}, bf16[128,4096]{1,0:T(8,128)(2,1)}, u32[]{:S(2)}, u32[]{:S(2)}) collective-permute-start(bf16[128,4096]{1,0:T(8,128)(2,1)} %get-tuple-element.85), channel_id=1, source_target_pairs={{0,1},{1,0},{2,3},{3,2},{4,5},{5,4},{6,7},{7,6},{8,9},{9,8},{10,11... | collective-permute-start | bytes 3145736 | tf_op jit(solution)/shard_map/ppermute | solution.py:46
  68.4 4.9 %collective-permute-start.10 = (bf16[2,1,256,512]{3,2,1,0:T(8,128)(2,1)}, bf16[2,1,256,512]{3,2,1,0:T(8,128)(2,1)}, u32[]{:S(2)}, u32[]{:S(2)}) collective-permute-start(bf16[2,1,256,512]{3,2,1,0:T(8,128)(2,1)} %get-tuple-element.86.own_ct.scaled_ref), channel_id=1, source_target_pairs={{0,1},{1,0},{2,3},{3,2},{4,5},{5,4},{6,7},{7,6},{8,9},{9,8},{10,11... | collective-permute-start | bytes 1572872 | tf_op jit(solution)/shard_map/ppermute | solution.py:46
  70.6 13.2 %collective-permute-start.11 = (bf16[448,512]{1,0:T(8,128)(2,1)}, bf16[448,512]{1,0:T(8,128)(2,1)}, u32[]{:S(2)}, u32[]{:S(2)}) collective-permute-start(bf16[448,512]{1,0:T(8,128)(2,1)} %get-tuple-element.92), channel_id=1, source_target_pairs={{0,2},{1,3},{2,4},{3,5},{4,6},{5,7},{6,0},{7,1},{8,10},{9,11},{10,... | collective-permute-start | bytes 1376264 | tf_op jit(solution)/shard_map/ppermute | solution.py:34
  70.6 13.2 %collective-permute-start.12 = (bf16[448,512]{1,0:T(8,128)(2,1)}, bf16[448,512]{1,0:T(8,128)(2,1)S(1)}, u32[]{:S(2)}, u32[]{:S(2)}) collective-permute-start(bf16[448,512]{1,0:T(8,128)(2,1)} %get-tuple-element.93), channel_id=1, source_target_pairs={{0,6},{1,7},{2,0},{3,1},{4,2},{5,3},{6,4},{7,5},{8,14},{9,15},{10,... | collective-permute-start | bytes 1376264 | tf_op jit(solution)/shard_map/ppermute | solution.py:38
  83.8 59.4 %copy-start = (bf16[448,512]{1,0:T(8,128)(2,1)}, bf16[448,512]{1,0:T(8,128)(2,1)S(1)}, u32[]{:S(2)}) copy-start(bf16[448,512]{1,0:T(8,128)(2,1)S(1)} %collective-permute-done.12.refs_2_) | copy-start | bytes 1376260
  83.8 24.7 %collective-permute-start.16 = (bf16[8,448,512]{2,1,0:T(8,128)(2,1)}, bf16[8,448,512]{2,1,0:T(8,128)(2,1)}, u32[]{:S(2)}, u32[]{:S(2)}) collective-permute-start(bf16[8,448,512]{2,1,0:T(8,128)(2,1)} %pack.4.refs_0_.weight1), channel_id=1, source_target_pairs={{0,1},{1,0},{2,3},{3,2},{4,5},{5,4},{6,7},{7,6},{8,9},{9,8},{10,11... | collective-permute-start | bytes 11010056 | tf_op jit(solution)/shard_map/ppermute | solution.py:46
  85.1 23.4 %collective-permute-start.13 = (bf16[896,512]{1,0:T(8,128)(2,1)}, bf16[896,512]{1,0:T(8,128)(2,1)}, u32[]{:S(2)}, u32[]{:S(2)}) collective-permute-start(bf16[896,512]{1,0:T(8,128)(2,1)} %get-tuple-element.98), channel_id=1, source_target_pairs={{0,2},{1,3},{2,4},{3,5},{4,6},{5,7},{6,0},{7,1},{8,10},{9,11},{10,... | collective-permute-start | bytes 2752520 | tf_op jit(solution)/shard_map/ppermute | solution.py:34
  85.1 23.4 %collective-permute-start.14 = (bf16[896,512]{1,0:T(8,128)(2,1)}, bf16[896,512]{1,0:T(8,128)(2,1)}, u32[]{:S(2)}, u32[]{:S(2)}) collective-permute-start(bf16[896,512]{1,0:T(8,128)(2,1)} %get-tuple-element.99), channel_id=1, source_target_pairs={{0,6},{1,7},{2,0},{3,1},{4,2},{5,3},{6,4},{7,5},{8,14},{9,15},{10,... | collective-permute-start | bytes 2752520 | tf_op jit(solution)/shard_map/ppermute | solution.py:38
  87.8 18.2 %collective-permute-start.15 = (bf16[672,512]{1,0:T(8,128)(2,1)}, bf16[672,512]{1,0:T(8,128)(2,1)}, u32[]{:S(2)}, u32[]{:S(2)}) collective-permute-start(bf16[672,512]{1,0:T(8,128)(2,1)} %get-tuple-element.100), channel_id=1, source_target_pairs={{0,8},{1,9},{2,10},{3,11},{4,12},{5,13},{6,14},{7,15},{8,0},{9,1},... | collective-permute-start | bytes 2064392 | tf_op jit(solution)/shard_map/ppermute | solution.py:42
  111.5 8.6 %collective-permute-start.20 = (bf16[6,448,512]{2,1,0:T(8,128)(2,1)}, bf16[6,448,512]{2,1,0:T(8,128)(2,1)}, u32[]{:S(2)}, u32[]{:S(2)}) collective-permute-start(bf16[6,448,512]{2,1,0:T(8,128)(2,1)} %pack.5.refs_1_), channel_id=1, source_target_pairs={{0,1},{1,0},{2,3},{3,2},{4,5},{5,4},{6,7},{7,6},{8,9},{9,8},{10,11... | collective-permute-start | bytes 8257544 | tf_op jit(solution)/shard_map/ppermute | solution.py:46
  112.3 32.6 %collective-permute-start.17 = (bf16[1120,512]{1,0:T(8,128)(2,1)}, bf16[1120,512]{1,0:T(8,128)(2,1)}, u32[]{:S(2)}, u32[]{:S(2)}) collective-permute-start(bf16[1120,512]{1,0:T(8,128)(2,1)} %get-tuple-element.114), channel_id=1, source_target_pairs={{0,8},{1,9},{2,10},{3,11},{4,12},{5,13},{6,14},{7,15},{8,0},{9,1},... | collective-permute-start | bytes 3440648 | tf_op jit(solution)/shard_map/ppermute | solution.py:42
  115.0 17.5 %collective-permute-start.19 = (bf16[672,512]{1,0:T(8,128)(2,1)}, bf16[672,512]{1,0:T(8,128)(2,1)}, u32[]{:S(2)}, u32[]{:S(2)}) collective-permute-start(bf16[672,512]{1,0:T(8,128)(2,1)} %get-tuple-element.115), channel_id=1, source_target_pairs={{0,6},{1,7},{2,0},{3,1},{4,2},{5,3},{6,4},{7,5},{8,14},{9,15},{10,... | collective-permute-start | bytes 2064392 | tf_op jit(solution)/shard_map/ppermute | solution.py:38
  117.7 18.0 %collective-permute-start.18 = (bf16[672,512]{1,0:T(8,128)(2,1)}, bf16[672,512]{1,0:T(8,128)(2,1)}, u32[]{:S(2)}, u32[]{:S(2)}) collective-permute-start(bf16[672,512]{1,0:T(8,128)(2,1)} %get-tuple-element.113), channel_id=1, source_target_pairs={{0,2},{1,3},{2,4},{3,5},{4,6},{5,7},{6,0},{7,1},{8,10},{9,11},{10,... | collective-permute-start | bytes 2064392 | tf_op jit(solution)/shard_map/ppermute | solution.py:34
  117.7 2.3 %collective-permute-start.21 = (bf16[448,512]{1,0:T(8,128)(2,1)}, bf16[448,512]{1,0:T(8,128)(2,1)}, u32[]{:S(2)}, u32[]{:S(2)}) collective-permute-start(bf16[448,512]{1,0:T(8,128)(2,1)} %collective-permute-done.11.refs_2_), channel_id=1, source_target_pairs={{0,1},{1,0},{2,3},{3,2},{4,5},{5,4},{6,7},{7,6},{8,9},{9,8},{10,11... | collective-permute-start | bytes 1376264 | tf_op jit(solution)/shard_map/ppermute | solution.py:46
  139.3 24.7 %collective-permute-start.25 = (bf16[464,512]{1,0:T(8,128)(2,1)}, bf16[464,512]{1,0:T(8,128)(2,1)}, u32[]{:S(2)}, u32[]{:S(2)}) collective-permute-start(bf16[464,512]{1,0:T(8,128)(2,1)} %get-tuple-element.136), channel_id=1, source_target_pairs={{0,112},{1,113},{2,114},{3,115},{4,116},{5,117},{6,118},{7,119},{8... | collective-permute-start | bytes 1425416 | tf_op jit(solution)/shard_map/ppermute | solution.py:56
  142.7 21.3 %collective-permute-start.26 = (bf16[464,512]{1,0:T(8,128)(2,1)}, bf16[464,512]{1,0:T(8,128)(2,1)}, u32[]{:S(2)}, u32[]{:S(2)}) collective-permute-start(bf16[464,512]{1,0:T(8,128)(2,1)} %get-tuple-element.137), channel_id=1, source_target_pairs={{0,120},{1,121},{2,122},{3,123},{4,124},{5,125},{6,126},{7,127},{8... | collective-permute-start | bytes 1425416 | tf_op jit(solution)/shard_map/ppermute | solution.py:56
  143.3 5.8 %collective-permute-start.22 = (bf16[448,512]{1,0:T(8,128)(2,1)S(1)}, bf16[448,512]{1,0:T(8,128)(2,1)}, u32[]{:S(2)}, u32[]{:S(2)}) collective-permute-start(bf16[448,512]{1,0:T(8,128)(2,1)S(1)} %collective-permute-done.12.refs_2_), channel_id=1, source_target_pairs={{0,1},{1,0},{2,3},{3,2},{4,5},{5,4},{6,7},{7,6},{8,9},{9,8},{10,11... | collective-permute-start | bytes 1376264 | tf_op jit(solution)/shard_map/ppermute | solution.py:46
  147.6 12.5 %collective-permute-start.24 = (bf16[448,512]{1,0:T(8,128)(2,1)}, bf16[448,512]{1,0:T(8,128)(2,1)}, u32[]{:S(2)}, u32[]{:S(2)}) collective-permute-start(bf16[448,512]{1,0:T(8,128)(2,1)} %get-tuple-element.130), channel_id=1, source_target_pairs={{0,6},{1,7},{2,0},{3,1},{4,2},{5,3},{6,4},{7,5},{8,14},{9,15},{10,... | collective-permute-start | bytes 1376264 | tf_op jit(solution)/shard_map/ppermute | solution.py:38
  147.6 13.4 %collective-permute-start.23 = (bf16[448,512]{1,0:T(8,128)(2,1)}, bf16[448,512]{1,0:T(8,128)(2,1)}, u32[]{:S(2)}, u32[]{:S(2)}) collective-permute-start(bf16[448,512]{1,0:T(8,128)(2,1)} %get-tuple-element.124), channel_id=1, source_target_pairs={{0,2},{1,3},{2,4},{3,5},{4,6},{5,7},{6,0},{7,1},{8,10},{9,11},{10,... | collective-permute-start | bytes 1376264 | tf_op jit(solution)/shard_map/ppermute | solution.py:34
